TPU v7x, 32 devices: a whole 2x2x4 slice. The times are simulated.
32 devices in a mesh: tm: 4 (over y, core), clip: 8 (over z, x).
Axes of the slice: x: 2, y: 2, z: 4, core: 2. Of those that a mesh axis runs over, the one named last changes fastest.
Arguments:
- tokens: bfloat16 [16, 8, 256, 1024], P('tm', 'clip'), may hold values from -6 to 6
- actions: int32 [16, 8], P('tm', 'clip'), may hold values from 0 to 7
- sides: int32 [8], P('clip'), may hold values from 8 to 16, as said below
- action_table: bfloat16 [8, 1024], P(None, ('tm', 'clip')), may hold values from -5 to 5
- norm_gains: bfloat16 [3, 1024], P(None, ('tm', 'clip')), may hold values from 0.099609375 to 1.8984375
- norm_shifts: bfloat16 [3, 1024], P(None, ('tm', 'clip')), may hold values from -1.5 to 1.5
- s_qkv: bfloat16 [1024, 3072], P(('tm', 'clip')), may hold values from -0.1875 to 0.1875
- s_out: bfloat16 [1024, 1024], P(('tm', 'clip')), may hold values from -0.75 to 0.75
- t_qkv: bfloat16 [1024, 3072], P(('tm', 'clip')), may hold values from -0.1875 to 0.1875
- t_out: bfloat16 [1024, 1024], P(('tm', 'clip')), may hold values from -0.375 to 0.375
- w_up: bfloat16 [1024, 4096], P(('tm', 'clip')), may hold values from -0.1875 to 0.1875
- b_up: bfloat16 [4096], P(('tm', 'clip')), may hold values from -2.5 to 2.5
- w_down: bfloat16 [4096, 1024], P(('tm', 'clip')), may hold values from -0.09375 to 0.09375
- b_down: bfloat16 [1024], P(('tm', 'clip')), may hold values from -1.5 to 1.5
- grad_out: bfloat16 [16, 8, 256, 1024], P('tm', 'clip'), may hold values from -6 to 6
Outputs:
- mixed: bfloat16 [16, 8, 256, 1024], P('tm', 'clip')
- input_grad: float32 [16, 8, 256, 1024], P('tm', 'clip')
- grad_actions: float32 [8, 1024], P(None, ('tm', 'clip'))
- grad_gains: float32 [3, 1024], P(None, ('tm', 'clip'))
- grad_shifts: float32 [3, 1024], P(None, ('tm', 'clip'))
- grad_s_qkv: float32 [1024, 3072], P(('tm', 'clip'))
- grad_s_out: float32 [1024, 1024], P(('tm', 'clip'))
- grad_t_qkv: float32 [1024, 3072], P(('tm', 'clip'))
- grad_t_out: float32 [1024, 1024], P(('tm', 'clip'))
- grad_w_up: float32 [1024, 4096], P(('tm', 'clip'))
- grad_b_up: float32 [4096], P(('tm', 'clip'))
- grad_w_down: float32 [4096, 1024], P(('tm', 'clip'))
- grad_b_down: float32 [1024], P(('tm', 'clip'))
Inputs may be any that keep to these rules, and one draw needn't show every extreme that they name: `sides`: each clip's frames are grids of 16 x 16 or of half that side; a smaller grid uses the first slots of each frame. Exactly 2 clips have the smaller side.
All inputs are finite; a program needn't handle non-finite values.
Results may differ from a plain program's by a relative error of at most 0.013.
Values may be sent and summed in bfloat16 or wider, within the bound.
No kernel may reach another device: no remote copies, remote signals or barrier semaphores. Data moves between devices by JAX's collectives and lax.ppermute only.
A program may use at most 448 MiB of HBM per device.

v0:
```python
from functools import partial

import jax
import jax.numpy as jnp
from jax import lax
from jax.sharding import PartitionSpec as P

H = 16
E = 64
ACTIONS = 8
FRAMES = 16


negative = -1e30
highest = lax.Precision.HIGHEST


def layer_norm(inputs, gain, shift):
    average = jnp.mean(inputs, axis=-1, keepdims=True)
    centered = inputs - average
    variance = jnp.mean(centered * centered, axis=-1, keepdims=True)
    return centered * lax.rsqrt(variance + 1e-05) * gain + shift


def matmul(inputs, weight):
    return jnp.dot(inputs, weight, preferred_element_type=jnp.float32)


def transpose_dot(inputs, grads):
    return lax.dot_general(
        inputs, grads, (((0,), (0,)), ((), ())), preferred_element_type=jnp.float32
    )


def backward_dot(grads, weight):
    return lax.dot_general(
        grads, weight, (((1,), (1,)), ((), ())), preferred_element_type=jnp.float32
    )


def on_device(
    tokens,
    actions,
    sides,
    action_table,
    norm_gains,
    norm_shifts,
    s_qkv,
    s_out,
    t_qkv,
    t_out,
    w_up,
    b_up,
    w_down,
    b_down,
    grad_out,
):
    frames_local, clip_count, cell_count, model_width = tokens.shape
    row_count = frames_local * clip_count * cell_count
    factor = E ** (-0.5)
    gathered = (
        lax.all_gather(action_table, ("tm", "clip"), axis=1, tiled=True),
        lax.all_gather(norm_gains, ("tm", "clip"), axis=1, tiled=True),
        lax.all_gather(norm_shifts, ("tm", "clip"), axis=1, tiled=True),
        lax.all_gather(s_qkv, ("tm", "clip"), axis=0, tiled=True),
        lax.all_gather(s_out, ("tm", "clip"), axis=0, tiled=True),
        lax.all_gather(t_qkv, ("tm", "clip"), axis=0, tiled=True),
        lax.all_gather(t_out, ("tm", "clip"), axis=0, tiled=True),
        lax.all_gather(w_up, ("tm", "clip"), axis=0, tiled=True),
        lax.all_gather(b_up, ("tm", "clip"), axis=0, tiled=True),
        lax.all_gather(w_down, ("tm", "clip"), axis=0, tiled=True),
        lax.all_gather(b_down, ("tm", "clip"), axis=0, tiled=True),
    )
    (
        action_rows,
        gain_rows,
        shift_rows,
        sq_full,
        so_full,
        tq_full,
        to_full,
        up_full,
        upb_full,
        down_full,
        downb_full,
    ) = gathered
    gain_rows = gain_rows.astype(jnp.float32)
    shift_rows = shift_rows.astype(jnp.float32)
    onehot = (actions[:, :, None] == jnp.arange(ACTIONS)[None, None, :]).astype(jnp.float32)
    embedded = jnp.einsum("fca,ad->fcd", onehot, action_rows.astype(jnp.float32), precision=highest)
    hidden0 = tokens.astype(jnp.float32) + embedded[:, :, None, :]
    visible = jnp.arange(cell_count)[None, :] < (sides * sides)[:, None]
    mask_rows = visible.astype(jnp.float32)[None, :, :, None]
    normed1, norm_back1 = jax.vjp(layer_norm, hidden0, gain_rows[0], shift_rows[0])
    normed1 = normed1.astype(jnp.bfloat16).reshape(row_count, model_width)
    spatial = (
        matmul(normed1, sq_full)
        .astype(jnp.bfloat16)
        .reshape(frames_local, clip_count, cell_count, 3, H, E)
    )
    sq_part = spatial[:, :, :, 0]
    sk_part = spatial[:, :, :, 1]
    sv_part = spatial[:, :, :, 2]
    scores = (
        jnp.einsum("fcphe,fcqhe->fchpq", sq_part, sk_part, preferred_element_type=jnp.float32)
        * factor
    )
    scores = jnp.where(visible[None, :, None, None, :], scores, negative)
    s_probs = jax.nn.softmax(scores, axis=-1)
    s_probs_low = s_probs.astype(jnp.bfloat16)
    s_mixed = jnp.einsum(
        "fchpq,fcqhe->fcphe", s_probs_low, sv_part, preferred_element_type=jnp.float32
    )
    s_mixed = s_mixed.astype(jnp.bfloat16).reshape(row_count, model_width)
    hidden1 = hidden0 + matmul(s_mixed, so_full).reshape(tokens.shape)
    normed2, norm_back2 = jax.vjp(layer_norm, hidden1, gain_rows[1], shift_rows[1])
    normed2 = normed2.astype(jnp.bfloat16).reshape(row_count, model_width)
    temporal = (
        matmul(normed2, tq_full)
        .astype(jnp.bfloat16)
        .reshape(frames_local, clip_count, cell_count, 3 * model_width)
    )
    query_low = temporal[..., :model_width]
    t_query = query_low.astype(jnp.float32).reshape(frames_local, clip_count, cell_count, H, E)
    key_value = temporal[..., model_width:]
    query_frames = lax.axis_index("tm") * frames_local + jnp.arange(frames_local)
    pieces = lax.all_gather(key_value, "tm", axis=0, tiled=True)
    running_max = jnp.full((clip_count, cell_count, H, frames_local), negative, jnp.float32)
    amount = pieces.shape[0]
    opened = pieces.astype(jnp.float32).reshape(amount, clip_count, cell_count, 2, H, E)
    part_scores = (
        jnp.einsum("fcphe,gcphe->cphfg", t_query, opened[:, :, :, 0], precision=highest) * factor
    )
    allowed = query_frames[:, None] >= jnp.arange(amount)[None, :]
    part_scores = jnp.where(allowed, part_scores, negative)
    new_max = jnp.maximum(running_max, jnp.max(part_scores, axis=-1))
    weights = jnp.where(allowed, jnp.exp(part_scores - new_max[..., None]), 0.0)
    new_sum = jnp.sum(weights, axis=-1)
    new_acc = jnp.einsum("cphfg,gcphe->cphfe", weights, opened[:, :, :, 1], precision=highest)
    t_result = new_acc / new_sum[..., None]
    log_total = new_max + jnp.log(new_sum)
    t_mixed = (
        jnp.transpose(t_result, (3, 0, 1, 2, 4))
        .reshape(row_count, model_width)
        .astype(jnp.bfloat16)
    )
    hidden2 = hidden1 + matmul(t_mixed, to_full).reshape(tokens.shape)
    normed3, norm_back3 = jax.vjp(layer_norm, hidden2, gain_rows[2], shift_rows[2])
    normed3 = normed3.astype(jnp.bfloat16).reshape(row_count, model_width)
    inner = matmul(normed3, up_full) + upb_full.astype(jnp.float32)
    active, gelu_back = jax.vjp(partial(jax.nn.gelu, approximate=False), inner)
    active = active.astype(jnp.bfloat16)
    hidden3 = hidden2 + (matmul(active, down_full) + downb_full.astype(jnp.float32)).reshape(
        tokens.shape
    )
    mixed = (hidden3 * mask_rows).astype(jnp.bfloat16)
    grad3 = grad_out.astype(jnp.float32) * mask_rows
    down_in = grad3.astype(jnp.bfloat16).reshape(row_count, model_width)
    g_w_down = transpose_dot(active, down_in)
    g_b_down = jnp.sum(down_in.astype(jnp.float32), axis=0)
    inner_grad = gelu_back(backward_dot(down_in, down_full))[0].astype(jnp.bfloat16)
    g_w_up = transpose_dot(normed3, inner_grad)
    g_b_up = jnp.sum(inner_grad.astype(jnp.float32), axis=0)
    back3 = norm_back3(backward_dot(inner_grad, up_full).reshape(tokens.shape))
    grad2 = grad3 + back3[0]
    t_in = grad2.astype(jnp.bfloat16).reshape(row_count, model_width)
    g_t_out = transpose_dot(t_mixed, t_in)
    t_mix_grad = jnp.transpose(
        backward_dot(t_in, to_full).reshape(frames_local, clip_count, cell_count, H, E),
        (1, 2, 3, 0, 4),
    )
    t_delta = jnp.sum(t_mix_grad * t_result, axis=-1)
    all_frames = (
        lax.all_gather(key_value, "tm", axis=0, tiled=True)
        .astype(jnp.float32)
        .reshape(FRAMES, clip_count, cell_count, 2, H, E)
    )
    full_scores = (
        jnp.einsum("fcphe,gcphe->cphfg", t_query, all_frames[:, :, :, 0], precision=highest)
        * factor
    )
    allowed = query_frames[:, None] >= jnp.arange(FRAMES)[None, :]
    t_probs = jnp.where(allowed, jnp.exp(full_scores - log_total[..., None]), 0.0)
    prob_grad = jnp.einsum(
        "cphfe,gcphe->cphfg", t_mix_grad, all_frames[:, :, :, 1], precision=highest
    )
    score_grad = t_probs * (prob_grad - t_delta[..., None])
    query_grad = (
        jnp.einsum("cphfg,gcphe->fcphe", score_grad, all_frames[:, :, :, 0], precision=highest)
        * factor
    )
    key_grad = jnp.einsum("cphfg,fcphe->gcphe", score_grad, t_query, precision=highest) * factor
    value_grad = jnp.einsum("cphfg,cphfe->gcphe", t_probs, t_mix_grad, precision=highest)
    kv_terms = jnp.stack((key_grad, value_grad), axis=3).reshape(
        FRAMES, clip_count, cell_count, 2 * model_width
    )
    kv_grad = lax.psum_scatter(
        kv_terms.astype(jnp.bfloat16), "tm", scatter_dimension=0, tiled=True
    ).astype(jnp.float32)
    t_grad = jnp.concatenate(
        (query_grad.reshape(frames_local, clip_count, cell_count, model_width), kv_grad), axis=-1
    )
    t_grad = t_grad.astype(jnp.bfloat16).reshape(row_count, 3 * model_width)
    g_t_qkv = transpose_dot(normed2, t_grad)
    back2 = norm_back2(backward_dot(t_grad, tq_full).reshape(tokens.shape))
    grad1 = grad2 + back2[0]
    s_in = grad1.astype(jnp.bfloat16).reshape(row_count, model_width)
    g_s_out = transpose_dot(s_mixed, s_in)
    mix_grad = (
        backward_dot(s_in, so_full)
        .astype(jnp.bfloat16)
        .reshape(frames_local, clip_count, cell_count, H, E)
    )
    s_prob_grad = jnp.einsum(
        "fcphe,fcqhe->fchpq", mix_grad, sv_part, preferred_element_type=jnp.float32
    )
    s_delta = jnp.sum(s_probs * s_prob_grad, axis=-1, keepdims=True)
    s_score_grad = (s_probs * (s_prob_grad - s_delta)).astype(jnp.bfloat16)
    s_query_grad = (
        jnp.einsum("fchpq,fcqhe->fcphe", s_score_grad, sk_part, preferred_element_type=jnp.float32)
        * factor
    )
    s_key_grad = (
        jnp.einsum("fchpq,fcphe->fcqhe", s_score_grad, sq_part, preferred_element_type=jnp.float32)
        * factor
    )
    s_value_grad = jnp.einsum(
        "fchpq,fcphe->fcqhe", s_probs_low, mix_grad, preferred_element_type=jnp.float32
    )
    s_grad = (
        jnp.stack((s_query_grad, s_key_grad, s_value_grad), axis=3)
        .astype(jnp.bfloat16)
        .reshape(row_count, 3 * model_width)
    )
    g_s_qkv = transpose_dot(normed1, s_grad)
    back1 = norm_back1(backward_dot(s_grad, sq_full).reshape(tokens.shape))
    input_grad = grad1 + back1[0]
    g_actions = jnp.einsum("fca,fcd->ad", onehot, jnp.sum(input_grad, axis=2), precision=highest)
    gain_terms = jnp.stack((back1[1], back2[1], back3[1]), axis=0)
    shift_terms = jnp.stack((back1[2], back2[2], back3[2]), axis=0)
    results = (
        lax.psum_scatter(g_actions, ("tm", "clip"), scatter_dimension=1, tiled=True),
        lax.psum_scatter(gain_terms, ("tm", "clip"), scatter_dimension=1, tiled=True),
        lax.psum_scatter(shift_terms, ("tm", "clip"), scatter_dimension=1, tiled=True),
        lax.psum_scatter(g_s_qkv, ("tm", "clip"), scatter_dimension=0, tiled=True),
        lax.psum_scatter(g_s_out, ("tm", "clip"), scatter_dimension=0, tiled=True),
        lax.psum_scatter(g_t_qkv, ("tm", "clip"), scatter_dimension=0, tiled=True),
        lax.psum_scatter(g_t_out, ("tm", "clip"), scatter_dimension=0, tiled=True),
        lax.psum_scatter(g_w_up, ("tm", "clip"), scatter_dimension=0, tiled=True),
        lax.psum_scatter(g_b_up, ("tm", "clip"), scatter_dimension=0, tiled=True),
        lax.psum_scatter(g_w_down, ("tm", "clip"), scatter_dimension=0, tiled=True),
        lax.psum_scatter(g_b_down, ("tm", "clip"), scatter_dimension=0, tiled=True),
    )
    return (
        mixed,
        input_grad,
        results[0],
        results[1],
        results[2],
        results[3],
        results[4],
        results[5],
        results[6],
        results[7],
        results[8],
        results[9],
        results[10],
    )


def solution(mesh):
    placed = (
        P("tm", "clip", None, None),
        P("tm", "clip"),
        P("clip"),
        P(None, ("tm", "clip")),
        P(None, ("tm", "clip")),
        P(None, ("tm", "clip")),
        P(("tm", "clip"), None),
        P(("tm", "clip"), None),
        P(("tm", "clip"), None),
        P(("tm", "clip"), None),
        P(("tm", "clip"), None),
        P(("tm", "clip")),
        P(("tm", "clip"), None),
        P(("tm", "clip")),
        P("tm", "clip", None, None),
    )
    return jax.shard_map(
        on_device,
        mesh=mesh,
        in_specs=placed,
        out_specs=(
            P("tm", "clip", None, None),
            P("tm", "clip", None, None),
            P(None, ("tm", "clip")),
            P(None, ("tm", "clip")),
            P(None, ("tm", "clip")),
            P(("tm", "clip"), None),
            P(("tm", "clip"), None),
            P(("tm", "clip"), None),
            P(("tm", "clip"), None),
            P(("tm", "clip"), None),
            P(("tm", "clip")),
            P(("tm", "clip"), None),
            P(("tm", "clip")),
        ),
        check_vma=False,
    )
```

profile of v0, /device:TPU:1, one launch (start us, length us, event | category | flops | bytes accessed | tf_op | source)
XLA Modules:
  0.0 2971.1 jit_solution(17290096965667128873)
XLA Ops:
  10.1 62.5 %all-gather.1 = bf16[32,32,3]{1,2,0:T(4,128)(2,1)S(1)} all-gather(bf16[1,32,3]{1,2,0:T(4,128)(2,1)} %bitcast.337), channel_id=1, replica_groups=mesh['tm'=4,'clip'=8] {'tm','clip'}, dimensions={0}, use_global_device_ids=true | all-gather | bytes 6336 | tf_op jit(solution)/shard_map/all_gather | solution.py:63
  72.7 63.0 %all-gather.2 = bf16[32,32,3]{1,2,0:T(4,128)(2,1)S(1)} all-gather(bf16[1,32,3]{1,2,0:T(4,128)(2,1)} %bitcast.338), channel_id=1, replica_groups=mesh['tm'=4,'clip'=8] {'tm','clip'}, dimensions={0}, use_global_device_ids=true | all-gather | bytes 6336 | tf_op jit(solution)/shard_map/all_gather | solution.py:64
  135.8 66.4 %all-gather = bf16[32,32,8]{1,2,0:T(8,128)(2,1)S(1)} all-gather(bf16[1,32,8]{1,2,0:T(8,128)(2,1)} %bitcast.336), channel_id=1, replica_groups=mesh['tm'=4,'clip'=8] {'tm','clip'}, dimensions={0}, use_global_device_ids=true | all-gather | bytes 16896 | tf_op jit(solution)/shard_map/all_gather | solution.py:62
  327.9 46.1 %all-reduce = bf16[1024]{0:T(1024)(128)(2,1)S(1)} all-reduce(bf16[1024]{0:T(1024)(128)(2,1)S(1)} %dynamic-update-slice), channel_id=1, replica_groups=mesh['tm'=4,'clip'=8] {'tm','clip'}, use_global_device_ids=true, to_apply=%add | all-reduce | flops 1024 | bytes 4096
  374.6 59.9 %all-gather.3 = bf16[32,1,128]{2,1,0:T(2,128)(2,1)S(1)} all-gather(bf16[1,1,128]{2,1,0:T(2,128)(2,1)S(1)} %bitcast.341), channel_id=1, replica_groups=mesh['tm'=4,'clip'=8] {'tm','clip'}, dimensions={0}, use_global_device_ids=true | all-gather | bytes 8448 | tf_op jit(solution)/shard_map/all_gather | solution.py:70
  482.9 24.0 copy.184
  506.9 24.1 copy.185
  547.3 60.2 %fusion.56 = f32[256,16,4]{2,1,0:T(8,128)S(1)} fusion(f32[256,16,4]{2,1,0:T(8,128)S(1)} %broadcast_maximum_fusion, f32[256,16,4,16]{3,2,1,0:T(4,128)} %get-tuple-element.100, pred[4,16]{1,0:T(4,128)(4,1)S(1)} %iota_compare_fusion), kind=kLoop, calls=%fused_computation.103 | loop fusion | flops 1294336 | bytes 1179712 | tf_op jit(solution)/shard_map/reduce_sum | solution.py:138
  670.5 51.9 %convert_reduce_fusion = (f32[4096]{0:T(1024)}, bf16[1024,4096]{1,0:T(8,128)(2,1)}, f32[1024,4096]{1,0:T(8,128)S(1)}) fusion(f32[1024,4096]{1,0:T(8,128)} %fusion.111, f32[4096]{0:T(1024)S(1)} %bitcast.317, bf16[1024,1024]{1,0:T(8,128)(2,1)} %bitcast.301, bf16[4096,1024]{1,0:T(8,128)(2,1)} %all-gather.24.cloned.1.call-done), kind=kOutput, calls=%fused_computation.14 | convolution fusion | flops 8904503296 | bytes 52461568 | tf_op jit(solution)/shard_map/dot_general | solution.py:36
  795.2 62.1 %convert_bitcast_fusion = bf16[16,1,256,1,16,64]{5,0,4,2,3,1:T(8,128)(2,1)} fusion(f32[4,256,16,64]{3,0,2,1:T(4,128)S(1)} %copy-done.2, f32[256,16,4,16]{3,2,1,0:T(4,128)} %get-tuple-element.100, f32[256,16,4]{2,1,0:T(8,128)S(1)} %copy-done.15, pred[4,16]{1,0:T(4,128)(4,1)S(1)} %copy-done.68), kind=kOutput, calls=%fused_computation.17 | convolution fusion | flops 206307328 | bytes 13697088 | tf_op jit(solution)/shard_map/cphfg,cphfe->gcphe/dot_general | solution.py:193
  857.3 30.4 %subtract_multiply_fusion = f32[256,16,4,16]{3,2,1,0:T(4,128)S(1)} fusion(bf16[16,1,256,1,16,64]{5,0,4,2,3,1:T(8,128)(2,1)} %copy.185, f32[4,256,16,64]{3,0,2,1:T(4,128)S(1)} %copy-done.2, f32[256,16,4,16]{3,2,1,0:T(4,128)S(1)} %bitcast.282, f32[256,16,4]{2,1,0:T(8,128)} %fusion.19, f32[256,16,4]{2,1,0:T(8,128)} %log_add_fusion, ...), kind=kOutput, calls=%fused_computation.43 | convolution fusion | flops 202637312 | bytes 14811200 | tf_op jit(solution)/shard_map/cphfe,gcphe->cphfg/dot_general | solution.py:184
  891.0 30.4 %fusion.2 = bf16[16,1,256,1,16,64]{5,0,4,2,3,1:T(8,128)(2,1)} fusion(bf16[4,256,16,64]{3,0,2,1:T(4,128)(2,1)} %copy.135, f32[256,16,4,16]{3,2,1,0:T(4,128)S(1)} %subtract_multiply_fusion), kind=kOutput, calls=%fused_computation.5 | convolution fusion | flops 209715200 | bytes 11534336 | tf_op jit(solution)/shard_map/cphfg,fcphe->gcphe/dot_general | solution.py:192
  921.4 22.7 pad_maximum_fusion
  944.1 38.3 %copy.143 = bf16[16,1,256,2,16,64]{2,5,4,3,0,1:T(8,128)(2,1)} copy(bf16[16,1,256,2,16,64]{5,0,4,2,3,1:T(8,128)(2,1)} %pad_maximum_fusion) | data formatting | bytes 33554432 | tf_op jit(solution)/shard_map/stack | solution.py:194
  1046.4 86.4 %reduce-scatter.17.cloned.1.call-done = bf16[4,1,256,2048]{3,2,0,1:T(8,128)(2,1)} async-done(((bf16[16,1,256,2048]{3,2,0,1:T(8,128)(2,1)}), bf16[4,1,256,2048]{3,2,0,1:T(8,128)(2,1)}) %reduce-scatter.17.cloned.1.call-update) | async-done | bytes 4194320 | tf_op jit(solution)/shard_map/reduce_scatter | solution.py:197
  1330.2 39.3 %all-reduce.3 = (f32[4096]{0:T(1024)S(1)}, f32[1024]{0:T(1024)S(1)}) all-reduce(f32[4096]{0:T(1024)S(1)} %copy-done.63, f32[1024]{0:T(1024)S(1)} %copy-done.64), channel_id=11, replica_groups=mesh['tm'=4,'clip'=8] {'tm','clip'}, use_global_device_ids=true, to_apply=%region_35.36.clone | all-reduce | flops 5120 | bytes 40960
  1372.0 125.5 %reduce-scatter.35.cloned.1.call-done = f32[32,3]{1,0:T(8,128)} async-done(((f32[1024,3]{1,0:T(8,128)}), f32[32,3]{1,0:T(8,128)}) %reduce-scatter.35.cloned.1.call-update) | async-done | bytes 400
  1498.9 131.2 %reduce-scatter.31.cloned.1.call-done = f32[32,8]{1,0:T(8,128)} async-done(((f32[1024,8]{1,0:T(8,128)}), f32[32,8]{1,0:T(8,128)}) %reduce-scatter.31.cloned.1.call-update) | async-done | bytes 1040
  1631.5 143.8 %reduce-scatter.25.cloned.1.call-done = f32[32,1024]{1,0:T(8,128)} async-done(((f32[1024,1024]{1,0:T(8,128)}), f32[32,1024]{1,0:T(8,128)}) %reduce-scatter.25.cloned.1.call-update) | async-done | bytes 131088 | tf_op jit(solution)/shard_map/reduce_scatter | solution.py:248
  1775.3 362.7 %reduce-scatter.29.cloned.1.call-done = f32[128,1024]{1,0:T(8,128)} async-done(((f32[4096,1024]{1,0:T(8,128)}), f32[128,1024]{1,0:T(8,128)}) %reduce-scatter.29.cloned.1.call-update) | async-done | bytes 524304 | tf_op jit(solution)/shard_map/reduce_scatter | solution.py:251
  2138.0 360.1 %reduce-scatter.27.cloned.1.call-done = f32[32,4096]{1,0:T(8,128)} async-done(((f32[1024,4096]{1,0:T(8,128)}), f32[32,4096]{1,0:T(8,128)}) %reduce-scatter.27.cloned.1.call-update) | async-done | bytes 524304 | tf_op jit(solution)/shard_map/reduce_scatter | solution.py:249
  2498.1 139.6 %reduce-scatter.21.cloned.1.call-done = f32[32,1024]{1,0:T(8,128)} async-done(((f32[1024,1024]{1,0:T(8,128)}), f32[32,1024]{1,0:T(8,128)}) %reduce-scatter.21.cloned.1.call-update) | async-done | bytes 131088 | tf_op jit(solution)/shard_map/reduce_scatter | solution.py:246
  2637.7 164.7 %reduce-scatter.23.cloned.1.call-done = f32[32,3072]{1,0:T(8,128)} async-done(((f32[1024,3072]{1,0:T(8,128)}), f32[32,3072]{1,0:T(8,128)}) %reduce-scatter.23.cloned.1.call-update) | async-done | bytes 393232 | tf_op jit(solution)/shard_map/reduce_scatter | solution.py:247
  2802.3 162.0 %reduce-scatter.19.cloned.1.call-done = f32[32,3072]{1,0:T(8,128)} async-done(((f32[1024,3072]{1,0:T(8,128)}), f32[32,3072]{1,0:T(8,128)}) %reduce-scatter.19.cloned.1.call-update) | async-done | bytes 393232 | tf_op jit(solution)/shard_map/reduce_scatter | solution.py:245
  (322 shorter events, 597.9 us)
Async XLA Ops:
  7.2 198.1 %copy-start.7 = (bf16[4,1,256,1024]{3,2,1,0:T(8,128)(2,1)S(1)}, bf16[4,1,256,1024]{3,2,1,0:T(8,128)(2,1)}, u32[]{:S(2)}) copy-start(bf16[4,1,256,1024]{3,2,1,0:T(8,128)(2,1)} %param.15) | copy-start | bytes 6291460
  7.2 203.1 %all-gather.12.cloned.1.call-start = ((), (), s32[]{:S(2)}) async-start(), calls=%async_computation.10 | async-start | bytes 6488064 | tf_op jit(solution)/shard_map/all_gather | solution.py:65
  7.9 294.7 %all-gather.14.cloned.1.call-start = ((), (), s32[]{:S(2)}) async-start(), calls=%async_computation.11 | async-start | bytes 2162688 | tf_op jit(solution)/shard_map/all_gather | solution.py:66
  8.7 301.5 %all-gather.16.cloned.1.call-start = ((), (), s32[]{:S(2)}) async-start(), calls=%async_computation.12 | async-start | bytes 6488064 | tf_op jit(solution)/shard_map/all_gather | solution.py:67
  9.4 439.9 %all-gather.18.cloned.1.call-start = ((), (), s32[]{:S(2)}) async-start(), calls=%async_computation.13 | async-start | bytes 20971520 | tf_op jit(solution)/shard_map/all_gather | solution.py:127
  203.2 99.4 %copy-start.33 = (f32[4,1024]{1,0:T(4,128)}, f32[4,1024]{1,0:T(4,128)S(1)}, u32[]{:S(2)}) copy-start(f32[4,1024]{1,0:T(4,128)S(1)} %fusion.85) | copy-start | bytes 49156
  207.3 100.7 %copy-start.39 = (f32[1,1024]{1,0:T(1,128)}, f32[1,1024]{1,0:T(1,128)S(1)}, u32[]{:S(2)}) copy-start(f32[1,1024]{1,0:T(1,128)S(1)} %get-tuple-element.90) | copy-start | bytes 12292
  325.7 109.0 %copy-start.13 = (bf16[4,1,256,1024]{3,2,1,0:T(8,128)(2,1)S(1)}, bf16[4,1,256,1024]{3,2,1,0:T(8,128)(2,1)}, u32[]{:S(2)}) copy-start(bf16[4,1,256,1024]{3,2,1,0:T(8,128)(2,1)} %param.29) | copy-start | bytes 6291460
  325.7 318.1 %all-gather.20.cloned.1.call-start = ((), (), s32[]{:S(2)}) async-start(), calls=%async_computation.14 | async-start | bytes 2162688 | tf_op jit(solution)/shard_map/all_gather | solution.py:68
  326.3 329.0 %all-gather.22.cloned.1.call-start = ((), (), s32[]{:S(2)}) async-start(), calls=%async_computation.15 | async-start | bytes 8650752 | tf_op jit(solution)/shard_map/all_gather | solution.py:69
  326.9 343.6 %all-gather.24.cloned.1.call-start = ((), (), s32[]{:S(2)}) async-start(), calls=%async_computation.16 | async-start | bytes 8650752 | tf_op jit(solution)/shard_map/all_gather | solution.py:71
  327.6 805.1 %reduce-scatter.17.cloned.1.call-start = ((), (), s32[]{:S(2)}) async-start(), calls=%async_computation.17 | async-start | bytes 20971520 | tf_op jit(solution)/shard_map/reduce_scatter | solution.py:197
  434.7 172.9 %copy-start.67 = (pred[4,16]{1,0:T(4,128)(4,1)}, pred[4,16]{1,0:T(4,128)(4,1)S(1)}, u32[]{:S(2)}) copy-start(pred[4,16]{1,0:T(4,128)(4,1)S(1)} %iota_compare_fusion) | copy-start | bytes 196
  784.7 72.6 %slice-start.2 = ((s8[8388608]{0:T(1024)(128)(4,1)}), s8[4194304]{0:T(1024)(128)(4,1)S(1)}, s32[]{:S(2)}) async-start(s8[8388608]{0:T(1024)(128)(4,1)} %bitcast.281), calls=%async_computation.29 | async-start | bytes 8388608
  795.2 62.1 %slice-start.3 = ((s8[8388608]{0:T(1024)(128)(4,1)}), s8[4194304]{0:T(1024)(128)(4,1)S(1)}, s32[]{:S(2)}) async-start(s8[8388608]{0:T(1024)(128)(4,1)} %bitcast.281), calls=%async_computation.30 | async-start | bytes 8388608
  1004.2 366.4 %reduce-scatter.33.cloned.1.call-start = ((), (), s32[]{:S(2)}) async-start(), calls=%async_computation.25 | async-start | bytes 540672
  1238.6 258.9 %reduce-scatter.35.cloned.1.call-start = ((), (), s32[]{:S(2)}) async-start(), calls=%async_computation.26 | async-start | bytes 540672
  1246.0 384.1 %reduce-scatter.31.cloned.1.call-start = ((), (), s32[]{:S(2)}) async-start(), calls=%async_computation.24 | async-start | bytes 540672
  1247.5 527.8 %reduce-scatter.25.cloned.1.call-start = ((), (), s32[]{:S(2)}) async-start(), calls=%async_computation.21 | async-start | bytes 4325376 | tf_op jit(solution)/shard_map/reduce_scatter | solution.py:248
  1253.5 884.5 %reduce-scatter.29.cloned.1.call-start = ((), (), s32[]{:S(2)}) async-start(), calls=%async_computation.23 | async-start | bytes 17301504 | tf_op jit(solution)/shard_map/reduce_scatter | solution.py:251
  1269.8 1228.2 %reduce-scatter.27.cloned.1.call-start = ((), (), s32[]{:S(2)}) async-start(), calls=%async_computation.22 | async-start | bytes 17301504 | tf_op jit(solution)/shard_map/reduce_scatter | solution.py:249
  1286.0 1351.7 %reduce-scatter.21.cloned.1.call-start = ((), (), s32[]{:S(2)}) async-start(), calls=%async_computation.19 | async-start | bytes 4325376 | tf_op jit(solution)/shard_map/reduce_scatter | solution.py:246
  1294.2 1508.1 %reduce-scatter.23.cloned.1.call-start = ((), (), s32[]{:S(2)}) async-start(), calls=%async_computation.20 | async-start | bytes 12976128 | tf_op jit(solution)/shard_map/reduce_scatter | solution.py:247
  1315.4 1648.9 %reduce-scatter.19.cloned.1.call-start = ((), (), s32[]{:S(2)}) async-start(), calls=%async_computation.18 | async-start | bytes 12976128 | tf_op jit(solution)/shard_map/reduce_scatter | solution.py:245
  (73 other events, 600.7 us)
Sparse Core Ops, SparseCore 0:
  11.0 72.2 all-gather.11
  86.2 55.1 all-gather.13
  144.4 68.7 all-gather.15
  325.8 112.3 all-gather.17
  441.0 56.4 all-gather.19
  500.3 76.2 all-gather.21
  579.6 76.0 all-gather.23
  1004.3 128.3 reduce-scatter.16
  1238.7 126.1 reduce-scatter.32
  1367.0 130.4 reduce-scatter.34
  1499.8 130.1 reduce-scatter.30
  1632.8 142.4 reduce-scatter.24
  1778.1 359.8 reduce-scatter.28
  2140.7 357.3 reduce-scatter.26
  2500.8 136.8 reduce-scatter.20
  2644.1 158.1 reduce-scatter.22
  2809.8 154.4 reduce-scatter.18
where the time goes:
time: 2980 us; the launch traced here: 2970 us
  waiting for transfers between devices  1680 us (56%)
  matrix products  450 us (15%)
  blocking collectives  337 us (11%)
  local copies, waits for them, and re-layouts  305 us (10%)
  other arithmetic  182 us (6%)
    reduce_scatter x1, waiting for transfers between devices, on_device(): lax.psum_scatter(g_w_down, ('tm', 'clip'), scatter_dimension=0, tiled=True)  363 us
    reduce_scatter x1, waiting for transfers between devices, on_device(): lax.psum_scatter(g_w_up, ('tm', 'clip'), scatter_dimension=0, tiled=True)  360 us
    unnamed x20, waiting for transfers between devices  261 us
    reduce_scatter x1, waiting for transfers between devices, on_device(): lax.psum_scatter(g_t_qkv, ('tm', 'clip'), scatter_dimension=0, tiled=True)  165 us
    reduce_scatter x1, waiting for transfers between devices, on_device(): lax.psum_scatter(g_s_qkv, ('tm', 'clip'), scatter_dimension=0, tiled=True)  162 us
    reduce_scatter x1, waiting for transfers between devices, on_device(): lax.psum_scatter(g_t_out, ('tm', 'clip'), scatter_dimension=0, tiled=True)  144 us
    reduce_scatter x1, waiting for transfers between devices, on_device(): lax.psum_scatter(g_s_out, ('tm', 'clip'), scatter_dimension=0, tiled=True)  140 us
    unnamed x179, local copies, waits for them, and re-layouts  113 us
  transfers between devices with their start and end apart: 17, of which 9 were waited for; matrix products, arithmetic and copies ran while one was open for 16% of the time, Pallas kernels for 0%

commit v1 on v0

v1 whole, which is shorter than its diff:
```python
from functools import partial

import jax
import jax.numpy as jnp
from jax import lax
from jax.experimental import pallas as pl
from jax.experimental.pallas import tpu as pltpu
from jax.sharding import PartitionSpec as P

H = 16
E = 64
ACTIONS = 8
FRAMES = 16
AXES = ("tm", "clip")
LANES = 128
GROUP = 16

negative = -1e30
highest = lax.Precision.HIGHEST
VMEM = 48 * 1024 * 1024


def flip(value, bit, total):
    return lax.ppermute(value, AXES, [(i, i ^ bit) for i in range(total)])


def unscramble(parts, me):
    bit = 1
    while bit < len(parts):
        swap = (me & bit) != 0
        parts = [jnp.where(swap, parts[p ^ bit], parts[p]) for p in range(len(parts))]
        bit *= 2
    return parts


def gather_small(value, me, total):
    blocks = value[None]
    bit = 1
    while bit < total:
        blocks = jnp.concatenate([blocks, flip(blocks, bit, total)], axis=0)
        bit *= 2
    bit = 1
    while bit < total:
        view = blocks.reshape(total // (2 * bit), 2, bit, *value.shape)
        view = jnp.where((me & bit) != 0, view[:, ::-1], view)
        blocks = view.reshape(total, *value.shape)
        bit *= 2
    return blocks


def scatter_small(value, me, total):
    bit = total // 2
    while bit:
        low_half, high_half = value[:bit], value[bit:]
        mine = (me & bit) != 0
        keep = jnp.where(mine, high_half, low_half)
        send = jnp.where(mine, low_half, high_half)
        value = keep + flip(send, bit, total)
        bit //= 2
    return value[0]


def scatter(value, order, me, total):
    _, rows, cols = value.shape
    left = [1 << i for i in reversed(range(total.bit_length() - 1))]
    for bit in order:
        at = left.index(bit)
        pre, post = 1 << at, 1 << (len(left) - at - 1)
        view = value.reshape(pre, 2, post, rows, cols)
        mine = (me // bit) % 2
        send = lax.dynamic_index_in_dim(view, 1 - mine, 1, keepdims=False)
        keep = lax.dynamic_index_in_dim(view, mine, 1, keepdims=False)
        got = flip(send, bit, total)
        value = keep.astype(jnp.float32) + got.astype(jnp.float32)
        left.pop(at)
        if left:
            value = value.astype(jnp.bfloat16)
    return value.reshape(rows, cols)


def spatial_bias(scalar, rows):
    column = lax.broadcasted_iota(jnp.int32, (1, rows), 1)
    return jnp.where(column < scalar * scalar, 0.0, negative)


def temporal_bias(frames_local, scalar, rows):
    def place(axis):
        index = lax.broadcasted_iota(jnp.int32, (rows, rows), axis)
        slot, at = index % GROUP, index // GROUP
        frame = ((at // frames_local) ^ scalar) * frames_local + at % frames_local
        return slot, frame

    slot_q, frame_q = place(0)
    slot_k, frame_k = place(1)
    return jnp.where((slot_q == slot_k) & (frame_q >= frame_k), 0.0, negative)


def lower_half(rows):
    return lax.broadcasted_iota(jnp.int32, (rows, LANES), 1) < E


def dot_t(a, b):
    return lax.dot_general(a, b, (((1,), (1,)), ((), ())), preferred_element_type=jnp.float32)


def t_dot(a, b):
    return lax.dot_general(a, b, (((0,), (0,)), ((), ())), preferred_element_type=jnp.float32)


def attention_forward(make_bias, scalar_ref, qkv_ref, out_ref):
    a, b, width = qkv_ref.shape
    rows, width = a * b, width // 3
    bias = make_bias(scalar_ref[0], rows)
    half = lower_half(rows)
    factor = E ** (-0.5)
    for c in range(0, width, LANES):
        q = qkv_ref[:, :, c : c + LANES].reshape(rows, LANES) * jnp.bfloat16(factor)
        k = qkv_ref[:, :, width + c : width + c + LANES].reshape(rows, LANES)
        v = qkv_ref[:, :, 2 * width + c : 2 * width + c + LANES].reshape(rows, LANES)
        pair = []
        for head in range(2):
            pick = half if head == 0 else ~half
            scores = dot_t(jnp.where(pick, q, 0), k) + bias
            weights = jnp.exp(scores - jnp.max(scores, axis=-1, keepdims=True))
            total = jnp.sum(weights, axis=-1, keepdims=True)
            probs = (weights * (1.0 / total)).astype(jnp.bfloat16)
            pair.append(jnp.dot(probs, v, preferred_element_type=jnp.float32))
        mixed = jnp.where(half, pair[0], pair[1]).astype(out_ref.dtype)
        out_ref[:, :, c : c + LANES] = mixed.reshape(a, b, LANES)


def attention_backward(make_bias, scalar_ref, qkv_ref, grad_ref, out_ref):
    a, b, width = qkv_ref.shape
    rows, width = a * b, width // 3
    bias = make_bias(scalar_ref[0], rows)
    half = lower_half(rows)
    factor = E ** (-0.5)
    for c in range(0, width, LANES):
        q = qkv_ref[:, :, c : c + LANES].reshape(rows, LANES) * jnp.bfloat16(factor)
        k = qkv_ref[:, :, width + c : width + c + LANES].reshape(rows, LANES)
        v = qkv_ref[:, :, 2 * width + c : 2 * width + c + LANES].reshape(rows, LANES)
        g = grad_ref[:, :, c : c + LANES].reshape(rows, LANES)
        dq, dk, dv = [], [], []
        for head in range(2):
            pick = half if head == 0 else ~half
            scores = dot_t(jnp.where(pick, q, 0), k) + bias
            weights = jnp.exp(scores - jnp.max(scores, axis=-1, keepdims=True))
            total = jnp.sum(weights, axis=-1, keepdims=True)
            probs = weights * (1.0 / total)
            prob_grad = dot_t(jnp.where(pick, g, 0), v)
            delta = jnp.sum(probs * prob_grad, axis=-1, keepdims=True)
            score_grad = (probs * (prob_grad - delta)).astype(jnp.bfloat16)
            dq.append(jnp.dot(score_grad, k, preferred_element_type=jnp.float32) * factor)
            dk.append(t_dot(score_grad, q))
            dv.append(t_dot(probs.astype(jnp.bfloat16), g))
        for index, pair in enumerate((dq, dk, dv)):
            merged = jnp.where(half, pair[0], pair[1]).astype(out_ref.dtype)
            start = index * width + c
            out_ref[:, :, start : start + LANES] = merged.reshape(a, b, LANES)


def run_attention(body, scalar, block, grid, index, inputs, out_width):
    a, b = block
    outer = inputs[0].shape[:2]
    rows = outer[0] * outer[1]
    return pl.pallas_call(
        body,
        grid=(grid,),
        in_specs=[pl.BlockSpec(memory_space=pltpu.SMEM)]
        + [pl.BlockSpec((a, b, x.shape[-1]), index) for x in inputs],
        out_specs=pl.BlockSpec((a, b, out_width), index),
        out_shape=jax.ShapeDtypeStruct((*outer, out_width), jnp.bfloat16),
        compiler_params=pltpu.CompilerParams(vmem_limit_bytes=VMEM),
        cost_estimate=pl.CostEstimate(
            flops=rows * H * E * 2 * a * b * 4,
            bytes_accessed=rows * 2 * (sum(x.shape[-1] for x in inputs) + out_width),
            transcendentals=rows * H * a * b,
        ),
    )(scalar, *inputs)


def normalise(inputs):
    average = jnp.mean(inputs, axis=-1, keepdims=True)
    centered = inputs - average
    variance = jnp.mean(centered * centered, axis=-1, keepdims=True)
    scale = lax.rsqrt(variance + 1e-05)
    return centered * scale, scale


def normalise_back(inputs, gain, grad):
    unit, scale = normalise(inputs)
    scaled = grad * gain
    first = jnp.mean(scaled, axis=-1, keepdims=True)
    second = jnp.mean(scaled * unit, axis=-1, keepdims=True)
    axes = tuple(range(grad.ndim - 1))
    return (
        scale * (scaled - first - unit * second),
        jnp.sum(grad * unit, axis=axes),
        jnp.sum(grad, axis=axes),
    )


def matmul(inputs, weight):
    return jnp.dot(inputs, weight, preferred_element_type=jnp.float32)


def on_device(
    tokens,
    actions,
    sides,
    action_table,
    norm_gains,
    norm_shifts,
    s_qkv,
    s_out,
    t_qkv,
    t_out,
    w_up,
    b_up,
    w_down,
    b_down,
    grad_out,
):
    frames_local, _, slots, width = tokens.shape
    tm_size, clip_size = lax.axis_size("tm"), lax.axis_size("clip")
    total = tm_size * clip_size
    me_tm, me_clip = lax.axis_index("tm"), lax.axis_index("clip")
    me = me_tm * clip_size + me_clip
    slots_local = slots // tm_size
    row_count = frames_local * slots
    bf16, f32 = jnp.bfloat16, jnp.float32

    clip_bits = [1 << i for i in reversed(range(clip_size.bit_length() - 1))]
    tm_bits = [clip_size << i for i in reversed(range(tm_size.bit_length() - 1))]
    z_bits, x_bits = clip_bits[:2], clip_bits[2:]
    y_bits, core_bits = tm_bits[:-1], tm_bits[-1:]
    order_xy = core_bits + x_bits + y_bits + z_bits
    order_yx = core_bits + y_bits + x_bits + z_bits

    def to_slots(value):
        view = value.reshape(frames_local, tm_size, slots_local, value.shape[-1])
        parts = []
        for o in range(tm_size):
            part = lax.dynamic_index_in_dim(view, me_tm ^ o, 1, keepdims=False)
            parts.append(flip(part, o * clip_size, total) if o else part)
        return jnp.concatenate(parts, axis=0)

    def from_slots(value):
        view = value.reshape(tm_size, frames_local, slots_local, value.shape[-1])
        parts = [flip(view[o], o * clip_size, total) if o else view[o] for o in range(tm_size)]
        parts = unscramble(parts, me_tm)
        return jnp.stack(parts, axis=1).reshape(frames_local, slots, value.shape[-1])

    small = jnp.concatenate(
        [x.reshape(-1) for x in (action_table, norm_gains, norm_shifts, b_up, b_down)]
    )
    sizes = [action_table.size, norm_gains.size, norm_shifts.size, b_up.size, b_down.size]
    padded = -(-sum(sizes) // 2048) * 2048
    small = jnp.pad(small, (0, padded - sum(sizes))).reshape(padded // LANES, LANES)
    small = gather_small(small, me, total).reshape(total, padded).astype(f32)
    ends = [sum(sizes[:i]) for i in range(len(sizes) + 1)]

    def unpack(i, rows):
        part = small[:, ends[i] : ends[i + 1]]
        return jnp.moveaxis(part.reshape(total, rows, -1), 1, 0).reshape(rows, -1)

    action_rows, gains, shifts = unpack(0, ACTIONS), unpack(1, 3), unpack(2, 3)
    up_bias, down_bias = unpack(3, 1), unpack(4, 1)

    def gathered(x):
        return lax.all_gather(x, AXES, axis=0, tiled=True)

    sq_full = gathered(s_qkv)
    middle = gathered(jnp.concatenate([s_out, t_qkv, t_out], axis=1))
    so_full = middle[:, :width]
    tq_full = middle[:, width : 4 * width]
    to_full = middle[:, 4 * width :]
    up_full = gathered(w_up)
    down_full = gathered(w_down)

    side = sides.reshape(1)
    onehot = (actions == jnp.arange(ACTIONS)[None, :]).astype(f32)
    embedded = jnp.dot(onehot, action_rows, precision=highest)
    hidden0 = tokens.reshape(frames_local, slots, width).astype(f32) + embedded[:, None, :]
    unit, _ = normalise(hidden0)
    normed1 = (unit * gains[0] + shifts[0]).astype(bf16).reshape(row_count, width)
    spatial = matmul(normed1, sq_full).astype(bf16).reshape(frames_local, slots, 3 * width)

    def frame_index(i):
        return (i, 0, 0)

    s_mixed = run_attention(
        partial(attention_forward, spatial_bias),
        side, (1, slots), frames_local, frame_index, [spatial], width,
    ).reshape(row_count, width)
    hidden1 = hidden0 + matmul(s_mixed, so_full).reshape(hidden0.shape)

    cotangent = to_slots(grad_out.reshape(frames_local, slots, width))
    hidden1 = to_slots(hidden1.astype(bf16)).astype(f32)
    frames = hidden1.shape[0]
    slot_at = me_tm * slots_local + jnp.arange(slots_local)
    mask = (slot_at < sides[0] * sides[0]).astype(f32)[None, :, None]
    unit, _ = normalise(hidden1)
    normed2 = (unit * gains[1] + shifts[1]).astype(bf16).reshape(row_count, width)
    temporal = matmul(normed2, tq_full).astype(bf16).reshape(frames, slots_local, 3 * width)

    def slot_index(i):
        return (0, i, 0)

    me_tm_array = me_tm.astype(jnp.int32).reshape(1)
    t_mixed = run_attention(
        partial(attention_forward, partial(temporal_bias, frames_local)),
        me_tm_array, (frames, GROUP), slots_local // GROUP, slot_index, [temporal], width,
    ).reshape(row_count, width)
    hidden2 = hidden1 + matmul(t_mixed, to_full).reshape(hidden1.shape)
    unit, _ = normalise(hidden2)
    normed3 = (unit * gains[2] + shifts[2]).astype(bf16).reshape(row_count, width)
    inner = matmul(normed3, up_full) + up_bias
    active, gelu_back = jax.vjp(partial(jax.nn.gelu, approximate=False), inner)
    active = active.astype(bf16)
    hidden3 = hidden2 + (matmul(active, down_full) + down_bias).reshape(hidden2.shape)
    mixed = from_slots((hidden3 * mask).astype(bf16))

    def blocks(grad):
        return grad.astype(bf16).reshape(total, grad.shape[0] // total, grad.shape[1])

    def halves(grad):
        half = grad.shape[1] // 2
        return jnp.concatenate(
            [
                scatter(blocks(grad[:, :half]), order_xy, me, total),
                scatter(blocks(grad[:, half:]), order_yx, me, total),
            ],
            axis=1,
        )

    grad3 = cotangent.astype(f32) * mask
    down_in = grad3.astype(bf16).reshape(row_count, width)
    g_w_down = scatter(blocks(t_dot(active, down_in)), order_xy, me, total)
    g_b_down = jnp.sum(down_in.astype(f32), axis=0)
    inner_grad = gelu_back(dot_t(down_in, down_full))[0].astype(bf16)
    g_w_up = scatter(blocks(t_dot(normed3, inner_grad)), order_yx, me, total)
    g_b_up = jnp.sum(inner_grad.astype(f32), axis=0)
    back3 = normalise_back(hidden2, gains[2], dot_t(inner_grad, up_full).reshape(hidden2.shape))
    grad2 = grad3 + back3[0]
    t_in = grad2.astype(bf16).reshape(row_count, width)
    g_t_out = scatter(blocks(t_dot(t_mixed, t_in)), order_yx, me, total)
    t_mix_grad = dot_t(t_in, to_full).astype(bf16).reshape(frames, slots_local, width)
    t_grad = run_attention(
        partial(attention_backward, partial(temporal_bias, frames_local)),
        me_tm_array, (frames, GROUP), slots_local // GROUP, slot_index, [temporal, t_mix_grad],
        3 * width,
    ).reshape(row_count, 3 * width)
    g_t_qkv = scatter(blocks(t_dot(normed2, t_grad)), order_xy, me, total)
    back2 = normalise_back(hidden1, gains[1], dot_t(t_grad, tq_full).reshape(hidden1.shape))
    grad1 = from_slots((grad2 + back2[0]).astype(bf16))
    s_in = grad1.reshape(row_count, width)
    g_s_out = scatter(blocks(t_dot(s_mixed, s_in)), order_yx, me, total)
    mix_grad = dot_t(s_in, so_full).astype(bf16).reshape(frames_local, slots, width)
    s_grad = run_attention(
        partial(attention_backward, spatial_bias),
        side, (1, slots), frames_local, frame_index, [spatial, mix_grad], 3 * width,
    ).reshape(row_count, 3 * width)
    g_s_qkv = halves(t_dot(normed1, s_grad))
    back1 = normalise_back(hidden0, gains[0], dot_t(s_grad, sq_full).reshape(hidden0.shape))
    input_grad = grad1.astype(f32) + back1[0]
    g_actions = jnp.dot(onehot.T, jnp.sum(input_grad, axis=1), precision=highest)

    terms = [
        g_actions,
        jnp.stack([back1[1], back2[1], back3[1]]),
        jnp.stack([back1[2], back2[2], back3[2]]),
        g_b_up[None],
        g_b_down[None],
    ]
    packed = [jnp.moveaxis(x.reshape(x.shape[0], total, -1), 1, 0).reshape(total, -1) for x in terms]
    packed = jnp.concatenate(packed, axis=1)
    packed = jnp.pad(packed, ((0, 0), (0, -packed.shape[1] % LANES)))
    summed = scatter_small(packed, me, total)

    def piece(i, rows):
        return summed[ends[i] : ends[i + 1]].reshape(rows, -1)

    shape = tokens.shape
    return (
        mixed.reshape(shape),
        input_grad.reshape(shape),
        piece(0, ACTIONS),
        piece(1, 3),
        piece(2, 3),
        g_s_qkv,
        g_s_out,
        g_t_qkv,
        g_t_out,
        g_w_up,
        piece(3, 1).reshape(-1),
        g_w_down,
        piece(4, 1).reshape(-1),
    )


def solution(mesh):
    whole = P(("tm", "clip"), None)
    columns = P(None, ("tm", "clip"))
    frames = P("tm", "clip", None, None)
    vector = P(("tm", "clip"))
    return jax.shard_map(
        on_device,
        mesh=mesh,
        in_specs=(
            frames, P("tm", "clip"), P("clip"), columns, columns, columns, whole, whole, whole,
            whole, whole, vector, whole, vector, frames,
        ),
        out_specs=(
            frames, frames, columns, columns, columns, whole, whole, whole, whole, whole, vector,
            whole, vector,
        ),
        check_vma=False,
    )
```

time: 2980 us -> 939 us (0.32)
  waiting for transfers between devices: 1680 us -> 410 us
  blocking collectives: 337 us -> 0 us
  matrix products: 450 us -> 204 us
  local copies, waits for them, and re-layouts: 305 us -> 61.1 us
  Pallas kernels: 0 us -> 101 us
  other arithmetic: 182 us -> 82.7 us
  starting transfers between devices: 0.9 us -> 58.9 us
    reduce_scatter x7 -> x0, waiting for transfers between devices: 1420 us -> none  [the longest x1 363 us: on_device(): lax.psum_scatter(g_w_down, ('tm', 'clip'), scatter_dimension=0, tiled=True)]
    unnamed x20 -> x4, waiting for transfers between devices: 261 us -> 1.9 us
    all_gather x4 -> x0, blocking collectives: 252 us -> none  [the longest x1 66.4 us: on_device(): lax.all_gather(action_table, ('tm', 'clip'), axis=1, tiled=True)]
    ppermute x0 -> x57, waiting for transfers between devices: none -> 247 us  [flip(): return lax.ppermute(value, AXES, [(i, i ^ bit) for i in range(total)])]
    dot_general x25 -> x14, matrix products: 389 us -> 144 us  [the longest x6 90.8 us: dot_t(): lax.dot_general(a, b, (((1,), (1,)), ((), ())), preferred_element_type=jn...]
    all_gather x7 -> x4, waiting for transfers between devices: 0.05 us -> 161 us  [gathered(): return lax.all_gather(x, AXES, axis=0, tiled=True)]
    unnamed x179 -> x164, local copies, waits for them, and re-layouts: 113 us -> 11.8 us
    pallas_call x0 -> x4, Pallas kernels: none -> 101 us  [run_attention(): pl.pallas_call(body, grid=(grid,), in_specs=[pl.BlockSpec(memory_space=pl...]
  transfers between devices with their start and end apart: 17 -> 61, of which waited for: 9 -> 33; matrix products, arithmetic and copies ran while one was open for 16% -> 22% of each run, Pallas kernels for 0% -> 11%
where the time goes in v1:
time: 939 us; the launch traced here: 933 us
  waiting for transfers between devices  410 us (44%)
  matrix products  204 us (22%)
  Pallas kernels  101 us (11%)
  other arithmetic  82.7 us (9%)
  local copies, waits for them, and re-layouts  61.1 us (7%)
  starting transfers between devices  58.9 us (6%)
  between operations  16.2 us (2%)
    ppermute x57, waiting for transfers between devices, flip(): return lax.ppermute(value, AXES, [(i, i ^ bit) for i in range(total)])  247 us
    all_gather x4, waiting for transfers between devices, gathered(): return lax.all_gather(x, AXES, axis=0, tiled=True)  161 us
    pallas_call x4, Pallas kernels, run_attention(): pl.pallas_call(body, grid=(grid,), in_specs=[pl.BlockSpec(memory_space=pl...  101 us
    dot_general x6, matrix products, dot_t(): lax.dot_general(a, b, (((1,), (1,)), ((), ())), preferred_element_type=jn...  90.8 us
    dot_general x6, matrix products, matmul(): return jnp.dot(inputs, weight, preferred_element_type=jnp.float32)  59.6 us
    ppermute x57, starting transfers between devices, flip(): return lax.ppermute(value, AXES, [(i, i ^ bit) for i in range(total)])  58.8 us
    dot_general x6, matrix products, t_dot(): lax.dot_general(a, b, (((0,), (0,)), ((), ())), preferred_element_type=jn...  52 us
    convert_element_type x28, other arithmetic, scatter(): value = value.astype(jnp.bfloat16)  27.9 us
  transfers between devices with their start and end apart: 61, of which 33 were waited for; matrix products, arithmetic and copies ran while one was open for 22% of the time, Pallas kernels for 11%

profile of v1, /device:TPU:1, one launch (start us, length us, event | category | flops | bytes accessed | tf_op | source)
XLA Modules:
  0.0 933.0 jit_solution(252911770802576232)
XLA Ops:
  35.3 13.6 %collective-permute-done.4 = bf16[16,16,128]{2,1,0:T(8,128)(2,1)S(1)} collective-permute-done((bf16[16,16,128]{2,1,0:T(8,128)(2,1)S(1)}, bf16[16,16,128]{2,1,0:T(8,128)(2,1)S(1)}, u32[]{:S(2)}, u32[]{:S(2)}) %collective-permute-start.4) | collective-permute-done | bytes 65568 | tf_op jit(solution)/shard_map/ppermute | solution.py:24
  65.0 20.4 %all-gather.5.cloned.1.call-done = bf16[1024,3072]{1,0:T(8,128)(2,1)} async-done(((bf16[32,3072]{1,0:T(8,128)(2,1)}), bf16[1024,3072]{1,0:T(8,128)(2,1)}) %all-gather.5.cloned.1.call-update) | async-done | bytes 6291472 | tf_op jit(solution)/shard_map/all_gather | solution.py:271
  85.4 11.3 %convolution_convert_fusion.3 = bf16[1024,3072]{1,0:T(8,128)(2,1)} fusion(bf16[1024,1024]{1,0:T(8,128)(2,1)} %fusion.25, bf16[1024,3072]{1,0:T(8,128)(2,1)} %all-gather.5.cloned.1.call-done), kind=kOutput, calls=%fused_computation.33 | convolution fusion | flops 6445596672 | bytes 14680064 | tf_op jit(solution)/shard_map/dot_general | solution.py:204
  96.7 11.4 %shard_map.246 = bf16[4,256,1024]{2,1,0:T(8,128)(2,1)S(1)} custom-call(s32[1]{0:T(128)S(6)} %copy.85.scalar_ref, bf16[4,256,3072]{2,1,0:T(8,128)(2,1)} %bitcast.402), custom_call_target="tpu_custom_call" | custom-call | flops 2147483648 | bytes 8388608 | tf_op jit(solution)/shard_map/pallas_call | solution.py:166
  108.1 66.1 %all-gather.7.cloned.1.call-done = bf16[1024,5120]{1,0:T(8,128)(2,1)} async-done(((bf16[32,5120]{1,0:T(8,128)(2,1)}), bf16[1024,5120]{1,0:T(8,128)(2,1)}) %all-gather.7.cloned.1.call-update) | async-done | bytes 10485776 | tf_op jit(solution)/shard_map/all_gather | solution.py:271
  184.4 11.0 %collective-permute-done.7 = bf16[4,64,1024]{2,1,0:T(8,128)(2,1)S(1)} collective-permute-done((bf16[4,64,1024]{2,1,0:T(8,128)(2,1)S(1)}, bf16[4,64,1024]{2,1,0:T(8,128)(2,1)S(1)}, u32[]{:S(2)}, u32[]{:S(2)}) %collective-permute-start.7) | collective-permute-done | bytes 524320 | tf_op jit(solution)/shard_map/ppermute | solution.py:24
  195.5 10.7 %collective-permute-done.6 = bf16[4,64,1024]{2,1,0:T(8,128)(2,1)S(1)} collective-permute-done((bf16[4,64,1024]{2,1,0:T(8,128)(2,1)S(1)}, bf16[4,64,1024]{2,1,0:T(8,128)(2,1)S(1)}, u32[]{:S(2)}, u32[]{:S(2)}) %collective-permute-start.6) | collective-permute-done | bytes 524320 | tf_op jit(solution)/shard_map/ppermute | solution.py:24
  210.3 11.5 %convolution_convert_fusion.2 = bf16[1024,3072]{1,0:T(8,128)(2,1)} fusion(bf16[1024,1024]{1,0:T(8,128)(2,1)S(1)} %fusion.20, bf16[1024,5120]{1,0:T(8,128)(2,1)} %all-gather.7.cloned.1.call-done), kind=kOutput, calls=%fused_computation.32 | convolution fusion | flops 6445596672 | bytes 14680064 | tf_op jit(solution)/shard_map/dot_general | solution.py:204
  221.9 11.8 %shard_map.247 = bf16[16,64,1024]{2,1,0:T(8,128)(2,1)S(1)} custom-call(s32[1]{0:T(128)} %bitcast.21.scalar_ref, bf16[16,64,3072]{2,1,0:T(8,128)(2,1)} %bitcast.404), custom_call_target="tpu_custom_call" | custom-call | flops 2147483648 | bytes 8388608 | tf_op jit(solution)/shard_map/pallas_call | solution.py:166
  243.1 11.6 %all-gather.9.cloned.1.call-done = bf16[1024,4096]{1,0:T(8,128)(2,1)} async-done(((bf16[32,4096]{1,0:T(8,128)(2,1)}), bf16[1024,4096]{1,0:T(8,128)(2,1)}) %all-gather.9.cloned.1.call-update) | async-done | bytes 8388624 | tf_op jit(solution)/shard_map/all_gather | solution.py:271
  254.7 16.2 %fusion.90 = f32[1024,4096]{1,0:T(8,128)} fusion(bf16[1024,1024]{1,0:T(8,128)(2,1)} %bitcast.453, bf16[1024,4096]{1,0:T(8,128)(2,1)} %all-gather.9.cloned.1.call-done), kind=kOutput, calls=%fused_computation.300 | convolution fusion | flops 8589934592 | bytes 27262976 | tf_op jit(solution)/shard_map/dot_general | solution.py:204
  270.9 62.6 %all-gather.11.cloned.1.call-done = bf16[4096,1024]{1,0:T(8,128)(2,1)} async-done(((bf16[128,1024]{1,0:T(8,128)(2,1)}), bf16[4096,1024]{1,0:T(8,128)(2,1)}) %all-gather.11.cloned.1.call-update) | async-done | bytes 8388624 | tf_op jit(solution)/shard_map/all_gather | solution.py:271
  333.6 51.5 %convert_reduce_fusion = (f32[4096]{0:T(1024)}, bf16[1024,4096]{1,0:T(8,128)(2,1)}, f32[1024,4096]{1,0:T(8,128)S(1)}) fusion(f32[1024,4096]{1,0:T(8,128)} %fusion.90, f32[4096]{0:T(1024)S(1)} %slice_bitcast_fusion, bf16[1024,1024]{1,0:T(8,128)(2,1)S(1)} %copy-done.33, bf16[4096,1024]{1,0:T(8,128)(2,1)} %all-gather.11.cloned.1.call-done), kind=kOutput, calls=%fused_computation.2 | convolution fusion | flops 8904503296 | bytes 52461568 | tf_op jit(solution)/shard_map/dot_general | solution.py:103
  393.2 11.3 %convolution_convert_fusion = bf16[4096,1024]{1,0:T(8,128)(2,1)} fusion(bf16[1024,4096]{1,0:T(8,128)(2,1)S(1)} %multiply_convert_fusion, bf16[1024,1024]{1,0:T(8,128)(2,1)S(1)} %copy-done.33), kind=kOutput, calls=%fused_computation.24 | convolution fusion | flops 8594128896 | bytes 18874368 | tf_op jit(solution)/shard_map/dot_general | solution.py:107
  404.6 14.9 %convolution_convert_fusion.1 = bf16[1024,4096]{1,0:T(8,128)(2,1)} fusion(bf16[1024,1024]{1,0:T(8,128)(2,1)S(1)} %bitcast.454, bf16[1024,4096]{1,0:T(8,128)(2,1)} %get-tuple-element.60), kind=kOutput, calls=%fused_computation.25 | convolution fusion | flops 8594128896 | bytes 18874368 | tf_op jit(solution)/shard_map/dot_general | solution.py:107
  437.4 11.4 %broadcast_add_fusion = f32[1024,1024]{1,0:T(8,128)S(1)} fusion(f32[1024]{0:T(1024)S(1)} %copy-done.63, bf16[1024,4096]{1,0:T(8,128)(2,1)S(1)} %copy-done.14, bf16[4096,1024]{1,0:T(8,128)(2,1)} %all-gather.11.cloned.1.call-done), kind=kOutput, calls=%fused_computation.115 | convolution fusion | flops 8590983168 | bytes 20975616 | tf_op jit(solution)/shard_map/dot_general | solution.py:204
  467.2 38.5 %shard_map.248 = bf16[16,64,3072]{2,1,0:T(8,128)(2,1)} custom-call(s32[1]{0:T(128)} %bitcast.21.scalar_ref, bf16[16,64,3072]{2,1,0:T(8,128)(2,1)} %bitcast.405, bf16[16,64,1024]{2,1,0:T(8,128)(2,1)S(1)} %bitcast.400), custom_call_target="tpu_custom_call" | custom-call | flops 2147483648 | bytes 14680064 | tf_op jit(solution)/shard_map/pallas_call | solution.py:166
  510.6 11.1 %multiply_reduce_fusion.1 = (f32[1024]{0:T(1024)S(1)}, f32[16,64]{1,0:T(8,128)S(1)}, f32[16,64]{1,0:T(8,128)S(1)}, f32[1024]{0:T(1024)S(1)}, f32[16,64,1024]{2,1,0:T(8,128)}) fusion(f32[16,64]{1,0:T(8,128)S(1)} %copy-done.47, f32[16,64]{1,0:T(8,128)S(1)} %copy-done.45, bf16[4,64,1024]{2,1,0:T(8,128)(2,1)S(1)} %copy-done.17, ...), kind=kOutput, calls=%fused_computation.61 | convolution fusion | flops 6456078336 | bytes 18903040 | tf_op jit(solution)/shard_map/dot_general | solution.py:103
  564.8 39.0 %shard_map.249 = bf16[4,256,3072]{2,1,0:T(8,128)(2,1)} custom-call(s32[1]{0:T(128)S(6)} %copy.85.scalar_ref, bf16[4,256,3072]{2,1,0:T(8,128)(2,1)} %bitcast.403, bf16[4,256,1024]{2,1,0:T(8,128)(2,1)S(1)} %bitcast.399), custom_call_target="tpu_custom_call" | custom-call | flops 2147483648 | bytes 14680064 | tf_op jit(solution)/shard_map/pallas_call | solution.py:166
  722.2 11.9 %collective-permute-done.28 = bf16[1,8,32,1536]{3,2,1,0:T(8,128)(2,1)S(1)} collective-permute-done((bf16[1,8,32,1536]{3,2,1,0:T(8,128)(2,1)S(1)}, bf16[1,8,32,1536]{3,2,1,0:T(8,128)(2,1)S(1)}, u32[]{:S(2)}, u32[]{:S(2)}) %collective-permute-start.28) | collective-permute-done | bytes 786464 | tf_op jit(solution)/shard_map/ppermute | solution.py:24
  745.3 13.5 %collective-permute-done.25 = bf16[1,2,32,1536]{3,2,1,0:T(8,128)(2,1)S(1)} collective-permute-done((bf16[1,2,32,1536]{3,2,1,0:T(8,128)(2,1)S(1)}, bf16[1,2,32,1536]{3,2,1,0:T(8,128)(2,1)S(1)}, u32[]{:S(2)}, u32[]{:S(2)}) %collective-permute-start.25) | collective-permute-done | bytes 196640 | tf_op jit(solution)/shard_map/ppermute | solution.py:24
  782.8 58.1 %collective-permute-done.39 = bf16[1,4,32,3072]{3,2,1,0:T(8,128)(2,1)S(1)} collective-permute-done((bf16[1,4,32,3072]{3,2,1,0:T(8,128)(2,1)S(1)}, bf16[1,4,32,3072]{3,2,1,0:T(8,128)(2,1)S(1)}, u32[]{:S(2)}, u32[]{:S(2)}) %collective-permute-start.39) | collective-permute-done | bytes 786464 | tf_op jit(solution)/shard_map/ppermute | solution.py:24
  845.2 15.9 %collective-permute-done.40 = bf16[1,2,32,3072]{3,2,1,0:T(8,128)(2,1)S(1)} collective-permute-done((bf16[1,2,32,3072]{3,2,1,0:T(8,128)(2,1)S(1)}, bf16[1,2,32,3072]{3,2,1,0:T(8,128)(2,1)S(1)}, u32[]{:S(2)}, u32[]{:S(2)}) %collective-permute-start.40) | collective-permute-done | bytes 393248 | tf_op jit(solution)/shard_map/ppermute | solution.py:24
  870.8 30.2 %collective-permute-done.55 = bf16[1,2,128,1024]{3,2,1,0:T(8,128)(2,1)S(1)} collective-permute-done((bf16[1,2,128,1024]{3,2,1,0:T(8,128)(2,1)S(1)}, bf16[1,2,128,1024]{3,2,1,0:T(8,128)(2,1)S(1)}, u32[]{:S(2)}, u32[]{:S(2)}) %collective-permute-start.55) | collective-permute-done | bytes 524320 | tf_op jit(solution)/shard_map/ppermute | solution.py:24
  (475 shorter events, 351.2 us)
Async XLA Ops:
  7.2 78.2 %all-gather.5.cloned.1.call-start = ((), (), s32[]{:S(2)}) async-start(), calls=%async_computation | async-start | bytes 6488064 | tf_op jit(solution)/shard_map/all_gather | solution.py:271
  7.9 166.3 %all-gather.7.cloned.1.call-start = ((), (), s32[]{:S(2)}) async-start(), calls=%async_computation.1 | async-start | bytes 10813440 | tf_op jit(solution)/shard_map/all_gather | solution.py:271
  9.7 245.0 %all-gather.9.cloned.1.call-start = ((), (), s32[]{:S(2)}) async-start(), calls=%async_computation.2 | async-start | bytes 8650752 | tf_op jit(solution)/shard_map/all_gather | solution.py:271
  10.4 323.1 %all-gather.11.cloned.1.call-start = ((), (), s32[]{:S(2)}) async-start(), calls=%async_computation.3 | async-start | bytes 8650752 | tf_op jit(solution)/shard_map/all_gather | solution.py:271
  19.5 161.2 %collective-permute-start.12 = (bf16[4,64,1024]{2,1,0:T(8,128)(2,1)}, bf16[4,64,1024]{2,1,0:T(8,128)(2,1)S(1)}, u32[]{:S(2)}, u32[]{:S(2)}) collective-permute-start(bf16[4,64,1024]{2,1,0:T(8,128)(2,1)} %get-tuple-element.87), channel_id=1, source_target_pairs={{0,16},{1,17},{2,18},{3,19},{4,20},{5,21},{6,22},{7,23},{8,24},{9,... | collective-permute-start | bytes 1572872 | tf_op jit(solution)/shard_map/ppermute | solution.py:24
  20.8 160.5 %collective-permute-start.11 = (bf16[4,64,1024]{2,1,0:T(8,128)(2,1)}, bf16[4,64,1024]{2,1,0:T(8,128)(2,1)}, u32[]{:S(2)}, u32[]{:S(2)}) collective-permute-start(bf16[4,64,1024]{2,1,0:T(8,128)(2,1)} %get-tuple-element.88), channel_id=1, source_target_pairs={{0,8},{1,9},{2,10},{3,11},{4,12},{5,13},{6,14},{7,15},{8,0},{9,1},... | collective-permute-start | bytes 1572872 | tf_op jit(solution)/shard_map/ppermute | solution.py:24
  22.0 159.3 %collective-permute-start.13 = (bf16[4,64,1024]{2,1,0:T(8,128)(2,1)}, bf16[4,64,1024]{2,1,0:T(8,128)(2,1)}, u32[]{:S(2)}, u32[]{:S(2)}) collective-permute-start(bf16[4,64,1024]{2,1,0:T(8,128)(2,1)} %get-tuple-element.89), channel_id=1, source_target_pairs={{0,24},{1,25},{2,26},{3,27},{4,28},{5,29},{6,30},{7,31},{8,16},{9,... | collective-permute-start | bytes 1572872 | tf_op jit(solution)/shard_map/ppermute | solution.py:24
  180.4 25.8 %collective-permute-start.6 = (bf16[4,64,1024]{2,1,0:T(8,128)(2,1)S(1)}, bf16[4,64,1024]{2,1,0:T(8,128)(2,1)S(1)}, u32[]{:S(2)}, u32[]{:S(2)}) collective-permute-start(bf16[4,64,1024]{2,1,0:T(8,128)(2,1)S(1)} %get-tuple-element.92), channel_id=1, source_target_pairs={{0,16},{1,17},{2,18},{3,19},{4,20},{5,21},{6,22},{7,23},{8,24},{9,... | collective-permute-start | bytes 1572872 | tf_op jit(solution)/shard_map/ppermute | solution.py:24
  461.0 192.5 %collective-permute-start.42 = (bf16[2,8,32,1024]{3,2,1,0:T(8,128)(2,1)}, bf16[2,8,32,1024]{3,2,1,0:T(8,128)(2,1)}, u32[]{:S(2)}, u32[]{:S(2)}) collective-permute-start(bf16[2,8,32,1024]{3,2,1,0:T(8,128)(2,1)} %dynamic-slice_bitcast_fusion.9), channel_id=1, source_target_pairs={{0,8},{1,9},{2,10},{3,11},{4,12},{5,13},{6,14},{7,15},{8,0},{9,1},... | collective-permute-start | bytes 3145736 | tf_op jit(solution)/shard_map/ppermute | solution.py:24
  462.5 177.2 %collective-permute-start.10 = (bf16[4,64,1024]{2,1,0:T(8,128)(2,1)}, bf16[4,64,1024]{2,1,0:T(8,128)(2,1)}, u32[]{:S(2)}, u32[]{:S(2)}) collective-permute-start(bf16[4,64,1024]{2,1,0:T(8,128)(2,1)} %get-tuple-element.83), channel_id=1, source_target_pairs={{0,8},{1,9},{2,10},{3,11},{4,12},{5,13},{6,14},{7,15},{8,0},{9,1},... | collective-permute-start | bytes 1572872 | tf_op jit(solution)/shard_map/ppermute | solution.py:24
  541.3 98.5 %collective-permute-start.9 = (bf16[4,64,1024]{2,1,0:T(8,128)(2,1)}, bf16[4,64,1024]{2,1,0:T(8,128)(2,1)}, u32[]{:S(2)}, u32[]{:S(2)}) collective-permute-start(bf16[4,64,1024]{2,1,0:T(8,128)(2,1)} %get-tuple-element.84), channel_id=1, source_target_pairs={{0,16},{1,17},{2,18},{3,19},{4,20},{5,21},{6,22},{7,23},{8,24},{9,... | collective-permute-start | bytes 1572872 | tf_op jit(solution)/shard_map/ppermute | solution.py:24
  542.5 97.7 %collective-permute-start.8 = (bf16[4,64,1024]{2,1,0:T(8,128)(2,1)}, bf16[4,64,1024]{2,1,0:T(8,128)(2,1)}, u32[]{:S(2)}, u32[]{:S(2)}) collective-permute-start(bf16[4,64,1024]{2,1,0:T(8,128)(2,1)} %get-tuple-element.85), channel_id=1, source_target_pairs={{0,24},{1,25},{2,26},{3,27},{4,28},{5,29},{6,30},{7,31},{8,16},{9,... | collective-permute-start | bytes 1572872 | tf_op jit(solution)/shard_map/ppermute | solution.py:24
  639.2 126.2 %collective-permute-start.52 = (bf16[2,8,128,1024]{3,2,1,0:T(8,128)(2,1)}, bf16[2,8,128,1024]{3,2,1,0:T(8,128)(2,1)}, u32[]{:S(2)}, u32[]{:S(2)}) collective-permute-start(bf16[2,8,128,1024]{3,2,1,0:T(8,128)(2,1)} %dynamic-slice_bitcast_fusion), channel_id=1, source_target_pairs={{0,8},{1,9},{2,10},{3,11},{4,12},{5,13},{6,14},{7,15},{8,0},{9,1},... | collective-permute-start | bytes 12582920 | tf_op jit(solution)/shard_map/ppermute | solution.py:24
  639.7 95.3 %collective-permute-start.37 = (bf16[2,8,32,3072]{3,2,1,0:T(8,128)(2,1)}, bf16[2,8,32,3072]{3,2,1,0:T(8,128)(2,1)}, u32[]{:S(2)}, u32[]{:S(2)}) collective-permute-start(bf16[2,8,32,3072]{3,2,1,0:T(8,128)(2,1)} %dynamic-slice_bitcast_fusion.2), channel_id=1, source_target_pairs={{0,8},{1,9},{2,10},{3,11},{4,12},{5,13},{6,14},{7,15},{8,0},{9,1},... | collective-permute-start | bytes 9437192 | tf_op jit(solution)/shard_map/ppermute | solution.py:24
  639.8 35.0 %collective-permute-start.32 = (bf16[2,8,32,1024]{3,2,1,0:T(8,128)(2,1)}, bf16[2,8,32,1024]{3,2,1,0:T(8,128)(2,1)}, u32[]{:S(2)}, u32[]{:S(2)}) collective-permute-start(bf16[2,8,32,1024]{3,2,1,0:T(8,128)(2,1)} %dynamic-slice_bitcast_fusion.10), channel_id=1, source_target_pairs={{0,8},{1,9},{2,10},{3,11},{4,12},{5,13},{6,14},{7,15},{8,0},{9,1},... | collective-permute-start | bytes 3145736 | tf_op jit(solution)/shard_map/ppermute | solution.py:24
  657.7 37.1 %collective-permute-start.22 = (bf16[2,8,32,1536]{3,2,1,0:T(8,128)(2,1)}, bf16[2,8,32,1536]{3,2,1,0:T(8,128)(2,1)}, u32[]{:S(2)}, u32[]{:S(2)}) collective-permute-start(bf16[2,8,32,1536]{3,2,1,0:T(8,128)(2,1)} %dynamic-slice_bitcast_fusion.6), channel_id=1, source_target_pairs={{0,8},{1,9},{2,10},{3,11},{4,12},{5,13},{6,14},{7,15},{8,0},{9,1},... | collective-permute-start | bytes 4718600 | tf_op jit(solution)/shard_map/ppermute | solution.py:24
  690.7 82.5 %collective-permute-start.47 = (bf16[2,8,32,4096]{3,2,1,0:T(8,128)(2,1)}, bf16[2,8,32,4096]{3,2,1,0:T(8,128)(2,1)}, u32[]{:S(2)}, u32[]{:S(2)}) collective-permute-start(bf16[2,8,32,4096]{3,2,1,0:T(8,128)(2,1)} %dynamic-slice_bitcast_fusion.1), channel_id=1, source_target_pairs={{0,8},{1,9},{2,10},{3,11},{4,12},{5,13},{6,14},{7,15},{8,0},{9,1},... | collective-permute-start | bytes 12582920 | tf_op jit(solution)/shard_map/ppermute | solution.py:24
  739.4 39.0 %collective-permute-start.38 = (bf16[8,1,32,3072]{3,2,0,1:T(8,128)(2,1)}, bf16[8,1,32,3072]{3,2,0,1:T(8,128)(2,1)}, u32[]{:S(2)}, u32[]{:S(2)}) collective-permute-start(bf16[8,1,32,3072]{3,2,0,1:T(8,128)(2,1)} %dynamic-slice_bitcast_fusion.4), channel_id=1, source_target_pairs={{0,1},{1,0},{2,3},{3,2},{4,5},{5,4},{6,7},{7,6},{8,9},{9,8},{10,11... | collective-permute-start | bytes 4718600 | tf_op jit(solution)/shard_map/ppermute | solution.py:24
  772.7 68.5 %collective-permute-start.53 = (bf16[8,1,128,1024]{3,2,0,1:T(8,128)(2,1)}, bf16[8,1,128,1024]{3,2,0,1:T(8,128)(2,1)S(1)}, u32[]{:S(2)}, u32[]{:S(2)}) collective-permute-start(bf16[8,1,128,1024]{3,2,0,1:T(8,128)(2,1)} %dynamic-slice_bitcast_fusion.3), channel_id=1, source_target_pairs={{0,1},{1,0},{2,3},{3,2},{4,5},{5,4},{6,7},{7,6},{8,9},{9,8},{10,11... | collective-permute-start | bytes 6291464 | tf_op jit(solution)/shard_map/ppermute | solution.py:24
  777.4 65.9 %collective-permute-start.48 = (bf16[1,8,32,4096]{3,2,1,0:T(8,128)(2,1)S(1)}, bf16[1,8,32,4096]{3,2,1,0:T(8,128)(2,1)S(1)}, u32[]{:S(2)}, u32[]{:S(2)}) collective-permute-start(bf16[1,8,32,4096]{3,2,1,0:T(8,128)(2,1)S(1)} %constant_dynamic-slice_fusion.2), channel_id=1, source_target_pairs={{0,16},{1,17},{2,18},{3,19},{4,20},{5,21},{6,22},{7,23},{8,24},{9,... | collective-permute-start | bytes 6291464 | tf_op jit(solution)/shard_map/ppermute | solution.py:24
  780.5 60.4 %collective-permute-start.39 = (bf16[1,4,32,3072]{3,2,1,0:T(8,128)(2,1)S(1)}, bf16[1,4,32,3072]{3,2,1,0:T(8,128)(2,1)S(1)}, u32[]{:S(2)}, u32[]{:S(2)}) collective-permute-start(bf16[1,4,32,3072]{3,2,1,0:T(8,128)(2,1)S(1)} %dynamic-slice_bitcast_fusion.11), channel_id=1, source_target_pairs={{0,16},{1,17},{2,18},{3,19},{4,20},{5,21},{6,22},{7,23},{8,24},{9,... | collective-permute-start | bytes 2359304 | tf_op jit(solution)/shard_map/ppermute | solution.py:24
  865.6 35.3 %collective-permute-start.55 = (bf16[1,2,128,1024]{3,2,1,0:T(8,128)(2,1)S(1)}, bf16[1,2,128,1024]{3,2,1,0:T(8,128)(2,1)S(1)}, u32[]{:S(2)}, u32[]{:S(2)}) collective-permute-start(bf16[1,2,128,1024]{3,2,1,0:T(8,128)(2,1)S(1)} %dynamic-slice_bitcast_fusion.13), channel_id=1, source_target_pairs={{0,4},{1,5},{2,6},{3,7},{4,0},{5,1},{6,2},{7,3},{8,12},{9,13},{10,... | collective-permute-start | bytes 1572872 | tf_op jit(solution)/shard_map/ppermute | solution.py:24
  868.4 43.8 %collective-permute-start.50 = (bf16[1,2,32,4096]{3,2,1,0:T(8,128)(2,1)S(1)}, bf16[1,2,32,4096]{3,2,1,0:T(8,128)(2,1)S(1)}, u32[]{:S(2)}, u32[]{:S(2)}) collective-permute-start(bf16[1,2,32,4096]{3,2,1,0:T(8,128)(2,1)S(1)} %dynamic-slice_bitcast_fusion.14), channel_id=1, source_target_pairs={{0,4},{1,5},{2,6},{3,7},{4,0},{5,1},{6,2},{7,3},{8,12},{9,13},{10,... | collective-permute-start | bytes 1572872 | tf_op jit(solution)/shard_map/ppermute | solution.py:24
  869.7 43.1 %collective-permute-start.41 = (bf16[1,1,32,3072]{3,2,1,0:T(8,128)(2,1)S(1)}, bf16[1,1,32,3072]{3,2,1,0:T(8,128)(2,1)S(1)}, u32[]{:S(2)}, u32[]{:S(2)}) collective-permute-start(bf16[1,1,32,3072]{3,2,1,0:T(8,128)(2,1)S(1)} %constant_dynamic-slice_fusion.5), channel_id=1, source_target_pairs={{0,2},{1,3},{2,0},{3,1},{4,6},{5,7},{6,4},{7,5},{8,10},{9,11},{10,... | collective-permute-start | bytes 589832 | tf_op jit(solution)/shard_map/ppermute | solution.py:24
  (116 other events, 2610.5 us)
Sparse Core Ops, SparseCore 0:
  11.0 74.3 all-gather.4
  88.8 85.3 all-gather.6
  177.2 77.4 all-gather.8
  257.6 75.9 all-gather.10

commit v2 on v1

v2 whole, which is shorter than its diff:
```python
from functools import partial

import jax
import jax.numpy as jnp
from jax import lax
from jax.experimental import pallas as pl
from jax.experimental.pallas import tpu as pltpu
from jax.sharding import PartitionSpec as P

H = 16
E = 64
ACTIONS = 8
FRAMES = 16
AXES = ("tm", "clip")
LANES = 128
GROUP = 16

negative = -1e30
highest = lax.Precision.HIGHEST
VMEM = 48 * 1024 * 1024
bf16, f32 = jnp.bfloat16, jnp.float32


class Place:
    def __init__(self):
        tm_size, clip_size = lax.axis_size("tm"), lax.axis_size("clip")
        self.tm_size, self.clip_size, self.total = tm_size, clip_size, tm_size * clip_size
        self.tm = lax.axis_index("tm")
        self.me = self.tm * clip_size + lax.axis_index("clip")
        self.core_bit = clip_size
        self.core = self.bit_of(clip_size)
        clip_bits = [1 << i for i in range(clip_size.bit_length() - 1)]
        tm_bits = [clip_size << i for i in range(tm_size.bit_length() - 1)]
        x, z, y = clip_bits[:-2], clip_bits[-2:], tm_bits[1:]
        self.z = [(b, b) for b in z]
        self.xy = list(zip(x + y, y + x))

    def bit_of(self, bit):
        return (self.me // bit) % 2

    def mine(self, pair):
        return jnp.where(self.core == 0, self.bit_of(pair[0]), self.bit_of(pair[1]))

    def choose(self, pair):
        return jnp.where(self.core == 0, pair[0], pair[1])

    def flip(self, value, pair):
        moves = [(i, i ^ pair[(i // self.core_bit) % 2]) for i in range(self.total)]
        return lax.ppermute(value, AXES, moves)

    def tm_flip(self, value, offset):
        moves = [(i, i ^ (offset * self.clip_size)) for i in range(self.total)]
        return lax.ppermute(value, AXES, moves)


def below(have, bit):
    return sum(1 for b in have if b < bit)


def unscramble(parts, me):
    bit = 1
    while bit < len(parts):
        swap = (me & bit) != 0
        parts = [jnp.where(swap, parts[p ^ bit], parts[p]) for p in range(len(parts))]
        bit *= 2
    return parts


def position(m, value, k):
    m = jnp.int32(m)
    high = lax.shift_left(lax.shift_right_logical(m, k), k + 1)
    return high | lax.shift_left(value, k) | (m & (lax.shift_left(jnp.int32(1), k) - 1))


def merge_body(info_ref, mine_ref, other_ref, out_ref):
    k, value = info_ref[0], info_ref[1]
    for m in range(mine_ref.shape[0]):
        out_ref[position(m, value, k)] = mine_ref[m]
        out_ref[position(m, 1 - value, k)] = other_ref[m]


def column_block(shape):
    blocks, rows, cols = shape
    return cols if blocks * rows * cols <= 512 * 1024 else min(cols, 512)


def merge(mine, other, k, value):
    m, r, n = mine.shape
    block = column_block((2 * m, r, n))
    spec = pl.BlockSpec((m, r, block), lambda j: (0, 0, j))
    return pl.pallas_call(
        merge_body,
        grid=(n // block,),
        in_specs=[pl.BlockSpec(memory_space=pltpu.SMEM), spec, spec],
        out_specs=pl.BlockSpec((2 * m, r, block), lambda j: (0, 0, j)),
        out_shape=jax.ShapeDtypeStruct((2 * m, r, n), mine.dtype),
        compiler_params=pltpu.CompilerParams(vmem_limit_bytes=VMEM),
        cost_estimate=pl.CostEstimate(
            flops=0, bytes_accessed=4 * m * r * n * mine.dtype.itemsize, transcendentals=0
        ),
    )(jnp.stack([jnp.int32(k), value.astype(jnp.int32)]), mine, other)


def split_body(ends, info_ref, *refs):
    k, value, step = info_ref[0], info_ref[1], pl.program_id(0)
    send_ref, keep_ref = refs[-2:]
    for p in range(len(ends) - 1):

        @pl.when((step >= ends[p]) & (step < ends[p + 1]))
        def _(a_ref=refs[2 * p], b_ref=refs[2 * p + 1]):
            for m in range(send_ref.shape[0]):
                for out_ref, at in ((send_ref, 1 - value), (keep_ref, value)):
                    i = position(m, at, k)
                    total = a_ref[i].astype(f32) + b_ref[i].astype(f32)
                    out_ref[m] = total.astype(out_ref.dtype)


def split(pairs, k, value, dtype):
    blocks, r, _ = pairs[0][0].shape
    widths = [a.shape[-1] for a, _ in pairs]
    n = sum(widths)
    block = min([column_block((blocks, r, n))] + widths)
    ends = [sum(widths[:i]) // block for i in range(len(widths) + 1)]
    in_specs = [pl.BlockSpec(memory_space=pltpu.SMEM)]
    for low, high in zip(ends[:-1], ends[1:]):

        def index(j, low=low, high=high):
            return (0, 0, jnp.clip(j - low, 0, high - low - 1))

        in_specs += [pl.BlockSpec((blocks, r, block), index)] * 2
    out = jax.ShapeDtypeStruct((blocks // 2, r, n), dtype)
    return pl.pallas_call(
        partial(split_body, ends),
        grid=(n // block,),
        in_specs=in_specs,
        out_specs=[pl.BlockSpec((blocks // 2, r, block), lambda j: (0, 0, j))] * 2,
        out_shape=[out, out],
        compiler_params=pltpu.CompilerParams(vmem_limit_bytes=VMEM),
        cost_estimate=pl.CostEstimate(
            flops=blocks * r * n, bytes_accessed=6 * blocks * r * n, transcendentals=0
        ),
    )(jnp.stack([jnp.int32(k), value.astype(jnp.int32)]), *[x for pair in pairs for x in pair])


def gather_small(place, value):
    core = (place.core_bit, place.core_bit)
    x_and_y = [(b, b) for b, _ in place.xy]
    count = len(x_and_y) // 2
    blocks, have = value[None], []
    for pair in x_and_y[:count] + [core] + x_and_y[count:] + place.z:
        (send,) = yield [blocks]
        (got,) = yield [place.flip(send, pair)]
        blocks = merge(blocks, got, below(have, pair[0]), place.bit_of(pair[0]))
        have.append(pair[0])
    return blocks


def scatter_small(place, value):
    bit = place.total // 2
    while bit:
        low_half, high_half = value[:bit], value[bit:]
        mine = (place.me & bit) != 0
        keep = jnp.where(mine, high_half, low_half)
        (send,) = yield [jnp.where(mine, low_half, high_half)]
        (got,) = yield [place.flip(send, (bit, bit))]
        value = keep + got
        bit //= 2
    return value[0]


def gather(place, keep, send):
    core = (place.core_bit, place.core_bit)
    have = ([], [])
    blocks, out = keep[None], send[None]
    for pair in [core] + place.z[::-1] + place.xy:
        (out,) = yield [out]
        (got,) = yield [place.flip(out, pair)]
        k = [below(h, b) for h, b in zip(have, pair)]
        blocks = out = merge(blocks, got, place.choose(k), place.mine(pair))
        have = (have[0] + [pair[0]], have[1] + [pair[1]])
    (out,) = yield [out]
    (got,) = yield [place.flip(out, core)]
    return blocks, got


def scatter(place, pairs):
    core = (place.core_bit, place.core_bit)
    bits = [1 << i for i in range(place.total.bit_length() - 1)]
    have = (bits, bits)
    for pair in place.xy[::-1] + place.z + [core]:
        have = tuple([b for b in h if b != bit] for h, bit in zip(have, pair))
        k = [below(h, b) for h, b in zip(have, pair)]
        dtype = f32 if pair == core else bf16
        send, keep = split(pairs, place.choose(k), place.mine(pair), dtype)
        (send,) = yield [send]
        (got,) = yield [place.flip(send, pair)]
        pairs = [(keep, got)]
    return keep[0], got[0]


class Chain:
    def __init__(self, steps):
        self.steps, self.flying, self.result = steps, False, None
        self.pending = next(steps)

    def done(self):
        return self.result is not None

    def move(self):
        try:
            self.pending = self.steps.send(self.pending)
        except StopIteration as stop:
            self.result = stop.value
        self.flying = not self.flying


def along(value, *chains):
    ending = [c for c in chains if c.flying]
    if ending:
        value, got = lax.optimization_barrier((value, [c.pending for c in ending]))
        for c, g in zip(ending, got):
            c.pending = g
            c.move()
    starting = [c for c in chains if not c.done()]
    if starting:
        value, sent = lax.optimization_barrier((value, [c.pending for c in starting]))
        for c, g in zip(starting, sent):
            c.pending = g
            c.move()
    return value


def finish(chain):
    while not chain.done():
        chain.move()
    return chain.result


def spatial_bias(scalar, rows, keys):
    key = lax.broadcasted_iota(jnp.int32, (1, rows) if keys == 1 else (rows, 1), keys)
    return jnp.where(key < scalar * scalar, 0.0, negative)


def temporal_bias(frames_local, scalar, rows, keys):
    def place(axis):
        index = lax.broadcasted_iota(jnp.int32, (rows, rows), axis)
        slot, at = index % GROUP, index // GROUP
        frame = ((at // frames_local) ^ scalar) * frames_local + at % frames_local
        return slot, frame

    slot_q, frame_q = place(1 - keys)
    slot_k, frame_k = place(keys)
    return jnp.where((slot_q == slot_k) & (frame_q >= frame_k), 0.0, negative)


def dot_t(a, b):
    return lax.dot_general(a, b, (((1,), (1,)), ((), ())), preferred_element_type=f32)


def t_dot(a, b):
    return lax.dot_general(a, b, (((0,), (0,)), ((), ())), preferred_element_type=f32)


def columns(scalar_ref, side, start):
    half = H * E // 2
    return pl.ds(pl.multiple_of((scalar_ref[1] ^ side) * half + start, LANES), LANES)


def two_heads(rows):
    half = lax.broadcasted_iota(jnp.int32, (rows, LANES), 1) < E

    def apart(x):
        return jnp.concatenate([jnp.where(half, x, 0), jnp.where(half, 0, x)], axis=0)

    def together(x):
        return jnp.where(half, x[:rows], x[rows:])

    return apart, together


def attention_forward(make_bias, scalar_ref, own_ref, other_ref, out_ref):
    a, b, width = own_ref.shape
    rows, width = a * b, width // 3
    bias = make_bias(scalar_ref[0], rows, 1)
    apart, together = two_heads(rows)
    factor = E ** (-0.5)
    for side, qkv_ref in enumerate((own_ref, other_ref)):
        for c in range(0, width, LANES):
            q = qkv_ref[:, :, c : c + LANES].reshape(rows, LANES) * bf16(factor)
            k = qkv_ref[:, :, width + c : width + c + LANES].reshape(rows, LANES)
            v = qkv_ref[:, :, 2 * width + c : 2 * width + c + LANES].reshape(rows, LANES)
            scores = dot_t(apart(q), k).reshape(2, rows, rows) + bias[None]
            weights = jnp.exp(scores - jnp.max(scores, axis=2, keepdims=True))
            scale = 1.0 / jnp.sum(weights, axis=2, keepdims=True)
            weights = weights.astype(bf16).reshape(2 * rows, rows)
            mixed = jnp.dot(weights, v, preferred_element_type=f32)
            mixed = together(mixed * scale.reshape(2 * rows, 1)).astype(out_ref.dtype)
            out_ref[:, :, columns(scalar_ref, side, c)] = mixed.reshape(a, b, LANES)


def attention_backward(make_bias, sides, scalar_ref, *refs):
    grad_ref = refs[len(sides)]
    a, b, width = refs[0].shape
    rows, width = a * b, width // 3
    bias = make_bias(scalar_ref[0], rows, 0)
    apart, together = two_heads(rows)
    factor = E ** (-0.5)
    for i, side in enumerate(sides):
        qkv_ref, out_ref = refs[i], refs[len(sides) + 1 + i]
        for c in range(0, width, LANES):
            q = qkv_ref[:, :, c : c + LANES].reshape(rows, LANES) * bf16(factor)
            k = qkv_ref[:, :, width + c : width + c + LANES].reshape(rows, LANES)
            v = qkv_ref[:, :, 2 * width + c : 2 * width + c + LANES].reshape(rows, LANES)
            g = grad_ref[:, :, columns(scalar_ref, side, c)].reshape(rows, LANES)
            scores = dot_t(apart(k), q).reshape(2, rows, rows) + bias[None]
            weights = jnp.exp(scores - jnp.max(scores, axis=1, keepdims=True))
            probs = weights * (1.0 / jnp.sum(weights, axis=1, keepdims=True))
            prob_grad = dot_t(apart(v), g).reshape(2, rows, rows)
            delta = jnp.sum(probs * prob_grad, axis=1, keepdims=True)
            score_grad = (probs * (prob_grad - delta)).astype(bf16)
            turned = jnp.concatenate([score_grad[0].T, score_grad[1].T], axis=0)
            dq = jnp.dot(turned, k, preferred_element_type=f32) * factor
            dk = jnp.dot(score_grad.reshape(2 * rows, rows), q, preferred_element_type=f32)
            dv = jnp.dot(
                probs.astype(bf16).reshape(2 * rows, rows), g, preferred_element_type=f32
            )
            for index, grad in enumerate((dq, dk, dv)):
                start = index * width + c
                merged = together(grad).astype(out_ref.dtype)
                out_ref[:, :, start : start + LANES] = merged.reshape(a, b, LANES)


def run_attention(body, scalars, block, grid, index, inputs, out_widths):
    a, b = block
    outer = inputs[0].shape[:2]
    rows = outer[0] * outer[1]
    return pl.pallas_call(
        body,
        grid=(grid,),
        in_specs=[pl.BlockSpec(memory_space=pltpu.SMEM)]
        + [pl.BlockSpec((a, b, x.shape[-1]), index) for x in inputs],
        out_specs=[pl.BlockSpec((a, b, width), index) for width in out_widths],
        out_shape=[jax.ShapeDtypeStruct((*outer, width), bf16) for width in out_widths],
        compiler_params=pltpu.CompilerParams(vmem_limit_bytes=VMEM),
        cost_estimate=pl.CostEstimate(
            flops=rows * H * E * 2 * a * b * 4,
            bytes_accessed=rows * 2 * (sum(x.shape[-1] for x in inputs) + sum(out_widths)),
            transcendentals=rows * H * a * b,
        ),
    )(scalars, *inputs)


def centre(x):
    average = jnp.mean(x, axis=-1, keepdims=True)
    centered = x - average
    variance = jnp.mean(centered * centered, axis=-1, keepdims=True)
    scale = lax.rsqrt(variance + 1e-05)
    return centered * scale, scale


def norm_body(x_ref, added_ref, gain_ref, shift_ref, out_ref):
    unit, _ = centre(x_ref[0].astype(f32) + added_ref[0])
    out_ref[0] = (unit * gain_ref[...] + shift_ref[...]).astype(out_ref.dtype)


def norm_back_body(x_ref, added_ref, gain_ref, grad_ref, rest_ref, out_ref, sums_ref):
    unit, scale = centre(x_ref[0].astype(f32) + added_ref[0])
    grad = grad_ref[0]
    scaled = grad * gain_ref[...]
    first = jnp.mean(scaled, axis=-1, keepdims=True)
    second = jnp.mean(scaled * unit, axis=-1, keepdims=True)
    out = rest_ref[0].astype(f32) + scale * (scaled - first - unit * second)
    out_ref[0] = out.astype(out_ref.dtype)
    terms = (grad * unit, grad, out)
    sums_ref[0] = jnp.concatenate([jnp.sum(x, axis=0, keepdims=True) for x in terms], axis=0)


def by_rows(body, arrays, rows, outs):
    blocks = arrays[0].shape[0]
    specs = []
    for x in arrays:
        if x.ndim == 2:
            specs.append(pl.BlockSpec(x.shape, lambda i: (0, 0)))
        else:
            at = (lambda i: (i, 0, 0)) if x.shape[0] == blocks else (lambda i: (0, 0, 0))
            specs.append(pl.BlockSpec((1, *x.shape[1:]), at))
    count = sum(x.size for x in arrays)
    return pl.pallas_call(
        body,
        grid=(blocks,),
        in_specs=specs,
        out_specs=[pl.BlockSpec((1, *shape[1:]), lambda i: (i, 0, 0)) for shape, _ in outs],
        out_shape=[jax.ShapeDtypeStruct(shape, dtype) for shape, dtype in outs],
        compiler_params=pltpu.CompilerParams(vmem_limit_bytes=VMEM),
        cost_estimate=pl.CostEstimate(
            flops=10 * count, bytes_accessed=4 * count, transcendentals=0
        ),
    )(*arrays)


def norm(x, added, gain, shift):
    shape = (x.shape[0] * x.shape[1] // 256, 256, x.shape[2])
    arrays = [x.reshape(shape), added, gain[None], shift[None]]
    (out,) = by_rows(norm_body, arrays, 256, [(shape, bf16)])
    return out.reshape(-1, shape[2])


def norm_back(x, added, gain, grad, rest, dtype):
    shape = (x.shape[0] * x.shape[1] // 256, 256, x.shape[2])
    arrays = [x.reshape(shape), added, gain[None], grad.reshape(shape), rest.reshape(shape)]
    sums = ((shape[0], 3, shape[2]), f32)
    out, sums = by_rows(norm_back_body, arrays, 256, [(shape, dtype), sums])
    return out.reshape(x.shape), sums


def matmul(inputs, weight):
    return jnp.dot(inputs, weight, preferred_element_type=f32)


TAIL = (
    0.14760860800743103, 0.14761532843112946, 0.127163827419281, 0.09018292278051376,
    0.013407237827777863, 0.06451446563005447, -0.19429759681224823, 0.13513216376304626,
    -0.031326886266469955,
)


def gelu(inner):
    size = jnp.abs(inner)
    t = 1.0 / (1.0 + 0.37 * size)
    bell = jnp.exp(inner * inner * -0.5)
    series = TAIL[-1]
    for term in reversed(TAIL[:-1]):
        series = series * t + term
    tail = series * t * bell
    cdf = jnp.where(inner > 0, 1.0 - tail, tail)
    return inner * cdf, cdf + inner * bell * 0.3989422804014327


def up_body(x_ref, w_ref, bias_ref, active_ref, slope_ref):
    rows = x_ref.shape[0]
    step = min(rows, 256)
    for r in range(0, rows, step):
        inner = jnp.dot(x_ref[r : r + step], w_ref[...], preferred_element_type=f32)
        active, slope = gelu(inner + bias_ref[...])
        active_ref[r : r + step] = active.astype(active_ref.dtype)
        slope_ref[r : r + step] = slope.astype(slope_ref.dtype)


def up_project(x, weight, bias):
    rows, width = x.shape
    cols, block = weight.shape[1], 512
    out = jax.ShapeDtypeStruct((rows, cols), bf16)
    return pl.pallas_call(
        up_body,
        grid=(cols // block,),
        in_specs=[
            pl.BlockSpec((rows, width), lambda i: (0, 0)),
            pl.BlockSpec((width, block), lambda i: (0, i)),
            pl.BlockSpec((1, block), lambda i: (0, i)),
        ],
        out_specs=[pl.BlockSpec((rows, block), lambda i: (0, i))] * 2,
        out_shape=[out, out],
        compiler_params=pltpu.CompilerParams(vmem_limit_bytes=VMEM),
        cost_estimate=pl.CostEstimate(
            flops=2 * rows * width * cols,
            bytes_accessed=2 * (rows * width + width * cols + 2 * rows * cols),
            transcendentals=rows * cols,
        ),
    )(x, weight, bias)


def on_device(
    tokens,
    actions,
    sides,
    action_table,
    norm_gains,
    norm_shifts,
    s_qkv,
    s_out,
    t_qkv,
    t_out,
    w_up,
    b_up,
    w_down,
    b_down,
    grad_out,
):
    shape = tokens.shape
    frames_local, _, slots, width = shape
    place = Place()
    total, core, tm_size = place.total, place.core, place.tm_size
    slots_local = slots // tm_size
    row_count = frames_local * slots
    half = width // 2

    def to_slots(value):
        view = value.reshape(frames_local, tm_size, slots_local, value.shape[-1])
        parts = []
        for o in range(tm_size):
            part = lax.dynamic_index_in_dim(view, place.tm ^ o, 1, keepdims=False)
            parts.append(place.tm_flip(part, o) if o else part)
        return parts

    def from_slots(value):
        view = value.reshape(tm_size, frames_local, slots_local, value.shape[-1])
        return [place.tm_flip(view[o], o) if o else view[o] for o in range(tm_size)]

    def in_slots(parts):
        return jnp.concatenate(parts, axis=0)

    def in_frames(parts):
        return jnp.stack(unscramble(parts, place.tm), axis=1).reshape(frames_local, slots, -1)

    def own_and_other(value, axis):
        first, second = (lax.index_in_dim(value, i, axis, keepdims=False) for i in (0, 1))
        return jnp.where(core == 0, first, second), jnp.where(core == 0, second, first)

    def in_order(own, other, axis):
        pair = [jnp.where(core == 0, own, other), jnp.where(core == 0, other, own)]
        return jnp.stack(pair, axis=axis)

    def halves(value):
        first, second = value[:, :half], value[:, half:]
        return jnp.where(core == 0, first, second), jnp.where(core == 0, second, first)

    def woven(own, other):
        cuts = [slice(i, i + half) for i in range(0, own.shape[1], half)]
        own_first = [x[:, cut] for cut in cuts for x in (own, other)]
        other_first = [x[:, cut] for cut in cuts for x in (other, own)]
        return jnp.where(
            core == 0,
            jnp.concatenate(own_first, axis=1),
            jnp.concatenate(other_first, axis=1),
        )

    def joined(own, other):
        return jnp.where(
            core == 0,
            jnp.concatenate([own, other], axis=1),
            jnp.concatenate([other, own], axis=1),
        )

    thin = width // total
    counts = [ACTIONS, 3, 3, 1]
    ends = [sum(counts[:i]) for i in range(len(counts) + 1)]
    small = jnp.concatenate([action_table, norm_gains, norm_shifts, b_down[None]], axis=0).T
    small = jnp.pad(small, ((0, 0), (0, LANES - ends[-1])))
    b_up = jnp.pad(b_up[None], ((0, GROUP - 1), (0, LANES - b_up.shape[0])))
    small = jnp.concatenate([small, b_up], axis=0)

    rows = s_qkv.shape[0]
    hidden_half = w_down.shape[0] // 2

    def attention_group(qkv, out):
        qkv = own_and_other(qkv.reshape(rows, 3, 2, half), 2)
        both = [
            jnp.concatenate([a.reshape(rows, 3 * half), b], axis=1)
            for a, b in zip(qkv, halves(out))
        ]
        return Chain(gather(place, *both))

    front = attention_group(s_qkv, s_out)
    tokens = along(tokens, front)
    tokens, small, grad_out = lax.optimization_barrier((tokens, small, grad_out))
    tokens = along(tokens, front)
    cotangent = to_slots(grad_out.reshape(frames_local, slots, width))
    small = Chain(gather_small(place, small))
    tokens = along(tokens, small)
    tokens = along(tokens, small)
    tokens, t_qkv, t_out = lax.optimization_barrier((tokens, t_qkv, t_out))
    tokens = along(tokens, front)
    middle = attention_group(t_qkv, t_out)
    tokens = along(tokens, middle)
    tokens, cotangent = lax.optimization_barrier((tokens, cotangent))
    tokens = along(tokens, front, small)
    tokens, w_up, w_down = lax.optimization_barrier((tokens, w_up, w_down))
    up_pair = own_and_other(w_up.reshape(rows, total, 2, hidden_half), 2)
    rising = Chain(gather(place, *[x.reshape(rows, -1) for x in up_pair]))
    falling = Chain(gather(place, *own_and_other(w_down.reshape(2, hidden_half, width), 0)))
    tokens = along(tokens, small, middle)
    while not small.done():
        tokens = along(tokens, small)
    small = small.result.astype(f32)
    table = small[:, :thin].reshape(width, LANES).T

    def unpack(i):
        return table[ends[i] : ends[i + 1]]

    action_rows, gains, shifts, down_bias = [unpack(i) for i in range(4)]
    up_bias = small[:, thin, : 2 * hidden_half].reshape(total, 2, hidden_half)
    up_bias = [x.reshape(1, -1) for x in own_and_other(up_bias, 1)]

    onehot = (actions == jnp.arange(ACTIONS)[None, :]).astype(f32)
    embedded = jnp.dot(onehot, action_rows, precision=highest)
    tokens = tokens.reshape(frames_local, slots, width)
    embedded = embedded[:, None, :]
    tokens, embedded = along((tokens, embedded), front, middle)
    normed1 = norm(tokens, embedded, gains[0], shifts[0])
    normed1 = along(normed1, rising)
    normed1 = along(normed1, front, middle)
    whole = [x.reshape(width, -1) for x in finish(front)]
    sq_halves = [x[:, : 3 * half] for x in whole]

    def project(x, halves, outer):
        return [matmul(x, w).astype(bf16).reshape(*outer, -1) for w in halves]

    spatial = project(normed1, sq_halves, (frames_local, slots))
    spatial = along(spatial, middle, rising)

    def frame_index(i):
        return (i, 0, 0)

    def slot_index(i):
        return (0, i, 0)

    spatial_place = (
        jnp.stack([sides[0], core.astype(jnp.int32)]), (1, slots), frames_local, frame_index,
    )
    (s_mixed,) = run_attention(
        partial(attention_forward, spatial_bias), *spatial_place, spatial, [width]
    )
    s_mixed = s_mixed.reshape(row_count, width)
    so_full = joined(*[x[:, 3 * half :] for x in whole])
    hidden0 = tokens.astype(f32) + embedded
    hidden1 = hidden0 + matmul(s_mixed, so_full).reshape(tokens.shape)

    hidden1 = along(hidden1.astype(bf16), middle, rising, falling)
    parts = to_slots(hidden1)
    hidden1 = in_slots(parts)
    frames = hidden1.shape[0]
    slot_at = place.tm * slots_local + jnp.arange(slots_local)
    mask = (slot_at < sides[0] * sides[0])[None, :, None]
    nothing = jnp.zeros((1, 1, width), f32)
    normed2 = norm(hidden1, nothing, gains[1], shifts[1])
    whole = [x.reshape(width, -1) for x in finish(middle)]
    tq_halves = [x[:, : 3 * half] for x in whole]
    to_full = joined(*[x[:, 3 * half :] for x in whole])
    normed2 = along(normed2, rising, falling)
    temporal = project(normed2, tq_halves, (frames, slots_local))
    temporal = along(temporal, rising, falling)
    temporal_place = (
        jnp.stack([place.tm.astype(jnp.int32), core.astype(jnp.int32)]), (frames, GROUP),
        slots_local // GROUP, slot_index,
    )
    make_bias = partial(temporal_bias, frames_local)
    (t_mixed,) = run_attention(
        partial(attention_forward, make_bias), *temporal_place, temporal, [width]
    )
    t_mixed = t_mixed.reshape(row_count, width)
    hidden2 = hidden1.astype(f32) + matmul(t_mixed, to_full).reshape(hidden1.shape)
    normed3 = norm(hidden2, nothing, gains[2], shifts[2])
    normed3 = along(normed3, rising, falling)
    up_halves = [x.reshape(width, -1) for x in finish(rising)]
    first = up_project(normed3, up_halves[0], up_bias[0])
    first = along(first, falling)
    normed3, first = lax.optimization_barrier((normed3, first))
    second = up_project(normed3, up_halves[1], up_bias[1])
    second = along(second, falling)
    (active, slope), (active2, slope2) = first, second
    down_halves = [x.reshape(-1, width) for x in finish(falling)]
    hidden3 = hidden2.reshape(row_count, width) + matmul(active, down_halves[0]) + down_bias
    hidden3 = hidden3 + matmul(active2, down_halves[1])
    mixed = from_slots(jnp.where(mask, hidden3.reshape(hidden2.shape), 0).astype(bf16))

    def blocks(grad):
        return grad.astype(bf16).reshape(total, grad.shape[0] // total, grad.shape[1])

    core_pair = (place.core_bit, place.core_bit)

    def exchanged(grad):
        return place.flip(blocks(grad), core_pair)

    def sums(keeps, gots):
        return Chain(scatter(place, [(blocks(x), y) for x, y in zip(keeps, gots)]))

    down_in = jnp.where(mask, in_slots(cotangent), 0).reshape(row_count, width)
    send = t_dot(active2, down_in).astype(bf16)
    down_in, send, active = lax.optimization_barrier((down_in, send, active))
    got = exchanged(send)
    keep = t_dot(active, down_in).astype(bf16)
    down_in, keep = lax.optimization_barrier((down_in, keep))
    inner_grad = (dot_t(down_in, down_halves[0]) * slope.astype(f32)).astype(bf16)
    s_down = sums([keep], [got])
    down_in, inner_grad = along((down_in, inner_grad), s_down)
    inner_grad2 = (dot_t(down_in, down_halves[1]) * slope2.astype(f32)).astype(bf16)
    send = t_dot(normed3, inner_grad2).astype(bf16)
    inner_grad, inner_grad2, send, mixed = lax.optimization_barrier(
        (inner_grad, inner_grad2, send, mixed)
    )
    mixed = in_frames(mixed)
    got = exchanged(send)
    keep = t_dot(normed3, inner_grad).astype(bf16)
    inner_grad, keep = lax.optimization_barrier((inner_grad, keep))
    normed3_grad = dot_t(inner_grad, up_halves[0])
    s_up = sums([keep], [got])
    normed3_grad, inner_grad2 = along((normed3_grad, inner_grad2), s_down, s_up)
    normed3_grad = normed3_grad + dot_t(inner_grad2, up_halves[1])
    g_b_down = jnp.sum(down_in.astype(f32), axis=0)
    g_b_up = in_order(
        *[jnp.sum(x.astype(f32), axis=0).reshape(total, -1) for x in (inner_grad, inner_grad2)], 1
    )
    grad2, sums3 = norm_back(hidden2, nothing, gains[2], normed3_grad, down_in, bf16)
    t_in = grad2.reshape(row_count, width)

    def out_grads(mixed_in, grad):
        return [t_dot(mixed_in, x).astype(bf16) for x in halves(grad)]

    g_t_out = out_grads(t_mixed, t_in)
    t_mix_grad = dot_t(t_in, to_full).astype(bf16).reshape(frames, slots_local, width)

    def back(side, where, make, values, grad):
        (out,) = run_attention(
            partial(attention_backward, make, (side,)), *where, [values[side], grad], [3 * half]
        )
        return out.reshape(row_count, -1)

    t_grad2 = back(1, temporal_place, make_bias, temporal, t_mix_grad)
    t_grad2, t_mix_grad, g_t_out = lax.optimization_barrier((t_grad2, t_mix_grad, g_t_out))
    t_mix_grad = along(t_mix_grad, s_down, s_up)
    t_grad = back(0, temporal_place, make_bias, temporal, t_mix_grad)
    t_grad, t_grad2 = lax.optimization_barrier((t_grad, t_grad2))
    normed2_grad = dot_t(t_grad, tq_halves[0]) + dot_t(t_grad2, tq_halves[1])
    grad1, sums2 = norm_back(hidden1, nothing, gains[1], normed2_grad, grad2, bf16)
    grad1, t_grad, t_grad2 = lax.optimization_barrier((grad1, t_grad, t_grad2))
    parts = from_slots(grad1)
    send = t_dot(normed2, t_grad2).astype(bf16)
    send, t_grad = lax.optimization_barrier((send, t_grad))
    t_gots = [exchanged(send), exchanged(g_t_out[1])]
    keep = t_dot(normed2, t_grad).astype(bf16)
    keep = along(keep, s_down, s_up)
    parts[0], keep = lax.optimization_barrier((parts[0], keep))
    s_time = sums([keep, g_t_out[0]], t_gots)
    grad1 = in_frames(parts)
    grad1 = along(grad1, s_time)
    s_in = grad1.reshape(row_count, width)
    g_s_out = out_grads(s_mixed, s_in)
    mix_grad = dot_t(s_in, so_full).astype(bf16).reshape(frames_local, slots, width)
    s_got = exchanged(g_s_out[1])
    mix_grad = along(mix_grad, s_up, s_down)
    s_grad2 = back(1, spatial_place, spatial_bias, spatial, mix_grad)
    mix_grad, s_grad2 = along((mix_grad, s_grad2), s_time, s_up)
    send = t_dot(normed1, s_grad2).astype(bf16)
    mix_grad, send = lax.optimization_barrier((mix_grad, send))
    got = exchanged(send)
    s_grad = back(0, spatial_place, spatial_bias, spatial, mix_grad)
    s_grad = along(s_grad, s_time)
    keep = t_dot(normed1, s_grad).astype(bf16)
    keep, s_grad, s_grad2, s_got = lax.optimization_barrier((keep, s_grad, s_grad2, s_got))
    s_space = sums([keep, g_s_out[0]], [got, s_got])
    s_grad, s_grad2 = along((s_grad, s_grad2), s_space)
    normed1_grad = dot_t(s_grad, sq_halves[0])
    normed1_grad, s_grad2 = along((normed1_grad, s_grad2), s_time)
    normed1_grad = normed1_grad + dot_t(s_grad2, sq_halves[1])
    input_grad, sums1 = norm_back(tokens, embedded, gains[0], normed1_grad, grad1, f32)
    sums1 = along(sums1, s_time, s_space)
    g_actions = jnp.dot(onehot.T, sums1[:, 2], precision=highest)

    terms = [
        g_actions,
        jnp.stack([jnp.sum(x[:, 0], axis=0) for x in (sums1, sums2, sums3)]),
        jnp.stack([jnp.sum(x[:, 1], axis=0) for x in (sums1, sums2, sums3)]),
        g_b_up.reshape(1, -1),
        g_b_down[None],
    ]
    packed = [jnp.moveaxis(x.reshape(x.shape[0], total, -1), 1, 0).reshape(total, -1) for x in terms]
    packed = jnp.concatenate(packed, axis=1)
    packed = jnp.pad(packed, ((0, 0), (0, -packed.shape[1] % LANES)))
    s_small = Chain(scatter_small(place, packed))
    g_w_down = in_order(*finish(s_down), 0).reshape(w_down.shape)
    g_w_up = in_order(*[x.reshape(rows, total, -1) for x in finish(s_up)], 2).reshape(w_up.shape)
    packed, g_w_down, g_w_up = lax.optimization_barrier((packed, g_w_down, g_w_up))
    while not (s_time.done() and s_space.done()):
        for _ in range(2):
            if not s_small.done():
                packed = along(packed, s_small)
        packed = along(packed, *[c for c in (s_space, s_time) if not c.done()])
    summed = finish(s_small)
    t_rows, s_rows = woven(*s_time.result), woven(*s_space.result)
    g_t_qkv, g_t_out = t_rows[:, : 3 * width], t_rows[:, 3 * width :]
    g_s_qkv, g_s_out = s_rows[:, : 3 * width], s_rows[:, 3 * width :]

    sizes = [x.size // total for x in terms]
    starts = [sum(sizes[:i]) for i in range(len(sizes) + 1)]

    def piece(i, count):
        return summed[starts[i] : starts[i + 1]].reshape(count, -1)

    return (
        mixed.reshape(shape),
        input_grad.reshape(shape),
        piece(0, ACTIONS),
        piece(1, 3),
        piece(2, 3),
        g_s_qkv,
        g_s_out,
        g_t_qkv,
        g_t_out,
        g_w_up,
        piece(3, 1).reshape(-1),
        g_w_down,
        piece(4, 1).reshape(-1),
    )


def solution(mesh):
    whole = P(("tm", "clip"), None)
    spread = P(None, ("tm", "clip"))
    frames = P("tm", "clip", None, None)
    vector = P(("tm", "clip"))
    return jax.shard_map(
        on_device,
        mesh=mesh,
        in_specs=(
            frames, P("tm", "clip"), P("clip"), spread, spread, spread, whole, whole, whole,
            whole, whole, vector, whole, vector, frames,
        ),
        out_specs=(
            frames, frames, spread, spread, spread, whole, whole, whole, whole, whole, vector,
            whole, vector,
        ),
        check_vma=False,
    )
```

time: 939 us -> 713 us (0.76)
  waiting for transfers between devices: 410 us -> 168 us
  Pallas kernels: 101 us -> 201 us
  other arithmetic: 82.7 us -> 25.5 us
  matrix products: 204 us -> 165 us
  starting transfers between devices: 58.9 us -> 76.8 us
  between operations: 16.2 us -> 3.77 us
    all_gather x4 -> x0, waiting for transfers between devices: 161 us -> none  [gathered(): return lax.all_gather(x, AXES, axis=0, tiled=True)]
    pallas_call x0 -> x53, Pallas kernels: none -> 139 us  [the longest x20 49 us: split(): pl.pallas_call(partial(split_body, ends), grid=(n // block,), in_specs=in...]
    ppermute x57 -> x72, waiting for transfers between devices: 247 us -> 168 us  [the longest x60 133 us: flip(): return lax.ppermute(value, AXES, moves)]
    convert_element_type x37 -> x2, other arithmetic: 56.7 us -> 0.82 us  [the longest x1 0.76 us: on_device(): jnp.where(mask, hidden3.reshape(hidden2.shape), 0).astype(bf16)]
    pallas_call x4 -> x6, Pallas kernels: 101 us -> 62 us  [run_attention(): pl.pallas_call(body, grid=(grid,), in_specs=[pl.BlockSpec(memory_space=pl...]
    dot_general x19 -> x31, matrix products: 203 us -> 165 us  [the longest x10 59 us: dot_t(): lax.dot_general(a, b, (((1,), (1,)), ((), ())), preferred_element_type=f32)]
    squeeze x37 -> x2, local copies, waits for them, and re-layouts: 22.4 us -> 1.61 us  [to_slots(): part = lax.dynamic_index_in_dim(view, place.tm ^ o, 1, keepdims=False)]
    ppermute x57 -> x72, starting transfers between devices: 58.8 us -> 76.8 us  [the longest x60 68.6 us: flip(): return lax.ppermute(value, AXES, moves)]
  transfers between devices with their start and end apart: 61 -> 72, of which waited for: 33 -> 35; matrix products, arithmetic and copies ran while one was open for 22% -> 29% of each run, Pallas kernels for 11% -> 17%
where the time goes in v2:
time: 713 us; the launch traced here: 707 us
  Pallas kernels  201 us (28%)
  waiting for transfers between devices  168 us (24%)
  matrix products  165 us (23%)
  starting transfers between devices  76.8 us (11%)
  local copies, waits for them, and re-layouts  68.1 us (10%)
  other arithmetic  25.5 us (4%)
    ppermute x60, waiting for transfers between devices, flip(): return lax.ppermute(value, AXES, moves)  133 us
    ppermute x60, starting transfers between devices, flip(): return lax.ppermute(value, AXES, moves)  68.6 us
    pallas_call x6, Pallas kernels, run_attention(): pl.pallas_call(body, grid=(grid,), in_specs=[pl.BlockSpec(memory_space=pl...  62 us
    dot_general x10, matrix products, dot_t(): lax.dot_general(a, b, (((1,), (1,)), ((), ())), preferred_element_type=f32)  59 us
    dot_general x12, matrix products, t_dot(): lax.dot_general(a, b, (((0,), (0,)), ((), ())), preferred_element_type=f32)  55 us
    dot_general x8, matrix products, matmul(): return jnp.dot(inputs, weight, preferred_element_type=f32)  50.4 us
    pallas_call x20, Pallas kernels, split(): pl.pallas_call(partial(split_body, ends), grid=(n // block,), in_specs=in...  49 us
    ppermute x12, waiting for transfers between devices, tm_flip(): return lax.ppermute(value, AXES, moves)  35 us
  transfers between devices with their start and end apart: 72, of which 35 were waited for; matrix products, arithmetic and copies ran while one was open for 29% of the time, Pallas kernels for 17%

profile of v2, /device:TPU:1, one launch (start us, length us, event | category | flops | bytes accessed | tf_op | source)
XLA Modules:
  0.0 707.5 jit_solution(10737376912888408175)
XLA Ops:
  19.0 10.5 %collective-permute-done.2.other_ref = bf16[2,32,2048]{2,1,0:T(8,128)(2,1)S(1)} collective-permute-done((bf16[2,32,2048]{2,1,0:T(8,128)(2,1)S(1)}, bf16[2,32,2048]{2,1,0:T(8,128)(2,1)S(1)}, u32[]{:S(2)}, u32[]{:S(2)}) %collective-permute-start.2) | collective-permute-done | bytes 262176 | tf_op jit(solution)/shard_map/ppermute | solution.py:49
  47.8 10.7 %collective-permute-done.8.other_ref = bf16[4,48,128]{2,1,0:T(8,128)(2,1)S(1)} collective-permute-done((bf16[4,48,128]{2,1,0:T(8,128)(2,1)S(1)}, bf16[4,48,128]{2,1,0:T(8,128)(2,1)S(1)}, u32[]{:S(2)}, u32[]{:S(2)}) %collective-permute-start.8) | collective-permute-done | bytes 49184 | tf_op jit(solution)/shard_map/ppermute | solution.py:49
  69.5 9.2 %collective-permute-done.11.other_ref = bf16[16,48,128]{2,1,0:T(8,128)(2,1)S(1)} collective-permute-done((bf16[16,48,128]{2,1,0:T(8,128)(2,1)S(1)}, bf16[16,48,128]{2,1,0:T(8,128)(2,1)S(1)}, u32[]{:S(2)}, u32[]{:S(2)}) %collective-permute-start.11) | collective-permute-done | bytes 196640 | tf_op jit(solution)/shard_map/ppermute | solution.py:49
  129.7 7.8 %convolution_convert_fusion.6 = bf16[1024,1536]{1,0:T(8,128)(2,1)} fusion(bf16[1024,1024]{1,0:T(8,128)(2,1)S(1)} %bitcast.280, bf16[1024,2048]{1,0:T(8,128)(2,1)} %bitcast.33), kind=kOutput, calls=%fused_computation.17 | convolution fusion | flops 3222798336 | bytes 8388608 | tf_op jit(solution)/shard_map/dot_general | solution.py:417
  144.4 7.8 %shard_map.262 = bf16[4,256,1024]{2,1,0:T(8,128)(2,1)S(1)} custom-call(s32[2]{0:T(128)S(1)} %pad_add_fusion.9.scalar_ref, bf16[4,256,1536]{2,1,0:T(8,128)(2,1)S(1)} %bitcast.249, bf16[4,256,1536]{2,1,0:T(8,128)(2,1)} %bitcast.307), custom_call_target="tpu_custom_call" | custom-call | flops 2147483648 | bytes 8388608 | tf_op jit(solution)/shard_map/pallas_call | solution.py:337
  183.3 11.8 %collective-permute-done.23 = bf16[4,64,1024]{2,1,0:T(8,128)(2,1)S(1)} collective-permute-done((bf16[4,64,1024]{2,1,0:T(8,128)(2,1)S(1)}, bf16[4,64,1024]{2,1,0:T(8,128)(2,1)S(1)}, u32[]{:S(2)}, u32[]{:S(2)}) %collective-permute-start.23) | collective-permute-done | bytes 524320 | tf_op jit(solution)/shard_map/ppermute | solution.py:53
  206.5 7.8 %convolution_convert_fusion.4 = bf16[1024,1536]{1,0:T(8,128)(2,1)} fusion(bf16[1024,1024]{1,0:T(8,128)(2,1)S(1)} %bitcast.276, bf16[1024,2048]{1,0:T(8,128)(2,1)} %bitcast.48), kind=kOutput, calls=%fused_computation.15 | convolution fusion | flops 3222798336 | bytes 8388608 | tf_op jit(solution)/shard_map/dot_general | solution.py:417
  224.0 7.9 %shard_map.270 = bf16[16,64,1024]{2,1,0:T(8,128)(2,1)S(1)} custom-call(s32[2]{0:T(128)S(1)} %pad_add_fusion.11.scalar_ref, bf16[16,64,1536]{2,1,0:T(8,128)(2,1)S(1)} %bitcast.251, bf16[16,64,1536]{2,1,0:T(8,128)(2,1)} %bitcast.309), custom_call_target="tpu_custom_call" | custom-call | flops 2147483648 | bytes 8388608 | tf_op jit(solution)/shard_map/pallas_call | solution.py:337
  249.2 16.5 %shard_map.274 = (bf16[1024,2048]{1,0:T(8,128)(2,1)}, bf16[1024,2048]{1,0:T(8,128)(2,1)}) custom-call(bf16[1024,1024]{1,0:T(8,128)(2,1)S(1)} %bitcast.283, bf16[1024,2048]{1,0:T(8,128)(2,1)} %bitcast.318, f32[1,2048]{1,0:T(1,128)S(1)} %select_n.824.bias_ref), custom_call_target="tpu_custom_call" | custom-call | flops 4294967296 | bytes 14680064 | tf_op jit(solution)/shard_map/pallas_call | solution.py:453
  272.7 16.4 %shard_map.276 = (bf16[1024,2048]{1,0:T(8,128)(2,1)}, bf16[1024,2048]{1,0:T(8,128)(2,1)}) custom-call(bf16[1024,1024]{1,0:T(8,128)(2,1)S(1)} %bitcast.284, bf16[1024,2048]{1,0:T(8,128)(2,1)} %bitcast.54.w_ref, f32[1,2048]{1,0:T(1,128)S(1)} %select_n.826.bias_ref), custom_call_target="tpu_custom_call" | custom-call | flops 4294967296 | bytes 14680064 | tf_op jit(solution)/shard_map/pallas_call | solution.py:453
  325.1 10.6 %fusion.1 = bf16[1024,1024]{1,0:T(8,128)(2,1)S(1)} fusion(f32[1024,1024]{1,0:T(8,128)} %fusion.66, f32[16,64,1024]{2,1,0:T(8,128)S(1)} %copy-done.87, f32[1024]{0:T(1024)S(1)} %bitcast.357, bf16[1024,2048]{1,0:T(8,128)(2,1)} %get-tuple-element.394, bf16[2048,1024]{1,0:T(8,128)(2,1)} %bitcast.58), kind=kOutput, calls=%fused_computation.6 | convolution fusion | flops 4299161600 | bytes 18878464 | tf_op jit(solution)/shard_map/dot_general | solution.py:417
  346.2 7.9 %multiply_convert_fusion = bf16[1024,2048]{1,0:T(8,128)(2,1)S(1)} fusion(bf16[1024,2048]{1,0:T(8,128)(2,1)} %get-tuple-element.406, bf16[1024,1024]{1,0:T(8,128)(2,1)S(1)} %bitcast_select_fusion, bf16[2048,1024]{1,0:T(8,128)(2,1)} %bitcast.58), kind=kOutput, calls=%fused_computation.2 | convolution fusion | flops 4301258752 | bytes 14680064 | tf_op jit(solution)/shard_map/dot_general | solution.py:257
  374.7 13.6 %collective-permute-done.39.refs_1_ = bf16[16,64,1024]{2,1,0:T(8,128)(2,1)S(1)} collective-permute-done((bf16[16,64,1024]{2,1,0:T(8,128)(2,1)S(1)}, bf16[16,64,1024]{2,1,0:T(8,128)(2,1)S(1)}, u32[]{:S(2)}, u32[]{:S(2)}) %collective-permute-start.39) | collective-permute-done | bytes 2097184 | tf_op jit(solution)/shard_map/ppermute | solution.py:49
  398.6 7.8 %fusion.68 = f32[1024,1024]{1,0:T(8,128)S(1)} fusion(bf16[1024,2048]{1,0:T(8,128)(2,1)} %copy-done.90, bf16[1024,2048]{1,0:T(8,128)(2,1)} %bitcast.54.w_ref), kind=kOutput, calls=%fused_computation.222 | convolution fusion | flops 4294967296 | bytes 12582912 | tf_op jit(solution)/shard_map/dot_general | solution.py:257
  418.2 11.6 %shard_map.282 = bf16[16,64,1536]{2,1,0:T(8,128)(2,1)S(1)} custom-call(s32[2]{0:T(128)S(1)} %copy-done.79, bf16[16,64,1536]{2,1,0:T(8,128)(2,1)} %bitcast.310, bf16[16,64,1024]{2,1,0:T(8,128)(2,1)S(1)} %bitcast.262), custom_call_target="tpu_custom_call" | custom-call | flops 2147483648 | bytes 8388608 | tf_op jit(solution)/shard_map/pallas_call | solution.py:337
  442.5 11.8 %shard_map.285 = bf16[16,64,1536]{2,1,0:T(8,128)(2,1)S(1)} custom-call(s32[2]{0:T(128)S(1)} %copy-done.79, bf16[16,64,1536]{2,1,0:T(8,128)(2,1)} %bitcast.252, bf16[16,64,1024]{2,1,0:T(8,128)(2,1)S(1)} %bitcast.263), custom_call_target="tpu_custom_call" | custom-call | flops 2147483648 | bytes 8388608 | tf_op jit(solution)/shard_map/pallas_call | solution.py:337
  487.9 9.5 %collective-permute-done.46.refs_1_ = bf16[4,64,1024]{2,1,0:T(8,128)(2,1)} collective-permute-done((bf16[4,64,1024]{2,1,0:T(8,128)(2,1)}, bf16[4,64,1024]{2,1,0:T(8,128)(2,1)}, u32[]{:S(2)}, u32[]{:S(2)}) %collective-permute-start.46) | collective-permute-done | bytes 524320 | tf_op jit(solution)/shard_map/ppermute | solution.py:49
  510.2 7.5 %collective-permute-done.44 = bf16[4,64,1024]{2,1,0:T(8,128)(2,1)S(1)} collective-permute-done((bf16[4,64,1024]{2,1,0:T(8,128)(2,1)S(1)}, bf16[4,64,1024]{2,1,0:T(8,128)(2,1)S(1)}, u32[]{:S(2)}, u32[]{:S(2)}) %collective-permute-start.44) | collective-permute-done | bytes 524320 | tf_op jit(solution)/shard_map/ppermute | solution.py:53
  532.2 9.7 %collective-permute-done.51.refs_1_ = bf16[2,64,1024]{2,1,0:T(8,128)(2,1)S(1)} collective-permute-done((bf16[2,64,1024]{2,1,0:T(8,128)(2,1)S(1)}, bf16[2,64,1024]{2,1,0:T(8,128)(2,1)S(1)}, u32[]{:S(2)}, u32[]{:S(2)}) %collective-permute-start.51) | collective-permute-done | bytes 262176 | tf_op jit(solution)/shard_map/ppermute | solution.py:49
  547.7 11.4 %shard_map.292 = bf16[4,256,1536]{2,1,0:T(8,128)(2,1)S(1)} custom-call(s32[2]{0:T(128)S(1)} %copy-done.77, bf16[4,256,1536]{2,1,0:T(8,128)(2,1)} %bitcast.308, bf16[4,256,1024]{2,1,0:T(8,128)(2,1)S(1)} %bitcast.260), custom_call_target="tpu_custom_call" | custom-call | flops 2147483648 | bytes 8388608 | tf_op jit(solution)/shard_map/pallas_call | solution.py:337
  585.2 11.4 %shard_map.295 = bf16[4,256,1536]{2,1,0:T(8,128)(2,1)S(1)} custom-call(s32[2]{0:T(128)S(1)} %copy-done.77, bf16[4,256,1536]{2,1,0:T(8,128)(2,1)} %bitcast.250, bf16[4,256,1024]{2,1,0:T(8,128)(2,1)S(1)} %bitcast.261), custom_call_target="tpu_custom_call" | custom-call | flops 2147483648 | bytes 8388608 | tf_op jit(solution)/shard_map/pallas_call | solution.py:337
  675.8 7.8 %collective-permute-done.69.refs_1_ = bf16[4,32,2048]{2,1,0:T(8,128)(2,1)S(1)} collective-permute-done((bf16[4,32,2048]{2,1,0:T(8,128)(2,1)S(1)}, bf16[4,32,2048]{2,1,0:T(8,128)(2,1)S(1)}, u32[]{:S(2)}, u32[]{:S(2)}) %collective-permute-start.69) | collective-permute-done | bytes 524320 | tf_op jit(solution)/shard_map/ppermute | solution.py:49
  684.8 8.4 %collective-permute-done.70.refs_1_ = bf16[2,32,2048]{2,1,0:T(8,128)(2,1)S(1)} collective-permute-done((bf16[2,32,2048]{2,1,0:T(8,128)(2,1)S(1)}, bf16[2,32,2048]{2,1,0:T(8,128)(2,1)S(1)}, u32[]{:S(2)}, u32[]{:S(2)}) %collective-permute-start.70) | collective-permute-done | bytes 262176 | tf_op jit(solution)/shard_map/ppermute | solution.py:49
  693.8 9.1 %collective-permute-start.71 = (f32[1,32,2048]{2,1,0:T(8,128)S(1)}, f32[1,32,2048]{2,1,0:T(8,128)S(1)}, u32[]{:S(2)}, u32[]{:S(2)}) collective-permute-start(f32[1,32,2048]{2,1,0:T(8,128)S(1)} %get-tuple-element.540), channel_id=1, source_target_pairs={{0,8},{1,9},{2,10},{3,11},{4,12},{5,13},{6,14},{7,15},{8,0},{9,1},... | collective-permute-start | bytes 786440 | tf_op jit(solution)/shard_map/ppermute | solution.py:49
  (606 shorter events, 459.1 us)
Async XLA Ops:
  9.1 23.4 %collective-permute-start.3 = (bf16[4,64,1024]{2,1,0:T(8,128)(2,1)}, bf16[4,64,1024]{2,1,0:T(8,128)(2,1)S(1)}, u32[]{:S(2)}, u32[]{:S(2)}) collective-permute-start(bf16[4,64,1024]{2,1,0:T(8,128)(2,1)} %get-tuple-element.601), channel_id=1, source_target_pairs={{0,8},{1,9},{2,10},{3,11},{4,12},{5,13},{6,14},{7,15},{8,0},{9,1},... | collective-permute-start | bytes 1572872 | tf_op jit(solution)/shard_map/ppermute | solution.py:53
  11.9 23.9 %collective-permute-start.5 = (bf16[4,64,1024]{2,1,0:T(8,128)(2,1)}, bf16[4,64,1024]{2,1,0:T(8,128)(2,1)S(1)}, u32[]{:S(2)}, u32[]{:S(2)}) collective-permute-start(bf16[4,64,1024]{2,1,0:T(8,128)(2,1)} %get-tuple-element.599), channel_id=1, source_target_pairs={{0,24},{1,25},{2,26},{3,27},{4,28},{5,29},{6,30},{7,31},{8,16},{9,... | collective-permute-start | bytes 1572872 | tf_op jit(solution)/shard_map/ppermute | solution.py:53
  43.4 38.1 %collective-permute-start.12 = (bf16[8,32,2048]{2,1,0:T(8,128)(2,1)S(1)}, bf16[8,32,2048]{2,1,0:T(8,128)(2,1)S(1)}, u32[]{:S(2)}, u32[]{:S(2)}) collective-permute-start(bf16[8,32,2048]{2,1,0:T(8,128)(2,1)S(1)} %shard_map.249.mine_ref), channel_id=1, source_target_pairs={{0,1},{1,0},{2,3},{3,2},{4,5},{5,4},{6,7},{7,6},{8,24},{9,25},{10,... | collective-permute-start | bytes 3145736 | tf_op jit(solution)/shard_map/ppermute | solution.py:49
  87.5 25.2 %collective-permute-start.14 = (bf16[16,32,2048]{2,1,0:T(8,128)(2,1)}, bf16[16,32,2048]{2,1,0:T(8,128)(2,1)}, u32[]{:S(2)}, u32[]{:S(2)}) collective-permute-start(bf16[16,32,2048]{2,1,0:T(8,128)(2,1)} %shard_map.255.mine_ref), channel_id=1, source_target_pairs={{0,16},{1,17},{2,18},{3,19},{4,20},{5,21},{6,22},{7,23},{8,9},{9,8... | collective-permute-start | bytes 6291464 | tf_op jit(solution)/shard_map/ppermute | solution.py:49
  139.3 25.2 %collective-permute-start.19 = (bf16[16,32,2048]{2,1,0:T(8,128)(2,1)S(1)}, bf16[16,32,2048]{2,1,0:T(8,128)(2,1)S(1)}, u32[]{:S(2)}, u32[]{:S(2)}) collective-permute-start(bf16[16,32,2048]{2,1,0:T(8,128)(2,1)S(1)} %shard_map.260.mine_ref), channel_id=1, source_target_pairs={{0,16},{1,17},{2,18},{3,19},{4,20},{5,21},{6,22},{7,23},{8,9},{9,8... | collective-permute-start | bytes 6291464 | tf_op jit(solution)/shard_map/ppermute | solution.py:49
  168.6 37.8 %collective-permute-start.26 = (bf16[32,32,2048]{2,1,0:T(8,128)(2,1)}, bf16[32,32,2048]{2,1,0:T(8,128)(2,1)}, u32[]{:S(2)}, u32[]{:S(2)}) collective-permute-start(bf16[32,32,2048]{2,1,0:T(8,128)(2,1)} %shard_map.263), channel_id=1, source_target_pairs={{0,8},{1,9},{2,10},{3,11},{4,12},{5,13},{6,14},{7,15},{8,0},{9,1},... | collective-permute-start | bytes 12582920 | tf_op jit(solution)/shard_map/ppermute | solution.py:49
  171.4 23.6 %collective-permute-start.23 = (bf16[4,64,1024]{2,1,0:T(8,128)(2,1)S(1)}, bf16[4,64,1024]{2,1,0:T(8,128)(2,1)S(1)}, u32[]{:S(2)}, u32[]{:S(2)}) collective-permute-start(bf16[4,64,1024]{2,1,0:T(8,128)(2,1)S(1)} %get-tuple-element.596), channel_id=1, source_target_pairs={{0,24},{1,25},{2,26},{3,27},{4,28},{5,29},{6,30},{7,31},{8,16},{9,... | collective-permute-start | bytes 1572872 | tf_op jit(solution)/shard_map/ppermute | solution.py:53
  172.3 26.2 %collective-permute-start.24 = (bf16[4,32,2048]{2,1,0:T(8,128)(2,1)S(1)}, bf16[4,32,2048]{2,1,0:T(8,128)(2,1)S(1)}, u32[]{:S(2)}, u32[]{:S(2)}) collective-permute-start(bf16[4,32,2048]{2,1,0:T(8,128)(2,1)S(1)} %shard_map.264.mine_ref), channel_id=1, source_target_pairs={{0,2},{1,3},{2,0},{3,1},{4,6},{5,7},{6,4},{7,5},{8,10},{9,11},{10,... | collective-permute-start | bytes 1572872 | tf_op jit(solution)/shard_map/ppermute | solution.py:49
  217.3 25.2 %collective-permute-start.29 = (bf16[16,32,2048]{2,1,0:T(8,128)(2,1)S(1)}, bf16[16,32,2048]{2,1,0:T(8,128)(2,1)S(1)}, u32[]{:S(2)}, u32[]{:S(2)}) collective-permute-start(bf16[16,32,2048]{2,1,0:T(8,128)(2,1)S(1)} %shard_map.268.mine_ref), channel_id=1, source_target_pairs={{0,16},{1,17},{2,18},{3,19},{4,20},{5,21},{6,22},{7,23},{8,9},{9,8... | collective-permute-start | bytes 6291464 | tf_op jit(solution)/shard_map/ppermute | solution.py:49
  246.5 24.6 %collective-permute-start.32 = (bf16[32,32,2048]{2,1,0:T(8,128)(2,1)}, bf16[32,32,2048]{2,1,0:T(8,128)(2,1)}, u32[]{:S(2)}, u32[]{:S(2)}) collective-permute-start(bf16[32,32,2048]{2,1,0:T(8,128)(2,1)} %shard_map.272), channel_id=1, source_target_pairs={{0,8},{1,9},{2,10},{3,11},{4,12},{5,13},{6,14},{7,15},{8,0},{9,1},... | collective-permute-start | bytes 12582920 | tf_op jit(solution)/shard_map/ppermute | solution.py:49
  267.2 25.4 %collective-permute-start.33 = (bf16[16,64,1024]{2,1,0:T(8,128)(2,1)S(1)}, bf16[16,64,1024]{2,1,0:T(8,128)(2,1)}, u32[]{:S(2)}, u32[]{:S(2)}) collective-permute-start(bf16[16,64,1024]{2,1,0:T(8,128)(2,1)S(1)} %shard_map.275.mine_ref), channel_id=1, source_target_pairs={{0,16},{1,17},{2,18},{3,19},{4,20},{5,21},{6,22},{7,23},{8,9},{9,8... | collective-permute-start | bytes 6291464 | tf_op jit(solution)/shard_map/ppermute | solution.py:49
  296.2 28.9 %collective-permute-start.35 = (bf16[32,64,1024]{2,1,0:T(8,128)(2,1)}, bf16[32,64,1024]{2,1,0:T(8,128)(2,1)}, u32[]{:S(2)}, u32[]{:S(2)}) collective-permute-start(bf16[32,64,1024]{2,1,0:T(8,128)(2,1)} %shard_map.277), channel_id=1, source_target_pairs={{0,8},{1,9},{2,10},{3,11},{4,12},{5,13},{6,14},{7,15},{8,0},{9,1},... | collective-permute-start | bytes 12582920 | tf_op jit(solution)/shard_map/ppermute | solution.py:49
  304.5 35.6 %collective-permute-start.34 = (bf16[32,64,1024]{2,1,0:T(8,128)(2,1)}, bf16[32,64,1024]{2,1,0:T(8,128)(2,1)S(1)}, u32[]{:S(2)}, u32[]{:S(2)}) collective-permute-start(bf16[32,64,1024]{2,1,0:T(8,128)(2,1)} %bitcast.57), channel_id=1, source_target_pairs={{0,8},{1,9},{2,10},{3,11},{4,12},{5,13},{6,14},{7,15},{8,0},{9,1},... | collective-permute-start | bytes 12582920 | tf_op jit(solution)/shard_map/ppermute | solution.py:49
  338.2 24.9 %collective-permute-start.38 = (bf16[4,64,1024]{2,1,0:T(8,128)(2,1)}, bf16[4,64,1024]{2,1,0:T(8,128)(2,1)S(1)}, u32[]{:S(2)}, u32[]{:S(2)}) collective-permute-start(bf16[4,64,1024]{2,1,0:T(8,128)(2,1)} %get-tuple-element.591), channel_id=1, source_target_pairs={{0,24},{1,25},{2,26},{3,27},{4,28},{5,29},{6,30},{7,31},{8,16},{9,... | collective-permute-start | bytes 1572872 | tf_op jit(solution)/shard_map/ppermute | solution.py:53
  363.1 29.3 %collective-permute-start.40 = (bf16[32,32,2048]{2,1,0:T(8,128)(2,1)}, bf16[32,32,2048]{2,1,0:T(8,128)(2,1)}, u32[]{:S(2)}, u32[]{:S(2)}) collective-permute-start(bf16[32,32,2048]{2,1,0:T(8,128)(2,1)} %bitcast.68), channel_id=1, source_target_pairs={{0,8},{1,9},{2,10},{3,11},{4,12},{5,13},{6,14},{7,15},{8,0},{9,1},... | collective-permute-start | bytes 12582920 | tf_op jit(solution)/shard_map/ppermute | solution.py:49
  363.1 25.2 %collective-permute-start.39 = (bf16[16,64,1024]{2,1,0:T(8,128)(2,1)S(1)}, bf16[16,64,1024]{2,1,0:T(8,128)(2,1)S(1)}, u32[]{:S(2)}, u32[]{:S(2)}) collective-permute-start(bf16[16,64,1024]{2,1,0:T(8,128)(2,1)S(1)} %get-tuple-element.414), channel_id=1, source_target_pairs={{0,16},{1,17},{2,18},{3,19},{4,20},{5,21},{6,22},{7,23},{8,9},{9,8... | collective-permute-start | bytes 6291464 | tf_op jit(solution)/shard_map/ppermute | solution.py:49
  397.9 36.7 %collective-permute-start.42 = (bf16[16,32,2048]{2,1,0:T(8,128)(2,1)}, bf16[16,32,2048]{2,1,0:T(8,128)(2,1)}, u32[]{:S(2)}, u32[]{:S(2)}) collective-permute-start(bf16[16,32,2048]{2,1,0:T(8,128)(2,1)} %get-tuple-element.428), channel_id=1, source_target_pairs={{0,16},{1,17},{2,18},{3,19},{4,20},{5,21},{6,22},{7,23},{8,9},{9,8... | collective-permute-start | bytes 6291464 | tf_op jit(solution)/shard_map/ppermute | solution.py:49
  406.4 27.1 %collective-permute-start.41 = (bf16[8,64,1024]{2,1,0:T(8,128)(2,1)}, bf16[8,64,1024]{2,1,0:T(8,128)(2,1)}, u32[]{:S(2)}, u32[]{:S(2)}) collective-permute-start(bf16[8,64,1024]{2,1,0:T(8,128)(2,1)} %get-tuple-element.427), channel_id=1, source_target_pairs={{0,1},{1,0},{2,3},{3,2},{4,5},{5,4},{6,7},{7,6},{8,24},{9,25},{10,... | collective-permute-start | bytes 3145736 | tf_op jit(solution)/shard_map/ppermute | solution.py:49
  479.3 39.0 %collective-permute-start.48 = (bf16[32,32,1536]{2,1,0:T(8,128)(2,1)}, bf16[32,32,1536]{2,1,0:T(8,128)(2,1)}, u32[]{:S(2)}, u32[]{:S(2)}) collective-permute-start(bf16[32,32,1536]{2,1,0:T(8,128)(2,1)} %bitcast.87), channel_id=1, source_target_pairs={{0,8},{1,9},{2,10},{3,11},{4,12},{5,13},{6,14},{7,15},{8,0},{9,1},... | collective-permute-start | bytes 9437192 | tf_op jit(solution)/shard_map/ppermute | solution.py:49
  484.9 33.3 %collective-permute-start.49 = (bf16[32,32,512]{2,1,0:T(8,128)(2,1)}, bf16[32,32,512]{2,1,0:T(8,128)(2,1)S(1)}, u32[]{:S(2)}, u32[]{:S(2)}) collective-permute-start(bf16[32,32,512]{2,1,0:T(8,128)(2,1)} %bitcast.363), channel_id=1, source_target_pairs={{0,8},{1,9},{2,10},{3,11},{4,12},{5,13},{6,14},{7,15},{8,0},{9,1},... | collective-permute-start | bytes 3145736 | tf_op jit(solution)/shard_map/ppermute | solution.py:49
  486.8 23.4 %collective-permute-start.43 = (bf16[4,64,1024]{2,1,0:T(8,128)(2,1)S(1)}, bf16[4,64,1024]{2,1,0:T(8,128)(2,1)S(1)}, u32[]{:S(2)}, u32[]{:S(2)}) collective-permute-start(bf16[4,64,1024]{2,1,0:T(8,128)(2,1)S(1)} %get-tuple-element.586), channel_id=1, source_target_pairs={{0,24},{1,25},{2,26},{3,27},{4,28},{5,29},{6,30},{7,31},{8,16},{9,... | collective-permute-start | bytes 1572872 | tf_op jit(solution)/shard_map/ppermute | solution.py:53
  525.2 33.9 %collective-permute-start.52 = (bf16[16,32,2048]{2,1,0:T(8,128)(2,1)}, bf16[16,32,2048]{2,1,0:T(8,128)(2,1)}, u32[]{:S(2)}, u32[]{:S(2)}) collective-permute-start(bf16[16,32,2048]{2,1,0:T(8,128)(2,1)} %get-tuple-element.472), channel_id=1, source_target_pairs={{0,16},{1,17},{2,18},{3,19},{4,20},{5,21},{6,22},{7,23},{8,9},{9,8... | collective-permute-start | bytes 6291464 | tf_op jit(solution)/shard_map/ppermute | solution.py:49
  570.1 33.9 %collective-permute-start.56 = (bf16[32,32,1536]{2,1,0:T(8,128)(2,1)}, bf16[32,32,1536]{2,1,0:T(8,128)(2,1)}, u32[]{:S(2)}, u32[]{:S(2)}) collective-permute-start(bf16[32,32,1536]{2,1,0:T(8,128)(2,1)} %bitcast.97), channel_id=1, source_target_pairs={{0,8},{1,9},{2,10},{3,11},{4,12},{5,13},{6,14},{7,15},{8,0},{9,1},... | collective-permute-start | bytes 9437192 | tf_op jit(solution)/shard_map/ppermute | solution.py:49
  610.2 32.5 %collective-permute-start.59 = (bf16[16,32,2048]{2,1,0:T(8,128)(2,1)}, bf16[16,32,2048]{2,1,0:T(8,128)(2,1)}, u32[]{:S(2)}, u32[]{:S(2)}) collective-permute-start(bf16[16,32,2048]{2,1,0:T(8,128)(2,1)} %get-tuple-element.510), channel_id=1, source_target_pairs={{0,16},{1,17},{2,18},{3,19},{4,20},{5,21},{6,22},{7,23},{8,9},{9,8... | collective-permute-start | bytes 6291464 | tf_op jit(solution)/shard_map/ppermute | solution.py:49
  (171 other events, 1787.9 us)

commit v3 on v2

--- a/solution.py
+++ b/solution.py
@@ -19,6 +19,7 @@
 highest = lax.Precision.HIGHEST
 VMEM = 48 * 1024 * 1024
 bf16, f32 = jnp.bfloat16, jnp.float32
+NO_COST = pl.CostEstimate(flops=0, bytes_accessed=0, transcendentals=0)
 
 
 class Place:
@@ -95,51 +96,39 @@
         out_specs=pl.BlockSpec((2 * m, r, block), lambda j: (0, 0, j)),
         out_shape=jax.ShapeDtypeStruct((2 * m, r, n), mine.dtype),
         compiler_params=pltpu.CompilerParams(vmem_limit_bytes=VMEM),
-        cost_estimate=pl.CostEstimate(
-            flops=0, bytes_accessed=4 * m * r * n * mine.dtype.itemsize, transcendentals=0
-        ),
+        cost_estimate=NO_COST,
     )(jnp.stack([jnp.int32(k), value.astype(jnp.int32)]), mine, other)
 
 
-def split_body(ends, info_ref, *refs):
-    k, value, step = info_ref[0], info_ref[1], pl.program_id(0)
-    send_ref, keep_ref = refs[-2:]
-    for p in range(len(ends) - 1):
-
-        @pl.when((step >= ends[p]) & (step < ends[p + 1]))
-        def _(a_ref=refs[2 * p], b_ref=refs[2 * p + 1]):
-            for m in range(send_ref.shape[0]):
-                for out_ref, at in ((send_ref, 1 - value), (keep_ref, value)):
-                    i = position(m, at, k)
-                    total = a_ref[i].astype(f32) + b_ref[i].astype(f32)
-                    out_ref[m] = total.astype(out_ref.dtype)
-
-
-def split(pairs, k, value, dtype):
-    blocks, r, _ = pairs[0][0].shape
-    widths = [a.shape[-1] for a, _ in pairs]
-    n = sum(widths)
-    block = min([column_block((blocks, r, n))] + widths)
-    ends = [sum(widths[:i]) // block for i in range(len(widths) + 1)]
-    in_specs = [pl.BlockSpec(memory_space=pltpu.SMEM)]
-    for low, high in zip(ends[:-1], ends[1:]):
-
-        def index(j, low=low, high=high):
-            return (0, 0, jnp.clip(j - low, 0, high - low - 1))
-
-        in_specs += [pl.BlockSpec((blocks, r, block), index)] * 2
+def part(info_ref, source_ref, send_ref, keep_ref):
+    k, value = info_ref[0], info_ref[1]
+    for m in range(send_ref.shape[0]):
+        for out_ref, at in ((send_ref, 1 - value), (keep_ref, value)):
+            out_ref[m] = source_ref[position(m, at, k)].astype(out_ref.dtype)
+
+
+def split_body(info_ref, a_ref, b_ref, send_ref, keep_ref):
+    k, value = info_ref[0], info_ref[1]
+    for m in range(send_ref.shape[0]):
+        for out_ref, at in ((send_ref, 1 - value), (keep_ref, value)):
+            i = position(m, at, k)
+            out_ref[m] = (a_ref[i].astype(f32) + b_ref[i].astype(f32)).astype(out_ref.dtype)
+
+
+def split(a, b, k, value, dtype):
+    blocks, r, n = a.shape
+    block = column_block(a.shape)
     out = jax.ShapeDtypeStruct((blocks // 2, r, n), dtype)
     return pl.pallas_call(
-        partial(split_body, ends),
+        split_body,
         grid=(n // block,),
-        in_specs=in_specs,
+        in_specs=[pl.BlockSpec(memory_space=pltpu.SMEM)]
+        + [pl.BlockSpec((blocks, r, block), lambda j: (0, 0, j))] * 2,
         out_specs=[pl.BlockSpec((blocks // 2, r, block), lambda j: (0, 0, j))] * 2,
         out_shape=[out, out],
         compiler_params=pltpu.CompilerParams(vmem_limit_bytes=VMEM),
-        cost_estimate=pl.CostEstimate(
-            flops=blocks * r * n, bytes_accessed=6 * blocks * r * n, transcendentals=0
-        ),
-    )(jnp.stack([jnp.int32(k), value.astype(jnp.int32)]), *[x for pair in pairs for x in pair])
+        cost_estimate=NO_COST,
+    )(jnp.stack([jnp.int32(k), value.astype(jnp.int32)]), a, b)
 
 
 def gather_small(place, value):
@@ -183,18 +172,21 @@
     return blocks, got
 
 
-def scatter(place, pairs):
+def scatter(place, first):
     core = (place.core_bit, place.core_bit)
     bits = [1 << i for i in range(place.total.bit_length() - 1)]
-    have = (bits, bits)
+    have, pairs = (bits, bits), None
     for pair in place.xy[::-1] + place.z + [core]:
         have = tuple([b for b in h if b != bit] for h, bit in zip(have, pair))
-        k = [below(h, b) for h, b in zip(have, pair)]
+        k = place.choose([below(h, b) for h, b in zip(have, pair)])
         dtype = f32 if pair == core else bf16
-        send, keep = split(pairs, place.choose(k), place.mine(pair), dtype)
+        if pairs is None:
+            send, keep = first(k, place.mine(pair))
+        else:
+            send, keep = split(*pairs, k, place.mine(pair), dtype)
         (send,) = yield [send]
         (got,) = yield [place.flip(send, pair)]
-        pairs = [(keep, got)]
+        pairs = (keep, got)
     return keep[0], got[0]
 
 
@@ -214,20 +206,26 @@
         self.flying = not self.flying
 
 
+def land(value, *chains, also=()):
+    chains = [c for c in chains if c.flying]
+    value, got, also = lax.optimization_barrier((value, [c.pending for c in chains], list(also)))
+    for c, g in zip(chains, got):
+        c.pending = g
+        c.move()
+    return (value, *also) if also else value
+
+
+def launch(value, *chains, also=()):
+    chains = [c for c in chains if not c.done() and not c.flying]
+    value, sent, also = lax.optimization_barrier((value, [c.pending for c in chains], list(also)))
+    for c, g in zip(chains, sent):
+        c.pending = g
+        c.move()
+    return (value, *also) if also else value
+
+
 def along(value, *chains):
-    ending = [c for c in chains if c.flying]
-    if ending:
-        value, got = lax.optimization_barrier((value, [c.pending for c in ending]))
-        for c, g in zip(ending, got):
-            c.pending = g
-            c.move()
-    starting = [c for c in chains if not c.done()]
-    if starting:
-        value, sent = lax.optimization_barrier((value, [c.pending for c in starting]))
-        for c, g in zip(starting, sent):
-            c.pending = g
-            c.move()
-    return value
+    return launch(land(value, *chains), *chains)
 
 
 def finish(chain):
@@ -333,7 +331,6 @@
 def run_attention(body, scalars, block, grid, index, inputs, out_widths):
     a, b = block
     outer = inputs[0].shape[:2]
-    rows = outer[0] * outer[1]
     return pl.pallas_call(
         body,
         grid=(grid,),
@@ -342,11 +339,7 @@
         out_specs=[pl.BlockSpec((a, b, width), index) for width in out_widths],
         out_shape=[jax.ShapeDtypeStruct((*outer, width), bf16) for width in out_widths],
         compiler_params=pltpu.CompilerParams(vmem_limit_bytes=VMEM),
-        cost_estimate=pl.CostEstimate(
-            flops=rows * H * E * 2 * a * b * 4,
-            bytes_accessed=rows * 2 * (sum(x.shape[-1] for x in inputs) + sum(out_widths)),
-            transcendentals=rows * H * a * b,
-        ),
+        cost_estimate=NO_COST,
     )(scalars, *inputs)
 
 
@@ -361,18 +354,6 @@
 def norm_body(x_ref, added_ref, gain_ref, shift_ref, out_ref):
     unit, _ = centre(x_ref[0].astype(f32) + added_ref[0])
     out_ref[0] = (unit * gain_ref[...] + shift_ref[...]).astype(out_ref.dtype)
-
-
-def norm_back_body(x_ref, added_ref, gain_ref, grad_ref, rest_ref, out_ref, sums_ref):
-    unit, scale = centre(x_ref[0].astype(f32) + added_ref[0])
-    grad = grad_ref[0]
-    scaled = grad * gain_ref[...]
-    first = jnp.mean(scaled, axis=-1, keepdims=True)
-    second = jnp.mean(scaled * unit, axis=-1, keepdims=True)
-    out = rest_ref[0].astype(f32) + scale * (scaled - first - unit * second)
-    out_ref[0] = out.astype(out_ref.dtype)
-    terms = (grad * unit, grad, out)
-    sums_ref[0] = jnp.concatenate([jnp.sum(x, axis=0, keepdims=True) for x in terms], axis=0)
 
 
 def by_rows(body, arrays, rows, outs):
@@ -384,7 +365,6 @@
         else:
             at = (lambda i: (i, 0, 0)) if x.shape[0] == blocks else (lambda i: (0, 0, 0))
             specs.append(pl.BlockSpec((1, *x.shape[1:]), at))
-    count = sum(x.size for x in arrays)
     return pl.pallas_call(
         body,
         grid=(blocks,),
@@ -392,9 +372,7 @@
         out_specs=[pl.BlockSpec((1, *shape[1:]), lambda i: (i, 0, 0)) for shape, _ in outs],
         out_shape=[jax.ShapeDtypeStruct(shape, dtype) for shape, dtype in outs],
         compiler_params=pltpu.CompilerParams(vmem_limit_bytes=VMEM),
-        cost_estimate=pl.CostEstimate(
-            flops=10 * count, bytes_accessed=4 * count, transcendentals=0
-        ),
+        cost_estimate=NO_COST,
     )(*arrays)
 
 
@@ -405,16 +383,232 @@
     return out.reshape(-1, shape[2])
 
 
-def norm_back(x, added, gain, grad, rest, dtype):
-    shape = (x.shape[0] * x.shape[1] // 256, 256, x.shape[2])
-    arrays = [x.reshape(shape), added, gain[None], grad.reshape(shape), rest.reshape(shape)]
-    sums = ((shape[0], 3, shape[2]), f32)
-    out, sums = by_rows(norm_back_body, arrays, 256, [(shape, dtype), sums])
-    return out.reshape(x.shape), sums
-
-
-def matmul(inputs, weight):
-    return jnp.dot(inputs, weight, preferred_element_type=f32)
+BLOCK = 512
+
+
+def dense(body, grid, scalars, inputs, outs, scratch=()):
+    return pl.pallas_call(
+        body,
+        grid_spec=pltpu.PrefetchScalarGridSpec(
+            num_scalar_prefetch=1,
+            grid=grid,
+            in_specs=[pl.BlockSpec(block, index) for _, block, index in inputs],
+            out_specs=[pl.BlockSpec(block, index) for _, _, block, index in outs],
+            scratch_shapes=list(scratch),
+        ),
+        out_shape=[jax.ShapeDtypeStruct(shape, dtype) for shape, dtype, _, _ in outs],
+        compiler_params=pltpu.CompilerParams(vmem_limit_bytes=VMEM),
+        cost_estimate=NO_COST,
+    )(scalars, *[x for x, _, _ in inputs])
+
+
+def at(*index):
+    return lambda j, ref: index
+
+
+def whole(x):
+    return (x, x.shape, at(*[0] * x.ndim))
+
+
+def rows_of(x, rows=256):
+    return (x, (rows, x.shape[1]), lambda i, ref: (i, 0))
+
+
+def project_body(_, x_ref, w_ref, out_ref):
+    out_ref[...] = jnp.dot(x_ref[...], w_ref[...], preferred_element_type=f32).astype(bf16)
+
+
+def project(x, w, cols, scalars):
+    index = lambda j, ref: (0, j)
+    rows = x.shape[0]
+    (out,) = dense(
+        project_body, (cols // BLOCK,), scalars,
+        [whole(x), (w, (w.shape[0], BLOCK), index)],
+        [((rows, cols), bf16, (rows, BLOCK), index)],
+    )
+    return out
+
+
+def sides(core, own_ref, other_ref):
+    for side, ref in ((core, own_ref), (1 - core, other_ref)):
+        yield pl.ds(pl.multiple_of(side * BLOCK, BLOCK), BLOCK), ref
+
+
+def hidden1_body(core_ref, mixed_ref, own_ref, other_ref, x_ref, added_ref, out_ref):
+    for cols, w_ref in sides(core_ref[0], own_ref, other_ref):
+        dot = jnp.dot(mixed_ref[...], w_ref[...], preferred_element_type=f32)
+        out_ref[:, cols] = (x_ref[:, cols].astype(f32) + added_ref[0, :, cols] + dot).astype(bf16)
+
+
+def out_half(w):
+    return (w, (w.shape[0], BLOCK), at(0, w.shape[1] // BLOCK - 1))
+
+
+def add_spatial(mixed, halves, x, added, scalars):
+    rows, width = x.shape
+    step = rows // added.shape[0]
+    (out,) = dense(
+        hidden1_body, (rows // step,), scalars,
+        [rows_of(mixed, step), *[out_half(w) for w in halves], rows_of(x, step),
+         (added, (1, 1, width), lambda i, ref: (i, 0, 0))],
+        [((rows, width), bf16, (step, width), lambda i, ref: (i, 0))],
+    )
+    return out
+
+
+def hidden2_body(
+    core_ref, mixed_ref, own_ref, other_ref, x_ref, gain_ref, shift_ref, out_ref, norm_ref
+):
+    for cols, w_ref in sides(core_ref[0], own_ref, other_ref):
+        dot = jnp.dot(mixed_ref[...], w_ref[...], preferred_element_type=f32)
+        out_ref[:, cols] = x_ref[:, cols].astype(f32) + dot
+    unit, _ = centre(out_ref[...])
+    norm_ref[...] = (unit * gain_ref[...] + shift_ref[...]).astype(bf16)
+
+
+def add_temporal(mixed, halves, x, gain, shift, scalars):
+    rows, width = x.shape
+    block = ((256, width), lambda i, ref: (i, 0))
+    return dense(
+        hidden2_body, (rows // 256,), scalars,
+        [rows_of(mixed), *[out_half(w) for w in halves], rows_of(x), whole(gain[None]),
+         whole(shift[None])],
+        [((rows, width), f32, *block), ((rows, width), bf16, *block)],
+    )
+
+
+def hidden3_body(_, a_ref, b_ref, own_ref, other_ref, x_ref, bias_ref, mask_ref, out_ref):
+    out = x_ref[...] + bias_ref[...]
+    out += jnp.dot(a_ref[...], own_ref[...], preferred_element_type=f32)
+    out += jnp.dot(b_ref[...], other_ref[...], preferred_element_type=f32)
+    out_ref[...] = jnp.where(mask_ref[...] > 0, out, 0).astype(bf16)
+
+
+def down_project(actives, halves, x, bias, mask, scalars):
+    rows, width = x.shape
+    (out,) = dense(
+        hidden3_body, (rows // 256,), scalars,
+        [*[rows_of(y) for y in actives], *[whole(w) for w in halves], rows_of(x), whole(bias),
+         rows_of(mask)],
+        [((rows, width), bf16, (256, width), lambda i, ref: (i, 0))],
+    )
+    return out
+
+
+def inner_back_body(_, x_ref, w_ref, slope_ref, out_ref, sum_ref):
+    grad = dot_t(x_ref[...], w_ref[...]) * slope_ref[...].astype(f32)
+    out_ref[...] = grad.astype(bf16)
+    sum_ref[...] = jnp.sum(out_ref[...].astype(f32), axis=0, keepdims=True)
+
+
+def inner_back(x, w, slope, scalars):
+    rows, cols = slope.shape
+    index = lambda j, ref: (0, j)
+    return dense(
+        inner_back_body, (cols // BLOCK,), scalars,
+        [whole(x), (w, (BLOCK, w.shape[1]), lambda j, ref: (j, 0)), (slope, (rows, BLOCK), index)],
+        [((rows, cols), bf16, (rows, BLOCK), index), ((1, cols), f32, (1, BLOCK), index)],
+    )
+
+
+def norm_back_body(
+    _, a_ref, b_ref, own_ref, other_ref, x_ref, added_ref, gain_ref, rest_ref, out_ref, sums_ref
+):
+    grad = dot_t(a_ref[...], own_ref[...]) + dot_t(b_ref[...], other_ref[...])
+    unit, scale = centre(x_ref[...].astype(f32) + added_ref[0])
+    scaled = grad * gain_ref[...]
+    first = jnp.mean(scaled, axis=-1, keepdims=True)
+    second = jnp.mean(scaled * unit, axis=-1, keepdims=True)
+    out = rest_ref[...].astype(f32) + scale * (scaled - first - unit * second)
+    out_ref[...] = out.astype(out_ref.dtype)
+    terms = (grad * unit, grad, out)
+    sums_ref[0] = jnp.concatenate([jnp.sum(x, axis=0, keepdims=True) for x in terms], axis=0)
+
+
+def norm_back(grads, halves, x, added, gain, rest, dtype, scalars):
+    rows, width = x.shape
+    step, cols = 256, grads[0].shape[1]
+    added_at = (lambda i, ref: (i, 0, 0)) if added.shape[0] > 1 else at(0, 0, 0)
+    return dense(
+        norm_back_body, (rows // step,), scalars,
+        [*[rows_of(g) for g in grads], *[(w, (w.shape[0], cols), at(0, 0)) for w in halves],
+         rows_of(x), (added, (1, 1, width), added_at), whole(gain[None]), rows_of(rest)],
+        [((rows, width), dtype, (step, width), lambda i, ref: (i, 0)),
+         ((rows // step, 3, width), f32, (1, 3, width), lambda i, ref: (i, 0, 0))],
+    )
+
+
+def mixed_back_body(core_ref, x_ref, own_ref, other_ref, out_ref):
+    grad = 0
+    for cols, w_ref in sides(core_ref[0], own_ref, other_ref):
+        grad += dot_t(x_ref[:, cols], w_ref[...])
+    out_ref[...] = grad.astype(bf16)
+
+
+def mixed_back(x, halves, scalars):
+    rows, width = x.shape
+    last = halves[0].shape[1] // BLOCK - 1
+    (out,) = dense(
+        mixed_back_body, (width // BLOCK,), scalars,
+        [whole(x), *[(w, (BLOCK, BLOCK), lambda j, ref: (j, last)) for w in halves]],
+        [((rows, width), bf16, (rows, BLOCK), lambda j, ref: (0, j))],
+    )
+    return out
+
+
+def weight_grad_body(_, x_ref, y_ref, out_ref):
+    out_ref[...] = t_dot(x_ref[...], y_ref[...]).astype(bf16).reshape(out_ref.shape)
+
+
+def weight_grad(x, y, total, scalars, half=None):
+    rows, count = x.shape
+    cols = y.shape[1] if half is None else BLOCK
+    shift = (lambda j, ref: (0, j)) if half is None else (lambda j, ref: (0, ref[0] ^ half))
+    shape = (total, count // total)
+    (out,) = dense(
+        weight_grad_body, (cols // BLOCK,), scalars,
+        [whole(x), (y, (rows, BLOCK), shift)],
+        [((*shape, cols), bf16, (*shape, BLOCK), lambda j, ref: (0, 0, j))],
+    )
+    return out
+
+
+def weight_split_body(ends, info_ref, *refs):
+    send_ref, keep_ref, sum_ref = refs[-3:]
+    step = pl.program_id(0)
+    for p in range(len(ends) - 1):
+
+        @pl.when((step >= ends[p]) & (step < ends[p + 1]))
+        def _(x_ref=refs[3 * p], y_ref=refs[3 * p + 1], got_ref=refs[3 * p + 2]):
+            grad = t_dot(x_ref[...], y_ref[...]).reshape(sum_ref.shape)
+            sum_ref[...] = grad + got_ref[...].astype(f32)
+
+    part(info_ref, sum_ref, send_ref, keep_ref)
+
+
+def weight_split(parts, k, value, core):
+    scalars = jnp.stack([jnp.int32(k), value.astype(jnp.int32), core.astype(jnp.int32)])
+    total, r, _ = parts[0][2].shape
+    widths = [got.shape[2] for _, _, got, _ in parts]
+    ends = [sum(widths[:i]) // BLOCK for i in range(len(parts) + 1)]
+    inputs = []
+    for (x, y, got, half), low, high in zip(parts, ends[:-1], ends[1:]):
+        place = lambda j, low=low, high=high: jnp.clip(j - low, 0, high - low - 1)
+        if half is None:
+            index = lambda j, ref, place=place: (0, place(j))
+        else:
+            index = lambda j, ref, half=half: (0, ref[2] ^ half)
+        inputs += [
+            whole(x),
+            (y, (y.shape[0], BLOCK), index),
+            (got, (total, r, BLOCK), lambda j, ref, place=place: (0, 0, place(j))),
+        ]
+    shape = (total // 2, r)
+    out = ((*shape, sum(widths)), bf16, (*shape, BLOCK), lambda j, ref: (0, 0, j))
+    return dense(
+        partial(weight_split_body, ends), (ends[-1],), scalars, inputs, [out, out],
+        [pltpu.VMEM((total, r, BLOCK), f32)],
+    )
 
 
 TAIL = (
@@ -438,7 +632,7 @@
 
 def up_body(x_ref, w_ref, bias_ref, active_ref, slope_ref):
     rows = x_ref.shape[0]
-    step = min(rows, 256)
+    step = min(rows, 128)
     for r in range(0, rows, step):
         inner = jnp.dot(x_ref[r : r + step], w_ref[...], preferred_element_type=f32)
         active, slope = gelu(inner + bias_ref[...])
@@ -461,11 +655,7 @@
         out_specs=[pl.BlockSpec((rows, block), lambda i: (0, i))] * 2,
         out_shape=[out, out],
         compiler_params=pltpu.CompilerParams(vmem_limit_bytes=VMEM),
-        cost_estimate=pl.CostEstimate(
-            flops=2 * rows * width * cols,
-            bytes_accessed=2 * (rows * width + width * cols + 2 * rows * cols),
-            transcendentals=rows * cols,
-        ),
+        cost_estimate=NO_COST,
     )(x, weight, bias)
 
 
@@ -520,10 +710,6 @@
         pair = [jnp.where(core == 0, own, other), jnp.where(core == 0, other, own)]
         return jnp.stack(pair, axis=axis)
 
-    def halves(value):
-        first, second = value[:, :half], value[:, half:]
-        return jnp.where(core == 0, first, second), jnp.where(core == 0, second, first)
-
     def woven(own, other):
         cuts = [slice(i, i + half) for i in range(0, own.shape[1], half)]
         own_first = [x[:, cut] for cut in cuts for x in (own, other)]
@@ -534,36 +720,31 @@
             jnp.concatenate(other_first, axis=1),
         )
 
-    def joined(own, other):
-        return jnp.where(
-            core == 0,
-            jnp.concatenate([own, other], axis=1),
-            jnp.concatenate([other, own], axis=1),
-        )
-
     thin = width // total
     counts = [ACTIONS, 3, 3, 1]
     ends = [sum(counts[:i]) for i in range(len(counts) + 1)]
+    rows = s_qkv.shape[0]
+    hidden_half = w_down.shape[0] // 2
+
+    def attention_group(qkv, out):
+        qkv = own_and_other(qkv.reshape(rows, 3, 2, half), 2)
+        both = [
+            jnp.concatenate([a.reshape(rows, 3 * half), b], axis=1)
+            for a, b in zip(qkv, own_and_other(out.reshape(rows, 2, half), 1))
+        ]
+        return Chain(gather(place, *both))
+
+    front = attention_group(s_qkv, s_out)
+    tokens = along(tokens, front)
+    rows_in = (action_table, norm_gains, norm_shifts, b_down)
+    tokens, rows_in, b_up, grad_out = lax.optimization_barrier((tokens, rows_in, b_up, grad_out))
+    action_table, norm_gains, norm_shifts, b_down = rows_in
     small = jnp.concatenate([action_table, norm_gains, norm_shifts, b_down[None]], axis=0).T
     small = jnp.pad(small, ((0, 0), (0, LANES - ends[-1])))
     b_up = jnp.pad(b_up[None], ((0, GROUP - 1), (0, LANES - b_up.shape[0])))
     small = jnp.concatenate([small, b_up], axis=0)
-
-    rows = s_qkv.shape[0]
-    hidden_half = w_down.shape[0] // 2
-
-    def attention_group(qkv, out):
-        qkv = own_and_other(qkv.reshape(rows, 3, 2, half), 2)
-        both = [
-            jnp.concatenate([a.reshape(rows, 3 * half), b], axis=1)
-            for a, b in zip(qkv, halves(out))
-        ]
-        return Chain(gather(place, *both))
-
-    front = attention_group(s_qkv, s_out)
     tokens = along(tokens, front)
-    tokens, small, grad_out = lax.optimization_barrier((tokens, small, grad_out))
-    tokens = along(tokens, front)
+    tokens, grad_out = lax.optimization_barrier((tokens, grad_out))
     cotangent = to_slots(grad_out.reshape(frames_local, slots, width))
     small = Chain(gather_small(place, small))
     tokens = along(tokens, small)
@@ -573,14 +754,16 @@
     middle = attention_group(t_qkv, t_out)
     tokens = along(tokens, middle)
     tokens, cotangent = lax.optimization_barrier((tokens, cotangent))
-    tokens = along(tokens, front, small)
+    tokens = along(tokens, front, middle)
+    tokens = along(tokens, small)
+    tokens = along(tokens, small)
+    tokens = along(tokens, front, middle)
+    while not small.done():
+        tokens = along(tokens, small)
     tokens, w_up, w_down = lax.optimization_barrier((tokens, w_up, w_down))
     up_pair = own_and_other(w_up.reshape(rows, total, 2, hidden_half), 2)
     rising = Chain(gather(place, *[x.reshape(rows, -1) for x in up_pair]))
     falling = Chain(gather(place, *own_and_other(w_down.reshape(2, hidden_half, width), 0)))
-    tokens = along(tokens, small, middle)
-    while not small.done():
-        tokens = along(tokens, small)
     small = small.result.astype(f32)
     table = small[:, :thin].reshape(width, LANES).T
 
@@ -595,17 +778,15 @@
     embedded = jnp.dot(onehot, action_rows, precision=highest)
     tokens = tokens.reshape(frames_local, slots, width)
     embedded = embedded[:, None, :]
-    tokens, embedded = along((tokens, embedded), front, middle)
     normed1 = norm(tokens, embedded, gains[0], shifts[0])
-    normed1 = along(normed1, rising)
-    normed1 = along(normed1, front, middle)
-    whole = [x.reshape(width, -1) for x in finish(front)]
-    sq_halves = [x[:, : 3 * half] for x in whole]
-
-    def project(x, halves, outer):
-        return [matmul(x, w).astype(bf16).reshape(*outer, -1) for w in halves]
-
-    spatial = project(normed1, sq_halves, (frames_local, slots))
+    normed1 = along(normed1, front, middle, rising)
+    s_halves = [x.reshape(width, -1) for x in finish(front)]
+    here = core.astype(jnp.int32).reshape(1)
+
+    def projected(x, w, outer):
+        return project(x, w, 3 * half, here).reshape(*outer, -1)
+
+    spatial = [projected(normed1, w, (frames_local, slots)) for w in s_halves]
     spatial = along(spatial, middle, rising)
 
     def frame_index(i):
@@ -621,23 +802,22 @@
         partial(attention_forward, spatial_bias), *spatial_place, spatial, [width]
     )
     s_mixed = s_mixed.reshape(row_count, width)
-    so_full = joined(*[x[:, 3 * half :] for x in whole])
-    hidden0 = tokens.astype(f32) + embedded
-    hidden1 = hidden0 + matmul(s_mixed, so_full).reshape(tokens.shape)
-
-    hidden1 = along(hidden1.astype(bf16), middle, rising, falling)
-    parts = to_slots(hidden1)
+    flat = tokens.reshape(row_count, width)
+    hidden1 = add_spatial(s_mixed, s_halves, flat, embedded, here)
+
+    hidden1 = along(hidden1, middle, rising, falling)
+    parts = to_slots(hidden1.reshape(tokens.shape))
+    parts = land(parts, middle, rising, falling)
     hidden1 = in_slots(parts)
     frames = hidden1.shape[0]
     slot_at = place.tm * slots_local + jnp.arange(slots_local)
     mask = (slot_at < sides[0] * sides[0])[None, :, None]
     nothing = jnp.zeros((1, 1, width), f32)
     normed2 = norm(hidden1, nothing, gains[1], shifts[1])
-    whole = [x.reshape(width, -1) for x in finish(middle)]
-    tq_halves = [x[:, : 3 * half] for x in whole]
-    to_full = joined(*[x[:, 3 * half :] for x in whole])
-    normed2 = along(normed2, rising, falling)
-    temporal = project(normed2, tq_halves, (frames, slots_local))
+    hidden1 = hidden1.reshape(row_count, width)
+    normed2 = launch(normed2, rising, falling)
+    t_halves = [x.reshape(width, -1) for x in finish(middle)]
+    temporal = [projected(normed2, w, (frames, slots_local)) for w in t_halves]
     temporal = along(temporal, rising, falling)
     temporal_place = (
         jnp.stack([place.tm.astype(jnp.int32), core.astype(jnp.int32)]), (frames, GROUP),
@@ -648,8 +828,7 @@
         partial(attention_forward, make_bias), *temporal_place, temporal, [width]
     )
     t_mixed = t_mixed.reshape(row_count, width)
-    hidden2 = hidden1.astype(f32) + matmul(t_mixed, to_full).reshape(hidden1.shape)
-    normed3 = norm(hidden2, nothing, gains[2], shifts[2])
+    hidden2, normed3 = add_temporal(t_mixed, t_halves, hidden1, gains[2], shifts[2], here)
     normed3 = along(normed3, rising, falling)
     up_halves = [x.reshape(width, -1) for x in finish(rising)]
     first = up_project(normed3, up_halves[0], up_bias[0])
@@ -658,56 +837,42 @@
     second = up_project(normed3, up_halves[1], up_bias[1])
     second = along(second, falling)
     (active, slope), (active2, slope2) = first, second
+
+    core_pair = (place.core_bit, place.core_bit)
+
+    def exchanged(grad):
+        return place.flip(grad, core_pair)
+
+    def sums(*parts):
+        return Chain(scatter(place, lambda k, value: weight_split(parts, k, value, core)))
+
+    down_in = jnp.where(mask, in_slots(cotangent), 0).reshape(row_count, width)
+    send = weight_grad(active2, down_in, total, here)
+    hidden2 = land(hidden2, falling)
     down_halves = [x.reshape(-1, width) for x in finish(falling)]
-    hidden3 = hidden2.reshape(row_count, width) + matmul(active, down_halves[0]) + down_bias
-    hidden3 = hidden3 + matmul(active2, down_halves[1])
-    mixed = from_slots(jnp.where(mask, hidden3.reshape(hidden2.shape), 0).astype(bf16))
-
-    def blocks(grad):
-        return grad.astype(bf16).reshape(total, grad.shape[0] // total, grad.shape[1])
-
-    core_pair = (place.core_bit, place.core_bit)
-
-    def exchanged(grad):
-        return place.flip(blocks(grad), core_pair)
-
-    def sums(keeps, gots):
-        return Chain(scatter(place, [(blocks(x), y) for x, y in zip(keeps, gots)]))
-
-    down_in = jnp.where(mask, in_slots(cotangent), 0).reshape(row_count, width)
-    send = t_dot(active2, down_in).astype(bf16)
-    down_in, send, active = lax.optimization_barrier((down_in, send, active))
+    hidden2, send = launch(hidden2, also=[send])
     got = exchanged(send)
-    keep = t_dot(active, down_in).astype(bf16)
-    down_in, keep = lax.optimization_barrier((down_in, keep))
-    inner_grad = (dot_t(down_in, down_halves[0]) * slope.astype(f32)).astype(bf16)
-    s_down = sums([keep], [got])
-    down_in, inner_grad = along((down_in, inner_grad), s_down)
-    inner_grad2 = (dot_t(down_in, down_halves[1]) * slope2.astype(f32)).astype(bf16)
-    send = t_dot(normed3, inner_grad2).astype(bf16)
-    inner_grad, inner_grad2, send, mixed = lax.optimization_barrier(
-        (inner_grad, inner_grad2, send, mixed)
-    )
-    mixed = in_frames(mixed)
+    mask_rows = jnp.broadcast_to(mask, (frames, slots_local, 1)).reshape(row_count, 1).astype(f32)
+    mixed = down_project([active, active2], down_halves, hidden2, down_bias, mask_rows, here)
+    down_in, mixed, got = lax.optimization_barrier((down_in, mixed, got))
+    s_down = sums((active, down_in, got, None))
+    down_in = launch(down_in, s_down)
+
+    inner_grad, b_sum = inner_back(down_in, down_halves[0], slope, here)
+    inner_grad2, b_sum2 = inner_back(down_in, down_halves[1], slope2, here)
+    send = weight_grad(normed3, inner_grad2, total, here)
+    inner_grad, inner_grad2, send = land((inner_grad, inner_grad2, send), s_down)
+    inner_grads, send = launch((inner_grad, inner_grad2), s_down, also=[send])
     got = exchanged(send)
-    keep = t_dot(normed3, inner_grad).astype(bf16)
-    inner_grad, keep = lax.optimization_barrier((inner_grad, keep))
-    normed3_grad = dot_t(inner_grad, up_halves[0])
-    s_up = sums([keep], [got])
-    normed3_grad, inner_grad2 = along((normed3_grad, inner_grad2), s_down, s_up)
-    normed3_grad = normed3_grad + dot_t(inner_grad2, up_halves[1])
-    g_b_down = jnp.sum(down_in.astype(f32), axis=0)
-    g_b_up = in_order(
-        *[jnp.sum(x.astype(f32), axis=0).reshape(total, -1) for x in (inner_grad, inner_grad2)], 1
-    )
-    grad2, sums3 = norm_back(hidden2, nothing, gains[2], normed3_grad, down_in, bf16)
-    t_in = grad2.reshape(row_count, width)
-
-    def out_grads(mixed_in, grad):
-        return [t_dot(mixed_in, x).astype(bf16) for x in halves(grad)]
-
-    g_t_out = out_grads(t_mixed, t_in)
-    t_mix_grad = dot_t(t_in, to_full).astype(bf16).reshape(frames, slots_local, width)
+
+    grad2, sums3 = norm_back(
+        inner_grads, up_halves, hidden2, nothing, gains[2], down_in, bf16, here
+    )
+    t_mix_grad = mixed_back(grad2, t_halves, here)
+    t_mix_grad, got = land(t_mix_grad, s_down, also=[got])
+    s_up = sums((normed3, inner_grads[0], got, None))
+    t_mix_grad = launch(t_mix_grad, s_down, s_up)
+    t_mix_grad = t_mix_grad.reshape(frames, slots_local, width)
 
     def back(side, where, make, values, grad):
         (out,) = run_attention(
@@ -716,45 +881,47 @@
         return out.reshape(row_count, -1)
 
     t_grad2 = back(1, temporal_place, make_bias, temporal, t_mix_grad)
-    t_grad2, t_mix_grad, g_t_out = lax.optimization_barrier((t_grad2, t_mix_grad, g_t_out))
-    t_mix_grad = along(t_mix_grad, s_down, s_up)
+    send = weight_grad(normed2, t_grad2, total, here)
+    send2 = weight_grad(t_mixed, grad2, total, here, 1)
     t_grad = back(0, temporal_place, make_bias, temporal, t_mix_grad)
-    t_grad, t_grad2 = lax.optimization_barrier((t_grad, t_grad2))
-    normed2_grad = dot_t(t_grad, tq_halves[0]) + dot_t(t_grad2, tq_halves[1])
-    grad1, sums2 = norm_back(hidden1, nothing, gains[1], normed2_grad, grad2, bf16)
-    grad1, t_grad, t_grad2 = lax.optimization_barrier((grad1, t_grad, t_grad2))
+    t_grads = land((t_grad, t_grad2), s_down, s_up)
+    t_grads, send, send2 = launch(t_grads, s_down, s_up, also=[send, send2])
+    gots = [exchanged(send), exchanged(send2)]
+
+    grad1, sums2 = norm_back(t_grads, t_halves, hidden1, nothing, gains[1], grad2, bf16, here)
+    grad1, *gots = land(grad1, s_down, s_up, also=gots)
+    grad1 = launch(grad1, s_down, s_up)
     parts = from_slots(grad1)
-    send = t_dot(normed2, t_grad2).astype(bf16)
-    send, t_grad = lax.optimization_barrier((send, t_grad))
-    t_gots = [exchanged(send), exchanged(g_t_out[1])]
-    keep = t_dot(normed2, t_grad).astype(bf16)
-    keep = along(keep, s_down, s_up)
-    parts[0], keep = lax.optimization_barrier((parts[0], keep))
-    s_time = sums([keep, g_t_out[0]], t_gots)
-    grad1 = in_frames(parts)
-    grad1 = along(grad1, s_time)
-    s_in = grad1.reshape(row_count, width)
-    g_s_out = out_grads(s_mixed, s_in)
-    mix_grad = dot_t(s_in, so_full).astype(bf16).reshape(frames_local, slots, width)
-    s_got = exchanged(g_s_out[1])
-    mix_grad = along(mix_grad, s_up, s_down)
+    s_time = sums((normed2, t_grads[0], gots[0], None), (t_mixed, grad2, gots[1], 0))
+    parts[0], s_time.pending = lax.optimization_barrier((parts[0], s_time.pending))
+    parts = land(parts, s_down, s_up)
+    grad1 = in_frames(parts).reshape(row_count, width)
+    grad1 = launch(grad1, s_down, s_up, s_time)
+
+    send2 = weight_grad(s_mixed, grad1, total, here, 1)
+    mix_grad = mixed_back(grad1, s_halves, here).reshape(frames_local, slots, width)
     s_grad2 = back(1, spatial_place, spatial_bias, spatial, mix_grad)
-    mix_grad, s_grad2 = along((mix_grad, s_grad2), s_time, s_up)
-    send = t_dot(normed1, s_grad2).astype(bf16)
-    mix_grad, send = lax.optimization_barrier((mix_grad, send))
-    got = exchanged(send)
+    send = weight_grad(normed1, s_grad2, total, here)
+    mix_grad, send, send2 = land((mix_grad, send, send2), s_down, s_up, s_time)
+    mix_grad, send, send2 = launch(mix_grad, s_down, s_up, s_time, also=[send, send2])
+    gots = [exchanged(send), exchanged(send2)]
+
     s_grad = back(0, spatial_place, spatial_bias, spatial, mix_grad)
-    s_grad = along(s_grad, s_time)
-    keep = t_dot(normed1, s_grad).astype(bf16)
-    keep, s_grad, s_grad2, s_got = lax.optimization_barrier((keep, s_grad, s_grad2, s_got))
-    s_space = sums([keep, g_s_out[0]], [got, s_got])
-    s_grad, s_grad2 = along((s_grad, s_grad2), s_space)
-    normed1_grad = dot_t(s_grad, sq_halves[0])
-    normed1_grad, s_grad2 = along((normed1_grad, s_grad2), s_time)
-    normed1_grad = normed1_grad + dot_t(s_grad2, sq_halves[1])
-    input_grad, sums1 = norm_back(tokens, embedded, gains[0], normed1_grad, grad1, f32)
-    sums1 = along(sums1, s_time, s_space)
+    s_grad, *gots = land(s_grad, s_down, s_up, s_time, also=gots)
+    s_space = sums((normed1, s_grad, gots[0], None), (s_mixed, grad1, gots[1], 0))
+    s_grads = launch((s_grad, s_grad2), s_time, s_space)
+
+    input_grad, sums1 = norm_back(
+        s_grads, s_halves, flat, embedded, gains[0], grad1, f32, here
+    )
+    sums1, input_grad = land((sums1, input_grad), s_time, s_space)
+    sums1, input_grad = launch((sums1, input_grad), s_time, s_space)
     g_actions = jnp.dot(onehot.T, sums1[:, 2], precision=highest)
+    sums1, b_sum, b_sum2, down_in, mixed = lax.optimization_barrier(
+        (sums1, b_sum, b_sum2, down_in, mixed)
+    )
+    g_b_down = jnp.sum(down_in.astype(f32), axis=0)
+    g_b_up = in_order(*[x.reshape(total, -1) for x in (b_sum, b_sum2)], 1)
 
     terms = [
         g_actions,
@@ -767,15 +934,21 @@
     packed = jnp.concatenate(packed, axis=1)
     packed = jnp.pad(packed, ((0, 0), (0, -packed.shape[1] % LANES)))
     s_small = Chain(scatter_small(place, packed))
+    packed = launch(packed, s_small)
+    packed = land(packed, s_time, s_space, s_small)
+    packed, mixed = launch((packed, mixed), s_time, s_space, s_small)
+    mixed = from_slots(mixed.reshape(frames, slots_local, width))
     g_w_down = in_order(*finish(s_down), 0).reshape(w_down.shape)
     g_w_up = in_order(*[x.reshape(rows, total, -1) for x in finish(s_up)], 2).reshape(w_up.shape)
     packed, g_w_down, g_w_up = lax.optimization_barrier((packed, g_w_down, g_w_up))
-    while not (s_time.done() and s_space.done()):
-        for _ in range(2):
-            if not s_small.done():
-                packed = along(packed, s_small)
-        packed = along(packed, *[c for c in (s_space, s_time) if not c.done()])
-    summed = finish(s_small)
+    packed = along(packed, s_small)
+    packed = along(packed, s_time, s_space, s_small)
+    packed, mixed = lax.optimization_barrier((packed, mixed))
+    mixed = in_frames(mixed)
+    packed = along(packed, s_small)
+    while not (s_time.done() and s_space.done() and s_small.done()):
+        packed = along(packed, s_time, s_space, s_small)
+    summed = s_small.result
     t_rows, s_rows = woven(*s_time.result), woven(*s_space.result)
     g_t_qkv, g_t_out = t_rows[:, : 3 * width], t_rows[:, 3 * width :]
     g_s_qkv, g_s_out = s_rows[:, : 3 * width], s_rows[:, 3 * width :]

time: 713 us -> 630 us (0.88)
  matrix products: 165 us -> 1.16 us
  Pallas kernels: 201 us -> 344 us
  waiting for transfers between devices: 168 us -> 128 us
  starting transfers between devices: 76.8 us -> 61.1 us
  other arithmetic: 25.5 us -> 16.1 us
    pallas_call x20 -> x40, Pallas kernels: 49 us -> 215 us  [the longest x24 190 us: dense(): pl.pallas_call(body, grid_spec=pltpu.PrefetchScalarGridSpec(num_scalar_pr...]
    dot_general x30 -> x0, matrix products: 164 us -> none  [the longest x10 59 us: dot_t(): lax.dot_general(a, b, (((1,), (1,)), ((), ())), preferred_element_type=f32)]
    ppermute x60, waiting for transfers between devices: 133 us -> 69.7 us  [flip(): return lax.ppermute(value, AXES, moves)]
    ppermute x12, waiting for transfers between devices: 35 us -> 58.2 us  [tm_flip(): return lax.ppermute(value, AXES, moves)]
    pallas_call x6 -> x2, Pallas kernels: 24.7 us -> 3.1 us  [by_rows(): pl.pallas_call(body, grid=(blocks,), in_specs=specs, out_specs=[pl.BlockS...]
    ppermute x60, starting transfers between devices: 68.6 us -> 49.6 us  [flip(): return lax.ppermute(value, AXES, moves)]
    unnamed x269 -> x262, local copies, waits for them, and re-layouts: 21.9 us -> 31.3 us
  transfers between devices with their start and end apart: 72 -> 72, of which waited for: 35 -> 24; matrix products, arithmetic and copies ran while one was open for 29% -> 8% of each run, Pallas kernels for 17% -> 42%
where the time goes in v3:
time: 630 us; the launch traced here: 625 us
  Pallas kernels  344 us (55%)
  waiting for transfers between devices  128 us (20%)
  local copies, waits for them, and re-layouts  70.5 us (11%)
  starting transfers between devices  61.1 us (10%)
  other arithmetic  16.1 us (3%)
    pallas_call x24, Pallas kernels, dense(): pl.pallas_call(body, grid_spec=pltpu.PrefetchScalarGridSpec(num_scalar_pr...  190 us
    ppermute x60, waiting for transfers between devices, flip(): return lax.ppermute(value, AXES, moves)  69.7 us
    pallas_call x6, Pallas kernels, run_attention(): pl.pallas_call(body, grid=(grid,), in_specs=[pl.BlockSpec(memory_space=pl...  61.7 us
    ppermute x12, waiting for transfers between devices, tm_flip(): return lax.ppermute(value, AXES, moves)  58.2 us
    ppermute x60, starting transfers between devices, flip(): return lax.ppermute(value, AXES, moves)  49.6 us
    pallas_call x25, Pallas kernels, merge(): pl.pallas_call(merge_body, grid=(n // block,), in_specs=[pl.BlockSpec(mem...  34.9 us
    unnamed x262, local copies, waits for them, and re-layouts  31.3 us
    pallas_call x2, Pallas kernels, up_project(): pl.pallas_call(up_body, grid=(cols // block,), in_specs=[pl.BlockSpec((ro...  29.8 us
  transfers between devices with their start and end apart: 72, of which 24 were waited for; matrix products, arithmetic and copies ran while one was open for 8% of the time, Pallas kernels for 42%

profile of v3, /device:TPU:1, one launch (start us, length us, event | category | flops | bytes accessed | tf_op | source)
XLA Modules:
  0.0 624.7 jit_solution(12578448948824580841)
XLA Ops:
  27.6 11.3 %collective-permute-done.5 = bf16[4,64,1024]{2,1,0:T(8,128)(2,1)S(1)} collective-permute-done((bf16[4,64,1024]{2,1,0:T(8,128)(2,1)}, bf16[4,64,1024]{2,1,0:T(8,128)(2,1)S(1)}, u32[]{:S(2)}, u32[]{:S(2)}) %collective-permute-start.5) | collective-permute-done | bytes 524320 | tf_op jit(solution)/shard_map/ppermute | solution.py:54
  45.1 11.0 %collective-permute-done.9.other_ref = bf16[4,48,128]{2,1,0:T(8,128)(2,1)S(1)} collective-permute-done((bf16[4,48,128]{2,1,0:T(8,128)(2,1)S(1)}, bf16[4,48,128]{2,1,0:T(8,128)(2,1)S(1)}, u32[]{:S(2)}, u32[]{:S(2)}) %collective-permute-start.9) | collective-permute-done | bytes 49184 | tf_op jit(solution)/shard_map/ppermute | solution.py:50
  128.6 11.4 %collective-permute-done.19.other_ref = bf16[16,32,2048]{2,1,0:T(8,128)(2,1)S(1)} collective-permute-done((bf16[16,32,2048]{2,1,0:T(8,128)(2,1)S(1)}, bf16[16,32,2048]{2,1,0:T(8,128)(2,1)S(1)}, u32[]{:S(2)}, u32[]{:S(2)}) %collective-permute-start.19) | collective-permute-done | bytes 2097184 | tf_op jit(solution)/shard_map/ppermute | solution.py:50
  159.0 11.4 %collective-permute-done.23 = bf16[4,64,1024]{2,1,0:T(8,128)(2,1)S(1)} collective-permute-done((bf16[4,64,1024]{2,1,0:T(8,128)(2,1)S(1)}, bf16[4,64,1024]{2,1,0:T(8,128)(2,1)S(1)}, u32[]{:S(2)}, u32[]{:S(2)}) %collective-permute-start.23) | collective-permute-done | bytes 524320 | tf_op jit(solution)/shard_map/ppermute | solution.py:54
  223.0 14.9 %shard_map.279 = (bf16[1024,2048]{1,0:T(8,128)(2,1)}, bf16[1024,2048]{1,0:T(8,128)(2,1)}) custom-call(bf16[1024,1024]{1,0:T(8,128)(2,1)S(1)} %get-tuple-element.417.x_ref.refs_0_, bf16[1024,2048]{1,0:T(8,128)(2,1)} %bitcast.244, f32[1,2048]{1,0:T(1,128)S(1)} %select_n.801.bias_ref), custom_call_target="tpu_custom_call" | custom-call | tf_op jit(solution)/shard_map/pallas_call | solution.py:647
  242.0 14.9 %shard_map.281 = (bf16[1024,2048]{1,0:T(8,128)(2,1)}, bf16[1024,2048]{1,0:T(8,128)(2,1)}) custom-call(bf16[1024,1024]{1,0:T(8,128)(2,1)S(1)} %get-tuple-element.417.x_ref.refs_0_, bf16[1024,2048]{1,0:T(8,128)(2,1)} %bitcast.58.w_ref.other_ref, f32[1,2048]{1,0:T(1,128)S(1)} %select_n.803.bias_ref), custom_call_target="tpu_custom_call" | custom-call | tf_op jit(solution)/shard_map/pallas_call | solution.py:647
  256.9 9.1 %collective-permute-done.33.other_ref = bf16[16,64,1024]{2,1,0:T(8,128)(2,1)} collective-permute-done((bf16[16,64,1024]{2,1,0:T(8,128)(2,1)}, bf16[16,64,1024]{2,1,0:T(8,128)(2,1)}, u32[]{:S(2)}, u32[]{:S(2)}) %collective-permute-start.33) | collective-permute-done | bytes 2097184 | tf_op jit(solution)/shard_map/ppermute | solution.py:50
  272.4 9.1 %shard_map.283 = bf16[32,64,1024]{2,1,0:T(8,128)(2,1)} custom-call(s32[1]{0:T(128)} %bitcast._.core_ref, bf16[1024,2048]{1,0:T(8,128)(2,1)} %get-tuple-element.425.x_ref.b_ref, bf16[1024,1024]{1,0:T(8,128)(2,1)S(1)} %bitcast_select_fusion.y_ref.refs_1_.x_ref.rest_ref), custom_call_target="tpu_custom_call" | custom-call | tf_op jit(solution)/shard_map/pallas_call | solution.py:390
  282.1 14.1 %shard_map.284 = bf16[1024,1024]{1,0:T(8,128)(2,1)S(1)} custom-call(s32[1]{0:T(128)} %bitcast._.core_ref, bf16[1024,2048]{1,0:T(8,128)(2,1)} %get-tuple-element.416.a_ref.refs_0_, bf16[1024,2048]{1,0:T(8,128)(2,1)} %get-tuple-element.425.x_ref.b_ref, bf16[2048,1024]{1,0:T(8,128)(2,1)} %bitcast.246, bf16[2048,1024]{1,0:T(8,128)(2,1)} %bitcast.60.other_ref.w_ref, ...), custom_call_target="tpu_custom_call" | custom-call | tf_op jit(solution)/shard_map/pallas_call | solution.py:390
  297.5 9.3 %shard_map.285 = (bf16[16,64,1024]{2,1,0:T(8,128)(2,1)S(1)}, bf16[16,64,1024]{2,1,0:T(8,128)(2,1)S(1)}) custom-call(s32[3]{0:T(128)S(1)} %pad_add_fusion.12.info_ref, bf16[1024,2048]{1,0:T(8,128)(2,1)} %get-tuple-element.416.a_ref.refs_0_, bf16[1024,1024]{1,0:T(8,128)(2,1)} %copy-done, bf16[32,64,1024]{2,1,0:T(8,128)(2,1)} %collective-permute-done.35.refs_2_), custom_call_target="tpu_custom_call" | custom-call | tf_op jit(solution)/shard_map/pallas_call | solution.py:390
  307.5 8.7 %shard_map.286 = (bf16[1024,2048]{1,0:T(8,128)(2,1)}, f32[1,2048]{1,0:T(1,128)S(1)}) custom-call(s32[1]{0:T(128)} %bitcast._.core_ref, bf16[1024,1024]{1,0:T(8,128)(2,1)S(1)} %copy-done.1, bf16[2048,1024]{1,0:T(8,128)(2,1)} %bitcast.247, bf16[1024,2048]{1,0:T(8,128)(2,1)} %get-tuple-element.436.slope_ref), custom_call_target="tpu_custom_call" | custom-call | tf_op jit(solution)/shard_map/pallas_call | solution.py:390
  316.2 8.8 %shard_map.287 = (bf16[1024,2048]{1,0:T(8,128)(2,1)}, f32[1,2048]{1,0:T(1,128)S(1)}) custom-call(s32[1]{0:T(128)} %bitcast._.core_ref, bf16[1024,1024]{1,0:T(8,128)(2,1)S(1)} %copy-done.1, bf16[2048,1024]{1,0:T(8,128)(2,1)} %bitcast.60.other_ref.w_ref, bf16[1024,2048]{1,0:T(8,128)(2,1)} %get-tuple-element.438.slope_ref), custom_call_target="tpu_custom_call" | custom-call | tf_op jit(solution)/shard_map/pallas_call | solution.py:390
  337.9 16.4 %shard_map.290 = (bf16[1024,1024]{1,0:T(8,128)(2,1)S(1)}, f32[4,3,1024]{2,1,0:T(4,128)S(1)}) custom-call(s32[1]{0:T(128)} %bitcast._.core_ref, bf16[1024,2048]{1,0:T(8,128)(2,1)} %get-tuple-element.447.a_ref.refs_1_, bf16[1024,2048]{1,0:T(8,128)(2,1)} %get-tuple-element.448.y_ref.b_ref, bf16[1024,2048]{1,0:T(8,128)(2,1)} %bitcast.245, ...), custom_call_target="tpu_custom_call" | custom-call | tf_op jit(solution)/shard_map/pallas_call | solution.py:390
  359.1 8.8 %shard_map.293 = (bf16[16,32,2048]{2,1,0:T(8,128)(2,1)S(1)}, bf16[16,32,2048]{2,1,0:T(8,128)(2,1)S(1)}) custom-call(s32[3]{0:T(128)S(1)} %pad_add_fusion.12.info_ref, bf16[1024,1024]{1,0:T(8,128)(2,1)} %copy-done.11, bf16[1024,2048]{1,0:T(8,128)(2,1)} %get-tuple-element.447.a_ref.refs_1_, bf16[32,32,2048]{2,1,0:T(8,128)(2,1)} %collective-permute-done.38.refs_2_), custom_call_target="tpu_custom_call" | custom-call | tf_op jit(solution)/shard_map/pallas_call | solution.py:390
  374.4 11.8 %shard_map.294 = bf16[16,64,1536]{2,1,0:T(8,128)(2,1)S(1)} custom-call(s32[2]{0:T(128)S(1)} %copy-done.89, bf16[16,64,1536]{2,1,0:T(8,128)(2,1)} %bitcast.208, bf16[16,64,1024]{2,1,0:T(8,128)(2,1)S(1)} %bitcast.218), custom_call_target="tpu_custom_call" | custom-call | tf_op jit(solution)/shard_map/pallas_call | solution.py:334
  387.9 11.6 %shard_map.295 = bf16[16,64,1536]{2,1,0:T(8,128)(2,1)S(1)} custom-call(s32[2]{0:T(128)S(1)} %copy-done.89, bf16[16,64,1536]{2,1,0:T(8,128)(2,1)} %bitcast.206, bf16[16,64,1024]{2,1,0:T(8,128)(2,1)S(1)} %bitcast.219), custom_call_target="tpu_custom_call" | custom-call | tf_op jit(solution)/shard_map/pallas_call | solution.py:334
  414.1 13.0 %shard_map.300 = (bf16[1024,1024]{1,0:T(8,128)(2,1)S(1)}, f32[4,3,1024]{2,1,0:T(4,128)S(1)}) custom-call(s32[1]{0:T(128)} %bitcast._.core_ref, bf16[1024,1536]{1,0:T(8,128)(2,1)} %bitcast.197, bf16[1024,1536]{1,0:T(8,128)(2,1)} %bitcast.200, bf16[1024,2048]{1,0:T(8,128)(2,1)} %bitcast.239, bf16[1024,2048]{1,0:T(8,128)(2,1)} %bitcast.243, ...), custom_call_target="tpu_custom_call" | custom-call | tf_op jit(solution)/shard_map/pallas_call | solution.py:390
  436.4 10.6 %shard_map.303 = (bf16[16,32,2048]{2,1,0:T(8,128)(2,1)}, bf16[16,32,2048]{2,1,0:T(8,128)(2,1)S(1)}) custom-call(s32[3]{0:T(128)S(1)} %pad_add_fusion.12.info_ref, bf16[1024,1024]{1,0:T(8,128)(2,1)} %bitcast.185, bf16[1024,1536]{1,0:T(8,128)(2,1)} %bitcast.198, bf16[32,32,1536]{2,1,0:T(8,128)(2,1)} %collective-permute-done.43.refs_2_, ...), custom_call_target="tpu_custom_call" | custom-call | tf_op jit(solution)/shard_map/pallas_call | solution.py:390
  447.0 10.1 %collective-permute-done.47 = bf16[4,64,1024]{2,1,0:T(8,128)(2,1)} collective-permute-done((bf16[4,64,1024]{2,1,0:T(8,128)(2,1)}, bf16[4,64,1024]{2,1,0:T(8,128)(2,1)}, u32[]{:S(2)}, u32[]{:S(2)}) %collective-permute-start.47) | collective-permute-done | bytes 524320 | tf_op jit(solution)/shard_map/ppermute | solution.py:54
  467.1 11.4 %shard_map.306 = bf16[4,256,1536]{2,1,0:T(8,128)(2,1)S(1)} custom-call(s32[2]{0:T(128)S(1)} %copy-done.87, bf16[4,256,1536]{2,1,0:T(8,128)(2,1)} %bitcast.204, bf16[4,256,1024]{2,1,0:T(8,128)(2,1)S(1)} %bitcast.216), custom_call_target="tpu_custom_call" | custom-call | tf_op jit(solution)/shard_map/pallas_call | solution.py:334
  493.4 11.2 %shard_map.311 = bf16[4,256,1536]{2,1,0:T(8,128)(2,1)S(1)} custom-call(s32[2]{0:T(128)S(1)} %copy-done.87, bf16[4,256,1536]{2,1,0:T(8,128)(2,1)} %bitcast.202, bf16[4,256,1024]{2,1,0:T(8,128)(2,1)S(1)} %bitcast.217), custom_call_target="tpu_custom_call" | custom-call | tf_op jit(solution)/shard_map/pallas_call | solution.py:334
  507.9 10.5 %shard_map.313 = (bf16[16,32,2048]{2,1,0:T(8,128)(2,1)}, bf16[16,32,2048]{2,1,0:T(8,128)(2,1)S(1)}) custom-call(s32[3]{0:T(128)S(1)} %pad_add_fusion.12.info_ref, bf16[1024,1024]{1,0:T(8,128)(2,1)} %bitcast.181, bf16[1024,1536]{1,0:T(8,128)(2,1)} %bitcast.211, bf16[32,32,1536]{2,1,0:T(8,128)(2,1)} %collective-permute-done.54.refs_2_, ...), custom_call_target="tpu_custom_call" | custom-call | tf_op jit(solution)/shard_map/pallas_call | solution.py:390
  530.6 13.4 %shard_map.314 = (f32[1024,1024]{1,0:T(8,128)}, f32[4,3,1024]{2,1,0:T(4,128)S(1)}) custom-call(s32[1]{0:T(128)} %bitcast._.core_ref, bf16[1024,1536]{1,0:T(8,128)(2,1)} %bitcast.212, bf16[1024,1536]{1,0:T(8,128)(2,1)} %bitcast.210, bf16[1024,2048]{1,0:T(8,128)(2,1)} %bitcast.235, bf16[1024,2048]{1,0:T(8,128)(2,1)} %bitcast.35.w_ref.other_ref, ...), custom_call_target="tpu_custom_call" | custom-call | tf_op jit(solution)/shard_map/pallas_call | solution.py:390
  591.0 11.9 %collective-permute-done.63 = bf16[4,64,1024]{2,1,0:T(8,128)(2,1)} collective-permute-done((bf16[4,64,1024]{2,1,0:T(8,128)(2,1)}, bf16[4,64,1024]{2,1,0:T(8,128)(2,1)}, u32[]{:S(2)}, u32[]{:S(2)}) %collective-permute-start.63) | collective-permute-done | bytes 524320 | tf_op jit(solution)/shard_map/ppermute | solution.py:54
  (589 shorter events, 346.1 us)
Async XLA Ops:
  15.1 23.9 %collective-permute-start.5 = (bf16[4,64,1024]{2,1,0:T(8,128)(2,1)}, bf16[4,64,1024]{2,1,0:T(8,128)(2,1)S(1)}, u32[]{:S(2)}, u32[]{:S(2)}) collective-permute-start(bf16[4,64,1024]{2,1,0:T(8,128)(2,1)} %get-tuple-element.643), channel_id=1, source_target_pairs={{0,24},{1,25},{2,26},{3,27},{4,28},{5,29},{6,30},{7,31},{8,16},{9,... | collective-permute-start | bytes 1572872 | tf_op jit(solution)/shard_map/ppermute | solution.py:54
  60.4 26.8 %collective-permute-start.14 = (bf16[16,32,2048]{2,1,0:T(8,128)(2,1)}, bf16[16,32,2048]{2,1,0:T(8,128)(2,1)}, u32[]{:S(2)}, u32[]{:S(2)}) collective-permute-start(bf16[16,32,2048]{2,1,0:T(8,128)(2,1)} %shard_map.253.mine_ref), channel_id=1, source_target_pairs={{0,16},{1,17},{2,18},{3,19},{4,20},{5,21},{6,22},{7,23},{8,9},{9,8... | collective-permute-start | bytes 6291464 | tf_op jit(solution)/shard_map/ppermute | solution.py:50
  114.7 25.2 %collective-permute-start.19 = (bf16[16,32,2048]{2,1,0:T(8,128)(2,1)S(1)}, bf16[16,32,2048]{2,1,0:T(8,128)(2,1)S(1)}, u32[]{:S(2)}, u32[]{:S(2)}) collective-permute-start(bf16[16,32,2048]{2,1,0:T(8,128)(2,1)S(1)} %shard_map.262.mine_ref), channel_id=1, source_target_pairs={{0,16},{1,17},{2,18},{3,19},{4,20},{5,21},{6,22},{7,23},{8,9},{9,8... | collective-permute-start | bytes 6291464 | tf_op jit(solution)/shard_map/ppermute | solution.py:50
  143.7 26.6 %collective-permute-start.24 = (bf16[32,32,2048]{2,1,0:T(8,128)(2,1)}, bf16[32,32,2048]{2,1,0:T(8,128)(2,1)S(1)}, u32[]{:S(2)}, u32[]{:S(2)}) collective-permute-start(bf16[32,32,2048]{2,1,0:T(8,128)(2,1)} %shard_map.266), channel_id=1, source_target_pairs={{0,8},{1,9},{2,10},{3,11},{4,12},{5,13},{6,14},{7,15},{8,0},{9,1},... | collective-permute-start | bytes 12582920 | tf_op jit(solution)/shard_map/ppermute | solution.py:50
  145.9 24.4 %collective-permute-start.23 = (bf16[4,64,1024]{2,1,0:T(8,128)(2,1)S(1)}, bf16[4,64,1024]{2,1,0:T(8,128)(2,1)S(1)}, u32[]{:S(2)}, u32[]{:S(2)}) collective-permute-start(bf16[4,64,1024]{2,1,0:T(8,128)(2,1)S(1)} %get-tuple-element.639), channel_id=1, source_target_pairs={{0,24},{1,25},{2,26},{3,27},{4,28},{5,29},{6,30},{7,31},{8,16},{9,... | collective-permute-start | bytes 1572872 | tf_op jit(solution)/shard_map/ppermute | solution.py:54
  150.7 19.6 %collective-permute-start.25 = (bf16[4,32,2048]{2,1,0:T(8,128)(2,1)S(1)}, bf16[4,32,2048]{2,1,0:T(8,128)(2,1)S(1)}, u32[]{:S(2)}, u32[]{:S(2)}) collective-permute-start(bf16[4,32,2048]{2,1,0:T(8,128)(2,1)S(1)} %shard_map.267.mine_ref), channel_id=1, source_target_pairs={{0,2},{1,3},{2,0},{3,1},{4,6},{5,7},{6,4},{7,5},{8,10},{9,11},{10,... | collective-permute-start | bytes 1572872 | tf_op jit(solution)/shard_map/ppermute | solution.py:50
  191.2 25.2 %collective-permute-start.29 = (bf16[16,32,2048]{2,1,0:T(8,128)(2,1)S(1)}, bf16[16,32,2048]{2,1,0:T(8,128)(2,1)S(1)}, u32[]{:S(2)}, u32[]{:S(2)}) collective-permute-start(bf16[16,32,2048]{2,1,0:T(8,128)(2,1)S(1)} %shard_map.273.mine_ref), channel_id=1, source_target_pairs={{0,16},{1,17},{2,18},{3,19},{4,20},{5,21},{6,22},{7,23},{8,9},{9,8... | collective-permute-start | bytes 6291464 | tf_op jit(solution)/shard_map/ppermute | solution.py:50
  220.3 21.7 %collective-permute-start.32 = (bf16[32,32,2048]{2,1,0:T(8,128)(2,1)}, bf16[32,32,2048]{2,1,0:T(8,128)(2,1)}, u32[]{:S(2)}, u32[]{:S(2)}) collective-permute-start(bf16[32,32,2048]{2,1,0:T(8,128)(2,1)} %shard_map.277), channel_id=1, source_target_pairs={{0,8},{1,9},{2,10},{3,11},{4,12},{5,13},{6,14},{7,15},{8,0},{9,1},... | collective-permute-start | bytes 12582920 | tf_op jit(solution)/shard_map/ppermute | solution.py:50
  240.5 25.5 %collective-permute-start.33 = (bf16[16,64,1024]{2,1,0:T(8,128)(2,1)}, bf16[16,64,1024]{2,1,0:T(8,128)(2,1)}, u32[]{:S(2)}, u32[]{:S(2)}) collective-permute-start(bf16[16,64,1024]{2,1,0:T(8,128)(2,1)} %shard_map.280.mine_ref), channel_id=1, source_target_pairs={{0,16},{1,17},{2,18},{3,19},{4,20},{5,21},{6,22},{7,23},{8,9},{9,8... | collective-permute-start | bytes 6291464 | tf_op jit(solution)/shard_map/ppermute | solution.py:50
  306.9 26.0 %collective-permute-start.36 = (bf16[16,64,1024]{2,1,0:T(8,128)(2,1)S(1)}, bf16[16,64,1024]{2,1,0:T(8,128)(2,1)S(1)}, u32[]{:S(2)}, u32[]{:S(2)}) collective-permute-start(bf16[16,64,1024]{2,1,0:T(8,128)(2,1)S(1)} %get-tuple-element.440), channel_id=1, source_target_pairs={{0,16},{1,17},{2,18},{3,19},{4,20},{5,21},{6,22},{7,23},{8,9},{9,8... | collective-permute-start | bytes 6291464 | tf_op jit(solution)/shard_map/ppermute | solution.py:50
  336.2 22.9 %collective-permute-start.38 = (bf16[32,32,2048]{2,1,0:T(8,128)(2,1)}, bf16[32,32,2048]{2,1,0:T(8,128)(2,1)}, u32[]{:S(2)}, u32[]{:S(2)}) collective-permute-start(bf16[32,32,2048]{2,1,0:T(8,128)(2,1)} %shard_map.288), channel_id=1, source_target_pairs={{0,8},{1,9},{2,10},{3,11},{4,12},{5,13},{6,14},{7,15},{8,0},{9,1},... | collective-permute-start | bytes 12582920 | tf_op jit(solution)/shard_map/ppermute | solution.py:50
  337.3 21.8 %collective-permute-start.37 = (bf16[8,64,1024]{2,1,0:T(8,128)(2,1)S(1)}, bf16[8,64,1024]{2,1,0:T(8,128)(2,1)S(1)}, u32[]{:S(2)}, u32[]{:S(2)}) collective-permute-start(bf16[8,64,1024]{2,1,0:T(8,128)(2,1)S(1)} %get-tuple-element.450), channel_id=1, source_target_pairs={{0,1},{1,0},{2,3},{3,2},{4,5},{5,4},{6,7},{7,6},{8,24},{9,25},{10,... | collective-permute-start | bytes 3145736 | tf_op jit(solution)/shard_map/ppermute | solution.py:50
  371.4 35.5 %collective-permute-start.40 = (bf16[16,32,2048]{2,1,0:T(8,128)(2,1)}, bf16[16,32,2048]{2,1,0:T(8,128)(2,1)}, u32[]{:S(2)}, u32[]{:S(2)}) collective-permute-start(bf16[16,32,2048]{2,1,0:T(8,128)(2,1)} %copy-done.90), channel_id=1, source_target_pairs={{0,16},{1,17},{2,18},{3,19},{4,20},{5,21},{6,22},{7,23},{8,9},{9,8... | collective-permute-start | bytes 6291464 | tf_op jit(solution)/shard_map/ppermute | solution.py:50
  372.0 34.9 %collective-permute-start.39 = (bf16[4,64,1024]{2,1,0:T(8,128)(2,1)S(1)}, bf16[4,64,1024]{2,1,0:T(8,128)(2,1)S(1)}, u32[]{:S(2)}, u32[]{:S(2)}) collective-permute-start(bf16[4,64,1024]{2,1,0:T(8,128)(2,1)S(1)} %get-tuple-element.459), channel_id=1, source_target_pairs={{0,2},{1,3},{2,0},{3,1},{4,6},{5,7},{6,4},{7,5},{8,10},{9,11},{10,... | collective-permute-start | bytes 1572872 | tf_op jit(solution)/shard_map/ppermute | solution.py:50
  432.6 24.5 %collective-permute-start.47 = (bf16[4,64,1024]{2,1,0:T(8,128)(2,1)}, bf16[4,64,1024]{2,1,0:T(8,128)(2,1)}, u32[]{:S(2)}, u32[]{:S(2)}) collective-permute-start(bf16[4,64,1024]{2,1,0:T(8,128)(2,1)} %bitcast.67), channel_id=1, source_target_pairs={{0,24},{1,25},{2,26},{3,27},{4,28},{5,29},{6,30},{7,31},{8,16},{9,... | collective-permute-start | bytes 1572872 | tf_op jit(solution)/shard_map/ppermute | solution.py:54
  433.6 23.5 %collective-permute-start.49 = (bf16[4,32,2048]{2,1,0:T(8,128)(2,1)}, bf16[4,32,2048]{2,1,0:T(8,128)(2,1)S(1)}, u32[]{:S(2)}, u32[]{:S(2)}) collective-permute-start(bf16[4,32,2048]{2,1,0:T(8,128)(2,1)} %get-tuple-element.489), channel_id=1, source_target_pairs={{0,2},{1,3},{2,0},{3,1},{4,6},{5,7},{6,4},{7,5},{8,10},{9,11},{10,... | collective-permute-start | bytes 1572872 | tf_op jit(solution)/shard_map/ppermute | solution.py:50
  460.2 26.0 %collective-permute-start.51 = (bf16[16,32,2048]{2,1,0:T(8,128)(2,1)}, bf16[16,32,2048]{2,1,0:T(8,128)(2,1)}, u32[]{:S(2)}, u32[]{:S(2)}) collective-permute-start(bf16[16,32,2048]{2,1,0:T(8,128)(2,1)} %get-tuple-element.500), channel_id=1, source_target_pairs={{0,16},{1,17},{2,18},{3,19},{4,20},{5,21},{6,22},{7,23},{8,9},{9,8... | collective-permute-start | bytes 6291464 | tf_op jit(solution)/shard_map/ppermute | solution.py:50
  461.3 24.9 %collective-permute-start.50 = (bf16[2,32,2048]{2,1,0:T(8,128)(2,1)}, bf16[2,32,2048]{2,1,0:T(8,128)(2,1)S(1)}, u32[]{:S(2)}, u32[]{:S(2)}) collective-permute-start(bf16[2,32,2048]{2,1,0:T(8,128)(2,1)} %get-tuple-element.499), channel_id=1, source_target_pairs={{0,4},{1,5},{2,6},{3,7},{4,0},{5,1},{6,2},{7,3},{8,12},{9,13},{10,... | collective-permute-start | bytes 786440 | tf_op jit(solution)/shard_map/ppermute | solution.py:50
  519.7 25.5 %collective-permute-start.57 = (bf16[16,32,2048]{2,1,0:T(8,128)(2,1)}, bf16[16,32,2048]{2,1,0:T(8,128)(2,1)}, u32[]{:S(2)}, u32[]{:S(2)}) collective-permute-start(bf16[16,32,2048]{2,1,0:T(8,128)(2,1)} %get-tuple-element.527), channel_id=1, source_target_pairs={{0,16},{1,17},{2,18},{3,19},{4,20},{5,21},{6,22},{7,23},{8,9},{9,8... | collective-permute-start | bytes 6291464 | tf_op jit(solution)/shard_map/ppermute | solution.py:50
  520.4 23.6 %collective-permute-start.56 = (bf16[4,32,2048]{2,1,0:T(8,128)(2,1)}, bf16[4,32,2048]{2,1,0:T(8,128)(2,1)S(1)}, u32[]{:S(2)}, u32[]{:S(2)}) collective-permute-start(bf16[4,32,2048]{2,1,0:T(8,128)(2,1)} %get-tuple-element.526), channel_id=1, source_target_pairs={{0,2},{1,3},{2,0},{3,1},{4,6},{5,7},{6,4},{7,5},{8,10},{9,11},{10,... | collective-permute-start | bytes 1572872 | tf_op jit(solution)/shard_map/ppermute | solution.py:50
  578.5 24.4 %collective-permute-start.63 = (bf16[4,64,1024]{2,1,0:T(8,128)(2,1)}, bf16[4,64,1024]{2,1,0:T(8,128)(2,1)}, u32[]{:S(2)}, u32[]{:S(2)}) collective-permute-start(bf16[4,64,1024]{2,1,0:T(8,128)(2,1)} %bitcast.87), channel_id=1, source_target_pairs={{0,24},{1,25},{2,26},{3,27},{4,28},{5,29},{6,30},{7,31},{8,16},{9,... | collective-permute-start | bytes 1572872 | tf_op jit(solution)/shard_map/ppermute | solution.py:54
  579.8 23.1 %collective-permute-start.65 = (f32[1,32,2048]{2,1,0:T(8,128)S(1)}, f32[1,32,2048]{2,1,0:T(8,128)S(1)}, u32[]{:S(2)}, u32[]{:S(2)}) collective-permute-start(f32[1,32,2048]{2,1,0:T(8,128)S(1)} %copy-done.94), channel_id=1, source_target_pairs={{0,8},{1,9},{2,10},{3,11},{4,12},{5,13},{6,14},{7,15},{8,0},{9,1},... | collective-permute-start | bytes 786440 | tf_op jit(solution)/shard_map/ppermute | solution.py:50
  579.8 23.1 %collective-permute-start.66 = (bf16[4,32,2048]{2,1,0:T(8,128)(2,1)S(1)}, bf16[4,32,2048]{2,1,0:T(8,128)(2,1)S(1)}, u32[]{:S(2)}, u32[]{:S(2)}) collective-permute-start(bf16[4,32,2048]{2,1,0:T(8,128)(2,1)S(1)} %copy-done.92), channel_id=1, source_target_pairs={{0,2},{1,3},{2,0},{3,1},{4,6},{5,7},{6,4},{7,5},{8,10},{9,11},{10,... | collective-permute-start | bytes 1572872 | tf_op jit(solution)/shard_map/ppermute | solution.py:50
  581.3 21.6 %collective-permute-start.67 = (f32[4,640]{1,0:T(4,128)S(1)}, f32[4,640]{1,0:T(4,128)S(1)}, u32[]{:S(2)}, u32[]{:S(2)}) collective-permute-start(f32[4,640]{1,0:T(4,128)S(1)} %slice_select_fusion.2), channel_id=1, source_target_pairs={{0,4},{1,5},{2,6},{3,7},{4,0},{5,1},{6,2},{7,3},{8,12},{9,13},{10,... | collective-permute-start | bytes 30728 | tf_op jit(solution)/shard_map/ppermute | solution.py:50
  (168 other events, 1467.1 us)

commit v4 on v3

--- a/solution.py
+++ b/solution.py
@@ -1,3 +1,4 @@
+import math
 from functools import partial
 
 import jax
@@ -17,9 +18,14 @@
 
 negative = -1e30
 highest = lax.Precision.HIGHEST
-VMEM = 48 * 1024 * 1024
+MIB = 1024 * 1024
 bf16, f32 = jnp.bfloat16, jnp.float32
 NO_COST = pl.CostEstimate(flops=0, bytes_accessed=0, transcendentals=0)
+
+
+def params(blocks, margin=6):
+    size = sum(math.prod(shape) * jnp.dtype(dtype).itemsize * n for shape, dtype, n in blocks)
+    return pltpu.CompilerParams(vmem_limit_bytes=(-(-size // MIB) + margin) * MIB)
 
 
 class Place:
@@ -95,7 +101,7 @@
         in_specs=[pl.BlockSpec(memory_space=pltpu.SMEM), spec, spec],
         out_specs=pl.BlockSpec((2 * m, r, block), lambda j: (0, 0, j)),
         out_shape=jax.ShapeDtypeStruct((2 * m, r, n), mine.dtype),
-        compiler_params=pltpu.CompilerParams(vmem_limit_bytes=VMEM),
+        compiler_params=params([((4 * m, r, block), mine.dtype, 2)], 2),
         cost_estimate=NO_COST,
     )(jnp.stack([jnp.int32(k), value.astype(jnp.int32)]), mine, other)
 
@@ -126,7 +132,7 @@
         + [pl.BlockSpec((blocks, r, block), lambda j: (0, 0, j))] * 2,
         out_specs=[pl.BlockSpec((blocks // 2, r, block), lambda j: (0, 0, j))] * 2,
         out_shape=[out, out],
-        compiler_params=pltpu.CompilerParams(vmem_limit_bytes=VMEM),
+        compiler_params=params([((3 * blocks, r, block), dtype, 2)], 3),
         cost_estimate=NO_COST,
     )(jnp.stack([jnp.int32(k), value.astype(jnp.int32)]), a, b)
 
@@ -147,21 +153,21 @@
 def scatter_small(place, value):
     bit = place.total // 2
     while bit:
-        low_half, high_half = value[:bit], value[bit:]
+        half = value.shape[1] // 2
+        low_half, high_half = value[:, :half], value[:, half:]
         mine = (place.me & bit) != 0
-        keep = jnp.where(mine, high_half, low_half)
         (send,) = yield [jnp.where(mine, low_half, high_half)]
         (got,) = yield [place.flip(send, (bit, bit))]
-        value = keep + got
+        value = jnp.where(mine, high_half, low_half) + got
         bit //= 2
-    return value[0]
-
-
-def gather(place, keep, send):
+    return value
+
+
+def gather(place, keep, send, ahead=0):
     core = (place.core_bit, place.core_bit)
     have = ([], [])
     blocks, out = keep[None], send[None]
-    for pair in [core] + place.z[::-1] + place.xy:
+    for pair in [core] + place.xy[:ahead] + place.z[::-1] + place.xy[ahead:]:
         (out,) = yield [out]
         (got,) = yield [place.flip(out, pair)]
         k = [below(h, b) for h, b in zip(have, pair)]
@@ -276,24 +282,46 @@
     return apart, together
 
 
+def head_pairs(sides, refs):
+    a, b, width = refs[0].shape
+    rows, width = a * b, width // 3
+    for i, side in enumerate(sides):
+        for c in range(0, width, LANES):
+            q, k, v = (
+                refs[i][:, :, at : at + LANES].reshape(rows, LANES)
+                for at in (c, width + c, 2 * width + c)
+            )
+            yield i, side, c, q * bf16(E ** (-0.5)), k, v
+
+
+def in_turn(items, first, last):
+    waiting = None
+    for item in items:
+        ready = first(*item)
+        if waiting is not None:
+            last(*waiting)
+        waiting = ready
+    last(*waiting)
+
+
 def attention_forward(make_bias, scalar_ref, own_ref, other_ref, out_ref):
     a, b, width = own_ref.shape
     rows, width = a * b, width // 3
     bias = make_bias(scalar_ref[0], rows, 1)
     apart, together = two_heads(rows)
-    factor = E ** (-0.5)
-    for side, qkv_ref in enumerate((own_ref, other_ref)):
-        for c in range(0, width, LANES):
-            q = qkv_ref[:, :, c : c + LANES].reshape(rows, LANES) * bf16(factor)
-            k = qkv_ref[:, :, width + c : width + c + LANES].reshape(rows, LANES)
-            v = qkv_ref[:, :, 2 * width + c : 2 * width + c + LANES].reshape(rows, LANES)
-            scores = dot_t(apart(q), k).reshape(2, rows, rows) + bias[None]
-            weights = jnp.exp(scores - jnp.max(scores, axis=2, keepdims=True))
-            scale = 1.0 / jnp.sum(weights, axis=2, keepdims=True)
-            weights = weights.astype(bf16).reshape(2 * rows, rows)
-            mixed = jnp.dot(weights, v, preferred_element_type=f32)
-            mixed = together(mixed * scale.reshape(2 * rows, 1)).astype(out_ref.dtype)
-            out_ref[:, :, columns(scalar_ref, side, c)] = mixed.reshape(a, b, LANES)
+
+    def first(i, side, c, q, k, v):
+        scores = dot_t(apart(q), k).reshape(2, rows, rows) + bias[None]
+        weights = jnp.exp(scores - jnp.max(scores, axis=2, keepdims=True))
+        scale = 1.0 / jnp.sum(weights, axis=2, keepdims=True)
+        return side, c, v, weights.astype(bf16).reshape(2 * rows, rows), scale
+
+    def last(side, c, v, weights, scale):
+        mixed = jnp.dot(weights, v, preferred_element_type=f32) * scale.reshape(2 * rows, 1)
+        mixed = together(mixed).astype(out_ref.dtype)
+        out_ref[:, :, columns(scalar_ref, side, c)] = mixed.reshape(a, b, LANES)
+
+    in_turn(head_pairs((0, 1), (own_ref, other_ref)), first, last)
 
 
 def attention_backward(make_bias, sides, scalar_ref, *refs):
@@ -302,30 +330,27 @@
     rows, width = a * b, width // 3
     bias = make_bias(scalar_ref[0], rows, 0)
     apart, together = two_heads(rows)
-    factor = E ** (-0.5)
-    for i, side in enumerate(sides):
-        qkv_ref, out_ref = refs[i], refs[len(sides) + 1 + i]
-        for c in range(0, width, LANES):
-            q = qkv_ref[:, :, c : c + LANES].reshape(rows, LANES) * bf16(factor)
-            k = qkv_ref[:, :, width + c : width + c + LANES].reshape(rows, LANES)
-            v = qkv_ref[:, :, 2 * width + c : 2 * width + c + LANES].reshape(rows, LANES)
-            g = grad_ref[:, :, columns(scalar_ref, side, c)].reshape(rows, LANES)
-            scores = dot_t(apart(k), q).reshape(2, rows, rows) + bias[None]
-            weights = jnp.exp(scores - jnp.max(scores, axis=1, keepdims=True))
-            probs = weights * (1.0 / jnp.sum(weights, axis=1, keepdims=True))
-            prob_grad = dot_t(apart(v), g).reshape(2, rows, rows)
-            delta = jnp.sum(probs * prob_grad, axis=1, keepdims=True)
-            score_grad = (probs * (prob_grad - delta)).astype(bf16)
-            turned = jnp.concatenate([score_grad[0].T, score_grad[1].T], axis=0)
-            dq = jnp.dot(turned, k, preferred_element_type=f32) * factor
-            dk = jnp.dot(score_grad.reshape(2 * rows, rows), q, preferred_element_type=f32)
-            dv = jnp.dot(
-                probs.astype(bf16).reshape(2 * rows, rows), g, preferred_element_type=f32
-            )
-            for index, grad in enumerate((dq, dk, dv)):
-                start = index * width + c
-                merged = together(grad).astype(out_ref.dtype)
-                out_ref[:, :, start : start + LANES] = merged.reshape(a, b, LANES)
+
+    def first(i, side, c, q, k, v):
+        g = grad_ref[:, :, columns(scalar_ref, side, c)].reshape(rows, LANES)
+        scores = dot_t(apart(k), q).reshape(2, rows, rows) + bias[None]
+        prob_grad = dot_t(apart(v), g).reshape(2, rows, rows)
+        weights = jnp.exp(scores - jnp.max(scores, axis=1, keepdims=True))
+        probs = weights * (1.0 / jnp.sum(weights, axis=1, keepdims=True))
+        delta = jnp.sum(probs * prob_grad, axis=1, keepdims=True)
+        return i, c, q, k, g, probs.astype(bf16), (probs * (prob_grad - delta)).astype(bf16)
+
+    def last(i, c, q, k, g, probs, score_grad):
+        turned = jnp.concatenate([score_grad[0].T, score_grad[1].T], axis=0)
+        dq = jnp.dot(turned, k, preferred_element_type=f32) * E ** (-0.5)
+        dk = jnp.dot(score_grad.reshape(2 * rows, rows), q, preferred_element_type=f32)
+        dv = jnp.dot(probs.reshape(2 * rows, rows), g, preferred_element_type=f32)
+        for index, grad in enumerate((dq, dk, dv)):
+            start = index * width + c
+            merged = together(grad).astype(bf16).reshape(a, b, LANES)
+            refs[len(sides) + 1 + i][:, :, start : start + LANES] = merged
+
+    in_turn(head_pairs(sides, refs), first, last)
 
 
 def run_attention(body, scalars, block, grid, index, inputs, out_widths):
@@ -338,7 +363,9 @@
         + [pl.BlockSpec((a, b, x.shape[-1]), index) for x in inputs],
         out_specs=[pl.BlockSpec((a, b, width), index) for width in out_widths],
         out_shape=[jax.ShapeDtypeStruct((*outer, width), bf16) for width in out_widths],
-        compiler_params=pltpu.CompilerParams(vmem_limit_bytes=VMEM),
+        compiler_params=params(
+            [((a, b, width), bf16, 2) for width in (*(x.shape[-1] for x in inputs), *out_widths)], 8
+        ),
         cost_estimate=NO_COST,
     )(scalars, *inputs)
 
@@ -371,7 +398,7 @@
         in_specs=specs,
         out_specs=[pl.BlockSpec((1, *shape[1:]), lambda i: (i, 0, 0)) for shape, _ in outs],
         out_shape=[jax.ShapeDtypeStruct(shape, dtype) for shape, dtype in outs],
-        compiler_params=pltpu.CompilerParams(vmem_limit_bytes=VMEM),
+        compiler_params=params([(x.shape[1:], f32, 4) for x in arrays]),
         cost_estimate=NO_COST,
     )(*arrays)
 
@@ -386,28 +413,41 @@
 BLOCK = 512
 
 
-def dense(body, grid, scalars, inputs, outs, scratch=()):
+def dense(body, grid, scalars, inputs, outs, scratch=(), margin=6):
+    used = [(block, x.dtype, 1 if index is FIXED else 2) for x, block, index in inputs]
+    used += [(block, dtype, 2) for _, dtype, block, _ in outs]
+    used += [(x.shape, x.dtype, 1) for x in scratch]
+
+    def spec(block, index):
+        if index is FIXED:
+            zeros = (0,) * len(block)
+            return pl.BlockSpec(block, lambda *_: zeros, pipeline_mode=pl.Buffered(1))
+        return pl.BlockSpec(block, index)
+
     return pl.pallas_call(
         body,
         grid_spec=pltpu.PrefetchScalarGridSpec(
             num_scalar_prefetch=1,
             grid=grid,
-            in_specs=[pl.BlockSpec(block, index) for _, block, index in inputs],
+            in_specs=[spec(block, index) for _, block, index in inputs],
             out_specs=[pl.BlockSpec(block, index) for _, _, block, index in outs],
             scratch_shapes=list(scratch),
         ),
         out_shape=[jax.ShapeDtypeStruct(shape, dtype) for shape, dtype, _, _ in outs],
-        compiler_params=pltpu.CompilerParams(vmem_limit_bytes=VMEM),
+        compiler_params=params(used, margin),
         cost_estimate=NO_COST,
     )(scalars, *[x for x, _, _ in inputs])
 
 
+FIXED = None
+
+
 def at(*index):
     return lambda j, ref: index
 
 
 def whole(x):
-    return (x, x.shape, at(*[0] * x.ndim))
+    return (x, x.shape, FIXED)
 
 
 def rows_of(x, rows=256):
@@ -490,7 +530,7 @@
         hidden3_body, (rows // 256,), scalars,
         [*[rows_of(y) for y in actives], *[whole(w) for w in halves], rows_of(x), whole(bias),
          rows_of(mask)],
-        [((rows, width), bf16, (256, width), lambda i, ref: (i, 0))],
+        [((rows, width), bf16, (256, width), lambda i, ref: (i, 0))], margin=30,
     )
     return out
 
@@ -531,10 +571,11 @@
     added_at = (lambda i, ref: (i, 0, 0)) if added.shape[0] > 1 else at(0, 0, 0)
     return dense(
         norm_back_body, (rows // step,), scalars,
-        [*[rows_of(g) for g in grads], *[(w, (w.shape[0], cols), at(0, 0)) for w in halves],
+        [*[rows_of(g) for g in grads], *[(w, (w.shape[0], cols), FIXED) for w in halves],
          rows_of(x), (added, (1, 1, width), added_at), whole(gain[None]), rows_of(rest)],
         [((rows, width), dtype, (step, width), lambda i, ref: (i, 0)),
          ((rows // step, 3, width), f32, (1, 3, width), lambda i, ref: (i, 0, 0))],
+        margin=30 if dtype == f32 else 6,
     )
 
 
@@ -619,9 +660,10 @@
 
 
 def gelu(inner):
-    size = jnp.abs(inner)
-    t = 1.0 / (1.0 + 0.37 * size)
-    bell = jnp.exp(inner * inner * -0.5)
+    size = 1.0 + 0.37 * jnp.abs(inner)
+    t = pl.reciprocal(size, approx=True)
+    t = t * (2.0 - size * t)
+    bell = jnp.exp2(inner * inner * -0.7213475204444817)
     series = TAIL[-1]
     for term in reversed(TAIL[:-1]):
         series = series * t + term
@@ -654,7 +696,9 @@
         ],
         out_specs=[pl.BlockSpec((rows, block), lambda i: (0, i))] * 2,
         out_shape=[out, out],
-        compiler_params=pltpu.CompilerParams(vmem_limit_bytes=VMEM),
+        compiler_params=params(
+            [(x.shape, bf16, 2), ((width, block), bf16, 2), ((rows, block), bf16, 4)]
+        ),
         cost_estimate=NO_COST,
     )(x, weight, bias)
 
@@ -692,9 +736,9 @@
             parts.append(place.tm_flip(part, o) if o else part)
         return parts
 
-    def from_slots(value):
+    def from_slots(value, offsets=range(tm_size)):
         view = value.reshape(tm_size, frames_local, slots_local, value.shape[-1])
-        return [place.tm_flip(view[o], o) if o else view[o] for o in range(tm_size)]
+        return [place.tm_flip(view[o], o) if o else view[o] for o in offsets]
 
     def in_slots(parts):
         return jnp.concatenate(parts, axis=0)
@@ -865,6 +909,13 @@
     inner_grads, send = launch((inner_grad, inner_grad2), s_down, also=[send])
     got = exchanged(send)
 
+    b_sums = [x.reshape(total, -1, thin).swapaxes(0, 1) for x in (b_sum, b_sum2)]
+    late_rows = [x.reshape(-1, width) for x in b_sums]
+    late_rows = jnp.where(
+        core == 0, jnp.concatenate(late_rows, axis=0), jnp.concatenate(late_rows[::-1], axis=0)
+    )
+    late_rows = jnp.concatenate([jnp.sum(down_in.astype(f32), axis=0)[None], late_rows], axis=0)
+
     grad2, sums3 = norm_back(
         inner_grads, up_halves, hidden2, nothing, gains[2], down_in, bf16, here
     )
@@ -916,36 +967,28 @@
     )
     sums1, input_grad = land((sums1, input_grad), s_time, s_space)
     sums1, input_grad = launch((sums1, input_grad), s_time, s_space)
-    g_actions = jnp.dot(onehot.T, sums1[:, 2], precision=highest)
-    sums1, b_sum, b_sum2, down_in, mixed = lax.optimization_barrier(
-        (sums1, b_sum, b_sum2, down_in, mixed)
-    )
-    g_b_down = jnp.sum(down_in.astype(f32), axis=0)
-    g_b_up = in_order(*[x.reshape(total, -1) for x in (b_sum, b_sum2)], 1)
-
-    terms = [
-        g_actions,
-        jnp.stack([jnp.sum(x[:, 0], axis=0) for x in (sums1, sums2, sums3)]),
-        jnp.stack([jnp.sum(x[:, 1], axis=0) for x in (sums1, sums2, sums3)]),
-        g_b_up.reshape(1, -1),
-        g_b_down[None],
-    ]
-    packed = [jnp.moveaxis(x.reshape(x.shape[0], total, -1), 1, 0).reshape(total, -1) for x in terms]
-    packed = jnp.concatenate(packed, axis=1)
-    packed = jnp.pad(packed, ((0, 0), (0, -packed.shape[1] % LANES)))
+    g_actions = jnp.sum(onehot[:, :, None] * sums1[:, 2][:, None, :], axis=0)
+    all_sums = [jnp.sum(x[:, :2], axis=0) for x in (sums1, sums2, sums3)]
+    both_norms = [jnp.stack([x[i] for x in all_sums]) for i in (0, 1)]
+    packed = jnp.concatenate([g_actions, *both_norms, late_rows], axis=0)
     s_small = Chain(scatter_small(place, packed))
     packed = launch(packed, s_small)
     packed = land(packed, s_time, s_space, s_small)
     packed, mixed = launch((packed, mixed), s_time, s_space, s_small)
-    mixed = from_slots(mixed.reshape(frames, slots_local, width))
-    g_w_down = in_order(*finish(s_down), 0).reshape(w_down.shape)
-    g_w_up = in_order(*[x.reshape(rows, total, -1) for x in finish(s_up)], 2).reshape(w_up.shape)
+    near = from_slots(mixed, range(tm_size // 2 + 1))
+    packed, down_sums, up_sums = lax.optimization_barrier((packed, finish(s_down), finish(s_up)))
+    g_w_down = in_order(*down_sums, 0).reshape(w_down.shape)
+    g_w_up = in_order(*[x.reshape(rows, total, -1) for x in up_sums], 2).reshape(w_up.shape)
+    packed = along(packed, s_small)
+    packed, *near = land(packed, s_time, s_space, s_small, also=near)
+    packed, mixed = launch((packed, mixed), s_time, s_space, s_small)
     packed, g_w_down, g_w_up = lax.optimization_barrier((packed, g_w_down, g_w_up))
+    far = from_slots(mixed, range(tm_size // 2 + 1, tm_size))
     packed = along(packed, s_small)
-    packed = along(packed, s_time, s_space, s_small)
+    packed, *far = land(packed, s_time, s_space, s_small, also=far)
+    packed = launch(packed, s_time, s_space, s_small)
+    mixed = in_frames(near + far)
     packed, mixed = lax.optimization_barrier((packed, mixed))
-    mixed = in_frames(mixed)
-    packed = along(packed, s_small)
     while not (s_time.done() and s_space.done() and s_small.done()):
         packed = along(packed, s_time, s_space, s_small)
     summed = s_small.result
@@ -953,26 +996,20 @@
     g_t_qkv, g_t_out = t_rows[:, : 3 * width], t_rows[:, 3 * width :]
     g_s_qkv, g_s_out = s_rows[:, : 3 * width], s_rows[:, 3 * width :]
 
-    sizes = [x.size // total for x in terms]
-    starts = [sum(sizes[:i]) for i in range(len(sizes) + 1)]
-
-    def piece(i, count):
-        return summed[starts[i] : starts[i + 1]].reshape(count, -1)
-
     return (
         mixed.reshape(shape),
         input_grad.reshape(shape),
-        piece(0, ACTIONS),
-        piece(1, 3),
-        piece(2, 3),
+        summed[:8],
+        summed[8:11],
+        summed[11:14],
         g_s_qkv,
         g_s_out,
         g_t_qkv,
         g_t_out,
         g_w_up,
-        piece(3, 1).reshape(-1),
+        summed[15:].reshape(-1),
         g_w_down,
-        piece(4, 1).reshape(-1),
+        summed[14],
     )
 
 

time: 630 us -> 597 us (0.948)
  Pallas kernels: 344 us -> 301 us
  waiting for transfers between devices: 128 us -> 145 us
    pallas_call x24, Pallas kernels: 190 us -> 159 us  [dense(): pl.pallas_call(body, grid_spec=pltpu.PrefetchScalarGridSpec(num_scalar_pr...]
    ppermute x60, waiting for transfers between devices: 69.7 us -> 99.9 us  [flip(): return lax.ppermute(value, AXES, moves)]
    ppermute x12, waiting for transfers between devices: 58.2 us -> 45.1 us  [tm_flip(): return lax.ppermute(value, AXES, moves)]
    pallas_call x6, Pallas kernels: 61.7 us -> 52.6 us  [run_attention(): pl.pallas_call(body, grid=(grid,), in_specs=[pl.BlockSpec(memory_space=pl...]
    unnamed x262 -> x274, local copies, waits for them, and re-layouts: 31.3 us -> 33.1 us
  transfers between devices with their start and end apart: 72 -> 72, of which waited for: 24 -> 31; matrix products, arithmetic and copies ran while one was open for 8% -> 8% of each run, Pallas kernels for 42% -> 38%
where the time goes in v4:
time: 597 us; the launch traced here: 592 us
  Pallas kernels  301 us (50%)
  waiting for transfers between devices  145 us (24%)
  local copies, waits for them, and re-layouts  66.8 us (11%)
  starting transfers between devices  58.1 us (10%)
  other arithmetic  17 us (3%)
    pallas_call x24, Pallas kernels, dense(): pl.pallas_call(body, grid_spec=pltpu.PrefetchScalarGridSpec(num_scalar_pr...  159 us
    ppermute x60, waiting for transfers between devices, flip(): return lax.ppermute(value, AXES, moves)  99.9 us
    pallas_call x6, Pallas kernels, run_attention(): pl.pallas_call(body, grid=(grid,), in_specs=[pl.BlockSpec(memory_space=pl...  52.6 us
    ppermute x60, starting transfers between devices, flip(): return lax.ppermute(value, AXES, moves)  47.6 us
    ppermute x12, waiting for transfers between devices, tm_flip(): return lax.ppermute(value, AXES, moves)  45.1 us
    pallas_call x25, Pallas kernels, merge(): pl.pallas_call(merge_body, grid=(n // block,), in_specs=[pl.BlockSpec(mem...  33.7 us
    unnamed x274, local copies, waits for them, and re-layouts  33.1 us
    pallas_call x2, Pallas kernels, up_project(): pl.pallas_call(up_body, grid=(cols // block,), in_specs=[pl.BlockSpec((ro...  29.1 us
  transfers between devices with their start and end apart: 72, of which 31 were waited for; matrix products, arithmetic and copies ran while one was open for 8% of the time, Pallas kernels for 38%

profile of v4, /device:TPU:1, one launch (start us, length us, event | category | flops | bytes accessed | tf_op | source)
XLA Modules:
  0.0 591.5 jit_solution(365829224790986354)
XLA Ops:
  27.6 11.4 %collective-permute-done.5 = bf16[4,64,1024]{2,1,0:T(8,128)(2,1)} collective-permute-done((bf16[4,64,1024]{2,1,0:T(8,128)(2,1)}, bf16[4,64,1024]{2,1,0:T(8,128)(2,1)}, u32[]{:S(2)}, u32[]{:S(2)}) %collective-permute-start.5) | collective-permute-done | bytes 524320 | tf_op jit(solution)/shard_map/ppermute | solution.py:60
  44.4 10.9 %collective-permute-done.9.other_ref = bf16[4,48,128]{2,1,0:T(8,128)(2,1)S(1)} collective-permute-done((bf16[4,48,128]{2,1,0:T(8,128)(2,1)S(1)}, bf16[4,48,128]{2,1,0:T(8,128)(2,1)S(1)}, u32[]{:S(2)}, u32[]{:S(2)}) %collective-permute-start.9) | collective-permute-done | bytes 49184 | tf_op jit(solution)/shard_map/ppermute | solution.py:56
  67.5 8.7 %collective-permute-done.13.other_ref = bf16[16,48,128]{2,1,0:T(8,128)(2,1)S(1)} collective-permute-done((bf16[16,48,128]{2,1,0:T(8,128)(2,1)S(1)}, bf16[16,48,128]{2,1,0:T(8,128)(2,1)S(1)}, u32[]{:S(2)}, u32[]{:S(2)}) %collective-permute-start.13) | collective-permute-done | bytes 196640 | tf_op jit(solution)/shard_map/ppermute | solution.py:56
  114.5 7.4 %shard_map.267 = bf16[4,256,1024]{2,1,0:T(8,128)(2,1)S(1)} custom-call(s32[2]{0:T(128)S(1)} %copy-done.99, bf16[4,256,1536]{2,1,0:T(8,128)(2,1)S(1)} %bitcast.206, bf16[4,256,1536]{2,1,0:T(8,128)(2,1)S(1)} %bitcast.208), custom_call_target="tpu_custom_call" | custom-call | tf_op jit(solution)/shard_map/pallas_call | solution.py:359
  127.9 11.4 %collective-permute-done.19.other_ref = bf16[16,32,2048]{2,1,0:T(8,128)(2,1)S(1)} collective-permute-done((bf16[16,32,2048]{2,1,0:T(8,128)(2,1)S(1)}, bf16[16,32,2048]{2,1,0:T(8,128)(2,1)S(1)}, u32[]{:S(2)}, u32[]{:S(2)}) %collective-permute-start.19) | collective-permute-done | bytes 2097184 | tf_op jit(solution)/shard_map/ppermute | solution.py:56
  156.6 11.4 %collective-permute-done.23 = bf16[4,64,1024]{2,1,0:T(8,128)(2,1)S(1)} collective-permute-done((bf16[4,64,1024]{2,1,0:T(8,128)(2,1)S(1)}, bf16[4,64,1024]{2,1,0:T(8,128)(2,1)S(1)}, u32[]{:S(2)}, u32[]{:S(2)}) %collective-permute-start.23) | collective-permute-done | bytes 524320 | tf_op jit(solution)/shard_map/ppermute | solution.py:60
  188.2 8.2 %shard_map.278 = bf16[16,64,1024]{2,1,0:T(8,128)(2,1)S(1)} custom-call(s32[2]{0:T(128)S(1)} %pad_add_fusion.8.scalar_ref, bf16[16,64,1536]{2,1,0:T(8,128)(2,1)S(1)} %bitcast.212, bf16[16,64,1536]{2,1,0:T(8,128)(2,1)S(1)} %bitcast.210), custom_call_target="tpu_custom_call" | custom-call | tf_op jit(solution)/shard_map/pallas_call | solution.py:359
  201.1 10.9 %collective-permute-done.29.other_ref = bf16[16,32,2048]{2,1,0:T(8,128)(2,1)S(1)} collective-permute-done((bf16[16,32,2048]{2,1,0:T(8,128)(2,1)S(1)}, bf16[16,32,2048]{2,1,0:T(8,128)(2,1)S(1)}, u32[]{:S(2)}, u32[]{:S(2)}) %collective-permute-start.29) | collective-permute-done | bytes 2097184 | tf_op jit(solution)/shard_map/ppermute | solution.py:56
  218.5 14.5 %shard_map.282 = (bf16[1024,2048]{1,0:T(8,128)(2,1)S(1)}, bf16[1024,2048]{1,0:T(8,128)(2,1)S(1)}) custom-call(bf16[1024,1024]{1,0:T(8,128)(2,1)S(1)} %get-tuple-element.417.x_ref.refs_0_, bf16[1024,2048]{1,0:T(8,128)(2,1)} %bitcast.57.w_ref.own_ref, f32[1,2048]{1,0:T(1,128)S(1)} %select_n.775.bias_ref), custom_call_target="tpu_custom_call" | custom-call | tf_op jit(solution)/shard_map/pallas_call | solution.py:689
  239.6 14.6 %shard_map.284 = (bf16[1024,2048]{1,0:T(8,128)(2,1)S(1)}, bf16[1024,2048]{1,0:T(8,128)(2,1)S(1)}) custom-call(bf16[1024,1024]{1,0:T(8,128)(2,1)S(1)} %get-tuple-element.417.x_ref.refs_0_, bf16[1024,2048]{1,0:T(8,128)(2,1)} %bitcast.58.w_ref.other_ref, f32[1,2048]{1,0:T(1,128)S(1)} %select_n.777.bias_ref), custom_call_target="tpu_custom_call" | custom-call | tf_op jit(solution)/shard_map/pallas_call | solution.py:689
  254.2 9.4 %collective-permute-done.33.other_ref = bf16[16,64,1024]{2,1,0:T(8,128)(2,1)} collective-permute-done((bf16[16,64,1024]{2,1,0:T(8,128)(2,1)}, bf16[16,64,1024]{2,1,0:T(8,128)(2,1)}, u32[]{:S(2)}, u32[]{:S(2)}) %collective-permute-start.33) | collective-permute-done | bytes 2097184 | tf_op jit(solution)/shard_map/ppermute | solution.py:56
  282.5 13.5 %shard_map.287 = bf16[1024,1024]{1,0:T(8,128)(2,1)S(1)} custom-call(s32[1]{0:T(128)} %bitcast.3._.core_ref, bf16[1024,2048]{1,0:T(8,128)(2,1)S(1)} %copy-done.39, bf16[1024,2048]{1,0:T(8,128)(2,1)} %copy-done.40, bf16[2048,1024]{1,0:T(8,128)(2,1)} %bitcast.59.own_ref.w_ref, bf16[2048,1024]{1,0:T(8,128)(2,1)} %bitcast.60.other_ref.w_ref, ...), custom_call_target="tpu_custom_call" | custom-call | tf_op jit(solution)/shard_map/pallas_call | solution.py:427
  296.0 8.9 %shard_map.288 = (bf16[16,64,1024]{2,1,0:T(8,128)(2,1)S(1)}, bf16[16,64,1024]{2,1,0:T(8,128)(2,1)S(1)}) custom-call(s32[3]{0:T(128)S(1)} %pad_add_fusion.12.info_ref, bf16[1024,2048]{1,0:T(8,128)(2,1)S(1)} %copy-done.39, bf16[1024,1024]{1,0:T(8,128)(2,1)S(1)} %bitcast_select_fusion.y_ref.refs_1_.x_ref.rest_ref, ...), custom_call_target="tpu_custom_call" | custom-call | tf_op jit(solution)/shard_map/pallas_call | solution.py:427
  334.5 15.4 %shard_map.293 = (bf16[1024,1024]{1,0:T(8,128)(2,1)S(1)}, f32[4,3,1024]{2,1,0:T(4,128)S(1)}) custom-call(s32[1]{0:T(128)} %bitcast.3._.core_ref, bf16[1024,2048]{1,0:T(8,128)(2,1)S(1)} %get-tuple-element.448.a_ref.refs_1_, bf16[1024,2048]{1,0:T(8,128)(2,1)S(1)} %get-tuple-element.449.y_ref.b_ref, bf16[1024,2048]{1,0:T(8,128)(2,1)} %bitcast.57.w_ref.own_ref, ...), custom_call_target="tpu_custom_call" | custom-call | tf_op jit(solution)/shard_map/pallas_call | solution.py:427
  352.9 8.1 %shard_map.296 = (bf16[16,32,2048]{2,1,0:T(8,128)(2,1)S(1)}, bf16[16,32,2048]{2,1,0:T(8,128)(2,1)S(1)}) custom-call(s32[3]{0:T(128)S(1)} %pad_add_fusion.12.info_ref, bf16[1024,1024]{1,0:T(8,128)(2,1)S(1)} %copy-done.16, bf16[1024,2048]{1,0:T(8,128)(2,1)S(1)} %get-tuple-element.448.a_ref.refs_1_, bf16[32,32,2048]{2,1,0:T(8,128)(2,1)} %collective-permute-done.38.refs_2_), custom_call_target="tpu_custom_call" | custom-call | tf_op jit(solution)/shard_map/pallas_call | solution.py:427
  363.9 9.4 %shard_map.297 = bf16[16,64,1536]{2,1,0:T(8,128)(2,1)S(1)} custom-call(s32[2]{0:T(128)S(1)} %copy-done.102, bf16[16,64,1536]{2,1,0:T(8,128)(2,1)S(1)} %bitcast.213, bf16[16,64,1024]{2,1,0:T(8,128)(2,1)S(1)} %bitcast.223), custom_call_target="tpu_custom_call" | custom-call | tf_op jit(solution)/shard_map/pallas_call | solution.py:359
  373.4 9.4 %shard_map.298 = bf16[16,64,1536]{2,1,0:T(8,128)(2,1)S(1)} custom-call(s32[2]{0:T(128)S(1)} %copy-done.102, bf16[16,64,1536]{2,1,0:T(8,128)(2,1)S(1)} %bitcast.211, bf16[16,64,1024]{2,1,0:T(8,128)(2,1)S(1)} %bitcast.224), custom_call_target="tpu_custom_call" | custom-call | tf_op jit(solution)/shard_map/pallas_call | solution.py:359
  393.7 9.7 %shard_map.303 = (bf16[1024,1024]{1,0:T(8,128)(2,1)S(1)}, f32[4,3,1024]{2,1,0:T(4,128)S(1)}) custom-call(s32[1]{0:T(128)} %bitcast.3._.core_ref, bf16[1024,1536]{1,0:T(8,128)(2,1)S(1)} %bitcast.202, bf16[1024,1536]{1,0:T(8,128)(2,1)S(1)} %bitcast.205, bf16[1024,2048]{1,0:T(8,128)(2,1)S(1)} %bitcast.179, bf16[1024,2048]{1,0:T(8,128)(2,1)S(1)} %bitcast.183, ...), custom_call_target="tpu_custom_call" | custom-call | tf_op jit(solution)/shard_map/pallas_call | solution.py:427
  429.9 7.6 %collective-permute-done.47 = bf16[4,64,1024]{2,1,0:T(8,128)(2,1)} collective-permute-done((bf16[4,64,1024]{2,1,0:T(8,128)(2,1)}, bf16[4,64,1024]{2,1,0:T(8,128)(2,1)}, u32[]{:S(2)}, u32[]{:S(2)}) %collective-permute-start.47) | collective-permute-done | bytes 524320 | tf_op jit(solution)/shard_map/ppermute | solution.py:60
  447.9 9.1 %shard_map.309 = bf16[4,256,1536]{2,1,0:T(8,128)(2,1)S(1)} custom-call(s32[2]{0:T(128)S(1)} %copy-done.100, bf16[4,256,1536]{2,1,0:T(8,128)(2,1)S(1)} %bitcast.209, bf16[4,256,1024]{2,1,0:T(8,128)(2,1)S(1)} %bitcast.221), custom_call_target="tpu_custom_call" | custom-call | tf_op jit(solution)/shard_map/pallas_call | solution.py:359
  470.7 9.1 %shard_map.314 = bf16[4,256,1536]{2,1,0:T(8,128)(2,1)S(1)} custom-call(s32[2]{0:T(128)S(1)} %copy-done.100, bf16[4,256,1536]{2,1,0:T(8,128)(2,1)S(1)} %bitcast.207, bf16[4,256,1024]{2,1,0:T(8,128)(2,1)S(1)} %bitcast.222), custom_call_target="tpu_custom_call" | custom-call | tf_op jit(solution)/shard_map/pallas_call | solution.py:359
  484.7 7.9 %shard_map.316 = (bf16[16,32,2048]{2,1,0:T(8,128)(2,1)}, bf16[16,32,2048]{2,1,0:T(8,128)(2,1)S(1)}) custom-call(s32[3]{0:T(128)S(1)} %pad_add_fusion.12.info_ref, bf16[1024,1024]{1,0:T(8,128)(2,1)S(1)} %bitcast.187, bf16[1024,1536]{1,0:T(8,128)(2,1)S(1)} %bitcast.216, bf16[32,32,1536]{2,1,0:T(8,128)(2,1)S(1)} %collective-permute-done.54.refs_2_, ...), custom_call_target="tpu_custom_call" | custom-call | tf_op jit(solution)/shard_map/pallas_call | solution.py:427
  506.7 13.1 %shard_map.317 = (f32[1024,1024]{1,0:T(8,128)}, f32[4,3,1024]{2,1,0:T(4,128)S(1)}) custom-call(s32[1]{0:T(128)} %bitcast.3._.core_ref, bf16[1024,1536]{1,0:T(8,128)(2,1)S(1)} %bitcast.217, bf16[1024,1536]{1,0:T(8,128)(2,1)} %bitcast.215, bf16[1024,2048]{1,0:T(8,128)(2,1)} %bitcast.36.w_ref.own_ref, bf16[1024,2048]{1,0:T(8,128)(2,1)} %bitcast.38.w_ref.other_ref, ...), custom_call_target="tpu_custom_call" | custom-call | tf_op jit(solution)/shard_map/pallas_call | solution.py:427
  532.4 8.0 %collective-permute-done.60 = f32[19,512]{1,0:T(8,128)S(1)} collective-permute-done((f32[19,512]{1,0:T(8,128)S(1)}, f32[19,512]{1,0:T(8,128)S(1)}, u32[]{:S(2)}, u32[]{:S(2)}) %collective-permute-start.60) | collective-permute-done | bytes 38944 | tf_op jit(solution)/shard_map/ppermute | solution.py:56
  (595 shorter events, 339.7 us)
Async XLA Ops:
  15.1 24.0 %collective-permute-start.5 = (bf16[4,64,1024]{2,1,0:T(8,128)(2,1)}, bf16[4,64,1024]{2,1,0:T(8,128)(2,1)}, u32[]{:S(2)}, u32[]{:S(2)}) collective-permute-start(bf16[4,64,1024]{2,1,0:T(8,128)(2,1)} %get-tuple-element.645), channel_id=1, source_target_pairs={{0,24},{1,25},{2,26},{3,27},{4,28},{5,29},{6,30},{7,31},{8,16},{9,... | collective-permute-start | bytes 1572872 | tf_op jit(solution)/shard_map/ppermute | solution.py:60
  59.7 26.8 %collective-permute-start.14 = (bf16[16,32,2048]{2,1,0:T(8,128)(2,1)}, bf16[16,32,2048]{2,1,0:T(8,128)(2,1)}, u32[]{:S(2)}, u32[]{:S(2)}) collective-permute-start(bf16[16,32,2048]{2,1,0:T(8,128)(2,1)} %shard_map.256.mine_ref), channel_id=1, source_target_pairs={{0,16},{1,17},{2,18},{3,19},{4,20},{5,21},{6,22},{7,23},{8,9},{9,8... | collective-permute-start | bytes 6291464 | tf_op jit(solution)/shard_map/ppermute | solution.py:56
  66.1 19.5 %collective-permute-start.15 = (bf16[4,32,2048]{2,1,0:T(8,128)(2,1)S(1)}, bf16[4,32,2048]{2,1,0:T(8,128)(2,1)S(1)}, u32[]{:S(2)}, u32[]{:S(2)}) collective-permute-start(bf16[4,32,2048]{2,1,0:T(8,128)(2,1)S(1)} %shard_map.257.mine_ref), channel_id=1, source_target_pairs={{0,2},{1,3},{2,0},{3,1},{4,6},{5,7},{6,4},{7,5},{8,10},{9,11},{10,... | collective-permute-start | bytes 1572872 | tf_op jit(solution)/shard_map/ppermute | solution.py:56
  114.0 25.2 %collective-permute-start.19 = (bf16[16,32,2048]{2,1,0:T(8,128)(2,1)S(1)}, bf16[16,32,2048]{2,1,0:T(8,128)(2,1)S(1)}, u32[]{:S(2)}, u32[]{:S(2)}) collective-permute-start(bf16[16,32,2048]{2,1,0:T(8,128)(2,1)S(1)} %shard_map.265.mine_ref), channel_id=1, source_target_pairs={{0,16},{1,17},{2,18},{3,19},{4,20},{5,21},{6,22},{7,23},{8,9},{9,8... | collective-permute-start | bytes 6291464 | tf_op jit(solution)/shard_map/ppermute | solution.py:56
  141.4 26.6 %collective-permute-start.24 = (bf16[32,32,2048]{2,1,0:T(8,128)(2,1)S(1)}, bf16[32,32,2048]{2,1,0:T(8,128)(2,1)S(1)}, u32[]{:S(2)}, u32[]{:S(2)}) collective-permute-start(bf16[32,32,2048]{2,1,0:T(8,128)(2,1)S(1)} %shard_map.269), channel_id=1, source_target_pairs={{0,8},{1,9},{2,10},{3,11},{4,12},{5,13},{6,14},{7,15},{8,0},{9,1},... | collective-permute-start | bytes 12582920 | tf_op jit(solution)/shard_map/ppermute | solution.py:56
  143.5 24.5 %collective-permute-start.23 = (bf16[4,64,1024]{2,1,0:T(8,128)(2,1)S(1)}, bf16[4,64,1024]{2,1,0:T(8,128)(2,1)S(1)}, u32[]{:S(2)}, u32[]{:S(2)}) collective-permute-start(bf16[4,64,1024]{2,1,0:T(8,128)(2,1)S(1)} %get-tuple-element.641), channel_id=1, source_target_pairs={{0,24},{1,25},{2,26},{3,27},{4,28},{5,29},{6,30},{7,31},{8,16},{9,... | collective-permute-start | bytes 1572872 | tf_op jit(solution)/shard_map/ppermute | solution.py:60
  149.3 18.7 %collective-permute-start.25 = (bf16[4,32,2048]{2,1,0:T(8,128)(2,1)S(1)}, bf16[4,32,2048]{2,1,0:T(8,128)(2,1)S(1)}, u32[]{:S(2)}, u32[]{:S(2)}) collective-permute-start(bf16[4,32,2048]{2,1,0:T(8,128)(2,1)S(1)} %shard_map.270.mine_ref), channel_id=1, source_target_pairs={{0,2},{1,3},{2,0},{3,1},{4,6},{5,7},{6,4},{7,5},{8,10},{9,11},{10,... | collective-permute-start | bytes 1572872 | tf_op jit(solution)/shard_map/ppermute | solution.py:56
  186.8 25.2 %collective-permute-start.29 = (bf16[16,32,2048]{2,1,0:T(8,128)(2,1)S(1)}, bf16[16,32,2048]{2,1,0:T(8,128)(2,1)S(1)}, u32[]{:S(2)}, u32[]{:S(2)}) collective-permute-start(bf16[16,32,2048]{2,1,0:T(8,128)(2,1)S(1)} %shard_map.276.mine_ref), channel_id=1, source_target_pairs={{0,16},{1,17},{2,18},{3,19},{4,20},{5,21},{6,22},{7,23},{8,9},{9,8... | collective-permute-start | bytes 6291464 | tf_op jit(solution)/shard_map/ppermute | solution.py:56
  215.8 23.8 %collective-permute-start.32 = (bf16[32,32,2048]{2,1,0:T(8,128)(2,1)}, bf16[32,32,2048]{2,1,0:T(8,128)(2,1)}, u32[]{:S(2)}, u32[]{:S(2)}) collective-permute-start(bf16[32,32,2048]{2,1,0:T(8,128)(2,1)} %shard_map.280), channel_id=1, source_target_pairs={{0,8},{1,9},{2,10},{3,11},{4,12},{5,13},{6,14},{7,15},{8,0},{9,1},... | collective-permute-start | bytes 12582920 | tf_op jit(solution)/shard_map/ppermute | solution.py:56
  217.8 17.2 %collective-permute-start.31 = (bf16[8,64,1024]{2,1,0:T(8,128)(2,1)S(1)}, bf16[8,64,1024]{2,1,0:T(8,128)(2,1)}, u32[]{:S(2)}, u32[]{:S(2)}) collective-permute-start(bf16[8,64,1024]{2,1,0:T(8,128)(2,1)S(1)} %shard_map.281.mine_ref), channel_id=1, source_target_pairs={{0,1},{1,0},{2,3},{3,2},{4,5},{5,4},{6,7},{7,6},{8,24},{9,25},{10,... | collective-permute-start | bytes 3145736 | tf_op jit(solution)/shard_map/ppermute | solution.py:56
  238.1 25.5 %collective-permute-start.33 = (bf16[16,64,1024]{2,1,0:T(8,128)(2,1)}, bf16[16,64,1024]{2,1,0:T(8,128)(2,1)}, u32[]{:S(2)}, u32[]{:S(2)}) collective-permute-start(bf16[16,64,1024]{2,1,0:T(8,128)(2,1)} %shard_map.283.mine_ref), channel_id=1, source_target_pairs={{0,16},{1,17},{2,18},{3,19},{4,20},{5,21},{6,22},{7,23},{8,9},{9,8... | collective-permute-start | bytes 6291464 | tf_op jit(solution)/shard_map/ppermute | solution.py:56
  305.0 25.2 %collective-permute-start.36 = (bf16[16,64,1024]{2,1,0:T(8,128)(2,1)S(1)}, bf16[16,64,1024]{2,1,0:T(8,128)(2,1)S(1)}, u32[]{:S(2)}, u32[]{:S(2)}) collective-permute-start(bf16[16,64,1024]{2,1,0:T(8,128)(2,1)S(1)} %get-tuple-element.441), channel_id=1, source_target_pairs={{0,16},{1,17},{2,18},{3,19},{4,20},{5,21},{6,22},{7,23},{8,9},{9,8... | collective-permute-start | bytes 6291464 | tf_op jit(solution)/shard_map/ppermute | solution.py:56
  332.2 20.7 %collective-permute-start.38 = (bf16[32,32,2048]{2,1,0:T(8,128)(2,1)S(1)}, bf16[32,32,2048]{2,1,0:T(8,128)(2,1)}, u32[]{:S(2)}, u32[]{:S(2)}) collective-permute-start(bf16[32,32,2048]{2,1,0:T(8,128)(2,1)S(1)} %shard_map.291), channel_id=1, source_target_pairs={{0,8},{1,9},{2,10},{3,11},{4,12},{5,13},{6,14},{7,15},{8,0},{9,1},... | collective-permute-start | bytes 12582920 | tf_op jit(solution)/shard_map/ppermute | solution.py:56
  333.6 19.3 %collective-permute-start.37 = (bf16[8,64,1024]{2,1,0:T(8,128)(2,1)}, bf16[8,64,1024]{2,1,0:T(8,128)(2,1)S(1)}, u32[]{:S(2)}, u32[]{:S(2)}) collective-permute-start(bf16[8,64,1024]{2,1,0:T(8,128)(2,1)} %get-tuple-element.451), channel_id=1, source_target_pairs={{0,1},{1,0},{2,3},{3,2},{4,5},{5,4},{6,7},{7,6},{8,24},{9,25},{10,... | collective-permute-start | bytes 3145736 | tf_op jit(solution)/shard_map/ppermute | solution.py:56
  361.8 25.3 %collective-permute-start.40 = (bf16[16,32,2048]{2,1,0:T(8,128)(2,1)S(1)}, bf16[16,32,2048]{2,1,0:T(8,128)(2,1)S(1)}, u32[]{:S(2)}, u32[]{:S(2)}) collective-permute-start(bf16[16,32,2048]{2,1,0:T(8,128)(2,1)S(1)} %get-tuple-element.461), channel_id=1, source_target_pairs={{0,16},{1,17},{2,18},{3,19},{4,20},{5,21},{6,22},{7,23},{8,9},{9,8... | collective-permute-start | bytes 6291464 | tf_op jit(solution)/shard_map/ppermute | solution.py:56
  362.0 25.1 %collective-permute-start.39 = (bf16[4,64,1024]{2,1,0:T(8,128)(2,1)S(1)}, bf16[4,64,1024]{2,1,0:T(8,128)(2,1)S(1)}, u32[]{:S(2)}, u32[]{:S(2)}) collective-permute-start(bf16[4,64,1024]{2,1,0:T(8,128)(2,1)S(1)} %get-tuple-element.460), channel_id=1, source_target_pairs={{0,2},{1,3},{2,0},{3,1},{4,6},{5,7},{6,4},{7,5},{8,10},{9,11},{10,... | collective-permute-start | bytes 1572872 | tf_op jit(solution)/shard_map/ppermute | solution.py:56
  411.6 18.3 %collective-permute-start.45 = (bf16[4,64,1024]{2,1,0:T(8,128)(2,1)}, bf16[4,64,1024]{2,1,0:T(8,128)(2,1)}, u32[]{:S(2)}, u32[]{:S(2)}) collective-permute-start(bf16[4,64,1024]{2,1,0:T(8,128)(2,1)} %bitcast.65), channel_id=1, source_target_pairs={{0,8},{1,9},{2,10},{3,11},{4,12},{5,13},{6,14},{7,15},{8,0},{9,1},... | collective-permute-start | bytes 1572872 | tf_op jit(solution)/shard_map/ppermute | solution.py:60
  412.4 17.5 %collective-permute-start.46 = (bf16[4,64,1024]{2,1,0:T(8,128)(2,1)}, bf16[4,64,1024]{2,1,0:T(8,128)(2,1)}, u32[]{:S(2)}, u32[]{:S(2)}) collective-permute-start(bf16[4,64,1024]{2,1,0:T(8,128)(2,1)} %bitcast.66), channel_id=1, source_target_pairs={{0,16},{1,17},{2,18},{3,19},{4,20},{5,21},{6,22},{7,23},{8,24},{9,... | collective-permute-start | bytes 1572872 | tf_op jit(solution)/shard_map/ppermute | solution.py:60
  413.2 24.3 %collective-permute-start.47 = (bf16[4,64,1024]{2,1,0:T(8,128)(2,1)}, bf16[4,64,1024]{2,1,0:T(8,128)(2,1)}, u32[]{:S(2)}, u32[]{:S(2)}) collective-permute-start(bf16[4,64,1024]{2,1,0:T(8,128)(2,1)} %bitcast.67), channel_id=1, source_target_pairs={{0,24},{1,25},{2,26},{3,27},{4,28},{5,29},{6,30},{7,31},{8,16},{9,... | collective-permute-start | bytes 1572872 | tf_op jit(solution)/shard_map/ppermute | solution.py:60
  414.0 23.6 %collective-permute-start.49 = (bf16[4,32,2048]{2,1,0:T(8,128)(2,1)}, bf16[4,32,2048]{2,1,0:T(8,128)(2,1)}, u32[]{:S(2)}, u32[]{:S(2)}) collective-permute-start(bf16[4,32,2048]{2,1,0:T(8,128)(2,1)} %get-tuple-element.491), channel_id=1, source_target_pairs={{0,2},{1,3},{2,0},{3,1},{4,6},{5,7},{6,4},{7,5},{8,10},{9,11},{10,... | collective-permute-start | bytes 1572872 | tf_op jit(solution)/shard_map/ppermute | solution.py:56
  440.7 25.2 %collective-permute-start.51 = (bf16[16,32,2048]{2,1,0:T(8,128)(2,1)S(1)}, bf16[16,32,2048]{2,1,0:T(8,128)(2,1)S(1)}, u32[]{:S(2)}, u32[]{:S(2)}) collective-permute-start(bf16[16,32,2048]{2,1,0:T(8,128)(2,1)S(1)} %get-tuple-element.502), channel_id=1, source_target_pairs={{0,16},{1,17},{2,18},{3,19},{4,20},{5,21},{6,22},{7,23},{8,9},{9,8... | collective-permute-start | bytes 6291464 | tf_op jit(solution)/shard_map/ppermute | solution.py:56
  441.3 20.5 %collective-permute-start.50 = (bf16[2,32,2048]{2,1,0:T(8,128)(2,1)S(1)}, bf16[2,32,2048]{2,1,0:T(8,128)(2,1)S(1)}, u32[]{:S(2)}, u32[]{:S(2)}) collective-permute-start(bf16[2,32,2048]{2,1,0:T(8,128)(2,1)S(1)} %get-tuple-element.501), channel_id=1, source_target_pairs={{0,4},{1,5},{2,6},{3,7},{4,0},{5,1},{6,2},{7,3},{8,12},{9,13},{10,... | collective-permute-start | bytes 786440 | tf_op jit(solution)/shard_map/ppermute | solution.py:56
  494.0 25.8 %collective-permute-start.57 = (bf16[16,32,2048]{2,1,0:T(8,128)(2,1)}, bf16[16,32,2048]{2,1,0:T(8,128)(2,1)}, u32[]{:S(2)}, u32[]{:S(2)}) collective-permute-start(bf16[16,32,2048]{2,1,0:T(8,128)(2,1)} %get-tuple-element.529), channel_id=1, source_target_pairs={{0,16},{1,17},{2,18},{3,19},{4,20},{5,21},{6,22},{7,23},{8,9},{9,8... | collective-permute-start | bytes 6291464 | tf_op jit(solution)/shard_map/ppermute | solution.py:56
  497.9 21.8 %collective-permute-start.56 = (bf16[4,32,2048]{2,1,0:T(8,128)(2,1)}, bf16[4,32,2048]{2,1,0:T(8,128)(2,1)S(1)}, u32[]{:S(2)}, u32[]{:S(2)}) collective-permute-start(bf16[4,32,2048]{2,1,0:T(8,128)(2,1)} %get-tuple-element.528), channel_id=1, source_target_pairs={{0,2},{1,3},{2,0},{3,1},{4,6},{5,7},{6,4},{7,5},{8,10},{9,11},{10,... | collective-permute-start | bytes 1572872 | tf_op jit(solution)/shard_map/ppermute | solution.py:56
  (174 other events, 1783.8 us)

commit v5 on v4

--- a/solution.py
+++ b/solution.py
@@ -210,6 +210,14 @@
         except StopIteration as stop:
             self.result = stop.value
         self.flying = not self.flying
+
+
+def hold(value, *chains):
+    chains = [c for c in chains if c.flying]
+    value, got = lax.optimization_barrier((value, [c.pending for c in chains]))
+    for c, g in zip(chains, got):
+        c.pending = g
+    return value
 
 
 def land(value, *chains, also=()):
@@ -797,17 +805,18 @@
     tokens = along(tokens, front)
     middle = attention_group(t_qkv, t_out)
     tokens = along(tokens, middle)
+    tokens, w_up = lax.optimization_barrier((tokens, w_up))
+    up_pair = own_and_other(w_up.reshape(rows, total, 2, hidden_half), 2)
+    rising = Chain(gather(place, *[x.reshape(rows, -1) for x in up_pair], len(place.xy) // 2))
     tokens, cotangent = lax.optimization_barrier((tokens, cotangent))
-    tokens = along(tokens, front, middle)
+    tokens = along(tokens, front, middle, rising)
     tokens = along(tokens, small)
     tokens = along(tokens, small)
-    tokens = along(tokens, front, middle)
+    tokens, w_down = lax.optimization_barrier((tokens, w_down))
+    falling = Chain(gather(place, *own_and_other(w_down.reshape(2, hidden_half, width), 0)))
+    tokens = along(tokens, front, middle, rising, falling)
     while not small.done():
         tokens = along(tokens, small)
-    tokens, w_up, w_down = lax.optimization_barrier((tokens, w_up, w_down))
-    up_pair = own_and_other(w_up.reshape(rows, total, 2, hidden_half), 2)
-    rising = Chain(gather(place, *[x.reshape(rows, -1) for x in up_pair]))
-    falling = Chain(gather(place, *own_and_other(w_down.reshape(2, hidden_half, width), 0)))
     small = small.result.astype(f32)
     table = small[:, :thin].reshape(width, LANES).T
 
@@ -823,7 +832,8 @@
     tokens = tokens.reshape(frames_local, slots, width)
     embedded = embedded[:, None, :]
     normed1 = norm(tokens, embedded, gains[0], shifts[0])
-    normed1 = along(normed1, front, middle, rising)
+    normed1 = land(normed1, front, middle, rising, falling)
+    normed1 = launch(normed1, front, middle, falling)
     s_halves = [x.reshape(width, -1) for x in finish(front)]
     here = core.astype(jnp.int32).reshape(1)
 
@@ -831,7 +841,8 @@
         return project(x, w, 3 * half, here).reshape(*outer, -1)
 
     spatial = [projected(normed1, w, (frames_local, slots)) for w in s_halves]
-    spatial = along(spatial, middle, rising)
+    spatial = land(spatial, middle, falling)
+    spatial = launch(spatial, middle, rising)
 
     def frame_index(i):
         return (i, 0, 0)
@@ -849,9 +860,10 @@
     flat = tokens.reshape(row_count, width)
     hidden1 = add_spatial(s_mixed, s_halves, flat, embedded, here)
 
-    hidden1 = along(hidden1, middle, rising, falling)
+    hidden1 = hold(hidden1, middle, rising)
     parts = to_slots(hidden1.reshape(tokens.shape))
-    parts = land(parts, middle, rising, falling)
+    parts[1] = along(parts[1], middle, rising)
+    parts = land(parts, middle, rising)
     hidden1 = in_slots(parts)
     frames = hidden1.shape[0]
     slot_at = place.tm * slots_local + jnp.arange(slots_local)
@@ -862,7 +874,6 @@
     normed2 = launch(normed2, rising, falling)
     t_halves = [x.reshape(width, -1) for x in finish(middle)]
     temporal = [projected(normed2, w, (frames, slots_local)) for w in t_halves]
-    temporal = along(temporal, rising, falling)
     temporal_place = (
         jnp.stack([place.tm.astype(jnp.int32), core.astype(jnp.int32)]), (frames, GROUP),
         slots_local // GROUP, slot_index,
@@ -879,7 +890,6 @@
     first = along(first, falling)
     normed3, first = lax.optimization_barrier((normed3, first))
     second = up_project(normed3, up_halves[1], up_bias[1])
-    second = along(second, falling)
     (active, slope), (active2, slope2) = first, second
 
     core_pair = (place.core_bit, place.core_bit)
@@ -892,23 +902,28 @@
 
     down_in = jnp.where(mask, in_slots(cotangent), 0).reshape(row_count, width)
     send = weight_grad(active2, down_in, total, here)
-    hidden2 = land(hidden2, falling)
+    down_in, send = land((down_in, send), falling)
+    own_rows = falling.pending[0].reshape(-1, width)
+    down_in, send = launch(down_in, falling, also=[send])
+    got = exchanged(send)
+    inner_grad, b_sum = inner_back(down_in, own_rows, slope, here)
+    hidden2, inner_grad = land((hidden2, inner_grad), falling)
     down_halves = [x.reshape(-1, width) for x in finish(falling)]
-    hidden2, send = launch(hidden2, also=[send])
-    got = exchanged(send)
     mask_rows = jnp.broadcast_to(mask, (frames, slots_local, 1)).reshape(row_count, 1).astype(f32)
     mixed = down_project([active, active2], down_halves, hidden2, down_bias, mask_rows, here)
     down_in, mixed, got = lax.optimization_barrier((down_in, mixed, got))
     s_down = sums((active, down_in, got, None))
     down_in = launch(down_in, s_down)
 
-    inner_grad, b_sum = inner_back(down_in, down_halves[0], slope, here)
     inner_grad2, b_sum2 = inner_back(down_in, down_halves[1], slope2, here)
     send = weight_grad(normed3, inner_grad2, total, here)
-    inner_grad, inner_grad2, send = land((inner_grad, inner_grad2, send), s_down)
-    inner_grads, send = launch((inner_grad, inner_grad2), s_down, also=[send])
+    inner_grads = (inner_grad, inner_grad2)
+    grad2, sums3 = norm_back(
+        inner_grads, up_halves, hidden2, nothing, gains[2], down_in, bf16, here
+    )
+    grad2, send = land((grad2, send), s_down)
+    grad2, send = launch(grad2, s_down, also=[send])
     got = exchanged(send)
-
     b_sums = [x.reshape(total, -1, thin).swapaxes(0, 1) for x in (b_sum, b_sum2)]
     late_rows = [x.reshape(-1, width) for x in b_sums]
     late_rows = jnp.where(
@@ -916,12 +931,10 @@
     )
     late_rows = jnp.concatenate([jnp.sum(down_in.astype(f32), axis=0)[None], late_rows], axis=0)
 
-    grad2, sums3 = norm_back(
-        inner_grads, up_halves, hidden2, nothing, gains[2], down_in, bf16, here
-    )
     t_mix_grad = mixed_back(grad2, t_halves, here)
-    t_mix_grad, got = land(t_mix_grad, s_down, also=[got])
-    s_up = sums((normed3, inner_grads[0], got, None))
+    send2 = weight_grad(t_mixed, grad2, total, here, 1)
+    (t_mix_grad, send2), got = land((t_mix_grad, send2), s_down, also=[got])
+    s_up = sums((normed3, inner_grad, got, None))
     t_mix_grad = launch(t_mix_grad, s_down, s_up)
     t_mix_grad = t_mix_grad.reshape(frames, slots_local, width)
 
@@ -933,16 +946,16 @@
 
     t_grad2 = back(1, temporal_place, make_bias, temporal, t_mix_grad)
     send = weight_grad(normed2, t_grad2, total, here)
-    send2 = weight_grad(t_mixed, grad2, total, here, 1)
     t_grad = back(0, temporal_place, make_bias, temporal, t_mix_grad)
     t_grads = land((t_grad, t_grad2), s_down, s_up)
     t_grads, send, send2 = launch(t_grads, s_down, s_up, also=[send, send2])
     gots = [exchanged(send), exchanged(send2)]
 
     grad1, sums2 = norm_back(t_grads, t_halves, hidden1, nothing, gains[1], grad2, bf16, here)
-    grad1, *gots = land(grad1, s_down, s_up, also=gots)
-    grad1 = launch(grad1, s_down, s_up)
+    grad1 = hold(grad1, s_down, s_up)
+    grad1, gots = lax.optimization_barrier((grad1, gots))
     parts = from_slots(grad1)
+    parts[1] = along(parts[1], s_down, s_up)
     s_time = sums((normed2, t_grads[0], gots[0], None), (t_mixed, grad2, gots[1], 0))
     parts[0], s_time.pending = lax.optimization_barrier((parts[0], s_time.pending))
     parts = land(parts, s_down, s_up)

time: 597 us -> 588 us (0.985)
  waiting for transfers between devices: 145 us -> 126 us
    ppermute x60, waiting for transfers between devices: 99.9 us -> 81.3 us  [flip(): return lax.ppermute(value, AXES, moves)]
    unnamed x274 -> x290, local copies, waits for them, and re-layouts: 33.1 us -> 39.8 us
  transfers between devices with their start and end apart: 72 -> 72, of which waited for: 31 -> 32; matrix products, arithmetic and copies ran while one was open for 8% -> 8% of each run, Pallas kernels for 38% -> 39%
where the time goes in v5:
time: 588 us; the launch traced here: 582 us
  Pallas kernels  300 us (51%)
  waiting for transfers between devices  126 us (21%)
  local copies, waits for them, and re-layouts  71.7 us (12%)
  starting transfers between devices  61.7 us (10%)
  other arithmetic  18.2 us (3%)
    pallas_call x24, Pallas kernels, dense(): pl.pallas_call(body, grid_spec=pltpu.PrefetchScalarGridSpec(num_scalar_pr...  159 us
    ppermute x60, waiting for transfers between devices, flip(): return lax.ppermute(value, AXES, moves)  81.3 us
    pallas_call x6, Pallas kernels, run_attention(): pl.pallas_call(body, grid=(grid,), in_specs=[pl.BlockSpec(memory_space=pl...  52.4 us
    ppermute x60, starting transfers between devices, flip(): return lax.ppermute(value, AXES, moves)  50.8 us
    ppermute x12, waiting for transfers between devices, tm_flip(): return lax.ppermute(value, AXES, moves)  44.6 us
    unnamed x290, local copies, waits for them, and re-layouts  39.8 us
    pallas_call x25, Pallas kernels, merge(): pl.pallas_call(merge_body, grid=(n // block,), in_specs=[pl.BlockSpec(mem...  34.8 us
    pallas_call x2, Pallas kernels, up_project(): pl.pallas_call(up_body, grid=(cols // block,), in_specs=[pl.BlockSpec((ro...  29.1 us
  transfers between devices with their start and end apart: 72, of which 32 were waited for; matrix products, arithmetic and copies ran while one was open for 8% of the time, Pallas kernels for 39%

profile of v5, /device:TPU:1, one launch (start us, length us, event | category | flops | bytes accessed | tf_op | source)
XLA Modules:
  0.0 582.2 jit_solution(9815815069378665863)
XLA Ops:
  27.7 11.3 %collective-permute-done.5 = bf16[4,64,1024]{2,1,0:T(8,128)(2,1)} collective-permute-done((bf16[4,64,1024]{2,1,0:T(8,128)(2,1)}, bf16[4,64,1024]{2,1,0:T(8,128)(2,1)}, u32[]{:S(2)}, u32[]{:S(2)}) %collective-permute-start.5) | collective-permute-done | bytes 524320 | tf_op jit(solution)/shard_map/ppermute | solution.py:60
  45.4 9.9 %collective-permute-done.9.other_ref = bf16[4,48,128]{2,1,0:T(8,128)(2,1)S(1)} collective-permute-done((bf16[4,48,128]{2,1,0:T(8,128)(2,1)S(1)}, bf16[4,48,128]{2,1,0:T(8,128)(2,1)S(1)}, u32[]{:S(2)}, u32[]{:S(2)}) %collective-permute-start.9) | collective-permute-done | bytes 49184 | tf_op jit(solution)/shard_map/ppermute | solution.py:56
  118.4 7.4 %shard_map.269 = bf16[4,256,1024]{2,1,0:T(8,128)(2,1)S(1)} custom-call(s32[2]{0:T(128)S(1)} %copy-done.106, bf16[4,256,1536]{2,1,0:T(8,128)(2,1)S(1)} %bitcast.208, bf16[4,256,1536]{2,1,0:T(8,128)(2,1)S(1)} %bitcast.210), custom_call_target="tpu_custom_call" | custom-call | tf_op jit(solution)/shard_map/pallas_call | solution.py:367
  131.1 12.3 %collective-permute-done.23.other_ref = bf16[4,32,2048]{2,1,0:T(8,128)(2,1)S(1)} collective-permute-done((bf16[4,32,2048]{2,1,0:T(8,128)(2,1)S(1)}, bf16[4,32,2048]{2,1,0:T(8,128)(2,1)S(1)}, u32[]{:S(2)}, u32[]{:S(2)}) %collective-permute-start.23) | collective-permute-done | bytes 524320 | tf_op jit(solution)/shard_map/ppermute | solution.py:56
  155.6 9.9 %collective-permute-done.25 = bf16[4,64,1024]{2,1,0:T(8,128)(2,1)S(1)} collective-permute-done((bf16[4,64,1024]{2,1,0:T(8,128)(2,1)S(1)}, bf16[4,64,1024]{2,1,0:T(8,128)(2,1)S(1)}, u32[]{:S(2)}, u32[]{:S(2)}) %collective-permute-start.25) | collective-permute-done | bytes 524320 | tf_op jit(solution)/shard_map/ppermute | solution.py:60
  165.5 11.7 %collective-permute-done.26 = bf16[4,64,1024]{2,1,0:T(8,128)(2,1)S(1)} collective-permute-done((bf16[4,64,1024]{2,1,0:T(8,128)(2,1)S(1)}, bf16[4,64,1024]{2,1,0:T(8,128)(2,1)S(1)}, u32[]{:S(2)}, u32[]{:S(2)}) %collective-permute-start.26) | collective-permute-done | bytes 524320 | tf_op jit(solution)/shard_map/ppermute | solution.py:60
  192.5 8.0 %shard_map.278 = bf16[16,64,1024]{2,1,0:T(8,128)(2,1)S(1)} custom-call(s32[2]{0:T(128)S(1)} %pad_add_fusion.8.scalar_ref, bf16[16,64,1536]{2,1,0:T(8,128)(2,1)S(1)} %bitcast.214, bf16[16,64,1536]{2,1,0:T(8,128)(2,1)S(1)} %bitcast.212), custom_call_target="tpu_custom_call" | custom-call | tf_op jit(solution)/shard_map/pallas_call | solution.py:367
  213.6 14.6 %shard_map.282 = (bf16[1024,2048]{1,0:T(8,128)(2,1)S(1)}, bf16[1024,2048]{1,0:T(8,128)(2,1)S(1)}) custom-call(bf16[1024,1024]{1,0:T(8,128)(2,1)S(1)} %get-tuple-element.418.x_ref.refs_0_, bf16[1024,2048]{1,0:T(8,128)(2,1)} %bitcast.59.w_ref.own_ref, f32[1,2048]{1,0:T(1,128)S(1)} %select_n.781.bias_ref), custom_call_target="tpu_custom_call" | custom-call | tf_op jit(solution)/shard_map/pallas_call | solution.py:697
  237.7 14.6 %shard_map.284 = (bf16[1024,2048]{1,0:T(8,128)(2,1)S(1)}, bf16[1024,2048]{1,0:T(8,128)(2,1)S(1)}) custom-call(bf16[1024,1024]{1,0:T(8,128)(2,1)S(1)} %copy-done.16, bf16[1024,2048]{1,0:T(8,128)(2,1)} %bitcast.60.w_ref.other_ref, f32[1,2048]{1,0:T(1,128)S(1)} %select_n.783.bias_ref), custom_call_target="tpu_custom_call" | custom-call | tf_op jit(solution)/shard_map/pallas_call | solution.py:697
  267.8 7.7 %shard_map.287 = (bf16[1024,2048]{1,0:T(8,128)(2,1)S(1)}, f32[1,2048]{1,0:T(1,128)S(1)}) custom-call(s32[1]{0:T(128)} %bitcast.3._.core_ref, bf16[1024,1024]{1,0:T(8,128)(2,1)S(1)} %bitcast_select_fusion.y_ref.x_ref.refs_1_.rest_ref, bf16[2048,1024]{1,0:T(8,128)(2,1)} %bitcast.61.w_ref.own_ref, bf16[1024,2048]{1,0:T(8,128)(2,1)S(1)} %copy-done.47), custom_call_target="tpu_custom_call" | custom-call | tf_op jit(solution)/shard_map/pallas_call | solution.py:435
  275.5 13.5 %shard_map.288 = bf16[1024,1024]{1,0:T(8,128)(2,1)S(1)} custom-call(s32[1]{0:T(128)} %bitcast.3._.core_ref, bf16[1024,2048]{1,0:T(8,128)(2,1)S(1)} %copy-done.40, bf16[1024,2048]{1,0:T(8,128)(2,1)} %copy-done.41, bf16[2048,1024]{1,0:T(8,128)(2,1)} %bitcast.61.w_ref.own_ref, bf16[2048,1024]{1,0:T(8,128)(2,1)} %bitcast.62.other_ref.w_ref, ...), custom_call_target="tpu_custom_call" | custom-call | tf_op jit(solution)/shard_map/pallas_call | solution.py:435
  289.1 9.8 %shard_map.289 = (bf16[16,64,1024]{2,1,0:T(8,128)(2,1)}, bf16[16,64,1024]{2,1,0:T(8,128)(2,1)S(1)}) custom-call(s32[3]{0:T(128)S(1)} %pad_add_fusion.13.info_ref, bf16[1024,2048]{1,0:T(8,128)(2,1)S(1)} %copy-done.40, bf16[1024,1024]{1,0:T(8,128)(2,1)S(1)} %bitcast_select_fusion.y_ref.x_ref.refs_1_.rest_ref, bf16[32,64,1024]{2,1,0:T(8,128)(2,1)} %collective-permute-done.35.refs_2_), custom_call_target="tpu_custom_call" | custom-call | tf_op jit(solution)/shard_map/pallas_call | solution.py:435
  300.1 7.3 %shard_map.290 = (bf16[1024,2048]{1,0:T(8,128)(2,1)S(1)}, f32[1,2048]{1,0:T(1,128)S(1)}) custom-call(s32[1]{0:T(128)} %bitcast.3._.core_ref, bf16[1024,1024]{1,0:T(8,128)(2,1)S(1)} %bitcast_select_fusion.y_ref.x_ref.refs_1_.rest_ref, bf16[2048,1024]{1,0:T(8,128)(2,1)} %bitcast.62.other_ref.w_ref, bf16[1024,2048]{1,0:T(8,128)(2,1)S(1)} %copy-done.49), custom_call_target="tpu_custom_call" | custom-call | tf_op jit(solution)/shard_map/pallas_call | solution.py:435
  315.2 15.3 %shard_map.291 = (bf16[1024,1024]{1,0:T(8,128)(2,1)S(1)}, f32[4,3,1024]{2,1,0:T(4,128)S(1)}) custom-call(s32[1]{0:T(128)} %bitcast.3._.core_ref, bf16[1024,2048]{1,0:T(8,128)(2,1)S(1)} %get-tuple-element.435.a_ref.refs_1_, bf16[1024,2048]{1,0:T(8,128)(2,1)S(1)} %get-tuple-element.441.b_ref.y_ref, bf16[1024,2048]{1,0:T(8,128)(2,1)} %bitcast.59.w_ref.own_ref, ...), custom_call_target="tpu_custom_call" | custom-call | tf_op jit(solution)/shard_map/pallas_call | solution.py:435
  337.8 8.6 %collective-permute-done.37.b_ref = bf16[8,64,1024]{2,1,0:T(8,128)(2,1)S(1)} collective-permute-done((bf16[8,64,1024]{2,1,0:T(8,128)(2,1)S(1)}, bf16[8,64,1024]{2,1,0:T(8,128)(2,1)S(1)}, u32[]{:S(2)}, u32[]{:S(2)}) %collective-permute-start.37) | collective-permute-done | bytes 1048608 | tf_op jit(solution)/shard_map/ppermute | solution.py:56
  346.5 7.3 %shard_map.297 = (bf16[16,32,2048]{2,1,0:T(8,128)(2,1)S(1)}, bf16[16,32,2048]{2,1,0:T(8,128)(2,1)S(1)}) custom-call(s32[3]{0:T(128)S(1)} %pad_add_fusion.13.info_ref, bf16[1024,1024]{1,0:T(8,128)(2,1)S(1)} %copy-done.17, bf16[1024,2048]{1,0:T(8,128)(2,1)S(1)} %get-tuple-element.435.a_ref.refs_1_, bf16[32,32,2048]{2,1,0:T(8,128)(2,1)S(1)} %collective-permute-done.38.refs_2_), custom_call_target="tpu_custom_call" | custom-call | tf_op jit(solution)/shard_map/pallas_call | solution.py:435
  355.7 9.4 %shard_map.298 = bf16[16,64,1536]{2,1,0:T(8,128)(2,1)S(1)} custom-call(s32[2]{0:T(128)S(1)} %copy-done.109, bf16[16,64,1536]{2,1,0:T(8,128)(2,1)S(1)} %bitcast.215, bf16[16,64,1024]{2,1,0:T(8,128)(2,1)S(1)} %bitcast.225), custom_call_target="tpu_custom_call" | custom-call | tf_op jit(solution)/shard_map/pallas_call | solution.py:367
  365.1 9.4 %shard_map.299 = bf16[16,64,1536]{2,1,0:T(8,128)(2,1)S(1)} custom-call(s32[2]{0:T(128)S(1)} %copy-done.109, bf16[16,64,1536]{2,1,0:T(8,128)(2,1)S(1)} %bitcast.213, bf16[16,64,1024]{2,1,0:T(8,128)(2,1)S(1)} %bitcast.226), custom_call_target="tpu_custom_call" | custom-call | tf_op jit(solution)/shard_map/pallas_call | solution.py:367
  386.1 9.9 %shard_map.303 = (bf16[1024,1024]{1,0:T(8,128)(2,1)S(1)}, f32[4,3,1024]{2,1,0:T(4,128)S(1)}) custom-call(s32[1]{0:T(128)} %bitcast.3._.core_ref, bf16[1024,1536]{1,0:T(8,128)(2,1)S(1)} %bitcast.204, bf16[1024,1536]{1,0:T(8,128)(2,1)S(1)} %bitcast.207, bf16[1024,2048]{1,0:T(8,128)(2,1)S(1)} %bitcast.181, bf16[1024,2048]{1,0:T(8,128)(2,1)S(1)} %bitcast.185, ...), custom_call_target="tpu_custom_call" | custom-call | tf_op jit(solution)/shard_map/pallas_call | solution.py:435
  437.5 9.1 %shard_map.309 = bf16[4,256,1536]{2,1,0:T(8,128)(2,1)S(1)} custom-call(s32[2]{0:T(128)S(1)} %copy-done.107, bf16[4,256,1536]{2,1,0:T(8,128)(2,1)S(1)} %bitcast.211, bf16[4,256,1024]{2,1,0:T(8,128)(2,1)S(1)} %bitcast.223), custom_call_target="tpu_custom_call" | custom-call | tf_op jit(solution)/shard_map/pallas_call | solution.py:367
  461.0 9.1 %shard_map.314 = bf16[4,256,1536]{2,1,0:T(8,128)(2,1)S(1)} custom-call(s32[2]{0:T(128)S(1)} %copy-done.107, bf16[4,256,1536]{2,1,0:T(8,128)(2,1)S(1)} %bitcast.209, bf16[4,256,1024]{2,1,0:T(8,128)(2,1)S(1)} %bitcast.224), custom_call_target="tpu_custom_call" | custom-call | tf_op jit(solution)/shard_map/pallas_call | solution.py:367
  474.6 7.9 %shard_map.316 = (bf16[16,32,2048]{2,1,0:T(8,128)(2,1)}, bf16[16,32,2048]{2,1,0:T(8,128)(2,1)S(1)}) custom-call(s32[3]{0:T(128)S(1)} %pad_add_fusion.13.info_ref, bf16[1024,1024]{1,0:T(8,128)(2,1)S(1)} %bitcast.189, bf16[1024,1536]{1,0:T(8,128)(2,1)S(1)} %bitcast.218, bf16[32,32,1536]{2,1,0:T(8,128)(2,1)S(1)} %collective-permute-done.54.refs_2_, ...), custom_call_target="tpu_custom_call" | custom-call | tf_op jit(solution)/shard_map/pallas_call | solution.py:435
  497.0 13.1 %shard_map.317 = (f32[1024,1024]{1,0:T(8,128)}, f32[4,3,1024]{2,1,0:T(4,128)S(1)}) custom-call(s32[1]{0:T(128)} %bitcast.3._.core_ref, bf16[1024,1536]{1,0:T(8,128)(2,1)S(1)} %bitcast.219, bf16[1024,1536]{1,0:T(8,128)(2,1)} %bitcast.217, bf16[1024,2048]{1,0:T(8,128)(2,1)} %bitcast.38.w_ref.own_ref, bf16[1024,2048]{1,0:T(8,128)(2,1)} %bitcast.40.w_ref.other_ref, ...), custom_call_target="tpu_custom_call" | custom-call | tf_op jit(solution)/shard_map/pallas_call | solution.py:435
  522.9 7.7 %collective-permute-done.60 = f32[19,512]{1,0:T(8,128)S(1)} collective-permute-done((f32[19,512]{1,0:T(8,128)S(1)}, f32[19,512]{1,0:T(8,128)S(1)}, u32[]{:S(2)}, u32[]{:S(2)}) %collective-permute-start.60) | collective-permute-done | bytes 38944 | tf_op jit(solution)/shard_map/ppermute | solution.py:56
  (614 shorter events, 333.4 us)
Async XLA Ops:
  15.1 24.0 %collective-permute-start.5 = (bf16[4,64,1024]{2,1,0:T(8,128)(2,1)}, bf16[4,64,1024]{2,1,0:T(8,128)(2,1)}, u32[]{:S(2)}, u32[]{:S(2)}) collective-permute-start(bf16[4,64,1024]{2,1,0:T(8,128)(2,1)} %get-tuple-element.649), channel_id=1, source_target_pairs={{0,24},{1,25},{2,26},{3,27},{4,28},{5,29},{6,30},{7,31},{8,16},{9,... | collective-permute-start | bytes 1572872 | tf_op jit(solution)/shard_map/ppermute | solution.py:60
  61.6 28.4 %collective-permute-start.15 = (bf16[16,32,2048]{2,1,0:T(8,128)(2,1)}, bf16[16,32,2048]{2,1,0:T(8,128)(2,1)}, u32[]{:S(2)}, u32[]{:S(2)}) collective-permute-start(bf16[16,32,2048]{2,1,0:T(8,128)(2,1)} %shard_map.256.mine_ref), channel_id=1, source_target_pairs={{0,16},{1,17},{2,18},{3,19},{4,20},{5,21},{6,22},{7,23},{8,9},{9,8... | collective-permute-start | bytes 6291464 | tf_op jit(solution)/shard_map/ppermute | solution.py:56
  117.0 26.5 %collective-permute-start.22 = (bf16[16,32,2048]{2,1,0:T(8,128)(2,1)S(1)}, bf16[16,32,2048]{2,1,0:T(8,128)(2,1)S(1)}, u32[]{:S(2)}, u32[]{:S(2)}) collective-permute-start(bf16[16,32,2048]{2,1,0:T(8,128)(2,1)S(1)} %shard_map.267.mine_ref), channel_id=1, source_target_pairs={{0,16},{1,17},{2,18},{3,19},{4,20},{5,21},{6,22},{7,23},{8,9},{9,8... | collective-permute-start | bytes 6291464 | tf_op jit(solution)/shard_map/ppermute | solution.py:56
  117.6 25.8 %collective-permute-start.23 = (bf16[4,32,2048]{2,1,0:T(8,128)(2,1)S(1)}, bf16[4,32,2048]{2,1,0:T(8,128)(2,1)S(1)}, u32[]{:S(2)}, u32[]{:S(2)}) collective-permute-start(bf16[4,32,2048]{2,1,0:T(8,128)(2,1)S(1)} %shard_map.268.mine_ref), channel_id=1, source_target_pairs={{0,4},{1,5},{2,6},{3,7},{4,0},{5,1},{6,2},{7,3},{8,12},{9,13},{10,... | collective-permute-start | bytes 1572872 | tf_op jit(solution)/shard_map/ppermute | solution.py:56
  151.6 25.6 %collective-permute-start.27 = (bf16[32,32,2048]{2,1,0:T(8,128)(2,1)S(1)}, bf16[32,32,2048]{2,1,0:T(8,128)(2,1)S(1)}, u32[]{:S(2)}, u32[]{:S(2)}) collective-permute-start(bf16[32,32,2048]{2,1,0:T(8,128)(2,1)S(1)} %shard_map.271), channel_id=1, source_target_pairs={{0,8},{1,9},{2,10},{3,11},{4,12},{5,13},{6,14},{7,15},{8,0},{9,1},... | collective-permute-start | bytes 12582920 | tf_op jit(solution)/shard_map/ppermute | solution.py:56
  152.0 25.2 %collective-permute-start.28 = (bf16[8,32,2048]{2,1,0:T(8,128)(2,1)S(1)}, bf16[8,32,2048]{2,1,0:T(8,128)(2,1)S(1)}, u32[]{:S(2)}, u32[]{:S(2)}) collective-permute-start(bf16[8,32,2048]{2,1,0:T(8,128)(2,1)S(1)} %shard_map.272.mine_ref), channel_id=1, source_target_pairs={{0,2},{1,3},{2,0},{3,1},{4,6},{5,7},{6,4},{7,5},{8,10},{9,11},{10,... | collective-permute-start | bytes 3145736 | tf_op jit(solution)/shard_map/ppermute | solution.py:56
  153.6 23.6 %collective-permute-start.26 = (bf16[4,64,1024]{2,1,0:T(8,128)(2,1)S(1)}, bf16[4,64,1024]{2,1,0:T(8,128)(2,1)S(1)}, u32[]{:S(2)}, u32[]{:S(2)}) collective-permute-start(bf16[4,64,1024]{2,1,0:T(8,128)(2,1)S(1)} %copy-done.119), channel_id=1, source_target_pairs={{0,24},{1,25},{2,26},{3,27},{4,28},{5,29},{6,30},{7,31},{8,16},{9,... | collective-permute-start | bytes 1572872 | tf_op jit(solution)/shard_map/ppermute | solution.py:60
  181.7 25.2 %collective-permute-start.29 = (bf16[16,32,2048]{2,1,0:T(8,128)(2,1)S(1)}, bf16[16,32,2048]{2,1,0:T(8,128)(2,1)S(1)}, u32[]{:S(2)}, u32[]{:S(2)}) collective-permute-start(bf16[16,32,2048]{2,1,0:T(8,128)(2,1)S(1)} %shard_map.274.mine_ref), channel_id=1, source_target_pairs={{0,16},{1,17},{2,18},{3,19},{4,20},{5,21},{6,22},{7,23},{8,9},{9,8... | collective-permute-start | bytes 6291464 | tf_op jit(solution)/shard_map/ppermute | solution.py:56
  182.7 22.7 %collective-permute-start.30 = (bf16[4,64,1024]{2,1,0:T(8,128)(2,1)S(1)}, bf16[4,64,1024]{2,1,0:T(8,128)(2,1)S(1)}, u32[]{:S(2)}, u32[]{:S(2)}) collective-permute-start(bf16[4,64,1024]{2,1,0:T(8,128)(2,1)S(1)} %shard_map.275.mine_ref), channel_id=1, source_target_pairs={{0,2},{1,3},{2,0},{3,1},{4,6},{5,7},{6,4},{7,5},{8,10},{9,11},{10,... | collective-permute-start | bytes 1572872 | tf_op jit(solution)/shard_map/ppermute | solution.py:56
  210.7 25.4 %collective-permute-start.32 = (bf16[32,32,2048]{2,1,0:T(8,128)(2,1)}, bf16[32,32,2048]{2,1,0:T(8,128)(2,1)}, u32[]{:S(2)}, u32[]{:S(2)}) collective-permute-start(bf16[32,32,2048]{2,1,0:T(8,128)(2,1)} %shard_map.280), channel_id=1, source_target_pairs={{0,8},{1,9},{2,10},{3,11},{4,12},{5,13},{6,14},{7,15},{8,0},{9,1},... | collective-permute-start | bytes 12582920 | tf_op jit(solution)/shard_map/ppermute | solution.py:56
  212.0 18.2 %collective-permute-start.31 = (bf16[8,64,1024]{2,1,0:T(8,128)(2,1)S(1)}, bf16[8,64,1024]{2,1,0:T(8,128)(2,1)}, u32[]{:S(2)}, u32[]{:S(2)}) collective-permute-start(bf16[8,64,1024]{2,1,0:T(8,128)(2,1)S(1)} %shard_map.281.mine_ref), channel_id=1, source_target_pairs={{0,1},{1,0},{2,3},{3,2},{4,5},{5,4},{6,7},{7,6},{8,24},{9,25},{10,... | collective-permute-start | bytes 3145736 | tf_op jit(solution)/shard_map/ppermute | solution.py:56
  233.7 26.9 %collective-permute-start.33 = (bf16[16,64,1024]{2,1,0:T(8,128)(2,1)}, bf16[16,64,1024]{2,1,0:T(8,128)(2,1)}, u32[]{:S(2)}, u32[]{:S(2)}) collective-permute-start(bf16[16,64,1024]{2,1,0:T(8,128)(2,1)} %shard_map.283.mine_ref), channel_id=1, source_target_pairs={{0,16},{1,17},{2,18},{3,19},{4,20},{5,21},{6,22},{7,23},{8,9},{9,8... | collective-permute-start | bytes 6291464 | tf_op jit(solution)/shard_map/ppermute | solution.py:56
  265.0 24.0 %collective-permute-start.35 = (bf16[32,64,1024]{2,1,0:T(8,128)(2,1)}, bf16[32,64,1024]{2,1,0:T(8,128)(2,1)}, u32[]{:S(2)}, u32[]{:S(2)}) collective-permute-start(bf16[32,64,1024]{2,1,0:T(8,128)(2,1)} %shard_map.285), channel_id=1, source_target_pairs={{0,8},{1,9},{2,10},{3,11},{4,12},{5,13},{6,14},{7,15},{8,0},{9,1},... | collective-permute-start | bytes 12582920 | tf_op jit(solution)/shard_map/ppermute | solution.py:56
  298.8 31.7 %collective-permute-start.36 = (bf16[16,64,1024]{2,1,0:T(8,128)(2,1)}, bf16[16,64,1024]{2,1,0:T(8,128)(2,1)S(1)}, u32[]{:S(2)}, u32[]{:S(2)}) collective-permute-start(bf16[16,64,1024]{2,1,0:T(8,128)(2,1)} %get-tuple-element.443), channel_id=1, source_target_pairs={{0,16},{1,17},{2,18},{3,19},{4,20},{5,21},{6,22},{7,23},{8,9},{9,8... | collective-permute-start | bytes 6291464 | tf_op jit(solution)/shard_map/ppermute | solution.py:56
  354.5 25.2 %collective-permute-start.40 = (bf16[16,32,2048]{2,1,0:T(8,128)(2,1)S(1)}, bf16[16,32,2048]{2,1,0:T(8,128)(2,1)S(1)}, u32[]{:S(2)}, u32[]{:S(2)}) collective-permute-start(bf16[16,32,2048]{2,1,0:T(8,128)(2,1)S(1)} %get-tuple-element.460), channel_id=1, source_target_pairs={{0,16},{1,17},{2,18},{3,19},{4,20},{5,21},{6,22},{7,23},{8,9},{9,8... | collective-permute-start | bytes 6291464 | tf_op jit(solution)/shard_map/ppermute | solution.py:56
  355.1 23.8 %collective-permute-start.39 = (bf16[4,64,1024]{2,1,0:T(8,128)(2,1)S(1)}, bf16[4,64,1024]{2,1,0:T(8,128)(2,1)S(1)}, u32[]{:S(2)}, u32[]{:S(2)}) collective-permute-start(bf16[4,64,1024]{2,1,0:T(8,128)(2,1)S(1)} %get-tuple-element.459), channel_id=1, source_target_pairs={{0,2},{1,3},{2,0},{3,1},{4,6},{5,7},{6,4},{7,5},{8,10},{9,11},{10,... | collective-permute-start | bytes 1572872 | tf_op jit(solution)/shard_map/ppermute | solution.py:56
  402.2 21.2 %collective-permute-start.46 = (bf16[4,64,1024]{2,1,0:T(8,128)(2,1)}, bf16[4,64,1024]{2,1,0:T(8,128)(2,1)}, u32[]{:S(2)}, u32[]{:S(2)}) collective-permute-start(bf16[4,64,1024]{2,1,0:T(8,128)(2,1)} %bitcast.68), channel_id=1, source_target_pairs={{0,16},{1,17},{2,18},{3,19},{4,20},{5,21},{6,22},{7,23},{8,24},{9,... | collective-permute-start | bytes 1572872 | tf_op jit(solution)/shard_map/ppermute | solution.py:60
  403.4 23.9 %collective-permute-start.47 = (bf16[4,64,1024]{2,1,0:T(8,128)(2,1)}, bf16[4,64,1024]{2,1,0:T(8,128)(2,1)}, u32[]{:S(2)}, u32[]{:S(2)}) collective-permute-start(bf16[4,64,1024]{2,1,0:T(8,128)(2,1)} %bitcast.69), channel_id=1, source_target_pairs={{0,24},{1,25},{2,26},{3,27},{4,28},{5,29},{6,30},{7,31},{8,16},{9,... | collective-permute-start | bytes 1572872 | tf_op jit(solution)/shard_map/ppermute | solution.py:60
  407.4 20.0 %collective-permute-start.49 = (bf16[4,32,2048]{2,1,0:T(8,128)(2,1)}, bf16[4,32,2048]{2,1,0:T(8,128)(2,1)}, u32[]{:S(2)}, u32[]{:S(2)}) collective-permute-start(bf16[4,32,2048]{2,1,0:T(8,128)(2,1)} %get-tuple-element.495), channel_id=1, source_target_pairs={{0,2},{1,3},{2,0},{3,1},{4,6},{5,7},{6,4},{7,5},{8,10},{9,11},{10,... | collective-permute-start | bytes 1572872 | tf_op jit(solution)/shard_map/ppermute | solution.py:56
  407.4 20.0 %collective-permute-start.48 = (f32[1,64,1024]{2,1,0:T(8,128)}, f32[1,64,1024]{2,1,0:T(8,128)}, u32[]{:S(2)}, u32[]{:S(2)}) collective-permute-start(f32[1,64,1024]{2,1,0:T(8,128)} %get-tuple-element.494), channel_id=1, source_target_pairs={{0,8},{1,9},{2,10},{3,11},{4,12},{5,13},{6,14},{7,15},{8,0},{9,1},... | collective-permute-start | bytes 786440 | tf_op jit(solution)/shard_map/ppermute | solution.py:56
  430.3 25.2 %collective-permute-start.51 = (bf16[16,32,2048]{2,1,0:T(8,128)(2,1)S(1)}, bf16[16,32,2048]{2,1,0:T(8,128)(2,1)S(1)}, u32[]{:S(2)}, u32[]{:S(2)}) collective-permute-start(bf16[16,32,2048]{2,1,0:T(8,128)(2,1)S(1)} %get-tuple-element.506), channel_id=1, source_target_pairs={{0,16},{1,17},{2,18},{3,19},{4,20},{5,21},{6,22},{7,23},{8,9},{9,8... | collective-permute-start | bytes 6291464 | tf_op jit(solution)/shard_map/ppermute | solution.py:56
  431.4 19.7 %collective-permute-start.50 = (bf16[2,32,2048]{2,1,0:T(8,128)(2,1)S(1)}, bf16[2,32,2048]{2,1,0:T(8,128)(2,1)S(1)}, u32[]{:S(2)}, u32[]{:S(2)}) collective-permute-start(bf16[2,32,2048]{2,1,0:T(8,128)(2,1)S(1)} %get-tuple-element.505), channel_id=1, source_target_pairs={{0,4},{1,5},{2,6},{3,7},{4,0},{5,1},{6,2},{7,3},{8,12},{9,13},{10,... | collective-permute-start | bytes 786440 | tf_op jit(solution)/shard_map/ppermute | solution.py:56
  483.9 26.2 %collective-permute-start.57 = (bf16[16,32,2048]{2,1,0:T(8,128)(2,1)}, bf16[16,32,2048]{2,1,0:T(8,128)(2,1)}, u32[]{:S(2)}, u32[]{:S(2)}) collective-permute-start(bf16[16,32,2048]{2,1,0:T(8,128)(2,1)} %get-tuple-element.533), channel_id=1, source_target_pairs={{0,16},{1,17},{2,18},{3,19},{4,20},{5,21},{6,22},{7,23},{8,9},{9,8... | collective-permute-start | bytes 6291464 | tf_op jit(solution)/shard_map/ppermute | solution.py:56
  488.3 21.8 %collective-permute-start.56 = (bf16[4,32,2048]{2,1,0:T(8,128)(2,1)}, bf16[4,32,2048]{2,1,0:T(8,128)(2,1)S(1)}, u32[]{:S(2)}, u32[]{:S(2)}) collective-permute-start(bf16[4,32,2048]{2,1,0:T(8,128)(2,1)} %get-tuple-element.532), channel_id=1, source_target_pairs={{0,2},{1,3},{2,0},{3,1},{4,6},{5,7},{6,4},{7,5},{8,10},{9,11},{10,... | collective-permute-start | bytes 1572872 | tf_op jit(solution)/shard_map/ppermute | solution.py:56
  (182 other events, 1750.0 us)

commit v6 on v5

--- a/solution.py
+++ b/solution.py
@@ -583,7 +583,7 @@
          rows_of(x), (added, (1, 1, width), added_at), whole(gain[None]), rows_of(rest)],
         [((rows, width), dtype, (step, width), lambda i, ref: (i, 0)),
          ((rows // step, 3, width), f32, (1, 3, width), lambda i, ref: (i, 0, 0))],
-        margin=30 if dtype == f32 else 6,
+        margin=30 if dtype == f32 or cols > 3 * BLOCK else 6,
     )
 
 
@@ -909,34 +909,31 @@
     inner_grad, b_sum = inner_back(down_in, own_rows, slope, here)
     hidden2, inner_grad = land((hidden2, inner_grad), falling)
     down_halves = [x.reshape(-1, width) for x in finish(falling)]
+    inner_grad2, b_sum2 = inner_back(down_in, down_halves[1], slope2, here)
+    send = weight_grad(normed3, inner_grad2, total, here)
+    down_in, hidden2, send, got = lax.optimization_barrier((down_in, hidden2, send, got))
+    got_up = exchanged(send)
+    s_down = sums((active, down_in, got, None))
+    down_in, hidden2 = launch((down_in, hidden2), s_down)
+
     mask_rows = jnp.broadcast_to(mask, (frames, slots_local, 1)).reshape(row_count, 1).astype(f32)
     mixed = down_project([active, active2], down_halves, hidden2, down_bias, mask_rows, here)
-    down_in, mixed, got = lax.optimization_barrier((down_in, mixed, got))
-    s_down = sums((active, down_in, got, None))
-    down_in = launch(down_in, s_down)
-
-    inner_grad2, b_sum2 = inner_back(down_in, down_halves[1], slope2, here)
-    send = weight_grad(normed3, inner_grad2, total, here)
-    inner_grads = (inner_grad, inner_grad2)
+    mixed, got_up = lax.optimization_barrier((mixed, got_up))
+    s_up = sums((normed3, inner_grad, got_up, None))
+    hidden2, s_up.pending, mixed = land((hidden2, s_up.pending, mixed), s_down)
+    hidden2 = launch(hidden2, s_down, s_up)
+
     grad2, sums3 = norm_back(
-        inner_grads, up_halves, hidden2, nothing, gains[2], down_in, bf16, here
-    )
-    grad2, send = land((grad2, send), s_down)
-    grad2, send = launch(grad2, s_down, also=[send])
-    got = exchanged(send)
+        (inner_grad, inner_grad2), up_halves, hidden2, nothing, gains[2], down_in, bf16, here
+    )
     b_sums = [x.reshape(total, -1, thin).swapaxes(0, 1) for x in (b_sum, b_sum2)]
     late_rows = [x.reshape(-1, width) for x in b_sums]
     late_rows = jnp.where(
         core == 0, jnp.concatenate(late_rows, axis=0), jnp.concatenate(late_rows[::-1], axis=0)
     )
     late_rows = jnp.concatenate([jnp.sum(down_in.astype(f32), axis=0)[None], late_rows], axis=0)
-
-    t_mix_grad = mixed_back(grad2, t_halves, here)
+    t_mix_grad = mixed_back(grad2, t_halves, here).reshape(frames, slots_local, width)
     send2 = weight_grad(t_mixed, grad2, total, here, 1)
-    (t_mix_grad, send2), got = land((t_mix_grad, send2), s_down, also=[got])
-    s_up = sums((normed3, inner_grad, got, None))
-    t_mix_grad = launch(t_mix_grad, s_down, s_up)
-    t_mix_grad = t_mix_grad.reshape(frames, slots_local, width)
 
     def back(side, where, make, values, grad):
         (out,) = run_attention(
@@ -945,14 +942,16 @@
         return out.reshape(row_count, -1)
 
     t_grad2 = back(1, temporal_place, make_bias, temporal, t_mix_grad)
+    t_mix_grad, t_grad2, late_rows = land((t_mix_grad, t_grad2, late_rows), s_down, s_up)
+    t_mix_grad, t_grad2 = launch((t_mix_grad, t_grad2), s_down, s_up)
+    t_grad = back(0, temporal_place, make_bias, temporal, t_mix_grad)
     send = weight_grad(normed2, t_grad2, total, here)
-    t_grad = back(0, temporal_place, make_bias, temporal, t_mix_grad)
-    t_grads = land((t_grad, t_grad2), s_down, s_up)
-    t_grads, send, send2 = launch(t_grads, s_down, s_up, also=[send, send2])
+    t_grads, send = land(((t_grad, t_grad2), send), s_down, s_up)
+    t_grads, send, send2 = launch(t_grads, s_down, also=[send, send2])
     gots = [exchanged(send), exchanged(send2)]
 
     grad1, sums2 = norm_back(t_grads, t_halves, hidden1, nothing, gains[1], grad2, bf16, here)
-    grad1 = hold(grad1, s_down, s_up)
+    grad1 = hold(grad1, s_down)
     grad1, gots = lax.optimization_barrier((grad1, gots))
     parts = from_slots(grad1)
     parts[1] = along(parts[1], s_down, s_up)
@@ -1005,9 +1004,10 @@
     while not (s_time.done() and s_space.done() and s_small.done()):
         packed = along(packed, s_time, s_space, s_small)
     summed = s_small.result
-    t_rows, s_rows = woven(*s_time.result), woven(*s_space.result)
-    g_t_qkv, g_t_out = t_rows[:, : 3 * width], t_rows[:, 3 * width :]
-    g_s_qkv, g_s_out = s_rows[:, : 3 * width], s_rows[:, 3 * width :]
+    (g_t_qkv, g_t_out), (g_s_qkv, g_s_out) = [
+        [woven(*[x[:, cut] for x in c.result]) for cut in (slice(3 * half), slice(3 * half, None))]
+        for c in (s_time, s_space)
+    ]
 
     return (
         mixed.reshape(shape),

time: 588 us -> 583 us (level)
  local copies, waits for them, and re-layouts: 71.7 us -> 59 us
  waiting for transfers between devices: 126 us -> 133 us
    ppermute x60, waiting for transfers between devices: 81.3 us -> 96.2 us  [flip(): return lax.ppermute(value, AXES, moves)]
    ppermute x12, waiting for transfers between devices: 44.6 us -> 36.3 us  [tm_flip(): return lax.ppermute(value, AXES, moves)]
    unnamed x290 -> x296, local copies, waits for them, and re-layouts: 39.8 us -> 32.4 us
  transfers between devices with their start and end apart: 72 -> 72, of which waited for: 32 -> 31; matrix products, arithmetic and copies ran while one was open for 8% -> 6% of each run, Pallas kernels for 39% -> 42%
where the time goes in v6:
time: 583 us; the launch traced here: 577 us
  Pallas kernels  300 us (51%)
  waiting for transfers between devices  133 us (23%)
  starting transfers between devices  63.1 us (11%)
  local copies, waits for them, and re-layouts  59 us (10%)
  other arithmetic  18.6 us (3%)
    pallas_call x24, Pallas kernels, dense(): pl.pallas_call(body, grid_spec=pltpu.PrefetchScalarGridSpec(num_scalar_pr...  157 us
    ppermute x60, waiting for transfers between devices, flip(): return lax.ppermute(value, AXES, moves)  96.2 us
    pallas_call x6, Pallas kernels, run_attention(): pl.pallas_call(body, grid=(grid,), in_specs=[pl.BlockSpec(memory_space=pl...  52.3 us
    ppermute x60, starting transfers between devices, flip(): return lax.ppermute(value, AXES, moves)  52.3 us
    ppermute x12, waiting for transfers between devices, tm_flip(): return lax.ppermute(value, AXES, moves)  36.3 us
    pallas_call x25, Pallas kernels, merge(): pl.pallas_call(merge_body, grid=(n // block,), in_specs=[pl.BlockSpec(mem...  33.7 us
    unnamed x296, local copies, waits for them, and re-layouts  32.4 us
    pallas_call x2, Pallas kernels, up_project(): pl.pallas_call(up_body, grid=(cols // block,), in_specs=[pl.BlockSpec((ro...  29.1 us
  transfers between devices with their start and end apart: 72, of which 31 were waited for; matrix products, arithmetic and copies ran while one was open for 6% of the time, Pallas kernels for 42%

profile of v6, /device:TPU:1, one launch (start us, length us, event | category | flops | bytes accessed | tf_op | source)
XLA Modules:
  0.0 577.5 jit_solution(15065902298294614481)
XLA Ops:
  16.6 10.5 %collective-permute-done.2.other_ref = bf16[2,32,2048]{2,1,0:T(8,128)(2,1)S(1)} collective-permute-done((bf16[2,32,2048]{2,1,0:T(8,128)(2,1)S(1)}, bf16[2,32,2048]{2,1,0:T(8,128)(2,1)S(1)}, u32[]{:S(2)}, u32[]{:S(2)}) %collective-permute-start.2) | collective-permute-done | bytes 262176 | tf_op jit(solution)/shard_map/ppermute | solution.py:56
  49.5 6.9 %collective-permute-done.9.other_ref = bf16[4,48,128]{2,1,0:T(8,128)(2,1)S(1)} collective-permute-done((bf16[4,48,128]{2,1,0:T(8,128)(2,1)S(1)}, bf16[4,48,128]{2,1,0:T(8,128)(2,1)S(1)}, u32[]{:S(2)}, u32[]{:S(2)}) %collective-permute-start.9) | collective-permute-done | bytes 49184 | tf_op jit(solution)/shard_map/ppermute | solution.py:56
  119.8 7.4 %shard_map.269 = bf16[4,256,1024]{2,1,0:T(8,128)(2,1)S(1)} custom-call(s32[2]{0:T(128)S(1)} %copy-done.107, bf16[4,256,1536]{2,1,0:T(8,128)(2,1)S(1)} %bitcast.210, bf16[4,256,1536]{2,1,0:T(8,128)(2,1)S(1)} %bitcast.212), custom_call_target="tpu_custom_call" | custom-call | tf_op jit(solution)/shard_map/pallas_call | solution.py:367
  132.5 12.7 %collective-permute-done.23.other_ref = bf16[4,32,2048]{2,1,0:T(8,128)(2,1)S(1)} collective-permute-done((bf16[4,32,2048]{2,1,0:T(8,128)(2,1)S(1)}, bf16[4,32,2048]{2,1,0:T(8,128)(2,1)S(1)}, u32[]{:S(2)}, u32[]{:S(2)}) %collective-permute-start.23) | collective-permute-done | bytes 524320 | tf_op jit(solution)/shard_map/ppermute | solution.py:56
  157.8 10.0 %collective-permute-done.25 = bf16[4,64,1024]{2,1,0:T(8,128)(2,1)S(1)} collective-permute-done((bf16[4,64,1024]{2,1,0:T(8,128)(2,1)S(1)}, bf16[4,64,1024]{2,1,0:T(8,128)(2,1)S(1)}, u32[]{:S(2)}, u32[]{:S(2)}) %collective-permute-start.25) | collective-permute-done | bytes 524320 | tf_op jit(solution)/shard_map/ppermute | solution.py:60
  167.8 11.7 %collective-permute-done.26 = bf16[4,64,1024]{2,1,0:T(8,128)(2,1)S(1)} collective-permute-done((bf16[4,64,1024]{2,1,0:T(8,128)(2,1)S(1)}, bf16[4,64,1024]{2,1,0:T(8,128)(2,1)S(1)}, u32[]{:S(2)}, u32[]{:S(2)}) %collective-permute-start.26) | collective-permute-done | bytes 524320 | tf_op jit(solution)/shard_map/ppermute | solution.py:60
  193.7 8.0 %shard_map.278 = bf16[16,64,1024]{2,1,0:T(8,128)(2,1)S(1)} custom-call(s32[2]{0:T(128)S(1)} %pad_add_fusion.8.scalar_ref, bf16[16,64,1536]{2,1,0:T(8,128)(2,1)S(1)} %bitcast.214, bf16[16,64,1536]{2,1,0:T(8,128)(2,1)S(1)} %bitcast.216), custom_call_target="tpu_custom_call" | custom-call | tf_op jit(solution)/shard_map/pallas_call | solution.py:367
  214.7 14.6 %shard_map.282 = (bf16[1024,2048]{1,0:T(8,128)(2,1)S(1)}, bf16[1024,2048]{1,0:T(8,128)(2,1)S(1)}) custom-call(bf16[1024,1024]{1,0:T(8,128)(2,1)S(1)} %get-tuple-element.423.x_ref.refs_0_, bf16[1024,2048]{1,0:T(8,128)(2,1)} %bitcast.59.w_ref.own_ref, f32[1,2048]{1,0:T(1,128)S(1)} %select_n.793.bias_ref), custom_call_target="tpu_custom_call" | custom-call | tf_op jit(solution)/shard_map/pallas_call | solution.py:697
  238.7 14.6 %shard_map.284 = (bf16[1024,2048]{1,0:T(8,128)(2,1)S(1)}, bf16[1024,2048]{1,0:T(8,128)(2,1)S(1)}) custom-call(bf16[1024,1024]{1,0:T(8,128)(2,1)S(1)} %copy-done.14, bf16[1024,2048]{1,0:T(8,128)(2,1)} %bitcast.60.w_ref.other_ref, f32[1,2048]{1,0:T(1,128)S(1)} %select_n.795.bias_ref), custom_call_target="tpu_custom_call" | custom-call | tf_op jit(solution)/shard_map/pallas_call | solution.py:697
  285.8 7.5 %shard_map.290 = (bf16[16,64,1024]{2,1,0:T(8,128)(2,1)}, bf16[16,64,1024]{2,1,0:T(8,128)(2,1)S(1)}) custom-call(s32[3]{0:T(128)S(1)} %pad_add_fusion.13.info_ref, bf16[1024,2048]{1,0:T(8,128)(2,1)S(1)} %copy-done.41, bf16[1024,1024]{1,0:T(8,128)(2,1)S(1)} %bitcast_select_fusion.y_ref.x_ref.refs_1_.rest_ref, ...), custom_call_target="tpu_custom_call" | custom-call | tf_op jit(solution)/shard_map/pallas_call | solution.py:435
  298.6 13.6 %shard_map.291 = bf16[1024,1024]{1,0:T(8,128)(2,1)S(1)} custom-call(s32[1]{0:T(128)} %bitcast.3._.core_ref, bf16[1024,2048]{1,0:T(8,128)(2,1)S(1)} %copy-done.42, bf16[1024,2048]{1,0:T(8,128)(2,1)} %copy-done.44, bf16[2048,1024]{1,0:T(8,128)(2,1)} %bitcast.199, bf16[2048,1024]{1,0:T(8,128)(2,1)} %bitcast.233, f32[1024,1024]{1,0:T(8,128)} %copy-done.46, ...), custom_call_target="tpu_custom_call" | custom-call | tf_op jit(solution)/shard_map/pallas_call | solution.py:435
  312.3 9.4 %shard_map.292 = (bf16[16,32,2048]{2,1,0:T(8,128)(2,1)}, bf16[16,32,2048]{2,1,0:T(8,128)(2,1)S(1)}) custom-call(s32[3]{0:T(128)S(1)} %pad_add_fusion.13.info_ref, bf16[1024,1024]{1,0:T(8,128)(2,1)S(1)} %copy-done.16, bf16[1024,2048]{1,0:T(8,128)(2,1)S(1)} %copy-done.39, bf16[32,32,2048]{2,1,0:T(8,128)(2,1)} %collective-permute-done.36.refs_2_), custom_call_target="tpu_custom_call" | custom-call | tf_op jit(solution)/shard_map/pallas_call | solution.py:435
  328.5 16.6 %shard_map.294 = (bf16[1024,1024]{1,0:T(8,128)(2,1)S(1)}, f32[4,3,1024]{2,1,0:T(4,128)S(1)}) custom-call(s32[1]{0:T(128)} %bitcast.3._.core_ref, bf16[1024,2048]{1,0:T(8,128)(2,1)} %copy-done.38, bf16[1024,2048]{1,0:T(8,128)(2,1)} %copy-done.43, bf16[1024,2048]{1,0:T(8,128)(2,1)} %bitcast.59.w_ref.own_ref, bf16[1024,2048]{1,0:T(8,128)(2,1)} %bitcast.60.w_ref.other_ref, ...), custom_call_target="tpu_custom_call" | custom-call | tf_op jit(solution)/shard_map/pallas_call | solution.py:435
  348.1 9.4 %shard_map.296 = bf16[16,64,1536]{2,1,0:T(8,128)(2,1)S(1)} custom-call(s32[2]{0:T(128)S(1)} %copy-done.110, bf16[16,64,1536]{2,1,0:T(8,128)(2,1)S(1)} %bitcast.217, bf16[16,64,1024]{2,1,0:T(8,128)(2,1)S(1)} %bitcast.227), custom_call_target="tpu_custom_call" | custom-call | tf_op jit(solution)/shard_map/pallas_call | solution.py:367
  373.2 9.4 %shard_map.299 = bf16[16,64,1536]{2,1,0:T(8,128)(2,1)S(1)} custom-call(s32[2]{0:T(128)S(1)} %copy-done.110, bf16[16,64,1536]{2,1,0:T(8,128)(2,1)S(1)} %bitcast.215, bf16[16,64,1024]{2,1,0:T(8,128)(2,1)S(1)} %bitcast.228), custom_call_target="tpu_custom_call" | custom-call | tf_op jit(solution)/shard_map/pallas_call | solution.py:367
  386.2 9.9 %shard_map.303 = (bf16[1024,1024]{1,0:T(8,128)(2,1)S(1)}, f32[4,3,1024]{2,1,0:T(4,128)S(1)}) custom-call(s32[1]{0:T(128)} %bitcast.3._.core_ref, bf16[1024,1536]{1,0:T(8,128)(2,1)S(1)} %bitcast.206, bf16[1024,1536]{1,0:T(8,128)(2,1)S(1)} %bitcast.209, bf16[1024,2048]{1,0:T(8,128)(2,1)S(1)} %bitcast.181, bf16[1024,2048]{1,0:T(8,128)(2,1)S(1)} %bitcast.185, ...), custom_call_target="tpu_custom_call" | custom-call | tf_op jit(solution)/shard_map/pallas_call | solution.py:435
  415.7 7.1 %shard_map.304 = (bf16[16,32,2048]{2,1,0:T(8,128)(2,1)S(1)}, bf16[16,32,2048]{2,1,0:T(8,128)(2,1)S(1)}) custom-call(s32[3]{0:T(128)S(1)} %pad_add_fusion.13.info_ref, bf16[1024,1024]{1,0:T(8,128)(2,1)S(1)} %bitcast.193, bf16[1024,1536]{1,0:T(8,128)(2,1)S(1)} %bitcast.207, bf16[32,32,1536]{2,1,0:T(8,128)(2,1)S(1)} %copy-done.52, ...), custom_call_target="tpu_custom_call" | custom-call | tf_op jit(solution)/shard_map/pallas_call | solution.py:435
  422.8 7.3 %collective-permute-done.47 = bf16[4,64,1024]{2,1,0:T(8,128)(2,1)} collective-permute-done((bf16[4,64,1024]{2,1,0:T(8,128)(2,1)}, bf16[4,64,1024]{2,1,0:T(8,128)(2,1)}, u32[]{:S(2)}, u32[]{:S(2)}) %collective-permute-start.47) | collective-permute-done | bytes 524320 | tf_op jit(solution)/shard_map/ppermute | solution.py:60
  439.8 9.0 %shard_map.309 = bf16[4,256,1536]{2,1,0:T(8,128)(2,1)S(1)} custom-call(s32[2]{0:T(128)S(1)} %copy-done.108, bf16[4,256,1536]{2,1,0:T(8,128)(2,1)S(1)} %bitcast.213, bf16[4,256,1024]{2,1,0:T(8,128)(2,1)S(1)} %bitcast.225), custom_call_target="tpu_custom_call" | custom-call | tf_op jit(solution)/shard_map/pallas_call | solution.py:367
  463.3 9.1 %shard_map.314 = bf16[4,256,1536]{2,1,0:T(8,128)(2,1)S(1)} custom-call(s32[2]{0:T(128)S(1)} %copy-done.108, bf16[4,256,1536]{2,1,0:T(8,128)(2,1)S(1)} %bitcast.211, bf16[4,256,1024]{2,1,0:T(8,128)(2,1)S(1)} %bitcast.226), custom_call_target="tpu_custom_call" | custom-call | tf_op jit(solution)/shard_map/pallas_call | solution.py:367
  477.6 7.8 %shard_map.316 = (bf16[16,32,2048]{2,1,0:T(8,128)(2,1)}, bf16[16,32,2048]{2,1,0:T(8,128)(2,1)S(1)}) custom-call(s32[3]{0:T(128)S(1)} %pad_add_fusion.13.info_ref, bf16[1024,1024]{1,0:T(8,128)(2,1)S(1)} %bitcast.189, bf16[1024,1536]{1,0:T(8,128)(2,1)S(1)} %bitcast.220, bf16[32,32,1536]{2,1,0:T(8,128)(2,1)S(1)} %collective-permute-done.54.refs_2_, ...), custom_call_target="tpu_custom_call" | custom-call | tf_op jit(solution)/shard_map/pallas_call | solution.py:435
  495.3 13.0 %shard_map.317 = (f32[1024,1024]{1,0:T(8,128)}, f32[4,3,1024]{2,1,0:T(4,128)S(1)}) custom-call(s32[1]{0:T(128)} %bitcast.3._.core_ref, bf16[1024,1536]{1,0:T(8,128)(2,1)S(1)} %bitcast.221, bf16[1024,1536]{1,0:T(8,128)(2,1)} %bitcast.219, bf16[1024,2048]{1,0:T(8,128)(2,1)} %bitcast.38.w_ref.own_ref, bf16[1024,2048]{1,0:T(8,128)(2,1)} %bitcast.40.w_ref.other_ref, ...), custom_call_target="tpu_custom_call" | custom-call | tf_op jit(solution)/shard_map/pallas_call | solution.py:435
  541.6 8.3 %collective-permute-done.64 = f32[19,128]{1,0:T(8,128)S(1)} collective-permute-done((f32[19,128]{1,0:T(8,128)S(1)}, f32[19,128]{1,0:T(8,128)S(1)}, u32[]{:S(2)}, u32[]{:S(2)}) %collective-permute-start.64) | collective-permute-done | bytes 9760 | tf_op jit(solution)/shard_map/ppermute | solution.py:56
  560.9 9.0 %collective-permute-done.67.b_ref = bf16[2,32,2048]{2,1,0:T(8,128)(2,1)S(1)} collective-permute-done((bf16[2,32,2048]{2,1,0:T(8,128)(2,1)S(1)}, bf16[2,32,2048]{2,1,0:T(8,128)(2,1)S(1)}, u32[]{:S(2)}, u32[]{:S(2)}) %collective-permute-start.67) | collective-permute-done | bytes 262176 | tf_op jit(solution)/shard_map/ppermute | solution.py:56
  (621 shorter events, 330.9 us)
Async XLA Ops:
  10.6 21.7 %collective-permute-start.3 = (bf16[4,64,1024]{2,1,0:T(8,128)(2,1)}, bf16[4,64,1024]{2,1,0:T(8,128)(2,1)}, u32[]{:S(2)}, u32[]{:S(2)}) collective-permute-start(bf16[4,64,1024]{2,1,0:T(8,128)(2,1)} %get-tuple-element.661), channel_id=1, source_target_pairs={{0,8},{1,9},{2,10},{3,11},{4,12},{5,13},{6,14},{7,15},{8,0},{9,1},... | collective-permute-start | bytes 1572872 | tf_op jit(solution)/shard_map/ppermute | solution.py:60
  11.3 21.1 %collective-permute-start.4 = (bf16[4,64,1024]{2,1,0:T(8,128)(2,1)}, bf16[4,64,1024]{2,1,0:T(8,128)(2,1)}, u32[]{:S(2)}, u32[]{:S(2)}) collective-permute-start(bf16[4,64,1024]{2,1,0:T(8,128)(2,1)} %get-tuple-element.660), channel_id=1, source_target_pairs={{0,16},{1,17},{2,18},{3,19},{4,20},{5,21},{6,22},{7,23},{8,24},{9,... | collective-permute-start | bytes 1572872 | tf_op jit(solution)/shard_map/ppermute | solution.py:60
  12.5 24.1 %collective-permute-start.5 = (bf16[4,64,1024]{2,1,0:T(8,128)(2,1)}, bf16[4,64,1024]{2,1,0:T(8,128)(2,1)}, u32[]{:S(2)}, u32[]{:S(2)}) collective-permute-start(bf16[4,64,1024]{2,1,0:T(8,128)(2,1)} %get-tuple-element.659), channel_id=1, source_target_pairs={{0,24},{1,25},{2,26},{3,27},{4,28},{5,29},{6,30},{7,31},{8,16},{9,... | collective-permute-start | bytes 1572872 | tf_op jit(solution)/shard_map/ppermute | solution.py:60
  62.7 28.3 %collective-permute-start.15 = (bf16[16,32,2048]{2,1,0:T(8,128)(2,1)}, bf16[16,32,2048]{2,1,0:T(8,128)(2,1)}, u32[]{:S(2)}, u32[]{:S(2)}) collective-permute-start(bf16[16,32,2048]{2,1,0:T(8,128)(2,1)} %shard_map.256.mine_ref), channel_id=1, source_target_pairs={{0,16},{1,17},{2,18},{3,19},{4,20},{5,21},{6,22},{7,23},{8,9},{9,8... | collective-permute-start | bytes 6291464 | tf_op jit(solution)/shard_map/ppermute | solution.py:56
  118.3 27.0 %collective-permute-start.22 = (bf16[16,32,2048]{2,1,0:T(8,128)(2,1)S(1)}, bf16[16,32,2048]{2,1,0:T(8,128)(2,1)S(1)}, u32[]{:S(2)}, u32[]{:S(2)}) collective-permute-start(bf16[16,32,2048]{2,1,0:T(8,128)(2,1)S(1)} %shard_map.267.mine_ref), channel_id=1, source_target_pairs={{0,16},{1,17},{2,18},{3,19},{4,20},{5,21},{6,22},{7,23},{8,9},{9,8... | collective-permute-start | bytes 6291464 | tf_op jit(solution)/shard_map/ppermute | solution.py:56
  119.8 25.5 %collective-permute-start.23 = (bf16[4,32,2048]{2,1,0:T(8,128)(2,1)S(1)}, bf16[4,32,2048]{2,1,0:T(8,128)(2,1)S(1)}, u32[]{:S(2)}, u32[]{:S(2)}) collective-permute-start(bf16[4,32,2048]{2,1,0:T(8,128)(2,1)S(1)} %shard_map.268.mine_ref), channel_id=1, source_target_pairs={{0,4},{1,5},{2,6},{3,7},{4,0},{5,1},{6,2},{7,3},{8,12},{9,13},{10,... | collective-permute-start | bytes 1572872 | tf_op jit(solution)/shard_map/ppermute | solution.py:56
  153.9 25.6 %collective-permute-start.27 = (bf16[32,32,2048]{2,1,0:T(8,128)(2,1)S(1)}, bf16[32,32,2048]{2,1,0:T(8,128)(2,1)S(1)}, u32[]{:S(2)}, u32[]{:S(2)}) collective-permute-start(bf16[32,32,2048]{2,1,0:T(8,128)(2,1)S(1)} %shard_map.271), channel_id=1, source_target_pairs={{0,8},{1,9},{2,10},{3,11},{4,12},{5,13},{6,14},{7,15},{8,0},{9,1},... | collective-permute-start | bytes 12582920 | tf_op jit(solution)/shard_map/ppermute | solution.py:56
  154.3 25.2 %collective-permute-start.28 = (bf16[8,32,2048]{2,1,0:T(8,128)(2,1)S(1)}, bf16[8,32,2048]{2,1,0:T(8,128)(2,1)S(1)}, u32[]{:S(2)}, u32[]{:S(2)}) collective-permute-start(bf16[8,32,2048]{2,1,0:T(8,128)(2,1)S(1)} %shard_map.272.mine_ref), channel_id=1, source_target_pairs={{0,2},{1,3},{2,0},{3,1},{4,6},{5,7},{6,4},{7,5},{8,10},{9,11},{10,... | collective-permute-start | bytes 3145736 | tf_op jit(solution)/shard_map/ppermute | solution.py:56
  155.5 24.0 %collective-permute-start.26 = (bf16[4,64,1024]{2,1,0:T(8,128)(2,1)S(1)}, bf16[4,64,1024]{2,1,0:T(8,128)(2,1)S(1)}, u32[]{:S(2)}, u32[]{:S(2)}) collective-permute-start(bf16[4,64,1024]{2,1,0:T(8,128)(2,1)S(1)} %copy-done.120), channel_id=1, source_target_pairs={{0,24},{1,25},{2,26},{3,27},{4,28},{5,29},{6,30},{7,31},{8,16},{9,... | collective-permute-start | bytes 1572872 | tf_op jit(solution)/shard_map/ppermute | solution.py:60
  183.8 25.2 %collective-permute-start.29 = (bf16[16,32,2048]{2,1,0:T(8,128)(2,1)S(1)}, bf16[16,32,2048]{2,1,0:T(8,128)(2,1)S(1)}, u32[]{:S(2)}, u32[]{:S(2)}) collective-permute-start(bf16[16,32,2048]{2,1,0:T(8,128)(2,1)S(1)} %shard_map.274.mine_ref), channel_id=1, source_target_pairs={{0,16},{1,17},{2,18},{3,19},{4,20},{5,21},{6,22},{7,23},{8,9},{9,8... | collective-permute-start | bytes 6291464 | tf_op jit(solution)/shard_map/ppermute | solution.py:56
  183.9 22.7 %collective-permute-start.30 = (bf16[4,64,1024]{2,1,0:T(8,128)(2,1)S(1)}, bf16[4,64,1024]{2,1,0:T(8,128)(2,1)S(1)}, u32[]{:S(2)}, u32[]{:S(2)}) collective-permute-start(bf16[4,64,1024]{2,1,0:T(8,128)(2,1)S(1)} %shard_map.275.mine_ref), channel_id=1, source_target_pairs={{0,2},{1,3},{2,0},{3,1},{4,6},{5,7},{6,4},{7,5},{8,10},{9,11},{10,... | collective-permute-start | bytes 1572872 | tf_op jit(solution)/shard_map/ppermute | solution.py:56
  212.8 24.3 %collective-permute-start.32 = (bf16[32,32,2048]{2,1,0:T(8,128)(2,1)}, bf16[32,32,2048]{2,1,0:T(8,128)(2,1)}, u32[]{:S(2)}, u32[]{:S(2)}) collective-permute-start(bf16[32,32,2048]{2,1,0:T(8,128)(2,1)} %shard_map.280), channel_id=1, source_target_pairs={{0,8},{1,9},{2,10},{3,11},{4,12},{5,13},{6,14},{7,15},{8,0},{9,1},... | collective-permute-start | bytes 12582920 | tf_op jit(solution)/shard_map/ppermute | solution.py:56
  234.6 25.5 %collective-permute-start.33 = (bf16[16,64,1024]{2,1,0:T(8,128)(2,1)}, bf16[16,64,1024]{2,1,0:T(8,128)(2,1)}, u32[]{:S(2)}, u32[]{:S(2)}) collective-permute-start(bf16[16,64,1024]{2,1,0:T(8,128)(2,1)} %shard_map.283.mine_ref), channel_id=1, source_target_pairs={{0,16},{1,17},{2,18},{3,19},{4,20},{5,21},{6,22},{7,23},{8,9},{9,8... | collective-permute-start | bytes 6291464 | tf_op jit(solution)/shard_map/ppermute | solution.py:56
  263.8 21.3 %collective-permute-start.35 = (bf16[32,64,1024]{2,1,0:T(8,128)(2,1)S(1)}, bf16[32,64,1024]{2,1,0:T(8,128)(2,1)S(1)}, u32[]{:S(2)}, u32[]{:S(2)}) collective-permute-start(bf16[32,64,1024]{2,1,0:T(8,128)(2,1)S(1)} %shard_map.285), channel_id=1, source_target_pairs={{0,8},{1,9},{2,10},{3,11},{4,12},{5,13},{6,14},{7,15},{8,0},{9,1},... | collective-permute-start | bytes 12582920 | tf_op jit(solution)/shard_map/ppermute | solution.py:56
  285.1 27.2 %collective-permute-start.36 = (bf16[32,32,2048]{2,1,0:T(8,128)(2,1)}, bf16[32,32,2048]{2,1,0:T(8,128)(2,1)}, u32[]{:S(2)}, u32[]{:S(2)}) collective-permute-start(bf16[32,32,2048]{2,1,0:T(8,128)(2,1)} %shard_map.289), channel_id=1, source_target_pairs={{0,8},{1,9},{2,10},{3,11},{4,12},{5,13},{6,14},{7,15},{8,0},{9,1},... | collective-permute-start | bytes 12582920 | tf_op jit(solution)/shard_map/ppermute | solution.py:56
  294.6 27.2 %collective-permute-start.37 = (bf16[16,64,1024]{2,1,0:T(8,128)(2,1)}, bf16[16,64,1024]{2,1,0:T(8,128)(2,1)}, u32[]{:S(2)}, u32[]{:S(2)}) collective-permute-start(bf16[16,64,1024]{2,1,0:T(8,128)(2,1)} %get-tuple-element.451), channel_id=1, source_target_pairs={{0,16},{1,17},{2,18},{3,19},{4,20},{5,21},{6,22},{7,23},{8,9},{9,8... | collective-permute-start | bytes 6291464 | tf_op jit(solution)/shard_map/ppermute | solution.py:56
  325.1 36.8 %collective-permute-start.39 = (bf16[16,32,2048]{2,1,0:T(8,128)(2,1)}, bf16[16,32,2048]{2,1,0:T(8,128)(2,1)}, u32[]{:S(2)}, u32[]{:S(2)}) collective-permute-start(bf16[16,32,2048]{2,1,0:T(8,128)(2,1)} %get-tuple-element.464), channel_id=1, source_target_pairs={{0,16},{1,17},{2,18},{3,19},{4,20},{5,21},{6,22},{7,23},{8,9},{9,8... | collective-permute-start | bytes 6291464 | tf_op jit(solution)/shard_map/ppermute | solution.py:56
  325.2 32.3 %collective-permute-start.38 = (bf16[8,64,1024]{2,1,0:T(8,128)(2,1)}, bf16[8,64,1024]{2,1,0:T(8,128)(2,1)}, u32[]{:S(2)}, u32[]{:S(2)}) collective-permute-start(bf16[8,64,1024]{2,1,0:T(8,128)(2,1)} %get-tuple-element.463), channel_id=1, source_target_pairs={{0,1},{1,0},{2,3},{3,2},{4,5},{5,4},{6,7},{7,6},{8,24},{9,25},{10,... | collective-permute-start | bytes 3145736 | tf_op jit(solution)/shard_map/ppermute | solution.py:56
  405.6 24.5 %collective-permute-start.47 = (bf16[4,64,1024]{2,1,0:T(8,128)(2,1)}, bf16[4,64,1024]{2,1,0:T(8,128)(2,1)}, u32[]{:S(2)}, u32[]{:S(2)}) collective-permute-start(bf16[4,64,1024]{2,1,0:T(8,128)(2,1)} %bitcast.72), channel_id=1, source_target_pairs={{0,24},{1,25},{2,26},{3,27},{4,28},{5,29},{6,30},{7,31},{8,16},{9,... | collective-permute-start | bytes 1572872 | tf_op jit(solution)/shard_map/ppermute | solution.py:60
  408.5 21.6 %collective-permute-start.49 = (bf16[4,32,2048]{2,1,0:T(8,128)(2,1)}, bf16[4,32,2048]{2,1,0:T(8,128)(2,1)}, u32[]{:S(2)}, u32[]{:S(2)}) collective-permute-start(bf16[4,32,2048]{2,1,0:T(8,128)(2,1)} %get-tuple-element.506), channel_id=1, source_target_pairs={{0,2},{1,3},{2,0},{3,1},{4,6},{5,7},{6,4},{7,5},{8,10},{9,11},{10,... | collective-permute-start | bytes 1572872 | tf_op jit(solution)/shard_map/ppermute | solution.py:56
  408.5 21.6 %collective-permute-start.48 = (f32[1,64,1024]{2,1,0:T(8,128)}, f32[1,64,1024]{2,1,0:T(8,128)}, u32[]{:S(2)}, u32[]{:S(2)}) collective-permute-start(f32[1,64,1024]{2,1,0:T(8,128)} %get-tuple-element.505), channel_id=1, source_target_pairs={{0,8},{1,9},{2,10},{3,11},{4,12},{5,13},{6,14},{7,15},{8,0},{9,1},... | collective-permute-start | bytes 786440 | tf_op jit(solution)/shard_map/ppermute | solution.py:56
  433.0 25.2 %collective-permute-start.51 = (bf16[16,32,2048]{2,1,0:T(8,128)(2,1)S(1)}, bf16[16,32,2048]{2,1,0:T(8,128)(2,1)S(1)}, u32[]{:S(2)}, u32[]{:S(2)}) collective-permute-start(bf16[16,32,2048]{2,1,0:T(8,128)(2,1)S(1)} %get-tuple-element.517), channel_id=1, source_target_pairs={{0,16},{1,17},{2,18},{3,19},{4,20},{5,21},{6,22},{7,23},{8,9},{9,8... | collective-permute-start | bytes 6291464 | tf_op jit(solution)/shard_map/ppermute | solution.py:56
  433.3 19.9 %collective-permute-start.50 = (bf16[2,32,2048]{2,1,0:T(8,128)(2,1)S(1)}, bf16[2,32,2048]{2,1,0:T(8,128)(2,1)S(1)}, u32[]{:S(2)}, u32[]{:S(2)}) collective-permute-start(bf16[2,32,2048]{2,1,0:T(8,128)(2,1)S(1)} %get-tuple-element.516), channel_id=1, source_target_pairs={{0,4},{1,5},{2,6},{3,7},{4,0},{5,1},{6,2},{7,3},{8,12},{9,13},{10,... | collective-permute-start | bytes 786440 | tf_op jit(solution)/shard_map/ppermute | solution.py:56
  486.8 25.5 %collective-permute-start.57 = (bf16[16,32,2048]{2,1,0:T(8,128)(2,1)}, bf16[16,32,2048]{2,1,0:T(8,128)(2,1)}, u32[]{:S(2)}, u32[]{:S(2)}) collective-permute-start(bf16[16,32,2048]{2,1,0:T(8,128)(2,1)} %get-tuple-element.544), channel_id=1, source_target_pairs={{0,16},{1,17},{2,18},{3,19},{4,20},{5,21},{6,22},{7,23},{8,9},{9,8... | collective-permute-start | bytes 6291464 | tf_op jit(solution)/shard_map/ppermute | solution.py:56
  (186 other events, 1689.5 us)

commit v7 on v6

--- a/solution.py
+++ b/solution.py
@@ -198,7 +198,7 @@
 
 class Chain:
     def __init__(self, steps):
-        self.steps, self.flying, self.result = steps, False, None
+        self.steps, self.flying, self.result, self.started = steps, False, None, 0
         self.pending = next(steps)
 
     def done(self):
@@ -210,6 +210,7 @@
         except StopIteration as stop:
             self.result = stop.value
         self.flying = not self.flying
+        self.started += self.flying
 
 
 def hold(value, *chains):
@@ -240,6 +241,12 @@
 
 def along(value, *chains):
     return launch(land(value, *chains), *chains)
+
+
+def up_to(chain, count):
+    while chain.started < count or chain.flying:
+        chain.move()
+    return chain.pending
 
 
 def finish(chain):
@@ -903,7 +910,8 @@
     down_in = jnp.where(mask, in_slots(cotangent), 0).reshape(row_count, width)
     send = weight_grad(active2, down_in, total, here)
     down_in, send = land((down_in, send), falling)
-    own_rows = falling.pending[0].reshape(-1, width)
+    (own_rows,) = up_to(falling, total.bit_length() - 1)
+    own_rows = own_rows.reshape(-1, width)
     down_in, send = launch(down_in, falling, also=[send])
     got = exchanged(send)
     inner_grad, b_sum = inner_back(down_in, own_rows, slope, here)

time: 583 us -> 583 us (level)
  no operation moved by 1% of the time
where the time goes in v7:
time: 583 us; the launch traced here: 577 us
  Pallas kernels  300 us (51%)
  waiting for transfers between devices  133 us (23%)
  starting transfers between devices  63.1 us (11%)
  local copies, waits for them, and re-layouts  59 us (10%)
  other arithmetic  18.6 us (3%)
    pallas_call x24, Pallas kernels, dense(): pl.pallas_call(body, grid_spec=pltpu.PrefetchScalarGridSpec(num_scalar_pr...  157 us
    ppermute x60, waiting for transfers between devices, flip(): return lax.ppermute(value, AXES, moves)  96.2 us
    pallas_call x6, Pallas kernels, run_attention(): pl.pallas_call(body, grid=(grid,), in_specs=[pl.BlockSpec(memory_space=pl...  52.3 us
    ppermute x60, starting transfers between devices, flip(): return lax.ppermute(value, AXES, moves)  52.3 us
    ppermute x12, waiting for transfers between devices, tm_flip(): return lax.ppermute(value, AXES, moves)  36.3 us
    pallas_call x25, Pallas kernels, merge(): pl.pallas_call(merge_body, grid=(n // block,), in_specs=[pl.BlockSpec(mem...  33.7 us
    unnamed x296, local copies, waits for them, and re-layouts  32.4 us
    pallas_call x2, Pallas kernels, up_project(): pl.pallas_call(up_body, grid=(cols // block,), in_specs=[pl.BlockSpec((ro...  29.1 us
  transfers between devices with their start and end apart: 72, of which 31 were waited for; matrix products, arithmetic and copies ran while one was open for 6% of the time, Pallas kernels for 42%

profile of v7, /device:TPU:1, one launch (start us, length us, event | category | flops | bytes accessed | tf_op | source)
XLA Modules:
  0.0 577.5 jit_solution(15065902298294614481)
XLA Ops:
  16.6 10.5 %collective-permute-done.2.other_ref = bf16[2,32,2048]{2,1,0:T(8,128)(2,1)S(1)} collective-permute-done((bf16[2,32,2048]{2,1,0:T(8,128)(2,1)S(1)}, bf16[2,32,2048]{2,1,0:T(8,128)(2,1)S(1)}, u32[]{:S(2)}, u32[]{:S(2)}) %collective-permute-start.2) | collective-permute-done | bytes 262176 | tf_op jit(solution)/shard_map/ppermute | solution.py:56
  49.5 6.9 %collective-permute-done.9.other_ref = bf16[4,48,128]{2,1,0:T(8,128)(2,1)S(1)} collective-permute-done((bf16[4,48,128]{2,1,0:T(8,128)(2,1)S(1)}, bf16[4,48,128]{2,1,0:T(8,128)(2,1)S(1)}, u32[]{:S(2)}, u32[]{:S(2)}) %collective-permute-start.9) | collective-permute-done | bytes 49184 | tf_op jit(solution)/shard_map/ppermute | solution.py:56
  119.8 7.4 %shard_map.269 = bf16[4,256,1024]{2,1,0:T(8,128)(2,1)S(1)} custom-call(s32[2]{0:T(128)S(1)} %copy-done.107, bf16[4,256,1536]{2,1,0:T(8,128)(2,1)S(1)} %bitcast.210, bf16[4,256,1536]{2,1,0:T(8,128)(2,1)S(1)} %bitcast.212), custom_call_target="tpu_custom_call" | custom-call | tf_op jit(solution)/shard_map/pallas_call | solution.py:374
  132.5 12.7 %collective-permute-done.23.other_ref = bf16[4,32,2048]{2,1,0:T(8,128)(2,1)S(1)} collective-permute-done((bf16[4,32,2048]{2,1,0:T(8,128)(2,1)S(1)}, bf16[4,32,2048]{2,1,0:T(8,128)(2,1)S(1)}, u32[]{:S(2)}, u32[]{:S(2)}) %collective-permute-start.23) | collective-permute-done | bytes 524320 | tf_op jit(solution)/shard_map/ppermute | solution.py:56
  157.8 10.0 %collective-permute-done.25 = bf16[4,64,1024]{2,1,0:T(8,128)(2,1)S(1)} collective-permute-done((bf16[4,64,1024]{2,1,0:T(8,128)(2,1)S(1)}, bf16[4,64,1024]{2,1,0:T(8,128)(2,1)S(1)}, u32[]{:S(2)}, u32[]{:S(2)}) %collective-permute-start.25) | collective-permute-done | bytes 524320 | tf_op jit(solution)/shard_map/ppermute | solution.py:60
  167.8 11.7 %collective-permute-done.26 = bf16[4,64,1024]{2,1,0:T(8,128)(2,1)S(1)} collective-permute-done((bf16[4,64,1024]{2,1,0:T(8,128)(2,1)S(1)}, bf16[4,64,1024]{2,1,0:T(8,128)(2,1)S(1)}, u32[]{:S(2)}, u32[]{:S(2)}) %collective-permute-start.26) | collective-permute-done | bytes 524320 | tf_op jit(solution)/shard_map/ppermute | solution.py:60
  193.7 8.0 %shard_map.278 = bf16[16,64,1024]{2,1,0:T(8,128)(2,1)S(1)} custom-call(s32[2]{0:T(128)S(1)} %pad_add_fusion.8.scalar_ref, bf16[16,64,1536]{2,1,0:T(8,128)(2,1)S(1)} %bitcast.214, bf16[16,64,1536]{2,1,0:T(8,128)(2,1)S(1)} %bitcast.216), custom_call_target="tpu_custom_call" | custom-call | tf_op jit(solution)/shard_map/pallas_call | solution.py:374
  214.7 14.6 %shard_map.282 = (bf16[1024,2048]{1,0:T(8,128)(2,1)S(1)}, bf16[1024,2048]{1,0:T(8,128)(2,1)S(1)}) custom-call(bf16[1024,1024]{1,0:T(8,128)(2,1)S(1)} %get-tuple-element.423.x_ref.refs_0_, bf16[1024,2048]{1,0:T(8,128)(2,1)} %bitcast.59.w_ref.own_ref, f32[1,2048]{1,0:T(1,128)S(1)} %select_n.793.bias_ref), custom_call_target="tpu_custom_call" | custom-call | tf_op jit(solution)/shard_map/pallas_call | solution.py:704
  238.7 14.6 %shard_map.284 = (bf16[1024,2048]{1,0:T(8,128)(2,1)S(1)}, bf16[1024,2048]{1,0:T(8,128)(2,1)S(1)}) custom-call(bf16[1024,1024]{1,0:T(8,128)(2,1)S(1)} %copy-done.14, bf16[1024,2048]{1,0:T(8,128)(2,1)} %bitcast.60.w_ref.other_ref, f32[1,2048]{1,0:T(1,128)S(1)} %select_n.795.bias_ref), custom_call_target="tpu_custom_call" | custom-call | tf_op jit(solution)/shard_map/pallas_call | solution.py:704
  285.8 7.5 %shard_map.290 = (bf16[16,64,1024]{2,1,0:T(8,128)(2,1)}, bf16[16,64,1024]{2,1,0:T(8,128)(2,1)S(1)}) custom-call(s32[3]{0:T(128)S(1)} %pad_add_fusion.13.info_ref, bf16[1024,2048]{1,0:T(8,128)(2,1)S(1)} %copy-done.41, bf16[1024,1024]{1,0:T(8,128)(2,1)S(1)} %bitcast_select_fusion.y_ref.x_ref.refs_1_.rest_ref, ...), custom_call_target="tpu_custom_call" | custom-call | tf_op jit(solution)/shard_map/pallas_call | solution.py:442
  298.6 13.6 %shard_map.291 = bf16[1024,1024]{1,0:T(8,128)(2,1)S(1)} custom-call(s32[1]{0:T(128)} %bitcast.3._.core_ref, bf16[1024,2048]{1,0:T(8,128)(2,1)S(1)} %copy-done.42, bf16[1024,2048]{1,0:T(8,128)(2,1)} %copy-done.44, bf16[2048,1024]{1,0:T(8,128)(2,1)} %bitcast.199, bf16[2048,1024]{1,0:T(8,128)(2,1)} %bitcast.233, f32[1024,1024]{1,0:T(8,128)} %copy-done.46, ...), custom_call_target="tpu_custom_call" | custom-call | tf_op jit(solution)/shard_map/pallas_call | solution.py:442
  312.3 9.4 %shard_map.292 = (bf16[16,32,2048]{2,1,0:T(8,128)(2,1)}, bf16[16,32,2048]{2,1,0:T(8,128)(2,1)S(1)}) custom-call(s32[3]{0:T(128)S(1)} %pad_add_fusion.13.info_ref, bf16[1024,1024]{1,0:T(8,128)(2,1)S(1)} %copy-done.16, bf16[1024,2048]{1,0:T(8,128)(2,1)S(1)} %copy-done.39, bf16[32,32,2048]{2,1,0:T(8,128)(2,1)} %collective-permute-done.36.refs_2_), custom_call_target="tpu_custom_call" | custom-call | tf_op jit(solution)/shard_map/pallas_call | solution.py:442
  328.5 16.6 %shard_map.294 = (bf16[1024,1024]{1,0:T(8,128)(2,1)S(1)}, f32[4,3,1024]{2,1,0:T(4,128)S(1)}) custom-call(s32[1]{0:T(128)} %bitcast.3._.core_ref, bf16[1024,2048]{1,0:T(8,128)(2,1)} %copy-done.38, bf16[1024,2048]{1,0:T(8,128)(2,1)} %copy-done.43, bf16[1024,2048]{1,0:T(8,128)(2,1)} %bitcast.59.w_ref.own_ref, bf16[1024,2048]{1,0:T(8,128)(2,1)} %bitcast.60.w_ref.other_ref, ...), custom_call_target="tpu_custom_call" | custom-call | tf_op jit(solution)/shard_map/pallas_call | solution.py:442
  348.1 9.4 %shard_map.296 = bf16[16,64,1536]{2,1,0:T(8,128)(2,1)S(1)} custom-call(s32[2]{0:T(128)S(1)} %copy-done.110, bf16[16,64,1536]{2,1,0:T(8,128)(2,1)S(1)} %bitcast.217, bf16[16,64,1024]{2,1,0:T(8,128)(2,1)S(1)} %bitcast.227), custom_call_target="tpu_custom_call" | custom-call | tf_op jit(solution)/shard_map/pallas_call | solution.py:374
  373.2 9.4 %shard_map.299 = bf16[16,64,1536]{2,1,0:T(8,128)(2,1)S(1)} custom-call(s32[2]{0:T(128)S(1)} %copy-done.110, bf16[16,64,1536]{2,1,0:T(8,128)(2,1)S(1)} %bitcast.215, bf16[16,64,1024]{2,1,0:T(8,128)(2,1)S(1)} %bitcast.228), custom_call_target="tpu_custom_call" | custom-call | tf_op jit(solution)/shard_map/pallas_call | solution.py:374
  386.2 9.9 %shard_map.303 = (bf16[1024,1024]{1,0:T(8,128)(2,1)S(1)}, f32[4,3,1024]{2,1,0:T(4,128)S(1)}) custom-call(s32[1]{0:T(128)} %bitcast.3._.core_ref, bf16[1024,1536]{1,0:T(8,128)(2,1)S(1)} %bitcast.206, bf16[1024,1536]{1,0:T(8,128)(2,1)S(1)} %bitcast.209, bf16[1024,2048]{1,0:T(8,128)(2,1)S(1)} %bitcast.181, bf16[1024,2048]{1,0:T(8,128)(2,1)S(1)} %bitcast.185, ...), custom_call_target="tpu_custom_call" | custom-call | tf_op jit(solution)/shard_map/pallas_call | solution.py:442
  415.7 7.1 %shard_map.304 = (bf16[16,32,2048]{2,1,0:T(8,128)(2,1)S(1)}, bf16[16,32,2048]{2,1,0:T(8,128)(2,1)S(1)}) custom-call(s32[3]{0:T(128)S(1)} %pad_add_fusion.13.info_ref, bf16[1024,1024]{1,0:T(8,128)(2,1)S(1)} %bitcast.193, bf16[1024,1536]{1,0:T(8,128)(2,1)S(1)} %bitcast.207, bf16[32,32,1536]{2,1,0:T(8,128)(2,1)S(1)} %copy-done.52, ...), custom_call_target="tpu_custom_call" | custom-call | tf_op jit(solution)/shard_map/pallas_call | solution.py:442
  422.8 7.3 %collective-permute-done.47 = bf16[4,64,1024]{2,1,0:T(8,128)(2,1)} collective-permute-done((bf16[4,64,1024]{2,1,0:T(8,128)(2,1)}, bf16[4,64,1024]{2,1,0:T(8,128)(2,1)}, u32[]{:S(2)}, u32[]{:S(2)}) %collective-permute-start.47) | collective-permute-done | bytes 524320 | tf_op jit(solution)/shard_map/ppermute | solution.py:60
  439.8 9.0 %shard_map.309 = bf16[4,256,1536]{2,1,0:T(8,128)(2,1)S(1)} custom-call(s32[2]{0:T(128)S(1)} %copy-done.108, bf16[4,256,1536]{2,1,0:T(8,128)(2,1)S(1)} %bitcast.213, bf16[4,256,1024]{2,1,0:T(8,128)(2,1)S(1)} %bitcast.225), custom_call_target="tpu_custom_call" | custom-call | tf_op jit(solution)/shard_map/pallas_call | solution.py:374
  463.3 9.1 %shard_map.314 = bf16[4,256,1536]{2,1,0:T(8,128)(2,1)S(1)} custom-call(s32[2]{0:T(128)S(1)} %copy-done.108, bf16[4,256,1536]{2,1,0:T(8,128)(2,1)S(1)} %bitcast.211, bf16[4,256,1024]{2,1,0:T(8,128)(2,1)S(1)} %bitcast.226), custom_call_target="tpu_custom_call" | custom-call | tf_op jit(solution)/shard_map/pallas_call | solution.py:374
  477.6 7.8 %shard_map.316 = (bf16[16,32,2048]{2,1,0:T(8,128)(2,1)}, bf16[16,32,2048]{2,1,0:T(8,128)(2,1)S(1)}) custom-call(s32[3]{0:T(128)S(1)} %pad_add_fusion.13.info_ref, bf16[1024,1024]{1,0:T(8,128)(2,1)S(1)} %bitcast.189, bf16[1024,1536]{1,0:T(8,128)(2,1)S(1)} %bitcast.220, bf16[32,32,1536]{2,1,0:T(8,128)(2,1)S(1)} %collective-permute-done.54.refs_2_, ...), custom_call_target="tpu_custom_call" | custom-call | tf_op jit(solution)/shard_map/pallas_call | solution.py:442
  495.3 13.0 %shard_map.317 = (f32[1024,1024]{1,0:T(8,128)}, f32[4,3,1024]{2,1,0:T(4,128)S(1)}) custom-call(s32[1]{0:T(128)} %bitcast.3._.core_ref, bf16[1024,1536]{1,0:T(8,128)(2,1)S(1)} %bitcast.221, bf16[1024,1536]{1,0:T(8,128)(2,1)} %bitcast.219, bf16[1024,2048]{1,0:T(8,128)(2,1)} %bitcast.38.w_ref.own_ref, bf16[1024,2048]{1,0:T(8,128)(2,1)} %bitcast.40.w_ref.other_ref, ...), custom_call_target="tpu_custom_call" | custom-call | tf_op jit(solution)/shard_map/pallas_call | solution.py:442
  541.6 8.3 %collective-permute-done.64 = f32[19,128]{1,0:T(8,128)S(1)} collective-permute-done((f32[19,128]{1,0:T(8,128)S(1)}, f32[19,128]{1,0:T(8,128)S(1)}, u32[]{:S(2)}, u32[]{:S(2)}) %collective-permute-start.64) | collective-permute-done | bytes 9760 | tf_op jit(solution)/shard_map/ppermute | solution.py:56
  560.9 9.0 %collective-permute-done.67.b_ref = bf16[2,32,2048]{2,1,0:T(8,128)(2,1)S(1)} collective-permute-done((bf16[2,32,2048]{2,1,0:T(8,128)(2,1)S(1)}, bf16[2,32,2048]{2,1,0:T(8,128)(2,1)S(1)}, u32[]{:S(2)}, u32[]{:S(2)}) %collective-permute-start.67) | collective-permute-done | bytes 262176 | tf_op jit(solution)/shard_map/ppermute | solution.py:56
  (621 shorter events, 330.9 us)
Async XLA Ops:
  10.6 21.7 %collective-permute-start.3 = (bf16[4,64,1024]{2,1,0:T(8,128)(2,1)}, bf16[4,64,1024]{2,1,0:T(8,128)(2,1)}, u32[]{:S(2)}, u32[]{:S(2)}) collective-permute-start(bf16[4,64,1024]{2,1,0:T(8,128)(2,1)} %get-tuple-element.661), channel_id=1, source_target_pairs={{0,8},{1,9},{2,10},{3,11},{4,12},{5,13},{6,14},{7,15},{8,0},{9,1},... | collective-permute-start | bytes 1572872 | tf_op jit(solution)/shard_map/ppermute | solution.py:60
  11.3 21.1 %collective-permute-start.4 = (bf16[4,64,1024]{2,1,0:T(8,128)(2,1)}, bf16[4,64,1024]{2,1,0:T(8,128)(2,1)}, u32[]{:S(2)}, u32[]{:S(2)}) collective-permute-start(bf16[4,64,1024]{2,1,0:T(8,128)(2,1)} %get-tuple-element.660), channel_id=1, source_target_pairs={{0,16},{1,17},{2,18},{3,19},{4,20},{5,21},{6,22},{7,23},{8,24},{9,... | collective-permute-start | bytes 1572872 | tf_op jit(solution)/shard_map/ppermute | solution.py:60
  12.5 24.1 %collective-permute-start.5 = (bf16[4,64,1024]{2,1,0:T(8,128)(2,1)}, bf16[4,64,1024]{2,1,0:T(8,128)(2,1)}, u32[]{:S(2)}, u32[]{:S(2)}) collective-permute-start(bf16[4,64,1024]{2,1,0:T(8,128)(2,1)} %get-tuple-element.659), channel_id=1, source_target_pairs={{0,24},{1,25},{2,26},{3,27},{4,28},{5,29},{6,30},{7,31},{8,16},{9,... | collective-permute-start | bytes 1572872 | tf_op jit(solution)/shard_map/ppermute | solution.py:60
  62.7 28.3 %collective-permute-start.15 = (bf16[16,32,2048]{2,1,0:T(8,128)(2,1)}, bf16[16,32,2048]{2,1,0:T(8,128)(2,1)}, u32[]{:S(2)}, u32[]{:S(2)}) collective-permute-start(bf16[16,32,2048]{2,1,0:T(8,128)(2,1)} %shard_map.256.mine_ref), channel_id=1, source_target_pairs={{0,16},{1,17},{2,18},{3,19},{4,20},{5,21},{6,22},{7,23},{8,9},{9,8... | collective-permute-start | bytes 6291464 | tf_op jit(solution)/shard_map/ppermute | solution.py:56
  118.3 27.0 %collective-permute-start.22 = (bf16[16,32,2048]{2,1,0:T(8,128)(2,1)S(1)}, bf16[16,32,2048]{2,1,0:T(8,128)(2,1)S(1)}, u32[]{:S(2)}, u32[]{:S(2)}) collective-permute-start(bf16[16,32,2048]{2,1,0:T(8,128)(2,1)S(1)} %shard_map.267.mine_ref), channel_id=1, source_target_pairs={{0,16},{1,17},{2,18},{3,19},{4,20},{5,21},{6,22},{7,23},{8,9},{9,8... | collective-permute-start | bytes 6291464 | tf_op jit(solution)/shard_map/ppermute | solution.py:56
  119.8 25.5 %collective-permute-start.23 = (bf16[4,32,2048]{2,1,0:T(8,128)(2,1)S(1)}, bf16[4,32,2048]{2,1,0:T(8,128)(2,1)S(1)}, u32[]{:S(2)}, u32[]{:S(2)}) collective-permute-start(bf16[4,32,2048]{2,1,0:T(8,128)(2,1)S(1)} %shard_map.268.mine_ref), channel_id=1, source_target_pairs={{0,4},{1,5},{2,6},{3,7},{4,0},{5,1},{6,2},{7,3},{8,12},{9,13},{10,... | collective-permute-start | bytes 1572872 | tf_op jit(solution)/shard_map/ppermute | solution.py:56
  153.9 25.6 %collective-permute-start.27 = (bf16[32,32,2048]{2,1,0:T(8,128)(2,1)S(1)}, bf16[32,32,2048]{2,1,0:T(8,128)(2,1)S(1)}, u32[]{:S(2)}, u32[]{:S(2)}) collective-permute-start(bf16[32,32,2048]{2,1,0:T(8,128)(2,1)S(1)} %shard_map.271), channel_id=1, source_target_pairs={{0,8},{1,9},{2,10},{3,11},{4,12},{5,13},{6,14},{7,15},{8,0},{9,1},... | collective-permute-start | bytes 12582920 | tf_op jit(solution)/shard_map/ppermute | solution.py:56
  154.3 25.2 %collective-permute-start.28 = (bf16[8,32,2048]{2,1,0:T(8,128)(2,1)S(1)}, bf16[8,32,2048]{2,1,0:T(8,128)(2,1)S(1)}, u32[]{:S(2)}, u32[]{:S(2)}) collective-permute-start(bf16[8,32,2048]{2,1,0:T(8,128)(2,1)S(1)} %shard_map.272.mine_ref), channel_id=1, source_target_pairs={{0,2},{1,3},{2,0},{3,1},{4,6},{5,7},{6,4},{7,5},{8,10},{9,11},{10,... | collective-permute-start | bytes 3145736 | tf_op jit(solution)/shard_map/ppermute | solution.py:56
  155.5 24.0 %collective-permute-start.26 = (bf16[4,64,1024]{2,1,0:T(8,128)(2,1)S(1)}, bf16[4,64,1024]{2,1,0:T(8,128)(2,1)S(1)}, u32[]{:S(2)}, u32[]{:S(2)}) collective-permute-start(bf16[4,64,1024]{2,1,0:T(8,128)(2,1)S(1)} %copy-done.120), channel_id=1, source_target_pairs={{0,24},{1,25},{2,26},{3,27},{4,28},{5,29},{6,30},{7,31},{8,16},{9,... | collective-permute-start | bytes 1572872 | tf_op jit(solution)/shard_map/ppermute | solution.py:60
  183.8 25.2 %collective-permute-start.29 = (bf16[16,32,2048]{2,1,0:T(8,128)(2,1)S(1)}, bf16[16,32,2048]{2,1,0:T(8,128)(2,1)S(1)}, u32[]{:S(2)}, u32[]{:S(2)}) collective-permute-start(bf16[16,32,2048]{2,1,0:T(8,128)(2,1)S(1)} %shard_map.274.mine_ref), channel_id=1, source_target_pairs={{0,16},{1,17},{2,18},{3,19},{4,20},{5,21},{6,22},{7,23},{8,9},{9,8... | collective-permute-start | bytes 6291464 | tf_op jit(solution)/shard_map/ppermute | solution.py:56
  183.9 22.7 %collective-permute-start.30 = (bf16[4,64,1024]{2,1,0:T(8,128)(2,1)S(1)}, bf16[4,64,1024]{2,1,0:T(8,128)(2,1)S(1)}, u32[]{:S(2)}, u32[]{:S(2)}) collective-permute-start(bf16[4,64,1024]{2,1,0:T(8,128)(2,1)S(1)} %shard_map.275.mine_ref), channel_id=1, source_target_pairs={{0,2},{1,3},{2,0},{3,1},{4,6},{5,7},{6,4},{7,5},{8,10},{9,11},{10,... | collective-permute-start | bytes 1572872 | tf_op jit(solution)/shard_map/ppermute | solution.py:56
  212.8 24.3 %collective-permute-start.32 = (bf16[32,32,2048]{2,1,0:T(8,128)(2,1)}, bf16[32,32,2048]{2,1,0:T(8,128)(2,1)}, u32[]{:S(2)}, u32[]{:S(2)}) collective-permute-start(bf16[32,32,2048]{2,1,0:T(8,128)(2,1)} %shard_map.280), channel_id=1, source_target_pairs={{0,8},{1,9},{2,10},{3,11},{4,12},{5,13},{6,14},{7,15},{8,0},{9,1},... | collective-permute-start | bytes 12582920 | tf_op jit(solution)/shard_map/ppermute | solution.py:56
  234.6 25.5 %collective-permute-start.33 = (bf16[16,64,1024]{2,1,0:T(8,128)(2,1)}, bf16[16,64,1024]{2,1,0:T(8,128)(2,1)}, u32[]{:S(2)}, u32[]{:S(2)}) collective-permute-start(bf16[16,64,1024]{2,1,0:T(8,128)(2,1)} %shard_map.283.mine_ref), channel_id=1, source_target_pairs={{0,16},{1,17},{2,18},{3,19},{4,20},{5,21},{6,22},{7,23},{8,9},{9,8... | collective-permute-start | bytes 6291464 | tf_op jit(solution)/shard_map/ppermute | solution.py:56
  263.8 21.3 %collective-permute-start.35 = (bf16[32,64,1024]{2,1,0:T(8,128)(2,1)S(1)}, bf16[32,64,1024]{2,1,0:T(8,128)(2,1)S(1)}, u32[]{:S(2)}, u32[]{:S(2)}) collective-permute-start(bf16[32,64,1024]{2,1,0:T(8,128)(2,1)S(1)} %shard_map.285), channel_id=1, source_target_pairs={{0,8},{1,9},{2,10},{3,11},{4,12},{5,13},{6,14},{7,15},{8,0},{9,1},... | collective-permute-start | bytes 12582920 | tf_op jit(solution)/shard_map/ppermute | solution.py:56
  285.1 27.2 %collective-permute-start.36 = (bf16[32,32,2048]{2,1,0:T(8,128)(2,1)}, bf16[32,32,2048]{2,1,0:T(8,128)(2,1)}, u32[]{:S(2)}, u32[]{:S(2)}) collective-permute-start(bf16[32,32,2048]{2,1,0:T(8,128)(2,1)} %shard_map.289), channel_id=1, source_target_pairs={{0,8},{1,9},{2,10},{3,11},{4,12},{5,13},{6,14},{7,15},{8,0},{9,1},... | collective-permute-start | bytes 12582920 | tf_op jit(solution)/shard_map/ppermute | solution.py:56
  294.6 27.2 %collective-permute-start.37 = (bf16[16,64,1024]{2,1,0:T(8,128)(2,1)}, bf16[16,64,1024]{2,1,0:T(8,128)(2,1)}, u32[]{:S(2)}, u32[]{:S(2)}) collective-permute-start(bf16[16,64,1024]{2,1,0:T(8,128)(2,1)} %get-tuple-element.451), channel_id=1, source_target_pairs={{0,16},{1,17},{2,18},{3,19},{4,20},{5,21},{6,22},{7,23},{8,9},{9,8... | collective-permute-start | bytes 6291464 | tf_op jit(solution)/shard_map/ppermute | solution.py:56
  325.1 36.8 %collective-permute-start.39 = (bf16[16,32,2048]{2,1,0:T(8,128)(2,1)}, bf16[16,32,2048]{2,1,0:T(8,128)(2,1)}, u32[]{:S(2)}, u32[]{:S(2)}) collective-permute-start(bf16[16,32,2048]{2,1,0:T(8,128)(2,1)} %get-tuple-element.464), channel_id=1, source_target_pairs={{0,16},{1,17},{2,18},{3,19},{4,20},{5,21},{6,22},{7,23},{8,9},{9,8... | collective-permute-start | bytes 6291464 | tf_op jit(solution)/shard_map/ppermute | solution.py:56
  325.2 32.3 %collective-permute-start.38 = (bf16[8,64,1024]{2,1,0:T(8,128)(2,1)}, bf16[8,64,1024]{2,1,0:T(8,128)(2,1)}, u32[]{:S(2)}, u32[]{:S(2)}) collective-permute-start(bf16[8,64,1024]{2,1,0:T(8,128)(2,1)} %get-tuple-element.463), channel_id=1, source_target_pairs={{0,1},{1,0},{2,3},{3,2},{4,5},{5,4},{6,7},{7,6},{8,24},{9,25},{10,... | collective-permute-start | bytes 3145736 | tf_op jit(solution)/shard_map/ppermute | solution.py:56
  405.6 24.5 %collective-permute-start.47 = (bf16[4,64,1024]{2,1,0:T(8,128)(2,1)}, bf16[4,64,1024]{2,1,0:T(8,128)(2,1)}, u32[]{:S(2)}, u32[]{:S(2)}) collective-permute-start(bf16[4,64,1024]{2,1,0:T(8,128)(2,1)} %bitcast.72), channel_id=1, source_target_pairs={{0,24},{1,25},{2,26},{3,27},{4,28},{5,29},{6,30},{7,31},{8,16},{9,... | collective-permute-start | bytes 1572872 | tf_op jit(solution)/shard_map/ppermute | solution.py:60
  408.5 21.6 %collective-permute-start.49 = (bf16[4,32,2048]{2,1,0:T(8,128)(2,1)}, bf16[4,32,2048]{2,1,0:T(8,128)(2,1)}, u32[]{:S(2)}, u32[]{:S(2)}) collective-permute-start(bf16[4,32,2048]{2,1,0:T(8,128)(2,1)} %get-tuple-element.506), channel_id=1, source_target_pairs={{0,2},{1,3},{2,0},{3,1},{4,6},{5,7},{6,4},{7,5},{8,10},{9,11},{10,... | collective-permute-start | bytes 1572872 | tf_op jit(solution)/shard_map/ppermute | solution.py:56
  408.5 21.6 %collective-permute-start.48 = (f32[1,64,1024]{2,1,0:T(8,128)}, f32[1,64,1024]{2,1,0:T(8,128)}, u32[]{:S(2)}, u32[]{:S(2)}) collective-permute-start(f32[1,64,1024]{2,1,0:T(8,128)} %get-tuple-element.505), channel_id=1, source_target_pairs={{0,8},{1,9},{2,10},{3,11},{4,12},{5,13},{6,14},{7,15},{8,0},{9,1},... | collective-permute-start | bytes 786440 | tf_op jit(solution)/shard_map/ppermute | solution.py:56
  433.0 25.2 %collective-permute-start.51 = (bf16[16,32,2048]{2,1,0:T(8,128)(2,1)S(1)}, bf16[16,32,2048]{2,1,0:T(8,128)(2,1)S(1)}, u32[]{:S(2)}, u32[]{:S(2)}) collective-permute-start(bf16[16,32,2048]{2,1,0:T(8,128)(2,1)S(1)} %get-tuple-element.517), channel_id=1, source_target_pairs={{0,16},{1,17},{2,18},{3,19},{4,20},{5,21},{6,22},{7,23},{8,9},{9,8... | collective-permute-start | bytes 6291464 | tf_op jit(solution)/shard_map/ppermute | solution.py:56
  433.3 19.9 %collective-permute-start.50 = (bf16[2,32,2048]{2,1,0:T(8,128)(2,1)S(1)}, bf16[2,32,2048]{2,1,0:T(8,128)(2,1)S(1)}, u32[]{:S(2)}, u32[]{:S(2)}) collective-permute-start(bf16[2,32,2048]{2,1,0:T(8,128)(2,1)S(1)} %get-tuple-element.516), channel_id=1, source_target_pairs={{0,4},{1,5},{2,6},{3,7},{4,0},{5,1},{6,2},{7,3},{8,12},{9,13},{10,... | collective-permute-start | bytes 786440 | tf_op jit(solution)/shard_map/ppermute | solution.py:56
  486.8 25.5 %collective-permute-start.57 = (bf16[16,32,2048]{2,1,0:T(8,128)(2,1)}, bf16[16,32,2048]{2,1,0:T(8,128)(2,1)}, u32[]{:S(2)}, u32[]{:S(2)}) collective-permute-start(bf16[16,32,2048]{2,1,0:T(8,128)(2,1)} %get-tuple-element.544), channel_id=1, source_target_pairs={{0,16},{1,17},{2,18},{3,19},{4,20},{5,21},{6,22},{7,23},{8,9},{9,8... | collective-permute-start | bytes 6291464 | tf_op jit(solution)/shard_map/ppermute | solution.py:56
  (186 other events, 1689.5 us)

commit v8 on v7

--- a/solution.py
+++ b/solution.py
@@ -712,7 +712,7 @@
         out_specs=[pl.BlockSpec((rows, block), lambda i: (0, i))] * 2,
         out_shape=[out, out],
         compiler_params=params(
-            [(x.shape, bf16, 2), ((width, block), bf16, 2), ((rows, block), bf16, 4)]
+            [(x.shape, bf16, 2), ((width, block), bf16, 2), ((rows, block), bf16, 4)], 30
         ),
         cost_estimate=NO_COST,
     )(x, weight, bias)

time: 583 us -> 582 us (level)
    unnamed x296 -> x294, local copies, waits for them, and re-layouts: 32.4 us -> 30.5 us
  transfers between devices with their start and end apart: 72 -> 72, of which waited for: 31 -> 32; matrix products, arithmetic and copies ran while one was open for 6% -> 6% of each run, Pallas kernels for 42% -> 42%
where the time goes in v8:
time: 582 us; the launch traced here: 575 us
  Pallas kernels  300 us (52%)
  waiting for transfers between devices  133 us (23%)
  starting transfers between devices  62.9 us (11%)
  local copies, waits for them, and re-layouts  57.2 us (10%)
  other arithmetic  18.6 us (3%)
    pallas_call x24, Pallas kernels, dense(): pl.pallas_call(body, grid_spec=pltpu.PrefetchScalarGridSpec(num_scalar_pr...  157 us
    ppermute x60, waiting for transfers between devices, flip(): return lax.ppermute(value, AXES, moves)  96.4 us
    pallas_call x6, Pallas kernels, run_attention(): pl.pallas_call(body, grid=(grid,), in_specs=[pl.BlockSpec(memory_space=pl...  52.3 us
    ppermute x60, starting transfers between devices, flip(): return lax.ppermute(value, AXES, moves)  52.1 us
    ppermute x12, waiting for transfers between devices, tm_flip(): return lax.ppermute(value, AXES, moves)  36.4 us
    pallas_call x25, Pallas kernels, merge(): pl.pallas_call(merge_body, grid=(n // block,), in_specs=[pl.BlockSpec(mem...  33.7 us
    unnamed x294, local copies, waits for them, and re-layouts  30.5 us
    pallas_call x2, Pallas kernels, up_project(): pl.pallas_call(up_body, grid=(cols // block,), in_specs=[pl.BlockSpec((ro...  29.1 us
  transfers between devices with their start and end apart: 72, of which 32 were waited for; matrix products, arithmetic and copies ran while one was open for 6% of the time, Pallas kernels for 42%

profile of v8, /device:TPU:1, one launch (start us, length us, event | category | flops | bytes accessed | tf_op | source)
XLA Modules:
  0.0 575.4 jit_solution(13630882817206311300)
XLA Ops:
  16.6 10.5 %collective-permute-done.2.other_ref = bf16[2,32,2048]{2,1,0:T(8,128)(2,1)S(1)} collective-permute-done((bf16[2,32,2048]{2,1,0:T(8,128)(2,1)S(1)}, bf16[2,32,2048]{2,1,0:T(8,128)(2,1)S(1)}, u32[]{:S(2)}, u32[]{:S(2)}) %collective-permute-start.2) | collective-permute-done | bytes 262176 | tf_op jit(solution)/shard_map/ppermute | solution.py:56
  49.5 6.9 %collective-permute-done.9.other_ref = bf16[4,48,128]{2,1,0:T(8,128)(2,1)S(1)} collective-permute-done((bf16[4,48,128]{2,1,0:T(8,128)(2,1)S(1)}, bf16[4,48,128]{2,1,0:T(8,128)(2,1)S(1)}, u32[]{:S(2)}, u32[]{:S(2)}) %collective-permute-start.9) | collective-permute-done | bytes 49184 | tf_op jit(solution)/shard_map/ppermute | solution.py:56
  119.8 7.4 %shard_map.269 = bf16[4,256,1024]{2,1,0:T(8,128)(2,1)S(1)} custom-call(s32[2]{0:T(128)S(1)} %copy-done.106, bf16[4,256,1536]{2,1,0:T(8,128)(2,1)S(1)} %bitcast.210, bf16[4,256,1536]{2,1,0:T(8,128)(2,1)S(1)} %bitcast.212), custom_call_target="tpu_custom_call" | custom-call | tf_op jit(solution)/shard_map/pallas_call | solution.py:374
  132.5 12.7 %collective-permute-done.23.other_ref = bf16[4,32,2048]{2,1,0:T(8,128)(2,1)S(1)} collective-permute-done((bf16[4,32,2048]{2,1,0:T(8,128)(2,1)S(1)}, bf16[4,32,2048]{2,1,0:T(8,128)(2,1)S(1)}, u32[]{:S(2)}, u32[]{:S(2)}) %collective-permute-start.23) | collective-permute-done | bytes 524320 | tf_op jit(solution)/shard_map/ppermute | solution.py:56
  157.8 10.0 %collective-permute-done.25 = bf16[4,64,1024]{2,1,0:T(8,128)(2,1)S(1)} collective-permute-done((bf16[4,64,1024]{2,1,0:T(8,128)(2,1)S(1)}, bf16[4,64,1024]{2,1,0:T(8,128)(2,1)S(1)}, u32[]{:S(2)}, u32[]{:S(2)}) %collective-permute-start.25) | collective-permute-done | bytes 524320 | tf_op jit(solution)/shard_map/ppermute | solution.py:60
  167.8 11.7 %collective-permute-done.26 = bf16[4,64,1024]{2,1,0:T(8,128)(2,1)S(1)} collective-permute-done((bf16[4,64,1024]{2,1,0:T(8,128)(2,1)S(1)}, bf16[4,64,1024]{2,1,0:T(8,128)(2,1)S(1)}, u32[]{:S(2)}, u32[]{:S(2)}) %collective-permute-start.26) | collective-permute-done | bytes 524320 | tf_op jit(solution)/shard_map/ppermute | solution.py:60
  193.7 8.0 %shard_map.278 = bf16[16,64,1024]{2,1,0:T(8,128)(2,1)S(1)} custom-call(s32[2]{0:T(128)S(1)} %pad_add_fusion.8.scalar_ref, bf16[16,64,1536]{2,1,0:T(8,128)(2,1)S(1)} %bitcast.214, bf16[16,64,1536]{2,1,0:T(8,128)(2,1)S(1)} %bitcast.216), custom_call_target="tpu_custom_call" | custom-call | tf_op jit(solution)/shard_map/pallas_call | solution.py:374
  214.7 14.6 %shard_map.282 = (bf16[1024,2048]{1,0:T(8,128)(2,1)S(1)}, bf16[1024,2048]{1,0:T(8,128)(2,1)S(1)}) custom-call(bf16[1024,1024]{1,0:T(8,128)(2,1)S(1)} %get-tuple-element.423.x_ref.refs_0_, bf16[1024,2048]{1,0:T(8,128)(2,1)} %bitcast.59.w_ref.own_ref, f32[1,2048]{1,0:T(1,128)S(1)} %select_n.793.bias_ref), custom_call_target="tpu_custom_call" | custom-call | tf_op jit(solution)/shard_map/pallas_call | solution.py:704
  238.7 14.6 %shard_map.284 = (bf16[1024,2048]{1,0:T(8,128)(2,1)S(1)}, bf16[1024,2048]{1,0:T(8,128)(2,1)S(1)}) custom-call(bf16[1024,1024]{1,0:T(8,128)(2,1)S(1)} %copy-done.14, bf16[1024,2048]{1,0:T(8,128)(2,1)} %bitcast.60.w_ref.other_ref, f32[1,2048]{1,0:T(1,128)S(1)} %select_n.795.bias_ref), custom_call_target="tpu_custom_call" | custom-call | tf_op jit(solution)/shard_map/pallas_call | solution.py:704
  283.8 7.4 %shard_map.290 = (bf16[16,64,1024]{2,1,0:T(8,128)(2,1)}, bf16[16,64,1024]{2,1,0:T(8,128)(2,1)S(1)}) custom-call(s32[3]{0:T(128)S(1)} %pad_add_fusion.13.info_ref, bf16[1024,2048]{1,0:T(8,128)(2,1)S(1)} %copy-done.40, bf16[1024,1024]{1,0:T(8,128)(2,1)S(1)} %bitcast_select_fusion.y_ref.x_ref.refs_1_.rest_ref, ...), custom_call_target="tpu_custom_call" | custom-call | tf_op jit(solution)/shard_map/pallas_call | solution.py:442
  296.5 13.6 %shard_map.291 = bf16[1024,1024]{1,0:T(8,128)(2,1)S(1)} custom-call(s32[1]{0:T(128)} %bitcast.3._.core_ref, bf16[1024,2048]{1,0:T(8,128)(2,1)S(1)} %copy-done.41, bf16[1024,2048]{1,0:T(8,128)(2,1)} %copy-done.43, bf16[2048,1024]{1,0:T(8,128)(2,1)} %bitcast.199, bf16[2048,1024]{1,0:T(8,128)(2,1)} %bitcast.233, f32[1024,1024]{1,0:T(8,128)} %copy-done.45, ...), custom_call_target="tpu_custom_call" | custom-call | tf_op jit(solution)/shard_map/pallas_call | solution.py:442
  310.2 9.4 %shard_map.292 = (bf16[16,32,2048]{2,1,0:T(8,128)(2,1)}, bf16[16,32,2048]{2,1,0:T(8,128)(2,1)S(1)}) custom-call(s32[3]{0:T(128)S(1)} %pad_add_fusion.13.info_ref, bf16[1024,1024]{1,0:T(8,128)(2,1)S(1)} %copy-done.15, bf16[1024,2048]{1,0:T(8,128)(2,1)S(1)} %copy-done.38, bf16[32,32,2048]{2,1,0:T(8,128)(2,1)} %collective-permute-done.36.refs_2_), custom_call_target="tpu_custom_call" | custom-call | tf_op jit(solution)/shard_map/pallas_call | solution.py:442
  326.4 16.6 %shard_map.294 = (bf16[1024,1024]{1,0:T(8,128)(2,1)S(1)}, f32[4,3,1024]{2,1,0:T(4,128)S(1)}) custom-call(s32[1]{0:T(128)} %bitcast.3._.core_ref, bf16[1024,2048]{1,0:T(8,128)(2,1)} %copy-done.37, bf16[1024,2048]{1,0:T(8,128)(2,1)} %copy-done.42, bf16[1024,2048]{1,0:T(8,128)(2,1)} %bitcast.59.w_ref.own_ref, bf16[1024,2048]{1,0:T(8,128)(2,1)} %bitcast.60.w_ref.other_ref, ...), custom_call_target="tpu_custom_call" | custom-call | tf_op jit(solution)/shard_map/pallas_call | solution.py:442
  346.0 9.4 %shard_map.296 = bf16[16,64,1536]{2,1,0:T(8,128)(2,1)S(1)} custom-call(s32[2]{0:T(128)S(1)} %copy-done.109, bf16[16,64,1536]{2,1,0:T(8,128)(2,1)S(1)} %bitcast.217, bf16[16,64,1024]{2,1,0:T(8,128)(2,1)S(1)} %bitcast.227), custom_call_target="tpu_custom_call" | custom-call | tf_op jit(solution)/shard_map/pallas_call | solution.py:374
  371.1 9.4 %shard_map.299 = bf16[16,64,1536]{2,1,0:T(8,128)(2,1)S(1)} custom-call(s32[2]{0:T(128)S(1)} %copy-done.109, bf16[16,64,1536]{2,1,0:T(8,128)(2,1)S(1)} %bitcast.215, bf16[16,64,1024]{2,1,0:T(8,128)(2,1)S(1)} %bitcast.228), custom_call_target="tpu_custom_call" | custom-call | tf_op jit(solution)/shard_map/pallas_call | solution.py:374
  384.2 9.9 %shard_map.303 = (bf16[1024,1024]{1,0:T(8,128)(2,1)S(1)}, f32[4,3,1024]{2,1,0:T(4,128)S(1)}) custom-call(s32[1]{0:T(128)} %bitcast.3._.core_ref, bf16[1024,1536]{1,0:T(8,128)(2,1)S(1)} %bitcast.206, bf16[1024,1536]{1,0:T(8,128)(2,1)S(1)} %bitcast.209, bf16[1024,2048]{1,0:T(8,128)(2,1)S(1)} %bitcast.181, bf16[1024,2048]{1,0:T(8,128)(2,1)S(1)} %bitcast.185, ...), custom_call_target="tpu_custom_call" | custom-call | tf_op jit(solution)/shard_map/pallas_call | solution.py:442
  413.7 7.1 %shard_map.304 = (bf16[16,32,2048]{2,1,0:T(8,128)(2,1)S(1)}, bf16[16,32,2048]{2,1,0:T(8,128)(2,1)S(1)}) custom-call(s32[3]{0:T(128)S(1)} %pad_add_fusion.13.info_ref, bf16[1024,1024]{1,0:T(8,128)(2,1)S(1)} %bitcast.193, bf16[1024,1536]{1,0:T(8,128)(2,1)S(1)} %bitcast.207, bf16[32,32,1536]{2,1,0:T(8,128)(2,1)S(1)} %copy-done.51, ...), custom_call_target="tpu_custom_call" | custom-call | tf_op jit(solution)/shard_map/pallas_call | solution.py:442
  420.8 7.3 %collective-permute-done.47 = bf16[4,64,1024]{2,1,0:T(8,128)(2,1)} collective-permute-done((bf16[4,64,1024]{2,1,0:T(8,128)(2,1)}, bf16[4,64,1024]{2,1,0:T(8,128)(2,1)}, u32[]{:S(2)}, u32[]{:S(2)}) %collective-permute-start.47) | collective-permute-done | bytes 524320 | tf_op jit(solution)/shard_map/ppermute | solution.py:60
  437.7 9.0 %shard_map.309 = bf16[4,256,1536]{2,1,0:T(8,128)(2,1)S(1)} custom-call(s32[2]{0:T(128)S(1)} %copy-done.107, bf16[4,256,1536]{2,1,0:T(8,128)(2,1)S(1)} %bitcast.213, bf16[4,256,1024]{2,1,0:T(8,128)(2,1)S(1)} %bitcast.225), custom_call_target="tpu_custom_call" | custom-call | tf_op jit(solution)/shard_map/pallas_call | solution.py:374
  461.2 9.1 %shard_map.314 = bf16[4,256,1536]{2,1,0:T(8,128)(2,1)S(1)} custom-call(s32[2]{0:T(128)S(1)} %copy-done.107, bf16[4,256,1536]{2,1,0:T(8,128)(2,1)S(1)} %bitcast.211, bf16[4,256,1024]{2,1,0:T(8,128)(2,1)S(1)} %bitcast.226), custom_call_target="tpu_custom_call" | custom-call | tf_op jit(solution)/shard_map/pallas_call | solution.py:374
  475.6 7.8 %shard_map.316 = (bf16[16,32,2048]{2,1,0:T(8,128)(2,1)}, bf16[16,32,2048]{2,1,0:T(8,128)(2,1)S(1)}) custom-call(s32[3]{0:T(128)S(1)} %pad_add_fusion.13.info_ref, bf16[1024,1024]{1,0:T(8,128)(2,1)S(1)} %bitcast.189, bf16[1024,1536]{1,0:T(8,128)(2,1)S(1)} %bitcast.220, bf16[32,32,1536]{2,1,0:T(8,128)(2,1)S(1)} %collective-permute-done.54.refs_2_, ...), custom_call_target="tpu_custom_call" | custom-call | tf_op jit(solution)/shard_map/pallas_call | solution.py:442
  493.2 13.0 %shard_map.317 = (f32[1024,1024]{1,0:T(8,128)}, f32[4,3,1024]{2,1,0:T(4,128)S(1)}) custom-call(s32[1]{0:T(128)} %bitcast.3._.core_ref, bf16[1024,1536]{1,0:T(8,128)(2,1)S(1)} %bitcast.221, bf16[1024,1536]{1,0:T(8,128)(2,1)} %bitcast.219, bf16[1024,2048]{1,0:T(8,128)(2,1)} %bitcast.38.w_ref.own_ref, bf16[1024,2048]{1,0:T(8,128)(2,1)} %bitcast.40.w_ref.other_ref, ...), custom_call_target="tpu_custom_call" | custom-call | tf_op jit(solution)/shard_map/pallas_call | solution.py:442
  539.6 8.3 %collective-permute-done.64 = f32[19,128]{1,0:T(8,128)S(1)} collective-permute-done((f32[19,128]{1,0:T(8,128)S(1)}, f32[19,128]{1,0:T(8,128)S(1)}, u32[]{:S(2)}, u32[]{:S(2)}) %collective-permute-start.64) | collective-permute-done | bytes 9760 | tf_op jit(solution)/shard_map/ppermute | solution.py:56
  558.9 9.0 %collective-permute-done.67.b_ref = bf16[2,32,2048]{2,1,0:T(8,128)(2,1)S(1)} collective-permute-done((bf16[2,32,2048]{2,1,0:T(8,128)(2,1)S(1)}, bf16[2,32,2048]{2,1,0:T(8,128)(2,1)S(1)}, u32[]{:S(2)}, u32[]{:S(2)}) %collective-permute-start.67) | collective-permute-done | bytes 262176 | tf_op jit(solution)/shard_map/ppermute | solution.py:56
  (619 shorter events, 328.9 us)
Async XLA Ops:
  10.6 21.7 %collective-permute-start.3 = (bf16[4,64,1024]{2,1,0:T(8,128)(2,1)}, bf16[4,64,1024]{2,1,0:T(8,128)(2,1)}, u32[]{:S(2)}, u32[]{:S(2)}) collective-permute-start(bf16[4,64,1024]{2,1,0:T(8,128)(2,1)} %get-tuple-element.661), channel_id=1, source_target_pairs={{0,8},{1,9},{2,10},{3,11},{4,12},{5,13},{6,14},{7,15},{8,0},{9,1},... | collective-permute-start | bytes 1572872 | tf_op jit(solution)/shard_map/ppermute | solution.py:60
  11.3 21.1 %collective-permute-start.4 = (bf16[4,64,1024]{2,1,0:T(8,128)(2,1)}, bf16[4,64,1024]{2,1,0:T(8,128)(2,1)}, u32[]{:S(2)}, u32[]{:S(2)}) collective-permute-start(bf16[4,64,1024]{2,1,0:T(8,128)(2,1)} %get-tuple-element.660), channel_id=1, source_target_pairs={{0,16},{1,17},{2,18},{3,19},{4,20},{5,21},{6,22},{7,23},{8,24},{9,... | collective-permute-start | bytes 1572872 | tf_op jit(solution)/shard_map/ppermute | solution.py:60
  12.5 24.1 %collective-permute-start.5 = (bf16[4,64,1024]{2,1,0:T(8,128)(2,1)}, bf16[4,64,1024]{2,1,0:T(8,128)(2,1)}, u32[]{:S(2)}, u32[]{:S(2)}) collective-permute-start(bf16[4,64,1024]{2,1,0:T(8,128)(2,1)} %get-tuple-element.659), channel_id=1, source_target_pairs={{0,24},{1,25},{2,26},{3,27},{4,28},{5,29},{6,30},{7,31},{8,16},{9,... | collective-permute-start | bytes 1572872 | tf_op jit(solution)/shard_map/ppermute | solution.py:60
  62.7 28.3 %collective-permute-start.15 = (bf16[16,32,2048]{2,1,0:T(8,128)(2,1)}, bf16[16,32,2048]{2,1,0:T(8,128)(2,1)}, u32[]{:S(2)}, u32[]{:S(2)}) collective-permute-start(bf16[16,32,2048]{2,1,0:T(8,128)(2,1)} %shard_map.256.mine_ref), channel_id=1, source_target_pairs={{0,16},{1,17},{2,18},{3,19},{4,20},{5,21},{6,22},{7,23},{8,9},{9,8... | collective-permute-start | bytes 6291464 | tf_op jit(solution)/shard_map/ppermute | solution.py:56
  118.3 27.0 %collective-permute-start.22 = (bf16[16,32,2048]{2,1,0:T(8,128)(2,1)S(1)}, bf16[16,32,2048]{2,1,0:T(8,128)(2,1)S(1)}, u32[]{:S(2)}, u32[]{:S(2)}) collective-permute-start(bf16[16,32,2048]{2,1,0:T(8,128)(2,1)S(1)} %shard_map.267.mine_ref), channel_id=1, source_target_pairs={{0,16},{1,17},{2,18},{3,19},{4,20},{5,21},{6,22},{7,23},{8,9},{9,8... | collective-permute-start | bytes 6291464 | tf_op jit(solution)/shard_map/ppermute | solution.py:56
  119.8 25.5 %collective-permute-start.23 = (bf16[4,32,2048]{2,1,0:T(8,128)(2,1)S(1)}, bf16[4,32,2048]{2,1,0:T(8,128)(2,1)S(1)}, u32[]{:S(2)}, u32[]{:S(2)}) collective-permute-start(bf16[4,32,2048]{2,1,0:T(8,128)(2,1)S(1)} %shard_map.268.mine_ref), channel_id=1, source_target_pairs={{0,4},{1,5},{2,6},{3,7},{4,0},{5,1},{6,2},{7,3},{8,12},{9,13},{10,... | collective-permute-start | bytes 1572872 | tf_op jit(solution)/shard_map/ppermute | solution.py:56
  153.9 25.6 %collective-permute-start.27 = (bf16[32,32,2048]{2,1,0:T(8,128)(2,1)S(1)}, bf16[32,32,2048]{2,1,0:T(8,128)(2,1)S(1)}, u32[]{:S(2)}, u32[]{:S(2)}) collective-permute-start(bf16[32,32,2048]{2,1,0:T(8,128)(2,1)S(1)} %shard_map.271), channel_id=1, source_target_pairs={{0,8},{1,9},{2,10},{3,11},{4,12},{5,13},{6,14},{7,15},{8,0},{9,1},... | collective-permute-start | bytes 12582920 | tf_op jit(solution)/shard_map/ppermute | solution.py:56
  154.3 25.2 %collective-permute-start.28 = (bf16[8,32,2048]{2,1,0:T(8,128)(2,1)S(1)}, bf16[8,32,2048]{2,1,0:T(8,128)(2,1)S(1)}, u32[]{:S(2)}, u32[]{:S(2)}) collective-permute-start(bf16[8,32,2048]{2,1,0:T(8,128)(2,1)S(1)} %shard_map.272.mine_ref), channel_id=1, source_target_pairs={{0,2},{1,3},{2,0},{3,1},{4,6},{5,7},{6,4},{7,5},{8,10},{9,11},{10,... | collective-permute-start | bytes 3145736 | tf_op jit(solution)/shard_map/ppermute | solution.py:56
  155.5 24.0 %collective-permute-start.26 = (bf16[4,64,1024]{2,1,0:T(8,128)(2,1)S(1)}, bf16[4,64,1024]{2,1,0:T(8,128)(2,1)S(1)}, u32[]{:S(2)}, u32[]{:S(2)}) collective-permute-start(bf16[4,64,1024]{2,1,0:T(8,128)(2,1)S(1)} %copy-done.119), channel_id=1, source_target_pairs={{0,24},{1,25},{2,26},{3,27},{4,28},{5,29},{6,30},{7,31},{8,16},{9,... | collective-permute-start | bytes 1572872 | tf_op jit(solution)/shard_map/ppermute | solution.py:60
  183.8 25.2 %collective-permute-start.29 = (bf16[16,32,2048]{2,1,0:T(8,128)(2,1)S(1)}, bf16[16,32,2048]{2,1,0:T(8,128)(2,1)S(1)}, u32[]{:S(2)}, u32[]{:S(2)}) collective-permute-start(bf16[16,32,2048]{2,1,0:T(8,128)(2,1)S(1)} %shard_map.274.mine_ref), channel_id=1, source_target_pairs={{0,16},{1,17},{2,18},{3,19},{4,20},{5,21},{6,22},{7,23},{8,9},{9,8... | collective-permute-start | bytes 6291464 | tf_op jit(solution)/shard_map/ppermute | solution.py:56
  183.9 22.7 %collective-permute-start.30 = (bf16[4,64,1024]{2,1,0:T(8,128)(2,1)S(1)}, bf16[4,64,1024]{2,1,0:T(8,128)(2,1)S(1)}, u32[]{:S(2)}, u32[]{:S(2)}) collective-permute-start(bf16[4,64,1024]{2,1,0:T(8,128)(2,1)S(1)} %shard_map.275.mine_ref), channel_id=1, source_target_pairs={{0,2},{1,3},{2,0},{3,1},{4,6},{5,7},{6,4},{7,5},{8,10},{9,11},{10,... | collective-permute-start | bytes 1572872 | tf_op jit(solution)/shard_map/ppermute | solution.py:56
  212.8 24.3 %collective-permute-start.32 = (bf16[32,32,2048]{2,1,0:T(8,128)(2,1)}, bf16[32,32,2048]{2,1,0:T(8,128)(2,1)}, u32[]{:S(2)}, u32[]{:S(2)}) collective-permute-start(bf16[32,32,2048]{2,1,0:T(8,128)(2,1)} %shard_map.280), channel_id=1, source_target_pairs={{0,8},{1,9},{2,10},{3,11},{4,12},{5,13},{6,14},{7,15},{8,0},{9,1},... | collective-permute-start | bytes 12582920 | tf_op jit(solution)/shard_map/ppermute | solution.py:56
  234.6 25.5 %collective-permute-start.33 = (bf16[16,64,1024]{2,1,0:T(8,128)(2,1)}, bf16[16,64,1024]{2,1,0:T(8,128)(2,1)}, u32[]{:S(2)}, u32[]{:S(2)}) collective-permute-start(bf16[16,64,1024]{2,1,0:T(8,128)(2,1)} %shard_map.283.mine_ref), channel_id=1, source_target_pairs={{0,16},{1,17},{2,18},{3,19},{4,20},{5,21},{6,22},{7,23},{8,9},{9,8... | collective-permute-start | bytes 6291464 | tf_op jit(solution)/shard_map/ppermute | solution.py:56
  283.2 27.0 %collective-permute-start.36 = (bf16[32,32,2048]{2,1,0:T(8,128)(2,1)}, bf16[32,32,2048]{2,1,0:T(8,128)(2,1)}, u32[]{:S(2)}, u32[]{:S(2)}) collective-permute-start(bf16[32,32,2048]{2,1,0:T(8,128)(2,1)} %shard_map.289), channel_id=1, source_target_pairs={{0,8},{1,9},{2,10},{3,11},{4,12},{5,13},{6,14},{7,15},{8,0},{9,1},... | collective-permute-start | bytes 12582920 | tf_op jit(solution)/shard_map/ppermute | solution.py:56
  292.5 27.2 %collective-permute-start.37 = (bf16[16,64,1024]{2,1,0:T(8,128)(2,1)}, bf16[16,64,1024]{2,1,0:T(8,128)(2,1)}, u32[]{:S(2)}, u32[]{:S(2)}) collective-permute-start(bf16[16,64,1024]{2,1,0:T(8,128)(2,1)} %get-tuple-element.451), channel_id=1, source_target_pairs={{0,16},{1,17},{2,18},{3,19},{4,20},{5,21},{6,22},{7,23},{8,9},{9,8... | collective-permute-start | bytes 6291464 | tf_op jit(solution)/shard_map/ppermute | solution.py:56
  323.0 36.8 %collective-permute-start.39 = (bf16[16,32,2048]{2,1,0:T(8,128)(2,1)}, bf16[16,32,2048]{2,1,0:T(8,128)(2,1)}, u32[]{:S(2)}, u32[]{:S(2)}) collective-permute-start(bf16[16,32,2048]{2,1,0:T(8,128)(2,1)} %get-tuple-element.464), channel_id=1, source_target_pairs={{0,16},{1,17},{2,18},{3,19},{4,20},{5,21},{6,22},{7,23},{8,9},{9,8... | collective-permute-start | bytes 6291464 | tf_op jit(solution)/shard_map/ppermute | solution.py:56
  323.1 32.3 %collective-permute-start.38 = (bf16[8,64,1024]{2,1,0:T(8,128)(2,1)}, bf16[8,64,1024]{2,1,0:T(8,128)(2,1)}, u32[]{:S(2)}, u32[]{:S(2)}) collective-permute-start(bf16[8,64,1024]{2,1,0:T(8,128)(2,1)} %get-tuple-element.463), channel_id=1, source_target_pairs={{0,1},{1,0},{2,3},{3,2},{4,5},{5,4},{6,7},{7,6},{8,24},{9,25},{10,... | collective-permute-start | bytes 3145736 | tf_op jit(solution)/shard_map/ppermute | solution.py:56
  403.5 24.6 %collective-permute-start.47 = (bf16[4,64,1024]{2,1,0:T(8,128)(2,1)}, bf16[4,64,1024]{2,1,0:T(8,128)(2,1)}, u32[]{:S(2)}, u32[]{:S(2)}) collective-permute-start(bf16[4,64,1024]{2,1,0:T(8,128)(2,1)} %bitcast.72), channel_id=1, source_target_pairs={{0,24},{1,25},{2,26},{3,27},{4,28},{5,29},{6,30},{7,31},{8,16},{9,... | collective-permute-start | bytes 1572872 | tf_op jit(solution)/shard_map/ppermute | solution.py:60
  406.5 21.6 %collective-permute-start.49 = (bf16[4,32,2048]{2,1,0:T(8,128)(2,1)}, bf16[4,32,2048]{2,1,0:T(8,128)(2,1)}, u32[]{:S(2)}, u32[]{:S(2)}) collective-permute-start(bf16[4,32,2048]{2,1,0:T(8,128)(2,1)} %get-tuple-element.506), channel_id=1, source_target_pairs={{0,2},{1,3},{2,0},{3,1},{4,6},{5,7},{6,4},{7,5},{8,10},{9,11},{10,... | collective-permute-start | bytes 1572872 | tf_op jit(solution)/shard_map/ppermute | solution.py:56
  406.5 21.6 %collective-permute-start.48 = (f32[1,64,1024]{2,1,0:T(8,128)}, f32[1,64,1024]{2,1,0:T(8,128)}, u32[]{:S(2)}, u32[]{:S(2)}) collective-permute-start(f32[1,64,1024]{2,1,0:T(8,128)} %get-tuple-element.505), channel_id=1, source_target_pairs={{0,8},{1,9},{2,10},{3,11},{4,12},{5,13},{6,14},{7,15},{8,0},{9,1},... | collective-permute-start | bytes 786440 | tf_op jit(solution)/shard_map/ppermute | solution.py:56
  431.0 25.2 %collective-permute-start.51 = (bf16[16,32,2048]{2,1,0:T(8,128)(2,1)S(1)}, bf16[16,32,2048]{2,1,0:T(8,128)(2,1)S(1)}, u32[]{:S(2)}, u32[]{:S(2)}) collective-permute-start(bf16[16,32,2048]{2,1,0:T(8,128)(2,1)S(1)} %get-tuple-element.517), channel_id=1, source_target_pairs={{0,16},{1,17},{2,18},{3,19},{4,20},{5,21},{6,22},{7,23},{8,9},{9,8... | collective-permute-start | bytes 6291464 | tf_op jit(solution)/shard_map/ppermute | solution.py:56
  431.2 19.9 %collective-permute-start.50 = (bf16[2,32,2048]{2,1,0:T(8,128)(2,1)S(1)}, bf16[2,32,2048]{2,1,0:T(8,128)(2,1)S(1)}, u32[]{:S(2)}, u32[]{:S(2)}) collective-permute-start(bf16[2,32,2048]{2,1,0:T(8,128)(2,1)S(1)} %get-tuple-element.516), channel_id=1, source_target_pairs={{0,4},{1,5},{2,6},{3,7},{4,0},{5,1},{6,2},{7,3},{8,12},{9,13},{10,... | collective-permute-start | bytes 786440 | tf_op jit(solution)/shard_map/ppermute | solution.py:56
  484.7 25.5 %collective-permute-start.57 = (bf16[16,32,2048]{2,1,0:T(8,128)(2,1)}, bf16[16,32,2048]{2,1,0:T(8,128)(2,1)}, u32[]{:S(2)}, u32[]{:S(2)}) collective-permute-start(bf16[16,32,2048]{2,1,0:T(8,128)(2,1)} %get-tuple-element.544), channel_id=1, source_target_pairs={{0,16},{1,17},{2,18},{3,19},{4,20},{5,21},{6,22},{7,23},{8,9},{9,8... | collective-permute-start | bytes 6291464 | tf_op jit(solution)/shard_map/ppermute | solution.py:56
  486.8 19.5 %collective-permute-start.56 = (bf16[4,32,2048]{2,1,0:T(8,128)(2,1)}, bf16[4,32,2048]{2,1,0:T(8,128)(2,1)S(1)}, u32[]{:S(2)}, u32[]{:S(2)}) collective-permute-start(bf16[4,32,2048]{2,1,0:T(8,128)(2,1)} %copy-done.110), channel_id=1, source_target_pairs={{0,2},{1,3},{2,0},{3,1},{4,6},{5,7},{6,4},{7,5},{8,10},{9,11},{10,... | collective-permute-start | bytes 1572872 | tf_op jit(solution)/shard_map/ppermute | solution.py:56
  (185 other events, 1685.5 us)

commit v9 on v8

--- a/solution.py
+++ b/solution.py
@@ -545,7 +545,7 @@
         hidden3_body, (rows // 256,), scalars,
         [*[rows_of(y) for y in actives], *[whole(w) for w in halves], rows_of(x), whole(bias),
          rows_of(mask)],
-        [((rows, width), bf16, (256, width), lambda i, ref: (i, 0))], margin=30,
+        [((rows, width), bf16, (256, width), lambda i, ref: (i, 0))], margin=40,
     )
     return out
 
@@ -590,7 +590,7 @@
          rows_of(x), (added, (1, 1, width), added_at), whole(gain[None]), rows_of(rest)],
         [((rows, width), dtype, (step, width), lambda i, ref: (i, 0)),
          ((rows // step, 3, width), f32, (1, 3, width), lambda i, ref: (i, 0, 0))],
-        margin=30 if dtype == f32 or cols > 3 * BLOCK else 6,
+        margin=42 if dtype == f32 else 30 if cols > 3 * BLOCK else 6,
     )
 
 

time: 582 us -> 579 us (level)
    unnamed x294 -> x272, local copies, waits for them, and re-layouts: 30.5 us -> 27.2 us
  transfers between devices with their start and end apart: 72 -> 72, of which waited for: 32 -> 31; matrix products, arithmetic and copies ran while one was open for 6% -> 8% of each run, Pallas kernels for 42% -> 43%
where the time goes in v9:
time: 579 us; the launch traced here: 573 us
  Pallas kernels  298 us (51%)
  waiting for transfers between devices  128 us (22%)
  starting transfers between devices  63.2 us (11%)
  local copies, waits for them, and re-layouts  57.9 us (10%)
  other arithmetic  21.7 us (4%)
    pallas_call x24, Pallas kernels, dense(): pl.pallas_call(body, grid_spec=pltpu.PrefetchScalarGridSpec(num_scalar_pr...  159 us
    ppermute x60, waiting for transfers between devices, flip(): return lax.ppermute(value, AXES, moves)  91.2 us
    ppermute x60, starting transfers between devices, flip(): return lax.ppermute(value, AXES, moves)  52.4 us
    pallas_call x6, Pallas kernels, run_attention(): pl.pallas_call(body, grid=(grid,), in_specs=[pl.BlockSpec(memory_space=pl...  52.3 us
    ppermute x12, waiting for transfers between devices, tm_flip(): return lax.ppermute(value, AXES, moves)  36.8 us
    pallas_call x25, Pallas kernels, merge(): pl.pallas_call(merge_body, grid=(n // block,), in_specs=[pl.BlockSpec(mem...  33.7 us
    pallas_call x2, Pallas kernels, up_project(): pl.pallas_call(up_body, grid=(cols // block,), in_specs=[pl.BlockSpec((ro...  29.1 us
    unnamed x272, local copies, waits for them, and re-layouts  27.2 us
  transfers between devices with their start and end apart: 72, of which 31 were waited for; matrix products, arithmetic and copies ran while one was open for 8% of the time, Pallas kernels for 43%

profile of v9, /device:TPU:1, one launch (start us, length us, event | category | flops | bytes accessed | tf_op | source)
XLA Modules:
  0.0 573.1 jit_solution(18034301632039602504)
XLA Ops:
  16.6 10.5 %collective-permute-done.2.other_ref = bf16[2,32,2048]{2,1,0:T(8,128)(2,1)S(1)} collective-permute-done((bf16[2,32,2048]{2,1,0:T(8,128)(2,1)S(1)}, bf16[2,32,2048]{2,1,0:T(8,128)(2,1)S(1)}, u32[]{:S(2)}, u32[]{:S(2)}) %collective-permute-start.2) | collective-permute-done | bytes 262176 | tf_op jit(solution)/shard_map/ppermute | solution.py:56
  49.5 6.9 %collective-permute-done.9.other_ref = bf16[4,48,128]{2,1,0:T(8,128)(2,1)S(1)} collective-permute-done((bf16[4,48,128]{2,1,0:T(8,128)(2,1)S(1)}, bf16[4,48,128]{2,1,0:T(8,128)(2,1)S(1)}, u32[]{:S(2)}, u32[]{:S(2)}) %collective-permute-start.9) | collective-permute-done | bytes 49184 | tf_op jit(solution)/shard_map/ppermute | solution.py:56
  119.7 7.4 %shard_map.269 = bf16[4,256,1024]{2,1,0:T(8,128)(2,1)S(1)} custom-call(s32[2]{0:T(128)S(1)} %copy-done.98, bf16[4,256,1536]{2,1,0:T(8,128)(2,1)S(1)} %bitcast.210, bf16[4,256,1536]{2,1,0:T(8,128)(2,1)S(1)} %bitcast.212), custom_call_target="tpu_custom_call" | custom-call | tf_op jit(solution)/shard_map/pallas_call | solution.py:374
  132.5 12.7 %collective-permute-done.23.other_ref = bf16[4,32,2048]{2,1,0:T(8,128)(2,1)S(1)} collective-permute-done((bf16[4,32,2048]{2,1,0:T(8,128)(2,1)S(1)}, bf16[4,32,2048]{2,1,0:T(8,128)(2,1)S(1)}, u32[]{:S(2)}, u32[]{:S(2)}) %collective-permute-start.23) | collective-permute-done | bytes 524320 | tf_op jit(solution)/shard_map/ppermute | solution.py:56
  157.6 10.0 %collective-permute-done.25 = bf16[4,64,1024]{2,1,0:T(8,128)(2,1)S(1)} collective-permute-done((bf16[4,64,1024]{2,1,0:T(8,128)(2,1)S(1)}, bf16[4,64,1024]{2,1,0:T(8,128)(2,1)S(1)}, u32[]{:S(2)}, u32[]{:S(2)}) %collective-permute-start.25) | collective-permute-done | bytes 524320 | tf_op jit(solution)/shard_map/ppermute | solution.py:60
  167.6 11.7 %collective-permute-done.26 = bf16[4,64,1024]{2,1,0:T(8,128)(2,1)S(1)} collective-permute-done((bf16[4,64,1024]{2,1,0:T(8,128)(2,1)S(1)}, bf16[4,64,1024]{2,1,0:T(8,128)(2,1)S(1)}, u32[]{:S(2)}, u32[]{:S(2)}) %collective-permute-start.26) | collective-permute-done | bytes 524320 | tf_op jit(solution)/shard_map/ppermute | solution.py:60
  193.4 8.0 %shard_map.278 = bf16[16,64,1024]{2,1,0:T(8,128)(2,1)S(1)} custom-call(s32[2]{0:T(128)S(1)} %pad_add_fusion.8.scalar_ref, bf16[16,64,1536]{2,1,0:T(8,128)(2,1)S(1)} %bitcast.214, bf16[16,64,1536]{2,1,0:T(8,128)(2,1)S(1)} %bitcast.216), custom_call_target="tpu_custom_call" | custom-call | tf_op jit(solution)/shard_map/pallas_call | solution.py:374
  214.4 14.6 %shard_map.282 = (bf16[1024,2048]{1,0:T(8,128)(2,1)S(1)}, bf16[1024,2048]{1,0:T(8,128)(2,1)S(1)}) custom-call(bf16[1024,1024]{1,0:T(8,128)(2,1)S(1)} %get-tuple-element.423.x_ref.refs_0_, bf16[1024,2048]{1,0:T(8,128)(2,1)} %bitcast.59.w_ref.own_ref, f32[1,2048]{1,0:T(1,128)S(1)} %select_n.793.bias_ref), custom_call_target="tpu_custom_call" | custom-call | tf_op jit(solution)/shard_map/pallas_call | solution.py:704
  238.5 14.5 %shard_map.284 = (bf16[1024,2048]{1,0:T(8,128)(2,1)S(1)}, bf16[1024,2048]{1,0:T(8,128)(2,1)S(1)}) custom-call(bf16[1024,1024]{1,0:T(8,128)(2,1)S(1)} %copy-done.15, bf16[1024,2048]{1,0:T(8,128)(2,1)} %bitcast.60.w_ref.other_ref, f32[1,2048]{1,0:T(1,128)S(1)} %select_n.795.bias_ref), custom_call_target="tpu_custom_call" | custom-call | tf_op jit(solution)/shard_map/pallas_call | solution.py:704
  283.6 7.4 %shard_map.290 = (bf16[16,64,1024]{2,1,0:T(8,128)(2,1)}, bf16[16,64,1024]{2,1,0:T(8,128)(2,1)S(1)}) custom-call(s32[3]{0:T(128)S(1)} %pad_add_fusion.13.info_ref, bf16[1024,2048]{1,0:T(8,128)(2,1)S(1)} %copy-done.39, bf16[1024,1024]{1,0:T(8,128)(2,1)S(1)} %bitcast_select_fusion.y_ref.x_ref.refs_1_.rest_ref, ...), custom_call_target="tpu_custom_call" | custom-call | tf_op jit(solution)/shard_map/pallas_call | solution.py:442
  295.0 15.1 %shard_map.291 = bf16[1024,1024]{1,0:T(8,128)(2,1)} custom-call(s32[1]{0:T(128)} %bitcast.3._.core_ref, bf16[1024,2048]{1,0:T(8,128)(2,1)} %copy-done.38, bf16[1024,2048]{1,0:T(8,128)(2,1)} %copy-done.41, bf16[2048,1024]{1,0:T(8,128)(2,1)} %bitcast.199, bf16[2048,1024]{1,0:T(8,128)(2,1)} %bitcast.233, f32[1024,1024]{1,0:T(8,128)} %copy-done.43, ...), custom_call_target="tpu_custom_call" | custom-call | tf_op jit(solution)/shard_map/pallas_call | solution.py:442
  312.3 8.7 %shard_map.292 = (bf16[16,32,2048]{2,1,0:T(8,128)(2,1)}, bf16[16,32,2048]{2,1,0:T(8,128)(2,1)S(1)}) custom-call(s32[3]{0:T(128)S(1)} %pad_add_fusion.13.info_ref, bf16[1024,1024]{1,0:T(8,128)(2,1)S(1)} %copy-done.16, bf16[1024,2048]{1,0:T(8,128)(2,1)S(1)} %copy-done.37, bf16[32,32,2048]{2,1,0:T(8,128)(2,1)} %collective-permute-done.36.refs_2_), custom_call_target="tpu_custom_call" | custom-call | tf_op jit(solution)/shard_map/pallas_call | solution.py:442
  328.2 16.5 %shard_map.294 = (bf16[1024,1024]{1,0:T(8,128)(2,1)S(1)}, f32[4,3,1024]{2,1,0:T(4,128)S(1)}) custom-call(s32[1]{0:T(128)} %bitcast.3._.core_ref, bf16[1024,2048]{1,0:T(8,128)(2,1)} %copy-done.36, bf16[1024,2048]{1,0:T(8,128)(2,1)} %copy-done.40, bf16[1024,2048]{1,0:T(8,128)(2,1)} %bitcast.59.w_ref.own_ref, bf16[1024,2048]{1,0:T(8,128)(2,1)} %bitcast.60.w_ref.other_ref, ...), custom_call_target="tpu_custom_call" | custom-call | tf_op jit(solution)/shard_map/pallas_call | solution.py:442
  347.8 9.4 %shard_map.296 = bf16[16,64,1536]{2,1,0:T(8,128)(2,1)S(1)} custom-call(s32[2]{0:T(128)S(1)} %copy-done.101, bf16[16,64,1536]{2,1,0:T(8,128)(2,1)S(1)} %bitcast.217, bf16[16,64,1024]{2,1,0:T(8,128)(2,1)S(1)} %bitcast.227), custom_call_target="tpu_custom_call" | custom-call | tf_op jit(solution)/shard_map/pallas_call | solution.py:374
  372.3 9.4 %shard_map.299 = bf16[16,64,1536]{2,1,0:T(8,128)(2,1)S(1)} custom-call(s32[2]{0:T(128)S(1)} %copy-done.101, bf16[16,64,1536]{2,1,0:T(8,128)(2,1)S(1)} %bitcast.215, bf16[16,64,1024]{2,1,0:T(8,128)(2,1)S(1)} %bitcast.228), custom_call_target="tpu_custom_call" | custom-call | tf_op jit(solution)/shard_map/pallas_call | solution.py:374
  385.4 9.9 %shard_map.303 = (bf16[1024,1024]{1,0:T(8,128)(2,1)S(1)}, f32[4,3,1024]{2,1,0:T(4,128)S(1)}) custom-call(s32[1]{0:T(128)} %bitcast.3._.core_ref, bf16[1024,1536]{1,0:T(8,128)(2,1)S(1)} %bitcast.206, bf16[1024,1536]{1,0:T(8,128)(2,1)S(1)} %bitcast.209, bf16[1024,2048]{1,0:T(8,128)(2,1)S(1)} %bitcast.181, bf16[1024,2048]{1,0:T(8,128)(2,1)S(1)} %bitcast.185, ...), custom_call_target="tpu_custom_call" | custom-call | tf_op jit(solution)/shard_map/pallas_call | solution.py:442
  414.2 7.1 %shard_map.304 = (bf16[16,32,2048]{2,1,0:T(8,128)(2,1)S(1)}, bf16[16,32,2048]{2,1,0:T(8,128)(2,1)S(1)}) custom-call(s32[3]{0:T(128)S(1)} %pad_add_fusion.13.info_ref, bf16[1024,1024]{1,0:T(8,128)(2,1)S(1)} %bitcast.193, bf16[1024,1536]{1,0:T(8,128)(2,1)S(1)} %bitcast.207, bf16[32,32,1536]{2,1,0:T(8,128)(2,1)S(1)} %copy-done.47, ...), custom_call_target="tpu_custom_call" | custom-call | tf_op jit(solution)/shard_map/pallas_call | solution.py:442
  421.3 8.0 %collective-permute-done.47 = bf16[4,64,1024]{2,1,0:T(8,128)(2,1)} collective-permute-done((bf16[4,64,1024]{2,1,0:T(8,128)(2,1)}, bf16[4,64,1024]{2,1,0:T(8,128)(2,1)}, u32[]{:S(2)}, u32[]{:S(2)}) %collective-permute-start.47) | collective-permute-done | bytes 524320 | tf_op jit(solution)/shard_map/ppermute | solution.py:60
  439.7 9.0 %shard_map.309 = bf16[4,256,1536]{2,1,0:T(8,128)(2,1)S(1)} custom-call(s32[2]{0:T(128)S(1)} %copy-done.99, bf16[4,256,1536]{2,1,0:T(8,128)(2,1)S(1)} %bitcast.213, bf16[4,256,1024]{2,1,0:T(8,128)(2,1)S(1)} %bitcast.225), custom_call_target="tpu_custom_call" | custom-call | tf_op jit(solution)/shard_map/pallas_call | solution.py:374
  462.4 9.1 %shard_map.314 = bf16[4,256,1536]{2,1,0:T(8,128)(2,1)S(1)} custom-call(s32[2]{0:T(128)S(1)} %copy-done.99, bf16[4,256,1536]{2,1,0:T(8,128)(2,1)S(1)} %bitcast.211, bf16[4,256,1024]{2,1,0:T(8,128)(2,1)S(1)} %bitcast.226), custom_call_target="tpu_custom_call" | custom-call | tf_op jit(solution)/shard_map/pallas_call | solution.py:374
  476.8 7.9 %shard_map.316 = (bf16[16,32,2048]{2,1,0:T(8,128)(2,1)}, bf16[16,32,2048]{2,1,0:T(8,128)(2,1)S(1)}) custom-call(s32[3]{0:T(128)S(1)} %copy-done.93, bf16[1024,1024]{1,0:T(8,128)(2,1)S(1)} %bitcast.189, bf16[1024,1536]{1,0:T(8,128)(2,1)S(1)} %bitcast.220, bf16[32,32,1536]{2,1,0:T(8,128)(2,1)S(1)} %collective-permute-done.54.refs_2_, ...), custom_call_target="tpu_custom_call" | custom-call | tf_op jit(solution)/shard_map/pallas_call | solution.py:442
  492.7 13.9 %shard_map.317 = (f32[1024,1024]{1,0:T(8,128)}, f32[4,3,1024]{2,1,0:T(4,128)}) custom-call(s32[1]{0:T(128)} %bitcast.3._.core_ref, bf16[1024,1536]{1,0:T(8,128)(2,1)} %bitcast.221, bf16[1024,1536]{1,0:T(8,128)(2,1)} %bitcast.219, bf16[1024,2048]{1,0:T(8,128)(2,1)} %bitcast.38.w_ref.own_ref, bf16[1024,2048]{1,0:T(8,128)(2,1)} %bitcast.40.w_ref.other_ref, ...), custom_call_target="tpu_custom_call" | custom-call | tf_op jit(solution)/shard_map/pallas_call | solution.py:442
  537.2 8.1 %collective-permute-done.64 = f32[19,128]{1,0:T(8,128)S(1)} collective-permute-done((f32[19,128]{1,0:T(8,128)S(1)}, f32[19,128]{1,0:T(8,128)S(1)}, u32[]{:S(2)}, u32[]{:S(2)}) %collective-permute-start.64) | collective-permute-done | bytes 9760 | tf_op jit(solution)/shard_map/ppermute | solution.py:56
  556.0 9.5 %collective-permute-done.67.b_ref = bf16[2,32,2048]{2,1,0:T(8,128)(2,1)S(1)} collective-permute-done((bf16[2,32,2048]{2,1,0:T(8,128)(2,1)S(1)}, bf16[2,32,2048]{2,1,0:T(8,128)(2,1)S(1)}, u32[]{:S(2)}, u32[]{:S(2)}) %collective-permute-start.67) | collective-permute-done | bytes 262176 | tf_op jit(solution)/shard_map/ppermute | solution.py:56
  (597 shorter events, 324.1 us)
Async XLA Ops:
  10.6 21.7 %collective-permute-start.3 = (bf16[4,64,1024]{2,1,0:T(8,128)(2,1)}, bf16[4,64,1024]{2,1,0:T(8,128)(2,1)}, u32[]{:S(2)}, u32[]{:S(2)}) collective-permute-start(bf16[4,64,1024]{2,1,0:T(8,128)(2,1)} %get-tuple-element.661), channel_id=1, source_target_pairs={{0,8},{1,9},{2,10},{3,11},{4,12},{5,13},{6,14},{7,15},{8,0},{9,1},... | collective-permute-start | bytes 1572872 | tf_op jit(solution)/shard_map/ppermute | solution.py:60
  11.2 21.1 %collective-permute-start.4 = (bf16[4,64,1024]{2,1,0:T(8,128)(2,1)}, bf16[4,64,1024]{2,1,0:T(8,128)(2,1)}, u32[]{:S(2)}, u32[]{:S(2)}) collective-permute-start(bf16[4,64,1024]{2,1,0:T(8,128)(2,1)} %get-tuple-element.660), channel_id=1, source_target_pairs={{0,16},{1,17},{2,18},{3,19},{4,20},{5,21},{6,22},{7,23},{8,24},{9,... | collective-permute-start | bytes 1572872 | tf_op jit(solution)/shard_map/ppermute | solution.py:60
  12.5 24.1 %collective-permute-start.5 = (bf16[4,64,1024]{2,1,0:T(8,128)(2,1)}, bf16[4,64,1024]{2,1,0:T(8,128)(2,1)}, u32[]{:S(2)}, u32[]{:S(2)}) collective-permute-start(bf16[4,64,1024]{2,1,0:T(8,128)(2,1)} %get-tuple-element.659), channel_id=1, source_target_pairs={{0,24},{1,25},{2,26},{3,27},{4,28},{5,29},{6,30},{7,31},{8,16},{9,... | collective-permute-start | bytes 1572872 | tf_op jit(solution)/shard_map/ppermute | solution.py:60
  62.7 28.3 %collective-permute-start.15 = (bf16[16,32,2048]{2,1,0:T(8,128)(2,1)}, bf16[16,32,2048]{2,1,0:T(8,128)(2,1)}, u32[]{:S(2)}, u32[]{:S(2)}) collective-permute-start(bf16[16,32,2048]{2,1,0:T(8,128)(2,1)} %shard_map.256.mine_ref), channel_id=1, source_target_pairs={{0,16},{1,17},{2,18},{3,19},{4,20},{5,21},{6,22},{7,23},{8,9},{9,8... | collective-permute-start | bytes 6291464 | tf_op jit(solution)/shard_map/ppermute | solution.py:56
  118.2 27.0 %collective-permute-start.22 = (bf16[16,32,2048]{2,1,0:T(8,128)(2,1)S(1)}, bf16[16,32,2048]{2,1,0:T(8,128)(2,1)S(1)}, u32[]{:S(2)}, u32[]{:S(2)}) collective-permute-start(bf16[16,32,2048]{2,1,0:T(8,128)(2,1)S(1)} %shard_map.267.mine_ref), channel_id=1, source_target_pairs={{0,16},{1,17},{2,18},{3,19},{4,20},{5,21},{6,22},{7,23},{8,9},{9,8... | collective-permute-start | bytes 6291464 | tf_op jit(solution)/shard_map/ppermute | solution.py:56
  119.7 25.5 %collective-permute-start.23 = (bf16[4,32,2048]{2,1,0:T(8,128)(2,1)S(1)}, bf16[4,32,2048]{2,1,0:T(8,128)(2,1)S(1)}, u32[]{:S(2)}, u32[]{:S(2)}) collective-permute-start(bf16[4,32,2048]{2,1,0:T(8,128)(2,1)S(1)} %shard_map.268.mine_ref), channel_id=1, source_target_pairs={{0,4},{1,5},{2,6},{3,7},{4,0},{5,1},{6,2},{7,3},{8,12},{9,13},{10,... | collective-permute-start | bytes 1572872 | tf_op jit(solution)/shard_map/ppermute | solution.py:56
  153.7 25.7 %collective-permute-start.27 = (bf16[32,32,2048]{2,1,0:T(8,128)(2,1)S(1)}, bf16[32,32,2048]{2,1,0:T(8,128)(2,1)S(1)}, u32[]{:S(2)}, u32[]{:S(2)}) collective-permute-start(bf16[32,32,2048]{2,1,0:T(8,128)(2,1)S(1)} %shard_map.271), channel_id=1, source_target_pairs={{0,8},{1,9},{2,10},{3,11},{4,12},{5,13},{6,14},{7,15},{8,0},{9,1},... | collective-permute-start | bytes 12582920 | tf_op jit(solution)/shard_map/ppermute | solution.py:56
  154.1 25.2 %collective-permute-start.28 = (bf16[8,32,2048]{2,1,0:T(8,128)(2,1)S(1)}, bf16[8,32,2048]{2,1,0:T(8,128)(2,1)S(1)}, u32[]{:S(2)}, u32[]{:S(2)}) collective-permute-start(bf16[8,32,2048]{2,1,0:T(8,128)(2,1)S(1)} %shard_map.272.mine_ref), channel_id=1, source_target_pairs={{0,2},{1,3},{2,0},{3,1},{4,6},{5,7},{6,4},{7,5},{8,10},{9,11},{10,... | collective-permute-start | bytes 3145736 | tf_op jit(solution)/shard_map/ppermute | solution.py:56
  155.3 24.1 %collective-permute-start.26 = (bf16[4,64,1024]{2,1,0:T(8,128)(2,1)S(1)}, bf16[4,64,1024]{2,1,0:T(8,128)(2,1)S(1)}, u32[]{:S(2)}, u32[]{:S(2)}) collective-permute-start(bf16[4,64,1024]{2,1,0:T(8,128)(2,1)S(1)} %copy-done.110), channel_id=1, source_target_pairs={{0,24},{1,25},{2,26},{3,27},{4,28},{5,29},{6,30},{7,31},{8,16},{9,... | collective-permute-start | bytes 1572872 | tf_op jit(solution)/shard_map/ppermute | solution.py:60
  183.5 25.2 %collective-permute-start.29 = (bf16[16,32,2048]{2,1,0:T(8,128)(2,1)S(1)}, bf16[16,32,2048]{2,1,0:T(8,128)(2,1)S(1)}, u32[]{:S(2)}, u32[]{:S(2)}) collective-permute-start(bf16[16,32,2048]{2,1,0:T(8,128)(2,1)S(1)} %shard_map.274.mine_ref), channel_id=1, source_target_pairs={{0,16},{1,17},{2,18},{3,19},{4,20},{5,21},{6,22},{7,23},{8,9},{9,8... | collective-permute-start | bytes 6291464 | tf_op jit(solution)/shard_map/ppermute | solution.py:56
  183.7 22.7 %collective-permute-start.30 = (bf16[4,64,1024]{2,1,0:T(8,128)(2,1)S(1)}, bf16[4,64,1024]{2,1,0:T(8,128)(2,1)S(1)}, u32[]{:S(2)}, u32[]{:S(2)}) collective-permute-start(bf16[4,64,1024]{2,1,0:T(8,128)(2,1)S(1)} %shard_map.275.mine_ref), channel_id=1, source_target_pairs={{0,2},{1,3},{2,0},{3,1},{4,6},{5,7},{6,4},{7,5},{8,10},{9,11},{10,... | collective-permute-start | bytes 1572872 | tf_op jit(solution)/shard_map/ppermute | solution.py:56
  212.6 24.4 %collective-permute-start.32 = (bf16[32,32,2048]{2,1,0:T(8,128)(2,1)}, bf16[32,32,2048]{2,1,0:T(8,128)(2,1)}, u32[]{:S(2)}, u32[]{:S(2)}) collective-permute-start(bf16[32,32,2048]{2,1,0:T(8,128)(2,1)} %shard_map.280), channel_id=1, source_target_pairs={{0,8},{1,9},{2,10},{3,11},{4,12},{5,13},{6,14},{7,15},{8,0},{9,1},... | collective-permute-start | bytes 12582920 | tf_op jit(solution)/shard_map/ppermute | solution.py:56
  234.4 25.5 %collective-permute-start.33 = (bf16[16,64,1024]{2,1,0:T(8,128)(2,1)}, bf16[16,64,1024]{2,1,0:T(8,128)(2,1)}, u32[]{:S(2)}, u32[]{:S(2)}) collective-permute-start(bf16[16,64,1024]{2,1,0:T(8,128)(2,1)} %shard_map.283.mine_ref), channel_id=1, source_target_pairs={{0,16},{1,17},{2,18},{3,19},{4,20},{5,21},{6,22},{7,23},{8,9},{9,8... | collective-permute-start | bytes 6291464 | tf_op jit(solution)/shard_map/ppermute | solution.py:56
  263.6 19.5 %collective-permute-start.35 = (bf16[32,64,1024]{2,1,0:T(8,128)(2,1)S(1)}, bf16[32,64,1024]{2,1,0:T(8,128)(2,1)S(1)}, u32[]{:S(2)}, u32[]{:S(2)}) collective-permute-start(bf16[32,64,1024]{2,1,0:T(8,128)(2,1)S(1)} %shard_map.285), channel_id=1, source_target_pairs={{0,8},{1,9},{2,10},{3,11},{4,12},{5,13},{6,14},{7,15},{8,0},{9,1},... | collective-permute-start | bytes 12582920 | tf_op jit(solution)/shard_map/ppermute | solution.py:56
  283.1 27.0 %collective-permute-start.36 = (bf16[32,32,2048]{2,1,0:T(8,128)(2,1)}, bf16[32,32,2048]{2,1,0:T(8,128)(2,1)}, u32[]{:S(2)}, u32[]{:S(2)}) collective-permute-start(bf16[32,32,2048]{2,1,0:T(8,128)(2,1)} %shard_map.289), channel_id=1, source_target_pairs={{0,8},{1,9},{2,10},{3,11},{4,12},{5,13},{6,14},{7,15},{8,0},{9,1},... | collective-permute-start | bytes 12582920 | tf_op jit(solution)/shard_map/ppermute | solution.py:56
  292.3 28.7 %collective-permute-start.37 = (bf16[16,64,1024]{2,1,0:T(8,128)(2,1)}, bf16[16,64,1024]{2,1,0:T(8,128)(2,1)}, u32[]{:S(2)}, u32[]{:S(2)}) collective-permute-start(bf16[16,64,1024]{2,1,0:T(8,128)(2,1)} %get-tuple-element.451), channel_id=1, source_target_pairs={{0,16},{1,17},{2,18},{3,19},{4,20},{5,21},{6,22},{7,23},{8,9},{9,8... | collective-permute-start | bytes 6291464 | tf_op jit(solution)/shard_map/ppermute | solution.py:56
  324.3 36.7 %collective-permute-start.39 = (bf16[16,32,2048]{2,1,0:T(8,128)(2,1)}, bf16[16,32,2048]{2,1,0:T(8,128)(2,1)}, u32[]{:S(2)}, u32[]{:S(2)}) collective-permute-start(bf16[16,32,2048]{2,1,0:T(8,128)(2,1)} %get-tuple-element.464), channel_id=1, source_target_pairs={{0,16},{1,17},{2,18},{3,19},{4,20},{5,21},{6,22},{7,23},{8,9},{9,8... | collective-permute-start | bytes 6291464 | tf_op jit(solution)/shard_map/ppermute | solution.py:56
  324.4 32.8 %collective-permute-start.38 = (bf16[8,64,1024]{2,1,0:T(8,128)(2,1)}, bf16[8,64,1024]{2,1,0:T(8,128)(2,1)}, u32[]{:S(2)}, u32[]{:S(2)}) collective-permute-start(bf16[8,64,1024]{2,1,0:T(8,128)(2,1)} %get-tuple-element.463), channel_id=1, source_target_pairs={{0,1},{1,0},{2,3},{3,2},{4,5},{5,4},{6,7},{7,6},{8,24},{9,25},{10,... | collective-permute-start | bytes 3145736 | tf_op jit(solution)/shard_map/ppermute | solution.py:56
  404.7 24.6 %collective-permute-start.47 = (bf16[4,64,1024]{2,1,0:T(8,128)(2,1)}, bf16[4,64,1024]{2,1,0:T(8,128)(2,1)}, u32[]{:S(2)}, u32[]{:S(2)}) collective-permute-start(bf16[4,64,1024]{2,1,0:T(8,128)(2,1)} %bitcast.72), channel_id=1, source_target_pairs={{0,24},{1,25},{2,26},{3,27},{4,28},{5,29},{6,30},{7,31},{8,16},{9,... | collective-permute-start | bytes 1572872 | tf_op jit(solution)/shard_map/ppermute | solution.py:60
  407.0 22.3 %collective-permute-start.49 = (bf16[4,32,2048]{2,1,0:T(8,128)(2,1)}, bf16[4,32,2048]{2,1,0:T(8,128)(2,1)}, u32[]{:S(2)}, u32[]{:S(2)}) collective-permute-start(bf16[4,32,2048]{2,1,0:T(8,128)(2,1)} %get-tuple-element.506), channel_id=1, source_target_pairs={{0,2},{1,3},{2,0},{3,1},{4,6},{5,7},{6,4},{7,5},{8,10},{9,11},{10,... | collective-permute-start | bytes 1572872 | tf_op jit(solution)/shard_map/ppermute | solution.py:56
  407.0 22.3 %collective-permute-start.48 = (f32[1,64,1024]{2,1,0:T(8,128)}, f32[1,64,1024]{2,1,0:T(8,128)}, u32[]{:S(2)}, u32[]{:S(2)}) collective-permute-start(f32[1,64,1024]{2,1,0:T(8,128)} %get-tuple-element.505), channel_id=1, source_target_pairs={{0,8},{1,9},{2,10},{3,11},{4,12},{5,13},{6,14},{7,15},{8,0},{9,1},... | collective-permute-start | bytes 786440 | tf_op jit(solution)/shard_map/ppermute | solution.py:56
  432.2 25.2 %collective-permute-start.51 = (bf16[16,32,2048]{2,1,0:T(8,128)(2,1)S(1)}, bf16[16,32,2048]{2,1,0:T(8,128)(2,1)S(1)}, u32[]{:S(2)}, u32[]{:S(2)}) collective-permute-start(bf16[16,32,2048]{2,1,0:T(8,128)(2,1)S(1)} %get-tuple-element.517), channel_id=1, source_target_pairs={{0,16},{1,17},{2,18},{3,19},{4,20},{5,21},{6,22},{7,23},{8,9},{9,8... | collective-permute-start | bytes 6291464 | tf_op jit(solution)/shard_map/ppermute | solution.py:56
  432.4 20.7 %collective-permute-start.50 = (bf16[2,32,2048]{2,1,0:T(8,128)(2,1)S(1)}, bf16[2,32,2048]{2,1,0:T(8,128)(2,1)S(1)}, u32[]{:S(2)}, u32[]{:S(2)}) collective-permute-start(bf16[2,32,2048]{2,1,0:T(8,128)(2,1)S(1)} %get-tuple-element.516), channel_id=1, source_target_pairs={{0,4},{1,5},{2,6},{3,7},{4,0},{5,1},{6,2},{7,3},{8,12},{9,13},{10,... | collective-permute-start | bytes 786440 | tf_op jit(solution)/shard_map/ppermute | solution.py:56
  486.0 25.4 %collective-permute-start.57 = (bf16[16,32,2048]{2,1,0:T(8,128)(2,1)}, bf16[16,32,2048]{2,1,0:T(8,128)(2,1)S(1)}, u32[]{:S(2)}, u32[]{:S(2)}) collective-permute-start(bf16[16,32,2048]{2,1,0:T(8,128)(2,1)} %get-tuple-element.544), channel_id=1, source_target_pairs={{0,16},{1,17},{2,18},{3,19},{4,20},{5,21},{6,22},{7,23},{8,9},{9,8... | collective-permute-start | bytes 6291464 | tf_op jit(solution)/shard_map/ppermute | solution.py:56
  (174 other events, 1784.5 us)
